TPU v7x, 32 devices: a whole 2x2x4 slice. The times are simulated.
32 devices in a mesh: dp: 2 (over x), context: 8 (over z, core), tensor: 2 (over y).
Axes of the slice: x: 2, y: 2, z: 4, core: 2. Of those that a mesh axis runs over, the one named last changes fastest.
Arguments:
- block_input: bfloat16 [2, 2048, 1600], P('dp', ('context', 'tensor')), may hold values from -6 to 6
- segment_ids: int32 [2, 2048], P('dp'), may hold values from 0 to 7, as said below
- slot_order: int32 [2, 16], P('dp'), may hold values from 0 to 15, as said below
- first_gain: bfloat16 [1600], P(('dp', 'context')), may hold values from 0.5 to 1.5
- first_shift: bfloat16 [1600], P(('dp', 'context')), may hold values from -3 to 3
- qkv_weight: bfloat16 [1600, 4800], P(('dp', 'context')), may hold values from -0.5 to 0.5
- qv_bias: bfloat16 [3200], P(('dp', 'context')), may hold values from -3 to 3
- out_weight: bfloat16 [1600, 1600], P(('dp', 'context')), may hold values from -0.3125 to 0.3125
- out_bias: bfloat16 [1600], P(('dp', 'context')), may hold values from -3 to 3
- second_gain: bfloat16 [1600], P(('dp', 'context')), may hold values from 0.5 to 1.5
- second_shift: bfloat16 [1600], P(('dp', 'context')), may hold values from -3 to 3
- fc_weight: bfloat16 [1600, 6400], P(('dp', 'context'), 'tensor'), may hold values from -0.15625 to 0.15625
- fc_bias: bfloat16 [6400], P('tensor'), may hold values from -3 to 3
- proj_weight: bfloat16 [6400, 1600], P('tensor', ('dp', 'context')), may hold values from -0.078125 to 0.078125
- proj_bias: bfloat16 [1600], P(('dp', 'context')), may hold values from -3 to 3
- out_grad: bfloat16 [2, 2048, 1600], P('dp', ('context', 'tensor')), may hold values from -6 to 6
Outputs:
- block_output: float32 [2, 2048, 1600], P('dp', ('context', 'tensor'))
- input_grad: float32 [2, 2048, 1600], P('dp', ('context', 'tensor'))
- qkv_weight_grad: float32 [1600, 4800], P(('dp', 'context'))
- qv_bias_grad: float32 [3200], P(('dp', 'context'))
- out_weight_grad: float32 [1600, 1600], P(('dp', 'context'))
- out_bias_grad: float32 [1600], P(('dp', 'context'))
- first_gain_grad: float32 [1600], P(('dp', 'context'))
- first_shift_grad: float32 [1600], P(('dp', 'context'))
- second_gain_grad: float32 [1600], P(('dp', 'context'))
- second_shift_grad: float32 [1600], P(('dp', 'context'))
- fc_weight_grad: float32 [1600, 6400], P(('dp', 'context'), 'tensor')
- fc_bias_grad: float32 [6400], P('tensor')
- proj_weight_grad: float32 [6400, 1600], P('tensor', ('dp', 'context'))
- proj_bias_grad: float32 [1600], P(('dp', 'context'))
Inputs may be any that keep to these rules, and one draw needn't show every extreme that they name: `segment_ids`: ids of the 8 documents of a row, not falling along position (not along slot order); every id appears in every row; one document of each row holds half of the row's positions or more, the others share the rest unevenly. `slot_order`: each row is a permutation of the slot numbers.
All inputs are finite; a program needn't handle non-finite values.
Results may differ from a plain program's by a relative error of at most 0.02.
Values may be sent and summed in bfloat16 or wider, within the bound.
A program may use at most 384 MiB of HBM per device.

v0:
```python
import math

import jax
import jax.numpy as jnp
from jax import lax
from jax.sharding import PartitionSpec as P

HEADS = 25


NORM_EPS = 1e-05
GELU_SCALE = 0.7978845608028654
GELU_CUBE = 0.044715
MASK_FLOOR = -1e30


def gelu_parts(values):
    inner_arg = GELU_SCALE * (values + GELU_CUBE * values * values * values)
    tanh_value = jnp.tanh(inner_arg)
    result = 0.5 * values * (1.0 + tanh_value)
    derivative = 0.5 * (1.0 + tanh_value) + 0.5 * values * (
        1.0 - tanh_value * tanh_value
    ) * GELU_SCALE * (1.0 + 3.0 * GELU_CUBE * values * values)
    return (result, derivative)


def norm_forward(values, norm_gain, norm_shift):
    mean_value = jnp.mean(values, axis=-1, keepdims=True)
    centered = values - mean_value
    inv_sigma = lax.rsqrt(jnp.mean(centered * centered, axis=-1, keepdims=True) + NORM_EPS)
    normed = centered * inv_sigma
    return (normed, inv_sigma, normed * norm_gain + norm_shift)


def norm_backward(upstream, normed, inv_sigma, norm_gain):
    scaled = upstream * norm_gain
    return inv_sigma * (
        scaled
        - jnp.mean(scaled, axis=-1, keepdims=True)
        - normed * jnp.mean(scaled * normed, axis=-1, keepdims=True)
    )


def contract(left_side, right_side, left_dim, right_dim):
    return lax.dot_general(
        left_side,
        right_side,
        (((left_dim,), (right_dim,)), ((), ())),
        preferred_element_type=jnp.float32,
    )


def key_places(slot_order, begin_row, length, slot_len):
    positions = begin_row + jnp.arange(length, dtype=jnp.int32)
    slot_ids = positions // slot_len
    within = positions - slot_ids * slot_len
    return jnp.take(slot_order, slot_ids, axis=1) * slot_len + within[None, :]


def permit(query_seg, query_place, key_seg, key_place):
    same_doc = key_seg[:, None, :] == query_seg[:, :, None]
    earlier = key_place[:, None, :] <= query_place[:, :, None]
    return jnp.logical_and(same_doc, earlier)


def block_grads(queries4, grads4, log_part, delta_part, allowed, keys4, values4, scale):
    scores = (
        jnp.einsum("rqhd,rkhd->rhqk", queries4, keys4, preferred_element_type=jnp.float32) * scale
    )
    weights = jnp.where(allowed[:, None], jnp.exp(scores - log_part[..., None]), 0.0)
    dprob = jnp.einsum("rqhd,rkhd->rhqk", grads4, values4, preferred_element_type=jnp.float32)
    dscore = (weights * (dprob - delta_part[..., None]) * scale).astype(jnp.bfloat16)
    dquery = jnp.einsum("rhqk,rkhd->rqhd", dscore, keys4, preferred_element_type=jnp.float32)
    dkey = jnp.einsum("rhqk,rqhd->rkhd", dscore, queries4, preferred_element_type=jnp.float32)
    dvalue = jnp.einsum(
        "rhqk,rqhd->rkhd", weights.astype(jnp.bfloat16), grads4, preferred_element_type=jnp.float32
    )
    return (dquery, dkey, dvalue)


def on_device(
    block_input,
    segment_ids,
    slot_order,
    first_gain,
    first_shift,
    qkv_weight,
    qv_bias,
    out_weight,
    out_bias,
    second_gain,
    second_shift,
    fc_weight,
    fc_bias,
    proj_weight,
    proj_bias,
    out_grad,
):
    gathered = (
        lax.all_gather(qkv_weight, ("dp", "context"), axis=0, tiled=True),
        lax.all_gather(out_weight, ("dp", "context"), axis=0, tiled=True),
        lax.all_gather(fc_weight, ("dp", "context"), axis=0, tiled=True),
        lax.all_gather(proj_weight, ("dp", "context"), axis=1, tiled=True),
        lax.all_gather(qv_bias, ("dp", "context"), axis=0, tiled=True),
        lax.all_gather(out_bias, ("dp", "context"), axis=0, tiled=True),
        lax.all_gather(first_gain, ("dp", "context"), axis=0, tiled=True),
        lax.all_gather(first_shift, ("dp", "context"), axis=0, tiled=True),
        lax.all_gather(second_gain, ("dp", "context"), axis=0, tiled=True),
        lax.all_gather(second_shift, ("dp", "context"), axis=0, tiled=True),
        lax.all_gather(proj_bias, ("dp", "context"), axis=0, tiled=True),
    )
    full_qkv, full_out, full_fc, full_proj = (gathered[0], gathered[1], gathered[2], gathered[3])
    bias_qv, bias_out, gain_one, shift_one, gain_two, shift_two, bias_proj = [
        member.astype(jnp.float32) for member in gathered[4:]
    ]
    bias_fc = fc_bias.astype(jnp.float32)
    row_count, slot_len, features = block_input.shape
    head_count = HEADS
    head_width = features // head_count
    token_count = row_count * slot_len
    scale = 1.0 / math.sqrt(head_width)
    own_begin = lax.axis_index(("context", "tensor")) * slot_len
    own_place = key_places(slot_order, own_begin, slot_len, slot_len)
    own_segment = lax.dynamic_slice_in_dim(segment_ids, own_begin, slot_len, 1)
    input_flat = block_input.reshape(token_count, features).astype(jnp.float32)
    normed_one, inv_one, pre_one = norm_forward(input_flat, gain_one, shift_one)
    norm_one = pre_one.astype(jnp.bfloat16)
    projected = jnp.dot(norm_one, full_qkv, preferred_element_type=jnp.float32)
    queries = (projected[:, :features] + bias_qv[:features]).astype(jnp.bfloat16)
    key_value = (
        jnp.concatenate(
            [
                projected[:, features : 2 * features],
                projected[:, 2 * features :] + bias_qv[features:],
            ],
            axis=1,
        )
        .astype(jnp.bfloat16)
        .reshape(row_count, slot_len, 2 * features)
    )
    own_key_rows = key_value[:, :, :features]
    query_four = queries.reshape(row_count, slot_len, head_count, head_width)
    own_keys = own_key_rows.reshape(row_count, slot_len, head_count, head_width)
    own_values = key_value[:, :, features:].reshape(row_count, slot_len, head_count, head_width)

    def block_allowed(offset, block_len):
        key_segment = lax.dynamic_slice_in_dim(segment_ids, offset, block_len, 1)
        return permit(
            own_segment, own_place, key_segment, key_places(slot_order, offset, block_len, slot_len)
        )

    start_stats = (
        jnp.full((row_count, head_count, slot_len), MASK_FLOOR, jnp.float32),
        jnp.zeros((row_count, head_count, slot_len), jnp.float32),
    )
    carried = start_stats
    piece = lax.all_gather(own_key_rows, ("context", "tensor"), axis=1, tiled=True)
    piece_len = piece.shape[1]
    block_len = math.gcd(piece_len, 1024)

    def stats_one_block(running, block_index):
        running_max, running_sum = running
        offset = block_index * block_len
        keys4 = lax.dynamic_slice_in_dim(piece, offset, block_len, 1).reshape(
            row_count, block_len, head_count, head_width
        )
        allowed = block_allowed(offset, block_len)
        scores = (
            jnp.einsum("rqhd,rkhd->rhqk", query_four, keys4, preferred_element_type=jnp.float32)
            * scale
        )
        scores = jnp.where(allowed[:, None], scores, MASK_FLOOR)
        new_max = jnp.maximum(running_max, jnp.max(scores, axis=-1))
        weights = jnp.where(allowed[:, None], jnp.exp(scores - new_max[..., None]), 0.0)
        running_sum = running_sum * jnp.exp(running_max - new_max) + jnp.sum(weights, axis=-1)
        return ((new_max, running_sum), None)

    carried, unused = lax.scan(
        stats_one_block, carried, jnp.arange(piece_len // block_len, dtype=jnp.int32)
    )
    running_max, running_sum = carried
    log_total = running_max + jnp.log(running_sum)
    start_weighted = jnp.zeros((row_count, slot_len, head_count, head_width), jnp.float32)
    weighted = start_weighted
    value_piece = lax.all_gather(key_value, ("context", "tensor"), axis=1, tiled=True)
    piece_len = value_piece.shape[1]
    value_block_len = math.gcd(piece_len, 1024)

    def value_one_block(running, block_index):
        offset = block_index * value_block_len
        kv_block = lax.dynamic_slice_in_dim(value_piece, offset, value_block_len, 1)
        keys4 = kv_block[:, :, :features].reshape(
            row_count, value_block_len, head_count, head_width
        )
        values4 = kv_block[:, :, features:].reshape(
            row_count, value_block_len, head_count, head_width
        )
        allowed = block_allowed(offset, value_block_len)
        scores = (
            jnp.einsum("rqhd,rkhd->rhqk", query_four, keys4, preferred_element_type=jnp.float32)
            * scale
        )
        weights = jnp.where(allowed[:, None], jnp.exp(scores - log_total[..., None]), 0.0).astype(
            jnp.bfloat16
        )
        return (
            running
            + jnp.einsum("rhqk,rkhd->rqhd", weights, values4, preferred_element_type=jnp.float32),
            None,
        )

    weighted, unused = lax.scan(
        value_one_block, weighted, jnp.arange(piece_len // value_block_len, dtype=jnp.int32)
    )
    attention = weighted.astype(jnp.bfloat16).reshape(token_count, features)
    hidden = (
        input_flat + jnp.dot(attention, full_out, preferred_element_type=jnp.float32) + bias_out
    )
    normed_two, inv_two, pre_two = norm_forward(hidden, gain_two, shift_two)
    norm_two = pre_two.astype(jnp.bfloat16)
    paired = lax.all_gather(norm_two, "tensor", axis=0, tiled=True)
    preact = jnp.dot(paired, full_fc, preferred_element_type=jnp.float32) + bias_fc
    activated, derivative = gelu_parts(preact)
    activation = activated.astype(jnp.bfloat16)
    mlp_output = lax.psum_scatter(
        jnp.dot(activation, full_proj, preferred_element_type=jnp.float32).astype(jnp.bfloat16),
        "tensor",
        scatter_dimension=0,
        tiled=True,
    ).astype(jnp.float32)
    block_output = hidden + mlp_output + bias_proj
    grad_flat = out_grad.reshape(token_count, features)
    grad_wide = grad_flat.astype(jnp.float32)
    grad_pair = lax.all_gather(grad_flat, "tensor", axis=0, tiled=True)
    proj_weight_term = contract(activation, grad_pair, 0, 0)
    dpreact = contract(grad_pair, full_proj, 1, 1) * derivative
    fc_bias_term = jnp.sum(dpreact, axis=0)
    dpreact_b = dpreact.astype(jnp.bfloat16)
    fc_weight_term = contract(paired, dpreact_b, 0, 0)
    dnorm_two = lax.psum_scatter(
        contract(dpreact_b, full_fc, 1, 1).astype(jnp.bfloat16),
        "tensor",
        scatter_dimension=0,
        tiled=True,
    ).astype(jnp.float32)
    second_gain_term = jnp.sum(dnorm_two * normed_two, axis=0)
    second_shift_term = jnp.sum(dnorm_two, axis=0)
    proj_bias_term = jnp.sum(grad_wide, axis=0)
    dhidden = grad_wide + norm_backward(dnorm_two, normed_two, inv_two, gain_two)
    out_bias_term = jnp.sum(dhidden, axis=0)
    dhidden_b = dhidden.astype(jnp.bfloat16)
    out_weight_term = contract(attention, dhidden_b, 0, 0)
    dattention = contract(dhidden_b, full_out, 1, 1).astype(jnp.bfloat16)
    dattention_four = dattention.reshape(row_count, slot_len, head_count, head_width)
    delta = jnp.sum(
        dattention_four.astype(jnp.float32)
        * attention.reshape(row_count, slot_len, head_count, head_width).astype(jnp.float32),
        axis=-1,
    )
    delta_heads = jnp.transpose(delta, (0, 2, 1))

    def query_fold(dquery_total, piece):
        piece_len = piece.shape[1]
        block_len = math.gcd(piece_len, 1024)

        def query_one_block(running, block_index):
            offset = block_index * block_len
            kv_block = lax.dynamic_slice_in_dim(piece, offset, block_len, 1)
            allowed = block_allowed(offset, block_len)
            keys4 = kv_block[:, :, :features].reshape(row_count, block_len, head_count, head_width)
            values4 = kv_block[:, :, features:].reshape(
                row_count, block_len, head_count, head_width
            )
            dquery, dkey, dvalue = block_grads(
                query_four, dattention_four, log_total, delta_heads, allowed, keys4, values4, scale
            )
            return (running + dquery, None)

        dquery_total, unused = lax.scan(
            query_one_block, dquery_total, jnp.arange(piece_len // block_len, dtype=jnp.int32)
        )
        return dquery_total

    dquery_start = jnp.zeros((row_count, slot_len, head_count, head_width), jnp.float32)
    dquery_total = query_fold(
        dquery_start, lax.all_gather(key_value, ("context", "tensor"), axis=1, tiled=True)
    )
    log_all, delta_all = (
        lax.all_gather(
            jnp.transpose(log_total, (0, 2, 1)), ("context", "tensor"), axis=1, tiled=True
        ),
        lax.all_gather(delta, ("context", "tensor"), axis=1, tiled=True),
    )
    running = jnp.zeros((row_count, slot_len, 2 * features), jnp.float32)
    query_piece = lax.all_gather(
        queries.reshape(row_count, slot_len, features), ("context", "tensor"), axis=1, tiled=True
    )
    grad_piece = lax.all_gather(
        dattention.reshape(row_count, slot_len, features), ("context", "tensor"), axis=1, tiled=True
    )
    piece_len = query_piece.shape[1]
    owner_block_len = math.gcd(piece_len, 1024)

    def owner_one_block(total_terms, block_index):
        offset = block_index * owner_block_len
        query_block = lax.dynamic_slice_in_dim(query_piece, offset, owner_block_len, 1).reshape(
            row_count, owner_block_len, head_count, head_width
        )
        grad_block = lax.dynamic_slice_in_dim(grad_piece, offset, owner_block_len, 1).reshape(
            row_count, owner_block_len, head_count, head_width
        )
        log_block = jnp.transpose(
            lax.dynamic_slice_in_dim(log_all, offset, owner_block_len, 1), (0, 2, 1)
        )
        delta_block = jnp.transpose(
            lax.dynamic_slice_in_dim(delta_all, offset, owner_block_len, 1), (0, 2, 1)
        )
        query_segment = lax.dynamic_slice_in_dim(segment_ids, offset, owner_block_len, 1)
        allowed = permit(
            query_segment,
            key_places(slot_order, offset, owner_block_len, slot_len),
            own_segment,
            own_place,
        )
        dquery, dkey, dvalue = block_grads(
            query_block, grad_block, log_block, delta_block, allowed, own_keys, own_values, scale
        )
        block_terms = jnp.concatenate(
            [
                dkey.reshape(row_count, slot_len, features),
                dvalue.reshape(row_count, slot_len, features),
            ],
            axis=2,
        )
        return (total_terms + block_terms, None)

    running, unused = lax.scan(
        owner_one_block, running, jnp.arange(piece_len // owner_block_len, dtype=jnp.int32)
    )
    dquery_flat = dquery_total.reshape(token_count, features)
    own_flat = running.reshape(token_count, 2 * features)
    dprojected = jnp.concatenate([dquery_flat, own_flat], axis=1)
    qv_bias_term = jnp.concatenate(
        [jnp.sum(dquery_flat, axis=0), jnp.sum(own_flat[:, features:], axis=0)]
    )
    dprojected_b = dprojected.astype(jnp.bfloat16)
    qkv_weight_term = contract(norm_one, dprojected_b, 0, 0)
    dnorm_one = contract(dprojected_b, full_qkv, 1, 1)
    first_gain_term = jnp.sum(dnorm_one * normed_one, axis=0)
    first_shift_term = jnp.sum(dnorm_one, axis=0)
    input_grad = dhidden + norm_backward(dnorm_one, normed_one, inv_one, gain_one)
    shards = (
        lax.psum_scatter(qkv_weight_term, ("dp", "context"), scatter_dimension=0, tiled=True),
        lax.psum_scatter(out_weight_term, ("dp", "context"), scatter_dimension=0, tiled=True),
        lax.psum_scatter(fc_weight_term, ("dp", "context"), scatter_dimension=0, tiled=True),
        lax.psum_scatter(proj_weight_term, ("dp", "context"), scatter_dimension=1, tiled=True),
        lax.psum_scatter(qv_bias_term, ("dp", "context"), scatter_dimension=0, tiled=True),
        lax.psum_scatter(out_bias_term, ("dp", "context"), scatter_dimension=0, tiled=True),
        lax.psum_scatter(first_gain_term, ("dp", "context"), scatter_dimension=0, tiled=True),
        lax.psum_scatter(first_shift_term, ("dp", "context"), scatter_dimension=0, tiled=True),
        lax.psum_scatter(second_gain_term, ("dp", "context"), scatter_dimension=0, tiled=True),
        lax.psum_scatter(second_shift_term, ("dp", "context"), scatter_dimension=0, tiled=True),
        lax.psum_scatter(proj_bias_term, ("dp", "context"), scatter_dimension=0, tiled=True),
    )
    joined = (
        lax.psum(shards[0].astype(jnp.bfloat16), "tensor").astype(jnp.float32),
        lax.psum(shards[1].astype(jnp.bfloat16), "tensor").astype(jnp.float32),
        lax.psum(shards[4].astype(jnp.bfloat16), "tensor").astype(jnp.float32),
        lax.psum(shards[5].astype(jnp.bfloat16), "tensor").astype(jnp.float32),
        lax.psum(shards[6].astype(jnp.bfloat16), "tensor").astype(jnp.float32),
        lax.psum(shards[7].astype(jnp.bfloat16), "tensor").astype(jnp.float32),
        lax.psum(shards[8].astype(jnp.bfloat16), "tensor").astype(jnp.float32),
        lax.psum(shards[9].astype(jnp.bfloat16), "tensor").astype(jnp.float32),
        lax.psum(shards[10].astype(jnp.bfloat16), "tensor").astype(jnp.float32),
    )
    fc_bias_grad = lax.psum(fc_bias_term, ("dp", "context"))
    return (
        block_output.reshape(row_count, slot_len, features),
        input_grad.reshape(row_count, slot_len, features),
        joined[0],
        joined[2],
        joined[1],
        joined[3],
        joined[4],
        joined[5],
        joined[6],
        joined[7],
        shards[2],
        fc_bias_grad,
        shards[3],
        joined[8],
    )


def solution(mesh):
    placed = (
        P("dp", ("context", "tensor"), None),
        P("dp", None),
        P("dp", None),
        P(("dp", "context")),
        P(("dp", "context")),
        P(("dp", "context"), None),
        P(("dp", "context")),
        P(("dp", "context"), None),
        P(("dp", "context")),
        P(("dp", "context")),
        P(("dp", "context")),
        P(("dp", "context"), "tensor"),
        P("tensor"),
        P("tensor", ("dp", "context")),
        P(("dp", "context")),
        P("dp", ("context", "tensor"), None),
    )
    return jax.shard_map(
        on_device,
        mesh=mesh,
        in_specs=placed,
        out_specs=(
            P("dp", ("context", "tensor"), None),
            P("dp", ("context", "tensor"), None),
            P(("dp", "context"), None),
            P(("dp", "context")),
            P(("dp", "context"), None),
            P(("dp", "context")),
            P(("dp", "context")),
            P(("dp", "context")),
            P(("dp", "context")),
            P(("dp", "context")),
            P(("dp", "context"), "tensor"),
            P("tensor"),
            P("tensor", ("dp", "context")),
            P(("dp", "context")),
        ),
        check_vma=False,
    )
```

profile of v0, /device:TPU:0, one launch (start us, length us, event | category | flops | bytes accessed | tf_op | source)
XLA Modules:
  0.0 2185.7 jit_solution(6737191822778418428)
XLA Ops:
  18.7 65.7 %all-reduce.23 = (bf16[1600]{0:T(1024)(128)(2,1)S(1)}, bf16[1600]{0:T(1024)(128)(2,1)S(1)}, bf16[3200]{0:T(1024)(128)(2,1)S(1)}, bf16[1600]{0:T(1024)(128)(2,1)S...) all-reduce(bf16[1600]{0:T(1024)(128)(2,1)S(1)} %dynamic-update-slic, ...), channel_id=1, replica_groups=mesh['dp'=2,'context'=8,'tensor'=2] {'dp','context'}, use_global_device_ids=true, to_apply=%add.1 | all-reduce | flops 12800 | bytes 51200
  85.8 51.2 %all-gather.26.cloned.1.call-done = bf16[16,100,4800]{2,1,0:T(8,128)(2,1)} async-done(((bf16[1,100,4800]{2,1,0:T(8,128)(2,1)}), bf16[16,100,4800]{2,1,0:T(8,128)(2,1)}) %all-gather.26.cloned.1.call-update) | async-done | bytes 15360016 | tf_op jit(solution)/shard_map/all_gather | solution.py:100
  137.0 16.0 reshape.1578
  153.1 10.5 fusion.93
  178.6 12.6 all-gather.1
  203.2 81.7 %all-gather.30.cloned.1.call-done = bf16[16,100,3200]{2,1,0:T(8,128)(2,1)} async-done(((bf16[1,100,3200]{2,1,0:T(8,128)(2,1)}), bf16[16,100,3200]{2,1,0:T(8,128)(2,1)}) %all-gather.30.cloned.1.call-update) | async-done | bytes 10240016 | tf_op jit(solution)/shard_map/all_gather | solution.py:102
  284.9 10.8 reshape.1582
  295.8 78.4 %all-gather.32.cloned.1.call-done = bf16[16,100,3200]{2,1,0:T(8,128)(2,1)} async-done(((bf16[1,100,3200]{2,1,0:T(8,128)(2,1)}), bf16[16,100,3200]{2,1,0:T(8,128)(2,1)}) %all-gather.32.cloned.1.call-update) | async-done | bytes 10240016 | tf_op jit(solution)/shard_map/all_gather | solution.py:103
  374.1 10.8 reshape.1584
  384.9 56.6 %all-gather.20.cloned.1.call-done = bf16[2048,1600]{0,1:T(8,128)(2,1)} async-done(((bf16[128,1600]{0,1:T(8,128)(2,1)}), bf16[2048,1600]{0,1:T(8,128)(2,1)}) %all-gather.20.cloned.1.call-update) | async-done | bytes 6553616 | tf_op jit(solution)/shard_map/all_gather | solution.py:157
  441.5 43.8 %while.54 = (s32[]{:T(128)}, f32[1,25,128]{2,1,0:T(8,128)S(1)}, f32[1,25,128]{2,1,0:T(8,128)S(1)}, s32[2]{0:T(128)S(1)}, s32[1,2048]{1,0:T(1,128)S(1)}, /*index=...) while((s32[]{:T(128)}, f32[1,25,128]{2,1,0:T(8,128)S(1)}, ...), condition=%wide.region_5.7_spmd.clone, body=%wide.region_2.0_spmd.clone.sunk | while | flops 446128768 | bytes 37044128 | solution.py:178
  485.3 64.2 %all-gather.18.cloned.1.call-done = bf16[1,2048,3200]{1,2,0:T(8,128)(2,1)} async-done(((bf16[1,128,3200]{1,2,0:T(8,128)(2,1)}), bf16[1,2048,3200]{1,2,0:T(8,128)(2,1)}) %all-gather.18.cloned.1.call-update) | async-done | bytes 13107216 | tf_op jit(solution)/shard_map/all_gather | solution.py:185
  549.4 50.4 %while.55 = (s32[]{:T(128)}, f32[1,128,25,64]{1,3,2,0:T(8,128)}, s32[2]{0:T(128)S(1)}, bf16[1,2048,3200]{1,2,0:T(8,128)(2,1)}, s32[1,2048]{1,0:T(1,128)S(1)}, /*...) while((s32[]{:T(128)}, f32[1,128,25,64]{1,3,2,0:T(8,128)}, ...), condition=%wide.region_7.9_spmd.clone, body=%wide.region_6.8_spmd.clone.sunk | while | flops 852845568 | bytes 22013880 | solution.py:212
  606.8 12.3 all_gather.68
  648.4 10.6 fusion.77
  685.1 547.2 %fusion.96 = (f32[112,3200]{1,0:T(8,128)S(1)}, f32[3200,112]{0,1:T(8,128)S(1)}) fusion(f32[1600,3200]{1,0:T(8,128)} %fusion.80, f32[3200,1600]{0,1:T(8,128)} %fusion.77), kind=kCustom, calls=%all-reduce-scatter.5 | all-reduce-scatter fusion | flops 11468801 | bytes 43827712
  1247.1 88.7 %all_gather.74 = f32[1,2048,25]{1,2,0:T(8,128)} all-gather(f32[1,128,25]{1,2,0:T(8,128)S(1)} %bitcast.740), channel_id=1, replica_groups=mesh['dp'=2,'context'=8,'tensor'=2] {'context','tensor'}, dimensions={1}, use_global_device_ids=true | all-gather | bytes 217600 | tf_op jit(solution)/shard_map/all_gather | solution.py:289
  1335.8 13.8 concatenate.36
  1349.6 13.8 concatenate.37
  1367.1 34.5 %all-gather.4 = f32[2048,25]{0,1:T(8,128)} all-gather(f32[128,25]{0,1:T(8,128)S(1)} %multiply_reduce_fusion), channel_id=6, replica_groups=mesh['dp'=2,'context'=8,'tensor'=2] {'context','tensor'}, dimensions={0}, use_global_device_ids=true | all-gather | bytes 217600 | tf_op jit(solution)/shard_map/all_gather | solution.py:292
  1401.6 74.8 %while.56 = (s32[]{:T(128)}, f32[1,128,25,64]{1,3,2,0:T(8,128)}, s32[2]{0:T(128)S(1)}, bf16[1,2048,3200]{1,2,0:T(8,128)(2,1)}, s32[1,2048]{1,0:T(1,128)S(1)}, /*...) while((s32[]{:T(128)}, f32[1,128,25,64]{1,3,2,0:T(8,128)}, ...), condition=%wide.region_16.18_spmd.clone, body=%wide.region_15.17_spmd.clone.sunk | while | flops 1282106368 | bytes 51927496 | solution.py:279
  1426.4 12.5 fusion.174
  1463.8 12.7 fusion.174
  1486.3 95.9 %while.57 = (s32[]{:T(128)}, f32[1,128,3200]{1,2,0:T(8,128)}, s32[2]{0:T(128)S(1)}, bf16[1,2048,1600]{1,2,0:T(8,128)(2,1)}, s32[1,128]{1,0:T(1,128)S(1)}, /*inde...) while((s32[]{:T(128)}, f32[1,128,3200]{1,2,0:T(8,128)}, ...), condition=%wide.region_18.20_spmd.clone, body=%wide.region_17.19_spmd.clone.sunk | while | flops 1705632768 | bytes 104945224 | solution.py:337
  1514.4 12.5 fusion.184
  1562.0 12.5 fusion.184
  1584.6 15.9 fusion.83
  1600.5 442.4 %fusion.95 = (f32[104,4800]{1,0:T(8,128)S(1)}, f32[112,1600]{1,0:T(8,128)S(1)}) fusion(f32[1600,4800]{1,0:T(8,128)} %fusion.83, f32[1600,1600]{1,0:T(8,128)} %fusion.85), kind=kCustom, calls=%all-reduce-scatter.4 | all-reduce-scatter fusion | flops 10854402 | bytes 43674112
  2043.7 18.4 collective-permute-start.2
  2079.4 10.7 concatenate.34
  2092.8 11.2 fusion.68
  2104.4 58.6 %all-reduce.22 = (bf16[3200]{0:T(1024)(128)(2,1)S(1)}, bf16[1600]{0:T(1024)(128)(2,1)S(1)}, bf16[1600]{0:T(1024)(128)(2,1)S(1)}, bf16[1600]{0:T(1024)(128)(2,1)S...) all-reduce(f32[3200]{0:T(1024)S(1)} %pad_maximum_fusion.4, ...), channel_id=10, replica_groups=mesh['dp'=2,'context'=8,'tensor'=2] {'dp','context'}, use_global_device_ids=true, to_apply=%region_25.27.clone | all-reduce | flops 16000 | bytes 102400
  (326 shorter events, 373.9 us)
Async XLA Ops:
  7.2 78.4 %copy-start.7 = (bf16[1,128,1600]{1,2,0:T(8,128)(2,1)S(1)}, bf16[1,128,1600]{1,2,0:T(8,128)(2,1)}, u32[]{:S(2)}) copy-start(bf16[1,128,1600]{1,2,0:T(8,128)(2,1)} %param.26) | copy-start | bytes 1228804
  7.2 129.8 %all-gather.26.cloned.1.call-start = ((), (), s32[]{:S(2)}) async-start(), calls=%async_computation.6 | async-start | bytes 17199104 | tf_op jit(solution)/shard_map/all_gather | solution.py:100
  7.9 187.2 %all-gather.28.cloned.1.call-start = ((), (), s32[]{:S(2)}) async-start(), calls=%async_computation.7 | async-start | bytes 5883904 | tf_op jit(solution)/shard_map/all_gather | solution.py:101
  8.7 276.3 %all-gather.30.cloned.1.call-start = ((), (), s32[]{:S(2)}) async-start(), calls=%async_computation.8 | async-start | bytes 11315200 | tf_op jit(solution)/shard_map/all_gather | solution.py:102
  9.4 364.7 %all-gather.32.cloned.1.call-start = ((), (), s32[]{:S(2)}) async-start(), calls=%async_computation.9 | async-start | bytes 11315200 | tf_op jit(solution)/shard_map/all_gather | solution.py:103
  10.0 431.5 %all-gather.20.cloned.1.call-start = ((), (), s32[]{:S(2)}) async-start(), calls=%async_computation.3 | async-start | bytes 6963200 | tf_op jit(solution)/shard_map/all_gather | solution.py:157
  84.3 68.7 %copy-start.28 = (f32[1600]{0:T(1024)}, f32[1600]{0:T(1024)S(1)}, u32[]{:S(2)}) copy-start(f32[1600]{0:T(1024)S(1)} %convert_element_type.177) | copy-start | bytes 19204
  84.3 68.7 %copy-start.25 = (f32[1600]{0:T(1024)}, f32[1600]{0:T(1024)S(1)}, u32[]{:S(2)}) copy-start(f32[1600]{0:T(1024)S(1)} %convert_element_type.176) | copy-start | bytes 19204
  85.6 67.5 %copy-start.36 = (f32[128]{0:T(128)}, f32[128]{0:T(128)S(1)}, u32[]{:S(2)}) copy-start(f32[128]{0:T(128)S(1)} %broadcast_multiply_fusion.5) | copy-start | bytes 1540
  85.8 67.3 %copy-start.39 = (f32[128]{0:T(128)}, f32[128]{0:T(128)S(1)}, u32[]{:S(2)}) copy-start(f32[128]{0:T(128)S(1)} %add_rsqrt_fusion.1) | copy-start | bytes 1540
  164.4 14.2 copy-start.14
  164.4 385.0 %all-gather.18.cloned.1.call-start = ((), (), s32[]{:S(2)}) async-start(), calls=%async_computation.2 | async-start | bytes 13926400 | tf_op jit(solution)/shard_map/all_gather | solution.py:185
  167.5 500.1 %reduce-scatter.17.cloned.1.call-start = ((), (), s32[]{:S(2)}) async-start(), calls=%async_computation.11 | async-start | bytes 1277952
  637.7 37.6 %reduce-scatter.15.cloned.1.call-start = ((), (), s32[]{:S(2)}) async-start(), calls=%async_computation.10 | async-start | bytes 1277952
  647.6 838.6 %all-gather.22.cloned.1.call-start = ((), (), s32[]{:S(2)}) async-start(), calls=%async_computation.4 | async-start | bytes 6963200 | tf_op jit(solution)/shard_map/all_gather | solution.py:295
  648.3 837.9 %all-gather.24.cloned.1.call-start = ((), (), s32[]{:S(2)}) async-start(), calls=%async_computation.5 | async-start | bytes 6963200 | tf_op jit(solution)/shard_map/all_gather | solution.py:298
  659.0 18.8 copy-start.15
  685.1 1489.4 %all-reduce.30.cloned.1.call-start = ((), (), s32[]{:S(2)}) async-start(), calls=%async_computation.12 | async-start | bytes 2715648 | tf_op jit(solution)/shard_map/psum | solution.py:366
  1232.3 103.5 %collective-permute-start.3 = (f32[112,3200]{1,0:T(8,128)S(1)}, f32[112,3200]{1,0:T(8,128)}, u32[]{:S(2)}, u32[]{:S(2)}) collective-permute-start(f32[112,3200]{1,0:T(8,128)S(1)} %get-tuple-element.930), channel_id=1, source_target_pairs={{0,2},{2,4},{4,6},{6,8},{8,10},{10,12},{12,14},{14,16},{16,18},{18... | collective-permute-start | bytes 4300808
  1234.8 114.9 %collective-permute-start.5 = (f32[3200,112]{0,1:T(8,128)S(1)}, f32[3200,112]{0,1:T(8,128)}, u32[]{:S(2)}, u32[]{:S(2)}) collective-permute-start(f32[3200,112]{0,1:T(8,128)S(1)} %get-tuple-element.931), channel_id=1, source_target_pairs={{0,2},{2,4},{4,6},{6,8},{8,10},{10,12},{12,14},{14,16},{16,18},{18... | collective-permute-start | bytes 4300808
  1238.2 97.7 %collective-permute-start.4 = (f32[68,3200]{1,0:T(8,128)}, f32[68,3200]{1,0:T(8,128)}, u32[]{:S(2)}, u32[]{:S(2)}) collective-permute-start(f32[68,3200]{1,0:T(8,128)} %slice.297), channel_id=1, source_target_pairs={{0,4},{2,6},{4,8},{6,10},{8,12},{10,14},{12,16},{14,18},{16,20},{1... | collective-permute-start | bytes 2611208
  1241.4 108.2 %collective-permute-start.6 = (f32[3200,68]{0,1:T(8,128)}, f32[3200,68]{0,1:T(8,128)}, u32[]{:S(2)}, u32[]{:S(2)}) collective-permute-start(f32[3200,68]{0,1:T(8,128)} %slice.298), channel_id=1, source_target_pairs={{0,4},{2,6},{4,8},{6,10},{8,12},{10,14},{12,16},{14,18},{16,20},{1... | collective-permute-start | bytes 2611208
  1349.6 16.4 copy-start.17
  1486.2 98.4 %copy-start.26 = (f32[1600]{0:T(1024)S(1)}, f32[1600]{0:T(1024)}, u32[]{:S(2)}) copy-start(f32[1600]{0:T(1024)} %copy-done.25) | copy-start | bytes 19204
  1486.2 98.4 %copy-start.29 = (f32[1600]{0:T(1024)S(1)}, f32[1600]{0:T(1024)}, u32[]{:S(2)}) copy-start(f32[1600]{0:T(1024)} %copy-done.28) | copy-start | bytes 19204
  1486.3 98.3 %copy-start.37 = (f32[128]{0:T(128)S(1)}, f32[128]{0:T(128)}, u32[]{:S(2)}) copy-start(f32[128]{0:T(128)} %copy-done.36) | copy-start | bytes 1540
  1486.3 98.3 %copy-start.40 = (f32[128]{0:T(128)S(1)}, f32[128]{0:T(128)}, u32[]{:S(2)}) copy-start(f32[128]{0:T(128)} %copy-done.39) | copy-start | bytes 1540
  2042.9 26.8 %copy-start.30 = (f32[25,64]{1,0:T(8,128)S(1)}, f32[25,64]{1,0:T(8,128)}, u32[]{:S(2)}) copy-start(f32[25,64]{1,0:T(8,128)} %get-tuple-element.1010) | copy-start | bytes 19204
  2043.7 26.6 %collective-permute-start.2 = (bf16[68,1600]{1,0:T(8,128)(2,1)}, bf16[68,1600]{1,0:T(8,128)(2,1)}, u32[]{:S(2)}, u32[]{:S(2)}) collective-permute-start(bf16[68,1600]{1,0:T(8,128)(2,1)} %slice.296), channel_id=1, source_target_pairs={{0,4},{2,6},{4,8},{6,10},{8,12},{10,14},{12,16},{14,18},{16,20},{1... | collective-permute-start | bytes 652808
  2062.1 8.2 collective-permute-start.1
  2064.3 15.1 collective-permute-start
  2092.8 79.4 %copy-start.11 = (f32[128,1600]{0,1:T(8,128)S(1)}, f32[128,1600]{0,1:T(8,128)}, u32[]{:S(2)}) copy-start(f32[128,1600]{0,1:T(8,128)} %copy-done.10) | copy-start | bytes 2457604
  (38 other events, 270.2 us)
Sparse Core Ops, SparseCore 0:
  10.3 126.7 all-gather.25
  139.3 55.8 all-gather.27
  197.4 87.4 all-gather.29
  287.0 87.0 all-gather.31
  376.0 65.3 all-gather.19
  444.0 105.3 all-gather.17
  637.8 16.3 reduce-scatter.16
  657.1 18.1 reduce-scatter.14
  678.0 99.0 all-gather.21
  779.0 101.6 all-gather.23
  2092.7 44.1 all-reduce.29
where the time goes:
time: 2200 us; the launch traced here: 2190 us
  blocking collectives  1270 us (58%)
  waiting for transfers between devices  346 us (16%)
  matrix products  213 us (10%)
  local copies, waits for them, and re-layouts  174 us (8%)
  other arithmetic  128 us (6%)
  starting transfers between devices  32.5 us (1%)
    unnamed x4, blocking collectives  1110 us
    unnamed x124, local copies, waits for them, and re-layouts  116 us
    all_gather x1, blocking collectives, on_device(): lax.all_gather(jnp.transpose(log_total, (0, 2, 1)), ('context', 'tensor')...  88.7 us
    select_n x8, other arithmetic, key_places(): return jnp.take(slot_order, slot_ids, axis=1) * slot_len + within[None, :]  81.9 us
    all_gather x1, waiting for transfers between devices, on_device(): lax.all_gather(fc_weight, ('dp', 'context'), axis=0, tiled=True)  81.7 us
    all_gather x1, waiting for transfers between devices, on_device(): lax.all_gather(proj_weight, ('dp', 'context'), axis=1, tiled=True)  78.4 us
    dot_general x8, matrix products, contract(): lax.dot_general(left_side, right_side, (((left_dim,), (right_dim,)), ((),...  67.2 us
    all_gather x1, waiting for transfers between devices, on_device(): lax.all_gather(key_value, ('context', 'tensor'), axis=1, tiled=True)  64.2 us
  transfers between devices with their start and end apart: 18, of which 7 were waited for; matrix products, arithmetic and copies ran while one was open for 39% of the time, Pallas kernels for 0%

commit v1 on v0

v1 whole, which is shorter than its diff:
```python
import functools
import math

import jax
import jax.numpy as jnp
import numpy as np
from jax import lax
from jax.experimental import pallas as pl
from jax.experimental.pallas import tpu as pltpu
from jax.sharding import Mesh
from jax.sharding import PartitionSpec as P

HEADS = 25
DOCS = 8
NORM_EPS = 1e-05
GELU_SCALE = 0.7978845608028654
GELU_CUBE = 0.044715
MASK_FLOOR = -1e30

F32 = jnp.float32
B16 = jnp.bfloat16
BLK = 256
VMEM_LIMIT = 60 * 1024 * 1024

ROW = ("h", "l", "c", "y")
CTX = ("h", "l", "c")
SHARD = ("x", "h", "l", "c")
FFG = ("l", "c", "y")


def gelu_parts(values):
    inner_arg = GELU_SCALE * (values + GELU_CUBE * values * values * values)
    tanh_value = jnp.tanh(inner_arg)
    result = 0.5 * values * (1.0 + tanh_value)
    derivative = 0.5 * (1.0 + tanh_value) + 0.5 * values * (
        1.0 - tanh_value * tanh_value
    ) * GELU_SCALE * (1.0 + 3.0 * GELU_CUBE * values * values)
    return (result, derivative)


def norm_forward(values):
    mean_value = jnp.mean(values, axis=-1, keepdims=True)
    centered = values - mean_value
    inv_sigma = lax.rsqrt(jnp.mean(centered * centered, axis=-1, keepdims=True) + NORM_EPS)
    return (centered * inv_sigma, inv_sigma)


def norm_backward(upstream, normed, inv_sigma, norm_gain):
    scaled = upstream * norm_gain
    return inv_sigma * (
        scaled
        - jnp.mean(scaled, axis=-1, keepdims=True)
        - normed * jnp.mean(scaled * normed, axis=-1, keepdims=True)
    )


def dot(left, right, left_dim, right_dim):
    return lax.dot_general(
        left, right, (((left_dim,), (right_dim,)), ((), ())), preferred_element_type=F32
    )


def sort_slots(inv_ref, src_ref, dst_ref, slot_len, start=0, width=None, factor=None):
    width = src_ref.shape[1] if width is None else width

    def body(piece, carry):
        slot = inv_ref[piece]
        rows = src_ref[pl.ds(pl.multiple_of(slot * slot_len, slot_len), slot_len), start : start + width]
        if factor is not None:
            rows = rows * jnp.asarray(factor, rows.dtype)
        dst_ref[pl.ds(pl.multiple_of(piece * slot_len, slot_len), slot_len), :] = rows
        return carry

    lax.fori_loop(0, src_ref.shape[0] // slot_len, body, 0)


def unsort_block(inv_ref, dst_ref, value, block, slot_len):
    for part in range(BLK // slot_len):
        slot = inv_ref[block * (BLK // slot_len) + part]
        dst_ref[pl.ds(pl.multiple_of(slot * slot_len, slot_len), slot_len), :] = value[
            part * slot_len : (part + 1) * slot_len
        ].astype(dst_ref.dtype)


def block_rows(block):
    return pl.ds(pl.multiple_of(block * BLK, BLK), BLK)


def mask_of(start_row, key_block, query_block, diagonal):
    key_at = key_block * BLK + lax.broadcasted_iota(jnp.int32, (BLK, BLK), 0)
    allowed = key_at >= start_row
    if diagonal:
        query_at = query_block * BLK + lax.broadcasted_iota(jnp.int32, (BLK, BLK), 1)
        allowed = jnp.logical_and(allowed, key_at <= query_at)
    return allowed


def attend_kernel(slot_len, head, inv_ref, low_ref, qkv_ref, start_ref, out_ref, lse_ref, q_s, k_s, vt_s):
    total = qkv_ref.shape[0]
    pair = 2 * head
    sort_slots(inv_ref, qkv_ref, q_s, slot_len, 0, pair, 1.0 / math.sqrt(head))
    sort_slots(inv_ref, qkv_ref, k_s, slot_len, pair, pair)

    def fill(piece, carry):
        slot = inv_ref[piece]
        rows = qkv_ref[pl.ds(pl.multiple_of(slot * slot_len, slot_len), slot_len), 2 * pair :]
        vt_s[:, pl.ds(pl.multiple_of(piece * slot_len, slot_len), slot_len)] = rows.astype(F32).T.astype(B16)
        return carry

    lax.fori_loop(0, total // slot_len, fill, 0)

    def per_query(block, carry):
        queries = q_s[block_rows(block), :]
        start_row = start_ref[block]

        def step(key_block, state, diagonal):
            allowed = mask_of(start_row, key_block, block, diagonal)
            keys = k_s[block_rows(key_block), :]
            values = vt_s[:, block_rows(key_block)]
            fresh = []
            for part in range(2):
                old_max, old_sum, old_acc = state[part]
                cols = slice(part * head, (part + 1) * head)
                scores = dot(keys[:, cols], queries[:, cols], 1, 1)
                scores = jnp.where(allowed, scores, MASK_FLOOR)
                new_max = jnp.maximum(old_max, jnp.max(scores, axis=0, keepdims=True))
                weights = jnp.where(allowed, jnp.exp(scores - new_max), 0.0)
                shrink = jnp.exp(old_max - new_max)
                new_sum = old_sum * shrink + jnp.sum(weights, axis=0, keepdims=True)
                new_acc = old_acc * shrink + dot(values[cols, :], weights.astype(B16), 1, 0)
                fresh.append((new_max, new_sum, new_acc))
            return tuple(fresh)

        first = tuple(
            (
                jnp.full((1, BLK), MASK_FLOOR, F32),
                jnp.zeros((1, BLK), F32),
                jnp.zeros((head, BLK), F32),
            )
            for part in range(2)
        )
        state = lax.fori_loop(low_ref[block], block, lambda j, s: step(j, s, False), first)
        state = step(block, state, True)
        lse_ref[block] = jnp.concatenate([s[0] + jnp.log(s[1]) for s in state], axis=0)
        result = jnp.concatenate([s[2] / s[1] for s in state], axis=0)
        unsort_block(inv_ref, out_ref, result.T, block, slot_len)
        return carry

    lax.fori_loop(0, total // BLK, per_query, 0)


def attend(inv, low, qkv, start3, slot_len, head):
    total = qkv.shape[0]
    vmem = pl.BlockSpec(memory_space=pltpu.VMEM)
    smem = pl.BlockSpec(memory_space=pltpu.SMEM)
    return pl.pallas_call(
        functools.partial(attend_kernel, slot_len, head),
        out_shape=(
            jax.ShapeDtypeStruct((total, 2 * head), B16),
            jax.ShapeDtypeStruct((total // BLK, 2, BLK), F32),
        ),
        in_specs=[smem, smem, vmem, vmem],
        out_specs=(vmem, vmem),
        scratch_shapes=[
            pltpu.VMEM((total, 2 * head), B16),
            pltpu.VMEM((total, 2 * head), B16),
            pltpu.VMEM((2 * head, total), B16),
        ],
        compiler_params=pltpu.CompilerParams(vmem_limit_bytes=VMEM_LIMIT),
        cost_estimate=pl.CostEstimate(
            flops=4 * total * total * head, bytes_accessed=8 * total * head * 2, transcendentals=total * total
        ),
        name="attend",
    )(inv, low, qkv, start3)


def attend_back_kernel(
    slot_len, head, inv_ref, low_ref, qkv_ref, out_ref, grad_ref, lse_ref, start_ref,
    dqkv_ref, q_s, k_s, v_s, kt_s, o_s, g_s, dk_s, dv_s,
):
    total = qkv_ref.shape[0]
    pair = 2 * head
    scale = 1.0 / math.sqrt(head)
    sort_slots(inv_ref, qkv_ref, q_s, slot_len, 0, pair, scale)
    sort_slots(inv_ref, qkv_ref, k_s, slot_len, pair, pair)
    sort_slots(inv_ref, qkv_ref, v_s, slot_len, 2 * pair, pair)
    sort_slots(inv_ref, out_ref, o_s, slot_len)
    sort_slots(inv_ref, grad_ref, g_s, slot_len)

    def fill(block, carry):
        kt_s[:, block_rows(block)] = k_s[block_rows(block), :].astype(F32).T.astype(B16)
        return carry

    lax.fori_loop(0, total // BLK, fill, 0)
    dk_s[...] = jnp.zeros_like(dk_s)
    dv_s[...] = jnp.zeros_like(dv_s)

    def per_query(block, carry):
        queries = q_s[block_rows(block), :]
        grads = g_s[block_rows(block), :]
        start_row = start_ref[block]
        lse = lse_ref[block]
        prod = (grads.astype(F32) * o_s[block_rows(block), :].astype(F32)).T
        delta = [jnp.sum(prod[part * head : (part + 1) * head], axis=0, keepdims=True) for part in range(2)]

        def step(key_block, state, diagonal):
            allowed = mask_of(start_row, key_block, block, diagonal)
            rows = block_rows(key_block)
            keys = k_s[rows, :]
            values = v_s[rows, :]
            flipped = kt_s[:, rows]
            fresh, dks, dvs = [], [], []
            for part in range(2):
                cols = slice(part * head, (part + 1) * head)
                scores = dot(keys[:, cols], queries[:, cols], 1, 1)
                weights = jnp.where(allowed, jnp.exp(scores - lse[part : part + 1]), 0.0)
                dprob = dot(values[:, cols], grads[:, cols], 1, 1)
                dscore = (weights * (dprob - delta[part])).astype(B16)
                dvs.append(dot(weights.astype(B16), grads[:, cols], 1, 0))
                dks.append(dot(dscore, queries[:, cols], 1, 0))
                fresh.append(state[part] + dot(flipped[cols, :], dscore, 1, 0))
            dk_s[rows, :] += jnp.concatenate(dks, axis=1)
            dv_s[rows, :] += jnp.concatenate(dvs, axis=1)
            return tuple(fresh)

        state = (jnp.zeros((head, BLK), F32), jnp.zeros((head, BLK), F32))
        state = lax.fori_loop(low_ref[block], block, lambda j, s: step(j, s, False), state)
        state = step(block, state, True)
        dq = jnp.concatenate(state, axis=0).T * scale
        for part in range(BLK // slot_len):
            slot = inv_ref[block * (BLK // slot_len) + part]
            dqkv_ref[pl.ds(pl.multiple_of(slot * slot_len, slot_len), slot_len), 0:pair] = dq[
                part * slot_len : (part + 1) * slot_len
            ]
        return carry

    lax.fori_loop(0, total // BLK, per_query, 0)

    def give(piece, carry):
        slot = inv_ref[piece]
        rows = pl.ds(pl.multiple_of(slot * slot_len, slot_len), slot_len)
        held = pl.ds(pl.multiple_of(piece * slot_len, slot_len), slot_len)
        dqkv_ref[rows, pair : 2 * pair] = dk_s[held, :]
        dqkv_ref[rows, 2 * pair :] = dv_s[held, :]
        return carry

    lax.fori_loop(0, total // slot_len, give, 0)


def attend_back(inv, low, qkv, out, grad, lse, start3, slot_len, head):
    total = qkv.shape[0]
    pair = 2 * head
    vmem = pl.BlockSpec(memory_space=pltpu.VMEM)
    smem = pl.BlockSpec(memory_space=pltpu.SMEM)
    held = pltpu.VMEM((total, pair), B16)
    return pl.pallas_call(
        functools.partial(attend_back_kernel, slot_len, head),
        out_shape=jax.ShapeDtypeStruct((total, 3 * pair), F32),
        in_specs=[smem, smem] + [vmem] * 5,
        out_specs=vmem,
        scratch_shapes=[
            held, held, held, pltpu.VMEM((pair, total), B16), held, held,
            pltpu.VMEM((total, pair), F32), pltpu.VMEM((total, pair), F32),
        ],
        compiler_params=pltpu.CompilerParams(vmem_limit_bytes=VMEM_LIMIT),
        cost_estimate=pl.CostEstimate(
            flops=10 * total * total * head, bytes_accessed=30 * total * head * 2, transcendentals=total * total
        ),
        name="attend_back",
    )(inv, low, qkv, out, grad, lse, start3)


def on_device(
    sizes, block_input, segment_ids, slot_order, first_gain, first_shift, qkv_weight, qv_bias, out_weight, out_bias,
    second_gain, second_shift, fc_weight, fc_bias, proj_weight, proj_bias, out_grad,
):
    n_x, n_ctx, n_y = sizes
    n_slot = n_ctx * n_y
    n_shard = n_x * n_ctx
    n_h = n_ctx // 4
    slot_len, feats = block_input.shape[1:]
    head = feats // HEADS
    pair = 2 * head
    rows = qkv_weight.shape[0]
    ff_own = fc_weight.shape[1] // 4
    padded = n_slot * pair
    y_at = lax.axis_index("y")
    ctx_at = lax.axis_index(CTX)
    slot_at = lax.axis_index(ROW)
    lc_at = lax.axis_index(("l", "c"))

    def gather(value, axes):
        return lax.all_gather(value, axes, axis=0, tiled=True)

    small = jnp.concatenate(
        [
            first_gain, first_shift, out_bias, second_gain, second_shift, proj_bias, qv_bias,
        ]
    )
    smalls = lax.all_gather(small, SHARD, axis=0, tiled=False).astype(F32)
    gain_one, shift_one, bias_out, gain_two, shift_two, bias_proj = [
        smalls[:, i * rows : (i + 1) * rows].reshape(feats) for i in range(6)
    ]
    bias_qv = smalls[:, 6 * rows :].reshape(2, feats)
    bias_pair = lax.dynamic_slice_in_dim(
        jnp.pad(bias_qv, ((0, 0), (0, padded - feats))), slot_at * pair, pair, 1
    )
    bias_qkv = jnp.concatenate([bias_pair[0], jnp.zeros((pair,), F32), bias_pair[1]])

    packed = jnp.pad(qkv_weight.reshape(rows, 3, feats), ((0, 0), (0, 0), (0, padded - feats)))
    packed = lax.dynamic_index_in_dim(packed.reshape(rows, 3, n_ctx, n_y, pair), y_at, 3, False)
    packed = packed.transpose(2, 0, 1, 3).reshape(n_ctx, rows, 3 * pair)
    packed = lax.all_to_all(packed, CTX, 0, 0, tiled=True)
    w_qkv = lax.all_gather(packed, "x", axis=0, tiled=False).reshape(feats, 3 * pair)

    ffn = jnp.concatenate(
        [
            fc_weight.reshape(rows, 4, ff_own).transpose(1, 0, 2),
            proj_weight.reshape(4, ff_own, rows).transpose(0, 2, 1),
        ],
        axis=2,
    )
    ffn = lax.all_to_all(ffn, ("l", "c"), 0, 0, tiled=True)
    ffn = gather(ffn.reshape(4 * rows, 2 * ff_own), ("x", "h"))
    w_fc, w_proj = ffn[:, :ff_own], ffn[:, ff_own:]
    w_out = gather(out_weight, SHARD)
    b_fc = lax.dynamic_slice_in_dim(fc_bias, lc_at * ff_own, ff_own, 0).astype(F32)

    order = slot_order[0]
    pieces = jnp.arange(n_slot, dtype=jnp.int32)
    inv = jnp.sum(jnp.where(order[None, :] == pieces[:, None], pieces[None, :], 0), axis=1).astype(jnp.int32)
    segs = jnp.take(segment_ids[0].reshape(n_slot, slot_len), inv, axis=0).reshape(-1)
    docs = jnp.arange(DOCS, dtype=jnp.int32)
    counts = jnp.sum((segs[None, :] == docs[:, None]).astype(jnp.int32), axis=1)
    starts = jnp.sum(jnp.where(segs[None, :] > docs[:, None], counts[:, None], 0), axis=0).astype(jnp.int32)
    start3 = starts.reshape(-1, 1, BLK)
    low = start3[:, 0, 0] // BLK

    own_input = block_input[0]
    own_wide = own_input.astype(F32)
    all_input = gather(own_input, ROW)
    normed_all, unused = norm_forward(all_input.astype(F32))
    norm_one = (normed_all * gain_one + shift_one).astype(B16)
    qkv = (dot(norm_one, w_qkv, 1, 0) + bias_qkv).astype(B16)
    heads_out, lse = attend(inv, low, qkv, start3, slot_len, head)
    attention = lax.all_to_all(heads_out.reshape(n_slot, slot_len, pair), ROW, 0, 0, tiled=True)
    attention = attention.transpose(1, 0, 2).reshape(slot_len, padded)[:, :feats]
    hidden = own_wide + dot(attention, w_out, 1, 0) + bias_out
    normed_two, inv_two = norm_forward(hidden)
    norm_two = (normed_two * gain_two + shift_two).astype(B16)
    grad_own = out_grad[0]
    grad_wide = grad_own.astype(F32)
    grad_all = gather(grad_own, FFG)
    norm_all = gather(norm_two, FFG)
    preact = dot(norm_all, w_fc, 1, 0) + b_fc
    activated, derivative = gelu_parts(preact)
    activation = activated.astype(B16)
    mlp_part = dot(activation, w_proj, 1, 1).astype(B16)
    mlp = lax.psum_scatter(mlp_part, FFG, scatter_dimension=0, tiled=True).astype(F32)
    block_output = hidden + mlp + bias_proj

    dpreact = dot(grad_all, w_proj, 1, 0) * derivative
    dpreact_b = dpreact.astype(B16)
    dnorm_part = dot(dpreact_b, w_fc, 1, 1).astype(B16)
    dnorm_two = lax.psum_scatter(dnorm_part, FFG, scatter_dimension=0, tiled=True).astype(F32)
    ffn_grad = jnp.concatenate([dot(norm_all, dpreact_b, 0, 0), dot(grad_all, activation, 0, 0)], axis=1).astype(B16)
    ffn_grad = lax.psum_scatter(ffn_grad, ("x", "h"), scatter_dimension=0, tiled=True)
    ffn_grad = lax.all_to_all(ffn_grad.reshape(4, rows, 2 * ff_own), ("l", "c"), 0, 0, tiled=True).astype(F32)
    fc_grad = ffn_grad[:, :, :ff_own].transpose(1, 0, 2).reshape(rows, 4 * ff_own)
    proj_grad = ffn_grad[:, :, ff_own:].transpose(0, 2, 1).reshape(4 * ff_own, rows)

    dhidden = grad_wide + norm_backward(dnorm_two, normed_two, inv_two, gain_two)
    dhidden_b = dhidden.astype(B16)
    out_part = dot(attention, dhidden_b, 0, 0).astype(B16).reshape(n_shard, rows, feats)
    row_pad = -rows % 16
    out_part = jnp.pad(out_part, ((0, 0), (0, row_pad), (0, 0))).reshape(-1, feats)
    out_grad_w = lax.psum_scatter(out_part, SHARD, scatter_dimension=0, tiled=True)[:rows]
    out_grad_w = lax.psum(out_grad_w, "y").astype(F32)

    dattention = dot(dhidden_b, w_out, 1, 1).astype(B16)
    dattention = jnp.pad(dattention, ((0, 0), (0, padded - feats))).reshape(slot_len, n_slot, pair).transpose(1, 0, 2)
    dattention = lax.all_to_all(dattention, ROW, 0, 0, tiled=True).reshape(n_slot * slot_len, pair)
    dqkv = attend_back(inv, low, qkv, heads_out, dattention, lse, start3, slot_len, head)
    dqkv_b = dqkv.astype(B16)
    dnorm_one_part = dot(dqkv_b, w_qkv, 1, 1).astype(B16)
    dnorm_one = lax.psum_scatter(dnorm_one_part, ROW, scatter_dimension=0, tiled=True).astype(F32)
    qkv_part = dot(norm_one, dqkv_b, 0, 0).astype(B16)
    qkv_part = lax.psum_scatter(qkv_part, "x", scatter_dimension=0, tiled=True).reshape(n_ctx, rows, 3 * pair)
    qkv_part = lax.all_to_all(qkv_part, CTX, 0, 0, tiled=True)
    qkv_all = lax.all_gather(qkv_part, "y", axis=0, tiled=False)
    qkv_grad = qkv_all.reshape(n_y, n_ctx, rows, 3, pair).transpose(2, 3, 1, 0, 4).reshape(rows, 3, padded)
    qkv_grad = qkv_grad[:, :, :feats].reshape(rows, 3 * feats).astype(F32)

    normed_one, inv_one = norm_forward(own_wide)
    input_grad = dhidden + norm_backward(dnorm_one, normed_one, inv_one, gain_one)

    dq_sum, dv_sum = jnp.sum(dqkv[:, :pair], axis=0), jnp.sum(dqkv[:, 2 * pair :], axis=0)

    def placed(value, width, at):
        return lax.dynamic_update_slice(jnp.zeros((width,), F32), value, (at,))

    vectors = jnp.concatenate(
        [
            jnp.sum(dhidden, axis=0),
            jnp.sum(dnorm_one * normed_one, axis=0),
            jnp.sum(dnorm_one, axis=0),
            jnp.sum(dnorm_two * normed_two, axis=0),
            jnp.sum(dnorm_two, axis=0),
            jnp.sum(grad_wide, axis=0),
            placed(dq_sum, padded, slot_at * pair)[:feats],
            placed(dv_sum, padded, slot_at * pair)[:feats],
            placed(jnp.sum(dpreact, axis=0), n_y * 4 * ff_own, (y_at * 4 + lc_at) * ff_own),
        ]
    )
    vectors = lax.psum(vectors, SHARD + ("y",))
    shard_at = lax.axis_index(SHARD)

    def own(index):
        return lax.dynamic_slice_in_dim(vectors, index * feats + shard_at * rows, rows, 0)

    qv_grad = lax.dynamic_slice_in_dim(vectors, 6 * feats + shard_at * 2 * rows, 2 * rows, 0)
    fc_bias_grad = lax.dynamic_slice_in_dim(vectors, 8 * feats + y_at * 4 * ff_own, 4 * ff_own, 0)
    return (
        block_output[None],
        input_grad[None],
        qkv_grad,
        qv_grad,
        out_grad_w,
        own(0),
        own(1),
        own(2),
        own(3),
        own(4),
        fc_grad,
        fc_bias_grad,
        proj_grad,
        own(5),
    )


def solution(mesh):
    n_x, n_ctx, n_y = (mesh.shape[axis] for axis in ("dp", "context", "tensor"))
    inner = Mesh(mesh.devices.reshape(n_x, n_ctx // 4, 2, 2, n_y), ("x", "h", "l", "c", "y"))
    tokens = P("x", ROW, None)
    shard = P(SHARD)
    shard_rows = P(SHARD, None)
    return jax.shard_map(
        functools.partial(on_device, (n_x, n_ctx, n_y)),
        mesh=inner,
        in_specs=(
            tokens, P("x", None), P("x", None), shard, shard, shard_rows, shard, shard_rows, shard, shard, shard,
            P(SHARD, "y"), P("y"), P("y", SHARD), shard, tokens,
        ),
        out_specs=(
            tokens, tokens, shard_rows, shard, shard_rows, shard, shard, shard, shard, shard,
            P(SHARD, "y"), P("y"), P("y", SHARD), shard,
        ),
        check_vma=False,
    )
```

time: 2200 us -> 1110 us (0.50)
  blocking collectives: 1270 us -> 143 us
  waiting for transfers between devices: 346 us -> 668 us
  matrix products: 213 us -> 75.2 us
  other arithmetic: 128 us -> 30 us
  local copies, waits for them, and re-layouts: 174 us -> 110 us
  Pallas kernels: 0 us -> 47.5 us
    unnamed x4 -> x1, blocking collectives: 1110 us -> 70.5 us
    unnamed x20 -> x18, waiting for transfers between devices: 9.77 us -> 226 us
    all_gather x8 -> x7, waiting for transfers between devices: 336 us -> 174 us  [the longest x5 174 us: gather(): return lax.all_gather(value, axes, axis=0, tiled=True)]
    all_gather x4 -> x0, blocking collectives: 148 us -> none  [the longest x1 88.7 us: on_device(): lax.all_gather(jnp.transpose(log_total, (0, 2, 1)), ('context', 'tensor')...]
    dot_general x26 -> x12, matrix products: 213 us -> 75.2 us  [dot(): lax.dot_general(left, right, (((left_dim,), (right_dim,)), ((), ())), pre...]
    reduce_scatter x0 -> x3, waiting for transfers between devices: none -> 133 us  [the longest x1 89.8 us: on_device(): lax.psum_scatter(ffn_grad, ('x', 'h'), scatter_dimension=0, tiled=True)]
    psum x1 -> x2, waiting for transfers between devices: 0.01 us -> 121 us  [the longest x1 120 us: on_device(): vectors = lax.psum(vectors, SHARD + ('y',))]
    select_n x8 -> x3, other arithmetic: 81.9 us -> 0.61 us  [the longest x1 0.53 us: on_device(): low = start3[:, 0, 0] // BLK]
  transfers between devices with their start and end apart: 18 -> 18, of which waited for: 7 -> 13; matrix products, arithmetic and copies ran while one was open for 39% -> 15% of each run, Pallas kernels for 0% -> 2%
where the time goes in v1:
time: 1110 us; the launch traced here: 1100 us
  waiting for transfers between devices  668 us (60%)
  blocking collectives  143 us (13%)
  local copies, waits for them, and re-layouts  110 us (10%)
  matrix products  75.2 us (7%)
  Pallas kernels  47.5 us (4%)
  other arithmetic  30 us (3%)
  between operations  15.6 us (1%)
  starting transfers between devices  12.1 us (1%)
    unnamed x18, waiting for transfers between devices  226 us
    all_gather x5, waiting for transfers between devices, gather(): return lax.all_gather(value, axes, axis=0, tiled=True)  174 us
    psum x1, waiting for transfers between devices, on_device(): vectors = lax.psum(vectors, SHARD + ('y',))  120 us
    reduce_scatter x1, waiting for transfers between devices, on_device(): lax.psum_scatter(ffn_grad, ('x', 'h'), scatter_dimension=0, tiled=True)  89.8 us
    dot_general x12, matrix products, dot(): lax.dot_general(left, right, (((left_dim,), (right_dim,)), ((), ())), pre...  75.2 us
    unnamed x1, blocking collectives  70.5 us
    unnamed x71, local copies, waits for them, and re-layouts  53.3 us
    reduce_scatter x1, waiting for transfers between devices, on_device(): lax.psum_scatter(out_part, SHARD, scatter_dimension=0, tiled=True)[:rows]  42.9 us
  transfers between devices with their start and end apart: 18, of which 13 were waited for; matrix products, arithmetic and copies ran while one was open for 15% of the time, Pallas kernels for 2%

profile of v1, /device:TPU:0, one launch (start us, length us, event | category | flops | bytes accessed | tf_op | source)
XLA Modules:
  0.0 1102.2 jit_solution(13884114447155547472)
XLA Ops:
  10.5 24.1 %all_to_all.30 = bf16[8,100,384]{2,1,0:T(8,128)(2,1)S(1)} all-to-all(bf16[8,100,384]{2,1,0:T(8,128)(2,1)S(1)} %copy.97), channel_id=1, replica_groups=mesh['x'=2,'h'=2,'l'=2,'c'=2,'y'=2] {'h','l','c'}, dimensions={0} | all-to-all | bytes 1228800 | tf_op jit(solution)/shard_map/all_to_all | solution.py:313
  45.1 70.5 %all-reduce.4 = bf16[12800]{0:T(1024)(128)(2,1)S(1)} all-reduce(bf16[12800]{0:T(1024)(128)(2,1)S(1)} %dynamic-update-slice), channel_id=3, replica_groups=mesh['x'=2,'h'=2,'l'=2,'c'=2,'y'=2] {'x','h','l','c'}, use_global_device_ids=true, to_apply=%add.4 | all-reduce | flops 12800 | bytes 51200
  121.3 7.4 all-gather.18.cloned.1.call-done
  145.9 23.2 %attend.1 = (bf16[2048,128]{1,0:T(8,128)(2,1)}, f32[8,2,256]{2,1,0:T(2,128)}) custom-call(s32[16]{0:T(128)} %copy-done.26, s32[8]{0:T(128)} %and_select_fusion.low_ref, bf16[2048,384]{1,0:T(8,128)(2,1)} %add_convert_fusion.qkv_ref, s32[8,1,256]{2,1,0:T(1,128)} %bitcast.155), custom_call_target="tpu_custom_call" | custom-call | flops 1073741824 | bytes 2097152 | tf_op jit(solution)/shard_map/attend/pallas_call | solution.py:156
  175.2 20.0 %all-gather.26.cloned.1.call-done = bf16[16,100,1600]{2,1,0:T(8,128)(2,1)} async-done(((bf16[1,100,1600]{2,1,0:T(8,128)(2,1)}), bf16[16,100,1600]{2,1,0:T(8,128)(2,1)}) %all-gather.26.cloned.1.call-update) | async-done | bytes 5120016 | tf_op jit(solution)/shard_map/all_gather | solution.py:293
  195.2 8.0 reshape.231
  203.2 5.4 fusion.64
  211.5 90.0 %all-gather.16.cloned.1.call-done = bf16[1600,1600]{1,0:T(8,128)(2,1)} async-done(((bf16[400,1600]{1,0:T(8,128)(2,1)}), bf16[1600,1600]{1,0:T(8,128)(2,1)}) %all-gather.16.cloned.1.call-update) | async-done | bytes 5120016 | tf_op jit(solution)/shard_map/all_gather | solution.py:293
  301.6 31.5 %all-gather.14.cloned.1.call-done = bf16[1024,1600]{0,1:T(8,128)(2,1)} async-done(((bf16[128,1600]{0,1:T(8,128)(2,1)}), bf16[1024,1600]{0,1:T(8,128)(2,1)}) %all-gather.14.cloned.1.call-update) | async-done | bytes 3276816 | tf_op jit(solution)/shard_map/all_gather | solution.py:293
  333.1 7.7 fusion.20
  340.8 25.1 %all-gather.22.cloned.1.call-done = bf16[1,1024,1600]{1,2,0:T(8,128)(2,1)} async-done(((bf16[1,128,1600]{1,2,0:T(8,128)(2,1)}), bf16[1,1024,1600]{1,2,0:T(8,128)(2,1)}) %all-gather.22.cloned.1.call-update) | async-done | bytes 3276816 | tf_op jit(solution)/shard_map/all_gather | solution.py:293
  365.9 9.5 fusion.65
  381.4 5.4 copy.114
  387.4 8.6 convolution_convert_fusion.3
  396.0 5.4 copy.112
  401.6 59.2 %reduce-scatter.21.cloned.1.call-done = bf16[128,1600]{1,0:T(8,128)(2,1)} async-done(((bf16[1024,1600]{1,0:T(8,128)(2,1)}), bf16[128,1600]{1,0:T(8,128)(2,1)}) %reduce-scatter.21.cloned.1.call-update) | async-done | bytes 409616
  463.3 73.6 %reduce-scatter.19.cloned.1.call-done = bf16[128,1600]{1,0:T(8,128)(2,1)} async-done(((bf16[1024,1600]{1,0:T(8,128)(2,1)}), bf16[128,1600]{1,0:T(8,128)(2,1)}) %reduce-scatter.19.cloned.1.call-update) | async-done | bytes 409616
  546.4 20.2 %all_to_all.31 = bf16[16,128,128]{2,1,0:T(8,128)(2,1)} all-to-all(bf16[16,128,128]{2,1,0:T(8,128)(2,1)S(1)} %bitcast.148), channel_id=1, replica_groups=mesh['x'=2,'h'=2,'l'=2,'c'=2,'y'=2] {'h','l','c','y'}, dimensions={0} | all-to-all | bytes 1048576 | tf_op jit(solution)/shard_map/all_to_all | solution.py:382
  566.6 24.3 %attend_back.1 = f32[2048,384]{1,0:T(8,128)} custom-call(s32[16]{0:T(128)} %copy-done.26, s32[8]{0:T(128)} %and_select_fusion.low_ref, bf16[2048,384]{1,0:T(8,128)(2,1)} %add_convert_fusion.qkv_ref, bf16[2048,128]{1,0:T(8,128)(2,1)} %get-tuple-element.16.out_ref, bf16[2048,128]{1,0:T(8,128)(2,1)} %bitcast.150, f32[8,2,256]{2,1,0:T(2,128)} %get-tuple-element.17.lse_ref, ...), custom_call_target="tpu_custom_call" | custom-call | flops 2684354560 | bytes 7864320 | tf_op jit(solution)/shard_map/attend_back/pallas_call | solution.py:256
  590.9 8.4 convolution_convert_fusion.6
  603.2 7.8 reshape.202
  611.1 5.6 pad.19
  616.8 5.8 convolution_convert_fusion.5
  629.6 9.6 copy.118
  640.6 28.7 %all_to_all.32 = bf16[8,100,384]{2,1,0:T(8,128)(2,1)S(1)} all-to-all(bf16[8,100,384]{2,1,0:T(8,128)(2,1)S(1)} %reshape.199), channel_id=1, replica_groups=mesh['x'=2,'h'=2,'l'=2,'c'=2,'y'=2] {'h','l','c'}, dimensions={0} | all-to-all | bytes 1228800 | tf_op jit(solution)/shard_map/all_to_all | solution.py:389
  670.6 42.9 %reduce-scatter.17.cloned.1.call-done = bf16[112,1600]{1,0:T(8,128)(2,1)} async-done(((bf16[1792,1600]{1,0:T(8,128)(2,1)}), bf16[112,1600]{1,0:T(8,128)(2,1)}) %reduce-scatter.17.cloned.1.call-update) | async-done | bytes 358416 | tf_op jit(solution)/shard_map/reduce_scatter | solution.py:377
  715.2 7.6 convolution_convert_fusion.1
  722.9 9.6 copy.116
  732.5 89.8 %reduce-scatter.25.cloned.1.call-done = bf16[400,1600]{1,0:T(8,128)(2,1)} async-done(((bf16[1600,1600]{1,0:T(8,128)(2,1)}), bf16[400,1600]{1,0:T(8,128)(2,1)}) %reduce-scatter.25.cloned.1.call-update) | async-done | bytes 1280016 | tf_op jit(solution)/shard_map/reduce_scatter | solution.py:367
  831.9 14.4 %all-to-all-done.5 = bf16[4,100,1600]{2,1,0:T(8,128)(2,1)S(1)} async-done(((bf16[4,100,1600]{2,1,0:T(8,128)(2,1)}), bf16[4,100,1600]{2,1,0:T(8,128)(2,1)S(1)}, u32[]{:S(2)}, u32[]{:S(2)}) %all-to-all-start.5) | async-done | bytes 1280032 | tf_op jit(solution)/shard_map/all_to_all | solution.py:368
  876.3 91.3 %reduce-scatter.23.cloned.1.call-done = bf16[128,1600]{1,0:T(8,128)(2,1)} async-done(((bf16[2048,1600]{1,0:T(8,128)(2,1)}), bf16[128,1600]{1,0:T(8,128)(2,1)}) %reduce-scatter.23.cloned.1.call-update) | async-done | bytes 409616
  971.5 119.8 %all-reduce.8.cloned.1.call-done = f32[19200]{0:T(1024)} async-done(((f32[19200]{0:T(1024)}), f32[19200]{0:T(1024)}) %all-reduce.8.cloned.1.call-update) | async-done | bytes 76816 | tf_op jit(solution)/shard_map/psum | solution.py:415
  (201 shorter events, 126.2 us)
Async XLA Ops:
  7.2 110.5 %copy-start = (s32[1,2048]{1,0:T(1,128)S(1)}, s32[1,2048]{1,0:T(1,128)}, u32[]{:S(2)}) copy-start(s32[1,2048]{1,0:T(1,128)} %param.17) | copy-start | bytes 24580
  7.2 112.2 %all-gather.20.cloned.1.call-start = ((), (), s32[]{:S(2)}) async-start(), calls=%async_computation.19 | async-start | bytes 1843200 | tf_op jit(solution)/shard_map/all_gather | solution.py:314
  9.9 27.0 %copy-start.9 = (bf16[100,3200]{1,0:T(8,128)(2,1)S(1)}, bf16[100,3200]{1,0:T(8,128)(2,1)}, u32[]{:S(2)}) copy-start(bf16[100,3200]{1,0:T(8,128)(2,1)} %param.27) | copy-start | bytes 1920004
  10.5 27.2 %copy-start.10 = (bf16[3200,100]{0,1:T(8,128)(2,1)S(1)}, bf16[3200,100]{0,1:T(8,128)(2,1)}, u32[]{:S(2)}) copy-start(bf16[3200,100]{0,1:T(8,128)(2,1)} %param.29) | copy-start | bytes 1920004
  35.5 93.2 %all-gather.18.cloned.1.call-start = ((), (), s32[]{:S(2)}) async-start(), calls=%async_computation.18 | async-start | bytes 6963200 | tf_op jit(solution)/shard_map/all_gather | solution.py:293
  36.2 159.0 %all-gather.26.cloned.1.call-start = ((), (), s32[]{:S(2)}) async-start(), calls=%async_computation.22 | async-start | bytes 5883904 | tf_op jit(solution)/shard_map/all_gather | solution.py:293
  38.4 77.3 %copy-start.24 = (s32[1,16]{1,0:T(1,128)S(1)}, s32[1,16]{1,0:T(1,128)}, u32[]{:S(2)}) copy-start(s32[1,16]{1,0:T(1,128)} %param.18) | copy-start | bytes 196
  39.8 76.1 %all-to-all-start.2 = ((bf16[4,100,1600]{2,1,0:T(8,128)(2,1)}), bf16[4,100,1600]{2,1,0:T(8,128)(2,1)S(1)}, u32[]{:S(2)}, u32[]{:S(2)}) async-start(bf16[4,100,1600]{2,1,0:T(8,128)(2,1)} %pad_maximum_fusion.1), calls=%async_computation.2 | async-start | bytes 2768896 | tf_op jit(solution)/shard_map/all_to_all | solution.py:323
  43.4 258.2 %all-gather.16.cloned.1.call-start = ((), (), s32[]{:S(2)}) async-start(), calls=%async_computation.13 | async-start | bytes 6656000 | tf_op jit(solution)/shard_map/all_gather | solution.py:293
  118.6 14.3 %copy-start.14 = (s32[2048]{0:T(1024)}, s32[2048]{0:T(1024)S(1)}, u32[]{:S(2)}) copy-start(s32[2048]{0:T(1024)S(1)} %select_reduce_fusion) | copy-start | bytes 24580
  121.3 16.8 %copy-start.7 = (bf16[1600,384]{1,0:T(8,128)(2,1)}, bf16[1600,384]{1,0:T(8,128)(2,1)S(1)}, u32[]{:S(2)}) copy-start(bf16[1600,384]{1,0:T(8,128)(2,1)S(1)} %reshape.190) | copy-start | bytes 3686404
  171.1 32.1 %all-to-all-start.1 = ((bf16[16,128,128]{1,2,0:T(8,128)(2,1)}), bf16[16,128,128]{1,2,0:T(8,128)(2,1)S(1)}, u32[]{:S(2)}, u32[]{:S(2)}) async-start(bf16[16,128,128]{1,2,0:T(8,128)(2,1)} %copy.100), calls=%async_computation.1 | async-start | bytes 1048576 | tf_op jit(solution)/shard_map/all_to_all | solution.py:346
  174.7 158.4 %all-gather.14.cloned.1.call-start = ((), (), s32[]{:S(2)}) async-start(), calls=%async_computation.12 | async-start | bytes 3686400 | tf_op jit(solution)/shard_map/all_gather | solution.py:293
  175.2 28.0 %copy-start.3 = (bf16[1,128,1600]{1,2,0:T(8,128)(2,1)S(1)}, bf16[1,128,1600]{1,2,0:T(8,128)(2,1)}, u32[]{:S(2)}) copy-start(bf16[1,128,1600]{1,2,0:T(8,128)(2,1)} %param.16) | copy-start | bytes 1228804
  210.1 155.7 %all-gather.22.cloned.1.call-start = ((), (), s32[]{:S(2)}) async-start(), calls=%async_computation.20 | async-start | bytes 3686400 | tf_op jit(solution)/shard_map/all_gather | solution.py:293
  210.7 250.1 %reduce-scatter.21.cloned.1.call-start = ((), (), s32[]{:S(2)}) async-start(), calls=%async_computation.24 | async-start | bytes 3833856
  386.9 150.0 %reduce-scatter.19.cloned.1.call-start = ((), (), s32[]{:S(2)}) async-start(), calls=%async_computation.23 | async-start | bytes 3833856
  401.4 137.4 %copy-start.5 = (bf16[1,128,1600]{1,2,0:T(8,128)(2,1)S(1)}, bf16[1,128,1600]{1,2,0:T(8,128)(2,1)}, u32[]{:S(2)}) copy-start(bf16[1,128,1600]{1,2,0:T(8,128)(2,1)} %param.31) | copy-start | bytes 1228804
  401.5 237.9 %reduce-scatter.15.cloned.1.call-start = ((), (), s32[]{:S(2)}) async-start(), calls=%async_computation.14 | async-start | bytes 1843200 | tf_op jit(solution)/shard_map/reduce_scatter | solution.py:388
  599.3 114.1 %reduce-scatter.17.cloned.1.call-start = ((), (), s32[]{:S(2)}) async-start(), calls=%async_computation.16 | async-start | bytes 6336512 | tf_op jit(solution)/shard_map/reduce_scatter | solution.py:377
  616.7 205.7 %reduce-scatter.25.cloned.1.call-start = ((), (), s32[]{:S(2)}) async-start(), calls=%async_computation.26 | async-start | bytes 6656000 | tf_op jit(solution)/shard_map/reduce_scatter | solution.py:367
  639.2 76.0 %copy-start.8 = (bf16[1600,384]{1,0:T(8,128)(2,1)S(1)}, bf16[1600,384]{1,0:T(8,128)(2,1)}, u32[]{:S(2)}) copy-start(bf16[1600,384]{1,0:T(8,128)(2,1)} %copy-done.7) | copy-start | bytes 3686404
  639.2 216.3 %all-gather.24.cloned.1.call-start = ((), (), s32[]{:S(2)}) async-start(), calls=%async_computation.21 | async-start | bytes 1843200 | tf_op jit(solution)/shard_map/all_gather | solution.py:390
  670.3 204.2 %all-reduce.10.cloned.1.call-start = ((), (), s32[]{:S(2)}) async-start(), calls=%async_computation.17 | async-start | bytes 692224 | tf_op jit(solution)/shard_map/psum | solution.py:378
  715.2 252.4 %reduce-scatter.23.cloned.1.call-start = ((), (), s32[]{:S(2)}) async-start(), calls=%async_computation.25 | async-start | bytes 7241728
  732.5 96.0 %copy-start.6 = (bf16[1,128,1600]{1,2,0:T(8,128)(2,1)S(1)}, bf16[1,128,1600]{1,2,0:T(8,128)(2,1)}, u32[]{:S(2)}) copy-start(bf16[1,128,1600]{1,2,0:T(8,128)(2,1)} %param.31) | copy-start | bytes 1228804
  824.7 21.6 %all-to-all-start.5 = ((bf16[4,100,1600]{2,1,0:T(8,128)(2,1)}), bf16[4,100,1600]{2,1,0:T(8,128)(2,1)S(1)}, u32[]{:S(2)}, u32[]{:S(2)}) async-start(bf16[4,100,1600]{2,1,0:T(8,128)(2,1)} %reshape.204), calls=%async_computation.7 | async-start | bytes 2768896 | tf_op jit(solution)/shard_map/all_to_all | solution.py:368
  828.2 263.1 %all-reduce.8.cloned.1.call-start = ((), (), s32[]{:S(2)}) async-start(), calls=%async_computation.15 | async-start | bytes 155648 | tf_op jit(solution)/shard_map/psum | solution.py:415
  870.1 99.4 %copy-start.11 = (f32[1600]{0:T(1024)S(1)}, f32[1600]{0:T(1024)}, u32[]{:S(2)}) copy-start(f32[1600]{0:T(1024)} %get-tuple-element.90) | copy-start | bytes 19204
  870.1 99.4 %copy-start.12 = (f32[1600]{0:T(1024)S(1)}, f32[1600]{0:T(1024)}, u32[]{:S(2)}) copy-start(f32[1600]{0:T(1024)} %get-tuple-element.96) | copy-start | bytes 19204
  870.1 99.4 %copy-start.13 = (f32[1600]{0:T(1024)S(1)}, f32[1600]{0:T(1024)}, u32[]{:S(2)}) copy-start(f32[1600]{0:T(1024)} %get-tuple-element.98) | copy-start | bytes 19204
  870.1 225.3 %copy-start.1 = (s32[1,2048]{1,0:T(1,128)S(1)}, s32[1,2048]{1,0:T(1,128)}, u32[]{:S(2)}) copy-start(s32[1,2048]{1,0:T(1,128)} %param.17) | copy-start | bytes 24580
  (15 other events, 86.8 us)
Sparse Core Ops, SparseCore 0:
  35.6 22.2 all-gather.19
  60.0 68.6 all-gather.17
  130.9 64.2 all-gather.25
  197.5 104.0 all-gather.15
  303.5 29.5 all-gather.13
  334.4 31.3 all-gather.21
  387.0 73.6 reduce-scatter.20
  463.1 73.7 reduce-scatter.18
  599.4 21.6 reduce-scatter.14
  625.5 87.8 reduce-scatter.16
  716.8 105.5 reduce-scatter.24
  824.4 22.3 all-gather.23
  849.7 24.6 all-reduce.9
  878.8 88.7 reduce-scatter.22
  973.0 118.2 all-reduce.7

commit v2 on v1

--- a/solution.py
+++ b/solution.py
@@ -270,6 +270,499 @@
     )(inv, low, qkv, out, grad, lse, start3)
 
 
+class Place:
+    def __init__(self, whole_line):
+        self.x, self.h, self.l, self.c, self.y = (lax.axis_index(a) for a in ("x", "h", "l", "c", "y"))
+        self.whole_line = whole_line
+        self.n_z = 2 * lax.axis_size("h") if whole_line else 2
+        self.z = self.h * 2 + self.l if whole_line else self.l
+        self.ctx = self.z * 2 + self.c
+        self.slot = self.ctx * 2 + self.y
+
+    def at_z(self, z):
+        return {"h": z // 2, "l": lax.rem(z, 2)} if self.whole_line else {"l": z}
+
+    def at_ctx(self, k):
+        return dict(self.at_z(k // 2), c=lax.rem(k, 2))
+
+    def at_slot(self, s):
+        return dict(self.at_ctx(s // 2), y=lax.rem(s, 2))
+
+    def far_z(self):
+        order = []
+        for step in range(1, self.n_z // 2 + 1):
+            order += [step] if 2 * step == self.n_z else [step, self.n_z - step]
+        return [lax.rem(self.z + step, self.n_z) for step in order]
+
+    def slot_of(self, z, c, y):
+        return (z * 2 + c) * 2 + y
+
+
+class Copies:
+    def __init__(self, sems):
+        self.sems = sems
+        self.begun = []
+
+    def send(self, src, dst, recv, peer):
+        at = len(self.begun)
+        copy = pltpu.make_async_remote_copy(
+            src_ref=src,
+            dst_ref=dst,
+            send_sem=self.sems.at[at],
+            recv_sem=recv,
+            device_id=peer,
+            device_id_type=pl.DeviceIdType.MESH,
+        )
+        copy.start()
+        self.begun.append(copy.wait_send)
+
+    def local(self, src, dst, sem=None):
+        copy = pltpu.make_async_copy(src, dst, self.sems.at[len(self.begun)] if sem is None else sem)
+        copy.start()
+        self.begun.append(copy.wait if sem is None else (lambda: None))
+        return copy
+
+    def arrived(self, dst, recv, peer):
+        pltpu.make_async_remote_copy(
+            src_ref=dst,
+            dst_ref=dst,
+            send_sem=self.sems.at[0],
+            recv_sem=recv,
+            device_id=peer,
+            device_id_type=pl.DeviceIdType.MESH,
+        ).wait_recv()
+
+    def finish(self):
+        for wait in self.begun:
+            wait()
+
+
+def meet(peers):
+    barrier = pltpu.get_barrier_semaphore()
+    for peer in peers:
+        pl.semaphore_signal(barrier, inc=1, device_id=peer, device_id_type=pl.DeviceIdType.MESH)
+    pl.semaphore_wait(barrier, len(peers))
+
+
+def others(me, count):
+    return [lax.rem(me + step, count) for step in range(1, count)]
+
+
+ANY = pl.BlockSpec(memory_space=pl.ANY)
+IN_VMEM = pl.BlockSpec(memory_space=pltpu.VMEM)
+
+
+def dma_sems(*counts):
+    return [pltpu.SemaphoreType.DMA((count,)) for count in counts]
+
+
+def comm_params(collective_id):
+    return pltpu.CompilerParams(
+        collective_id=collective_id, has_side_effects=True, vmem_limit_bytes=VMEM_LIMIT
+    )
+
+
+def gather_begin(place, own, out, copies, recv):
+    peer_y, peer_c = {"y": 1 - place.y}, {"c": 1 - place.c}
+    copies.local(own, out.at[place.slot])
+    for z in place.far_z():
+        copies.send(own, out.at[place.slot], recv.at[place.slot], place.at_z(z))
+    copies.send(own, out.at[place.slot], recv.at[place.slot], peer_y)
+    copies.send(own, out.at[place.slot], recv.at[place.slot], peer_c)
+
+
+def gather_middle(place, out, copies, recv):
+    peer_y, peer_c = {"y": 1 - place.y}, {"c": 1 - place.c}
+    for z in place.far_z():
+        at = place.slot_of(z, place.c, place.y)
+        copies.arrived(out.at[at], recv.at[at], place.at_z(z))
+        copies.send(out.at[at], out.at[at], recv.at[at], peer_y)
+        copies.send(out.at[at], out.at[at], recv.at[at], peer_c)
+    for z in [place.z] + place.far_z():
+        at = place.slot_of(z, place.c, 1 - place.y)
+        copies.arrived(out.at[at], recv.at[at], peer_y)
+        copies.send(out.at[at], out.at[at], recv.at[at], peer_c)
+
+
+def gather_end(place, out, copies, recv):
+    for z in [place.z] + place.far_z():
+        for y in (place.y, 1 - place.y):
+            at = place.slot_of(z, 1 - place.c, y)
+            copies.arrived(out.at[at], recv.at[at], {"c": 1 - place.c})
+
+
+def gather_copies(n_z):
+    return 4 * n_z
+
+
+def group_gather_kernel(own, out, send, recv):
+    place = Place(False)
+    copies = Copies(send)
+    meet([place.at_z(1 - place.z), {"y": 1 - place.y}, {"c": 1 - place.c}])
+    gather_begin(place, own, out, copies, recv)
+    gather_middle(place, out, copies, recv)
+    gather_end(place, out, copies, recv)
+    copies.finish()
+
+
+def group_gather(value, collective_id):
+    return pl.pallas_call(
+        group_gather_kernel,
+        out_shape=jax.ShapeDtypeStruct((8,) + value.shape, value.dtype),
+        in_specs=[ANY],
+        out_specs=ANY,
+        scratch_shapes=dma_sems(gather_copies(2), 8),
+        compiler_params=comm_params(collective_id),
+        name="group_gather",
+    )(value)
+
+
+def opening_kernel(own, blocks, out, blocks_all, send, recv, recv_w):
+    place = Place(True)
+    n_ctx = blocks.shape[0]
+    copies = Copies(send)
+    peer_x = {"x": 1 - place.x}
+    far_ctx = others(place.ctx, n_ctx)
+    meet([place.at_ctx(k) for k in far_ctx] + [{"y": 1 - place.y}, peer_x])
+    mine = blocks_all.at[place.x, place.ctx]
+
+    def sem_w(x, k):
+        return recv_w.at[x * n_ctx + k]
+
+    gather_begin(place, own, out, copies, recv)
+    for k in far_ctx:
+        copies.send(blocks.at[k], mine, sem_w(place.x, place.ctx), place.at_ctx(k))
+    copies.local(blocks.at[place.ctx], mine)
+    copies.send(blocks.at[place.ctx], mine, sem_w(place.x, place.ctx), peer_x)
+    gather_middle(place, out, copies, recv)
+    for k in far_ctx:
+        block = blocks_all.at[place.x, k]
+        copies.arrived(block, sem_w(place.x, k), place.at_ctx(k))
+        copies.send(block, block, sem_w(place.x, k), peer_x)
+    gather_end(place, out, copies, recv)
+    for k in [place.ctx] + far_ctx:
+        copies.arrived(blocks_all.at[1 - place.x, k], sem_w(1 - place.x, k), peer_x)
+    copies.finish()
+
+
+def opening(own, blocks):
+    n_ctx = blocks.shape[0]
+    return pl.pallas_call(
+        opening_kernel,
+        out_shape=(
+            jax.ShapeDtypeStruct((2 * n_ctx,) + own.shape, own.dtype),
+            jax.ShapeDtypeStruct((2,) + blocks.shape, blocks.dtype),
+        ),
+        in_specs=[ANY, ANY],
+        out_specs=(ANY, ANY),
+        scratch_shapes=dma_sems(gather_copies(n_ctx // 2) + 2 * n_ctx, 2 * n_ctx, 2 * n_ctx),
+        compiler_params=comm_params(1),
+        name="opening",
+    )(own, blocks)
+
+
+def to_tokens_kernel(src, dst, send, recv):
+    place = Place(True)
+    copies = Copies(send)
+    count, width = src.shape[0], src.shape[2]
+    far = others(place.slot, count)
+    meet([place.at_slot(s) for s in far])
+
+    def columns(s):
+        return dst.at[:, pl.ds(pl.multiple_of(s * width, width), width)]
+
+    for s in far:
+        copies.send(src.at[s], columns(place.slot), recv.at[place.slot], place.at_slot(s))
+    copies.local(src.at[place.slot], columns(place.slot))
+    for s in far:
+        copies.arrived(columns(s), recv.at[s], place.at_slot(s))
+    copies.finish()
+
+
+def to_tokens(value):
+    count, tokens, width = value.shape
+    return pl.pallas_call(
+        to_tokens_kernel,
+        out_shape=jax.ShapeDtypeStruct((tokens, count * width), value.dtype),
+        in_specs=[ANY],
+        out_specs=ANY,
+        scratch_shapes=dma_sems(count, count),
+        compiler_params=comm_params(2),
+        name="to_tokens",
+    )(value)
+
+
+def to_heads_kernel(src, dst, send, recv):
+    place = Place(True)
+    copies = Copies(send)
+    count, width = dst.shape[0], dst.shape[2]
+    far = others(place.slot, count)
+    meet([place.at_slot(s) for s in far])
+
+    def columns(s):
+        return src.at[:, pl.ds(pl.multiple_of(s * width, width), width)]
+
+    for s in far:
+        copies.send(columns(s), dst.at[place.slot], recv.at[place.slot], place.at_slot(s))
+    copies.local(columns(place.slot), dst.at[place.slot])
+    for s in far:
+        copies.arrived(dst.at[s], recv.at[s], place.at_slot(s))
+    copies.finish()
+
+
+def to_heads(value, count):
+    tokens, width = value.shape[0], value.shape[1] // count
+    return pl.pallas_call(
+        to_heads_kernel,
+        out_shape=jax.ShapeDtypeStruct((count, tokens, width), value.dtype),
+        in_specs=[ANY],
+        out_specs=ANY,
+        scratch_shapes=dma_sems(count, count),
+        compiler_params=comm_params(3),
+        name="to_heads",
+    )(value)
+
+
+class Scatter:
+    def __init__(self, place, part, held, from_c, from_y, from_z, out, copies, loads, rc, ry, rz):
+        self.__dict__.update(locals())
+
+    def order(self):
+        return self.place.far_z() + [self.place.z]
+
+    def begin(self):
+        p = self.place
+        for y in (1 - p.y, p.y):
+            for z in self.order():
+                at = z * 2 + y
+                self.copies.send(
+                    self.part.at[p.slot_of(z, 1 - p.c, y)], self.from_c.at[at], self.rc.at[at], {"c": 1 - p.c}
+                )
+                self.copies.local(self.part.at[p.slot_of(z, p.c, y)], self.held.at[at], self.loads.at[at])
+
+    def add_c(self, z, y):
+        at = z * 2 + y
+        self.copies.arrived(self.from_c.at[at], self.rc.at[at], {"c": 1 - self.place.c})
+        pltpu.make_async_copy(self.held.at[at], self.held.at[at], self.loads.at[at]).wait()
+        self.from_c[at] = self.from_c[at] + self.held[at]
+
+    def over_c_far(self):
+        p = self.place
+        for z in self.order():
+            self.add_c(z, 1 - p.y)
+            self.copies.send(self.from_c.at[z * 2 + 1 - p.y], self.from_y.at[z], self.ry.at[z], {"y": 1 - p.y})
+
+    def over_c_near(self):
+        for z in self.order():
+            self.add_c(z, self.place.y)
+
+    def over_y(self):
+        p = self.place
+        for z in self.order():
+            self.copies.arrived(self.from_y.at[z], self.ry.at[z], {"y": 1 - p.y})
+            self.from_y[z] = self.from_y[z] + self.from_c[z * 2 + p.y]
+            if z is not p.z:
+                self.copies.send(self.from_y.at[z], self.from_z.at[p.z], self.rz.at[p.z], p.at_z(z))
+
+    def over_z(self):
+        p = self.place
+        total = self.from_y[p.z].astype(F32)
+        for z in p.far_z():
+            self.copies.arrived(self.from_z.at[z], self.rz.at[z], p.at_z(z))
+            total = total + self.from_z[z].astype(F32)
+        self.out[...] = total
+
+
+def scatter_scratch(n_z, block):
+    return [
+        pltpu.VMEM((2 * n_z,) + block, B16),
+        pltpu.VMEM((2 * n_z,) + block, B16),
+        pltpu.VMEM((n_z,) + block, B16),
+        pltpu.VMEM((n_z,) + block, B16),
+    ]
+
+
+def scatter_sems(n_z, more=0):
+    return dma_sems(6 * n_z + more, 2 * n_z, 2 * n_z, n_z, n_z)
+
+
+def group_scatter_kernel(part, out, held, from_c, from_y, from_z, send, loads, rc, ry, rz):
+    place = Place(False)
+    copies = Copies(send)
+    meet([place.at_z(1 - place.z), {"y": 1 - place.y}, {"c": 1 - place.c}])
+    sums = Scatter(place, part, held, from_c, from_y, from_z, out, copies, loads, rc, ry, rz)
+    sums.begin()
+    sums.over_c_far()
+    sums.over_c_near()
+    sums.over_y()
+    sums.over_z()
+    copies.finish()
+
+
+def group_scatter(part, collective_id):
+    block = part.shape[1:]
+    return pl.pallas_call(
+        group_scatter_kernel,
+        out_shape=jax.ShapeDtypeStruct(block, F32),
+        in_specs=[ANY],
+        out_specs=IN_VMEM,
+        scratch_shapes=scatter_scratch(2, block) + scatter_sems(2),
+        compiler_params=comm_params(collective_id),
+        name="group_scatter",
+    )(part)
+
+
+def closing_kernel(
+    part, grads, out, grads_out, held, from_c, from_y, from_z, own_x, from_x,
+    send, loads, rc, ry, rz, load_x, rx, rk, rg,
+):
+    place = Place(True)
+    n_ctx = grads.shape[1]
+    copies = Copies(send)
+    far_ctx = others(place.ctx, n_ctx)
+    peer_x, peer_y = {"x": 1 - place.x}, {"y": 1 - place.y}
+    meet([place.at_ctx(k) for k in far_ctx] + [peer_y, peer_x])
+    sums = Scatter(place, part, held, from_c, from_y, from_z, out, copies, loads, rc, ry, rz)
+    sums.begin()
+    for k in far_ctx + [place.ctx]:
+        copies.send(grads.at[1 - place.x, k], from_x.at[k], rx.at[k], peer_x)
+        copies.local(grads.at[place.x, k], own_x.at[k], load_x.at[k])
+    sums.over_c_far()
+    mine = grads_out.at[place.y, place.ctx]
+    for k in far_ctx + [place.ctx]:
+        copies.arrived(from_x.at[k], rx.at[k], peer_x)
+        pltpu.make_async_copy(own_x.at[k], own_x.at[k], load_x.at[k]).wait()
+        from_x[k] = from_x[k] + own_x[k]
+        if k is not place.ctx:
+            copies.send(from_x.at[k], mine, rk.at[place.ctx], place.at_ctx(k))
+    copies.local(from_x.at[place.ctx], mine)
+    copies.send(from_x.at[place.ctx], mine, rg.at[place.ctx], peer_y)
+    sums.over_c_near()
+    sums.over_y()
+    for k in far_ctx:
+        block = grads_out.at[place.y, k]
+        copies.arrived(block, rk.at[k], place.at_ctx(k))
+        copies.send(block, block, rg.at[k], peer_y)
+    sums.over_z()
+    for k in [place.ctx] + far_ctx:
+        copies.arrived(grads_out.at[1 - place.y, k], rg.at[k], peer_y)
+    copies.finish()
+
+
+def closing(part, grads):
+    block = part.shape[1:]
+    n_ctx = grads.shape[1]
+    n_z = n_ctx // 2
+    piece = grads.shape[1:]
+    return pl.pallas_call(
+        closing_kernel,
+        out_shape=(jax.ShapeDtypeStruct(block, F32), jax.ShapeDtypeStruct((2,) + piece, B16)),
+        in_specs=[ANY, ANY],
+        out_specs=(IN_VMEM, ANY),
+        scratch_shapes=scatter_scratch(n_z, block)
+        + [pltpu.VMEM(piece, B16), pltpu.VMEM(piece, B16)]
+        + scatter_sems(n_z, 5 * n_ctx)
+        + dma_sems(n_ctx, n_ctx, n_ctx, n_ctx),
+        compiler_params=comm_params(4),
+        name="closing",
+    )(part, grads)
+
+
+def vectors_kernel(src, own_out, ff_out, from_all, half, from_y, send, recv, ry):
+    place = Place(True)
+    count = src.shape[0]
+    n_ctx = count // 2
+    copies = Copies(send)
+    me = place.x * n_ctx + place.ctx
+    far = others(me, count)
+    peer_y = {"y": 1 - place.y}
+
+    def peer(k):
+        return dict(place.at_ctx(lax.rem(k, n_ctx)), x=k // n_ctx)
+
+    meet([peer(k) for k in far] + [peer_y])
+    for k in far:
+        copies.send(src.at[k], from_all.at[me], recv.at[me], peer(k))
+    from_all[me] = src[me]
+    for k in far:
+        copies.arrived(from_all.at[k], recv.at[k], peer(k))
+    total = from_all[0, 0:8, :]
+    for k in range(1, count):
+        total = total + from_all[k, 0:8, :]
+    half[...] = total
+    copies.send(half, from_y, ry.at[0], peer_y)
+    for part in range(4):
+        total = from_all[part, 8:16, :]
+        for k in range(part + 4, count, 4):
+            total = total + from_all[k, 8:16, :]
+        ff_out[part] = total
+    copies.arrived(from_y, ry.at[0], peer_y)
+    own_out[...] = half[...] + from_y[...]
+    copies.finish()
+
+
+def vectors_sum(value):
+    count = value.shape[0]
+    flat = jax.ShapeDtypeStruct((8, 128), F32)
+    return pl.pallas_call(
+        vectors_kernel,
+        out_shape=(flat, jax.ShapeDtypeStruct((4, 8, 128), F32)),
+        in_specs=[IN_VMEM],
+        out_specs=(IN_VMEM, IN_VMEM),
+        scratch_shapes=[
+            pltpu.VMEM(value.shape, F32),
+            pltpu.VMEM((8, 128), F32),
+            pltpu.VMEM((8, 128), F32),
+        ]
+        + dma_sems(count + 1, count, 1),
+        compiler_params=comm_params(5),
+        name="vectors_sum",
+    )(value)
+
+
+def shift_perm(count, step):
+    return [(i, (i + step) % count) for i in range(count)]
+
+
+def spread(blocks, n_h):
+    lc, h, x = lax.axis_index(("l", "c")), lax.axis_index("h"), lax.axis_index("x")
+
+    def pick(value, at):
+        return lax.dynamic_index_in_dim(value, at, 0, False)
+
+    whole = jnp.zeros((2, n_h) + blocks.shape, blocks.dtype)
+    mine = jnp.zeros(blocks.shape, blocks.dtype)
+    mine = lax.dynamic_update_index_in_dim(mine, pick(blocks, lc), lc, 0)
+    for step in range(1, 4):
+        got = lax.ppermute(pick(blocks, lc ^ step), ("l", "c"), [(i, i ^ step) for i in range(4)])
+        mine = lax.dynamic_update_index_in_dim(mine, got, lc ^ step, 0)
+    line = jnp.zeros((n_h,) + blocks.shape, blocks.dtype)
+    line = lax.dynamic_update_index_in_dim(line, mine, h, 0)
+    for step in range(1, n_h):
+        got = lax.ppermute(mine, "h", shift_perm(n_h, step))
+        line = lax.dynamic_update_index_in_dim(line, got, lax.rem(h + n_h - step, n_h), 0)
+    whole = lax.dynamic_update_index_in_dim(whole, line, x, 0)
+    got = lax.ppermute(line, "x", shift_perm(2, 1))
+    return lax.dynamic_update_index_in_dim(whole, got, 1 - x, 0)
+
+
+def unspread(grad, n_h):
+    lc, h, x = lax.axis_index(("l", "c")), lax.axis_index("h"), lax.axis_index("x")
+
+    def pick(value, at):
+        return lax.dynamic_index_in_dim(value, at, 0, False)
+
+    line = pick(grad, x) + lax.ppermute(pick(grad, 1 - x), "x", shift_perm(2, 1))
+    mine = pick(line, h)
+    for step in range(1, n_h):
+        mine = mine + lax.ppermute(pick(line, lax.rem(h + step, n_h)), "h", shift_perm(n_h, step))
+    out = lax.dynamic_update_index_in_dim(jnp.zeros_like(mine), pick(mine, lc), lc, 0)
+    for step in range(1, 4):
+        got = lax.ppermute(pick(mine, lc ^ step), ("l", "c"), [(i, i ^ step) for i in range(4)])
+        out = lax.dynamic_update_index_in_dim(out, got, lc ^ step, 0)
+    return out
+
+
 def on_device(
     sizes, block_input, segment_ids, slot_order, first_gain, first_shift, qkv_weight, qv_bias, out_weight, out_bias,
     second_gain, second_shift, fc_weight, fc_bias, proj_weight, proj_bias, out_grad,
@@ -297,7 +790,17 @@
             first_gain, first_shift, out_bias, second_gain, second_shift, proj_bias, qv_bias,
         ]
     )
-    smalls = lax.all_gather(small, SHARD, axis=0, tiled=False).astype(F32)
+    row_pad = -rows % 16
+    packed = jnp.pad(qkv_weight.reshape(rows, 3, feats), ((0, 0), (0, 0), (0, padded - feats)))
+    packed = lax.dynamic_index_in_dim(packed.reshape(rows, 3, n_ctx, n_y, pair), y_at, 3, False)
+    packed = packed.transpose(2, 0, 1, 3).reshape(n_ctx, rows, 3 * pair)
+    small = jnp.pad(small, (0, row_pad * 3 * pair - small.shape[0])).reshape(1, row_pad, 3 * pair)
+    packed = jnp.concatenate([packed, jnp.broadcast_to(small, (n_ctx, row_pad, 3 * pair))], axis=1)
+    all_input, packed = opening(block_input[0], packed)
+    all_input = all_input.reshape(n_slot * slot_len, feats)
+    packed = packed.reshape(n_shard, rows + row_pad, 3 * pair)
+    w_qkv = packed[:, :rows].reshape(feats, 3 * pair)
+    smalls = packed[:, rows:].reshape(n_shard, -1)[:, : 8 * rows].astype(F32)
     gain_one, shift_one, bias_out, gain_two, shift_two, bias_proj = [
         smalls[:, i * rows : (i + 1) * rows].reshape(feats) for i in range(6)
     ]
@@ -307,22 +810,8 @@
     )
     bias_qkv = jnp.concatenate([bias_pair[0], jnp.zeros((pair,), F32), bias_pair[1]])
 
-    packed = jnp.pad(qkv_weight.reshape(rows, 3, feats), ((0, 0), (0, 0), (0, padded - feats)))
-    packed = lax.dynamic_index_in_dim(packed.reshape(rows, 3, n_ctx, n_y, pair), y_at, 3, False)
-    packed = packed.transpose(2, 0, 1, 3).reshape(n_ctx, rows, 3 * pair)
-    packed = lax.all_to_all(packed, CTX, 0, 0, tiled=True)
-    w_qkv = lax.all_gather(packed, "x", axis=0, tiled=False).reshape(feats, 3 * pair)
-
-    ffn = jnp.concatenate(
-        [
-            fc_weight.reshape(rows, 4, ff_own).transpose(1, 0, 2),
-            proj_weight.reshape(4, ff_own, rows).transpose(0, 2, 1),
-        ],
-        axis=2,
-    )
-    ffn = lax.all_to_all(ffn, ("l", "c"), 0, 0, tiled=True)
-    ffn = gather(ffn.reshape(4 * rows, 2 * ff_own), ("x", "h"))
-    w_fc, w_proj = ffn[:, :ff_own], ffn[:, ff_own:]
+    w_fc = spread(fc_weight.reshape(rows, 4, ff_own).transpose(1, 0, 2), n_h).reshape(feats, ff_own)
+    w_proj = spread(proj_weight.reshape(4, ff_own, rows).transpose(0, 2, 1), n_h).reshape(feats, ff_own)
     w_out = gather(out_weight, SHARD)
     b_fc = lax.dynamic_slice_in_dim(fc_bias, lc_at * ff_own, ff_own, 0).astype(F32)
 
@@ -338,20 +827,18 @@
 
     own_input = block_input[0]
     own_wide = own_input.astype(F32)
-    all_input = gather(own_input, ROW)
     normed_all, unused = norm_forward(all_input.astype(F32))
     norm_one = (normed_all * gain_one + shift_one).astype(B16)
     qkv = (dot(norm_one, w_qkv, 1, 0) + bias_qkv).astype(B16)
     heads_out, lse = attend(inv, low, qkv, start3, slot_len, head)
-    attention = lax.all_to_all(heads_out.reshape(n_slot, slot_len, pair), ROW, 0, 0, tiled=True)
-    attention = attention.transpose(1, 0, 2).reshape(slot_len, padded)[:, :feats]
+    attention = to_tokens(heads_out.reshape(n_slot, slot_len, pair))[:, :feats]
     hidden = own_wide + dot(attention, w_out, 1, 0) + bias_out
     normed_two, inv_two = norm_forward(hidden)
     norm_two = (normed_two * gain_two + shift_two).astype(B16)
     grad_own = out_grad[0]
     grad_wide = grad_own.astype(F32)
     grad_all = gather(grad_own, FFG)
-    norm_all = gather(norm_two, FFG)
+    norm_all = group_gather(norm_two, 6).reshape(-1, feats)
     preact = dot(norm_all, w_fc, 1, 0) + b_fc
     activated, derivative = gelu_parts(preact)
     activation = activated.astype(B16)
@@ -362,33 +849,31 @@
     dpreact = dot(grad_all, w_proj, 1, 0) * derivative
     dpreact_b = dpreact.astype(B16)
     dnorm_part = dot(dpreact_b, w_fc, 1, 1).astype(B16)
-    dnorm_two = lax.psum_scatter(dnorm_part, FFG, scatter_dimension=0, tiled=True).astype(F32)
-    ffn_grad = jnp.concatenate([dot(norm_all, dpreact_b, 0, 0), dot(grad_all, activation, 0, 0)], axis=1).astype(B16)
-    ffn_grad = lax.psum_scatter(ffn_grad, ("x", "h"), scatter_dimension=0, tiled=True)
-    ffn_grad = lax.all_to_all(ffn_grad.reshape(4, rows, 2 * ff_own), ("l", "c"), 0, 0, tiled=True).astype(F32)
-    fc_grad = ffn_grad[:, :, :ff_own].transpose(1, 0, 2).reshape(rows, 4 * ff_own)
-    proj_grad = ffn_grad[:, :, ff_own:].transpose(0, 2, 1).reshape(4 * ff_own, rows)
+    dnorm_two = group_scatter(dnorm_part.reshape(8, slot_len, feats), 7)
+    ffn_shape = (n_x, n_h, 4, rows, ff_own)
+    proj_grad = unspread(dot(grad_all, activation, 0, 0).astype(B16).reshape(ffn_shape), n_h)
+    proj_grad = proj_grad.transpose(0, 2, 1).reshape(4 * ff_own, rows).astype(F32)
+    fc_grad = unspread(dot(norm_all, dpreact_b, 0, 0).astype(B16).reshape(ffn_shape), n_h)
+    fc_grad = fc_grad.transpose(1, 0, 2).reshape(rows, 4 * ff_own).astype(F32)
 
     dhidden = grad_wide + norm_backward(dnorm_two, normed_two, inv_two, gain_two)
     dhidden_b = dhidden.astype(B16)
     out_part = dot(attention, dhidden_b, 0, 0).astype(B16).reshape(n_shard, rows, feats)
-    row_pad = -rows % 16
     out_part = jnp.pad(out_part, ((0, 0), (0, row_pad), (0, 0))).reshape(-1, feats)
     out_grad_w = lax.psum_scatter(out_part, SHARD, scatter_dimension=0, tiled=True)[:rows]
     out_grad_w = lax.psum(out_grad_w, "y").astype(F32)
 
     dattention = dot(dhidden_b, w_out, 1, 1).astype(B16)
-    dattention = jnp.pad(dattention, ((0, 0), (0, padded - feats))).reshape(slot_len, n_slot, pair).transpose(1, 0, 2)
-    dattention = lax.all_to_all(dattention, ROW, 0, 0, tiled=True).reshape(n_slot * slot_len, pair)
+    dattention = jnp.pad(dattention, ((0, 0), (0, padded - feats)))
+    dattention = to_heads(dattention, n_slot).reshape(n_slot * slot_len, pair)
     dqkv = attend_back(inv, low, qkv, heads_out, dattention, lse, start3, slot_len, head)
     dqkv_b = dqkv.astype(B16)
     dnorm_one_part = dot(dqkv_b, w_qkv, 1, 1).astype(B16)
-    dnorm_one = lax.psum_scatter(dnorm_one_part, ROW, scatter_dimension=0, tiled=True).astype(F32)
-    qkv_part = dot(norm_one, dqkv_b, 0, 0).astype(B16)
-    qkv_part = lax.psum_scatter(qkv_part, "x", scatter_dimension=0, tiled=True).reshape(n_ctx, rows, 3 * pair)
-    qkv_part = lax.all_to_all(qkv_part, CTX, 0, 0, tiled=True)
-    qkv_all = lax.all_gather(qkv_part, "y", axis=0, tiled=False)
-    qkv_grad = qkv_all.reshape(n_y, n_ctx, rows, 3, pair).transpose(2, 3, 1, 0, 4).reshape(rows, 3, padded)
+    qkv_part = dot(norm_one, dqkv_b, 0, 0).astype(B16).reshape(n_x, n_ctx, rows, 3 * pair)
+    qkv_part = jnp.pad(qkv_part, ((0, 0), (0, 0), (0, row_pad), (0, 0)))
+    dnorm_one, qkv_all = closing(dnorm_one_part.reshape(n_slot, slot_len, feats), qkv_part)
+    qkv_all = qkv_all[:, :, :rows].reshape(n_y, n_ctx, rows, 3, pair)
+    qkv_grad = qkv_all.transpose(2, 3, 1, 0, 4).reshape(rows, 3, padded)
     qkv_grad = qkv_grad[:, :, :feats].reshape(rows, 3 * feats).astype(F32)
 
     normed_one, inv_one = norm_forward(own_wide)
@@ -407,19 +892,29 @@
             jnp.sum(dnorm_two * normed_two, axis=0),
             jnp.sum(dnorm_two, axis=0),
             jnp.sum(grad_wide, axis=0),
-            placed(dq_sum, padded, slot_at * pair)[:feats],
-            placed(dv_sum, padded, slot_at * pair)[:feats],
-            placed(jnp.sum(dpreact, axis=0), n_y * 4 * ff_own, (y_at * 4 + lc_at) * ff_own),
         ]
     )
-    vectors = lax.psum(vectors, SHARD + ("y",))
-    shard_at = lax.axis_index(SHARD)
+    qv_sums = jnp.concatenate(
+        [placed(dq_sum, padded, slot_at * pair)[:feats], placed(dv_sum, padded, slot_at * pair)[:feats]]
+    )
+    vectors = jnp.concatenate(
+        [
+            vectors.reshape(6, n_shard, rows).transpose(1, 0, 2).reshape(n_shard, 6 * rows),
+            qv_sums.reshape(n_shard, 2 * rows),
+            jnp.zeros((n_shard, 1024 - 8 * rows), F32),
+            jnp.broadcast_to(jnp.sum(dpreact, axis=0)[None], (n_shard, ff_own)),
+            jnp.zeros((n_shard, 1024 - ff_own), F32),
+        ],
+        axis=1,
+    )
+    owned, ff_sums = vectors_sum(vectors.reshape(n_shard, 16, 128))
+    owned = owned.reshape(1024)
+    fc_bias_grad = ff_sums.reshape(4, 1024)[:, :ff_own].reshape(4 * ff_own)
+    qv_grad = owned[6 * rows : 8 * rows]
 
     def own(index):
-        return lax.dynamic_slice_in_dim(vectors, index * feats + shard_at * rows, rows, 0)
-
-    qv_grad = lax.dynamic_slice_in_dim(vectors, 6 * feats + shard_at * 2 * rows, 2 * rows, 0)
-    fc_bias_grad = lax.dynamic_slice_in_dim(vectors, 8 * feats + y_at * 4 * ff_own, 4 * ff_own, 0)
+        return owned[index * rows : (index + 1) * rows]
+
     return (
         block_output[None],
         input_grad[None],

time: 1110 us -> 868 us (0.78)
  waiting for transfers between devices: 668 us -> 132 us
  Pallas kernels: 47.5 us -> 319 us
  local copies, waits for them, and re-layouts: 110 us -> 253 us
  blocking collectives: 143 us -> 0 us
  other arithmetic: 30 us -> 46 us
  starting transfers between devices: 12.1 us -> 23.6 us
    pallas_call x0 -> x7, Pallas kernels: none -> 277 us  [the longest x1 99.5 us: opening(): pl.pallas_call(opening_kernel, out_shape=(jax.ShapeDtypeStruct((2 * n_ctx...]
    unnamed x18 -> x5, waiting for transfers between devices: 226 us -> 0.74 us
    all_gather x5 -> x2, waiting for transfers between devices: 174 us -> 0.01 us  [gather(): return lax.all_gather(value, axes, axis=0, tiled=True)]
    ppermute x0 -> x20, waiting for transfers between devices: none -> 121 us  [the longest x2 45.9 us: unspread(): lax.ppermute(pick(grad, 1 - x), 'x', shift_perm(2, 1))]
    psum x1 -> x0, waiting for transfers between devices: 120 us -> none  [on_device(): vectors = lax.psum(vectors, SHARD + ('y',))]
    reduce_scatter x2 -> x1, waiting for transfers between devices: 89.9 us -> 3 us  [on_device(): lax.psum_scatter(mlp_part, FFG, scatter_dimension=0, tiled=True).astype(F32)]
    all_to_all x3 -> x0, blocking collectives: 73 us -> none  [the longest x1 28.7 us: on_device(): qkv_part = lax.all_to_all(qkv_part, CTX, 0, 0, tiled=True)]
    unnamed x1 -> x0, blocking collectives: 70.5 us -> none
  transfers between devices with their start and end apart: 18 -> 25, of which waited for: 13 -> 9; matrix products, arithmetic and copies ran while one was open for 15% -> 40% of each run, Pallas kernels for 2% -> 37%
where the time goes in v2:
time: 868 us; the launch traced here: 863 us
  Pallas kernels  319 us (37%)
  local copies, waits for them, and re-layouts  253 us (29%)
  waiting for transfers between devices  132 us (15%)
  matrix products  74.8 us (9%)
  other arithmetic  46 us (5%)
  starting transfers between devices  23.6 us (3%)
  between operations  15.5 us (2%)
    pallas_call x1, Pallas kernels, opening(): pl.pallas_call(opening_kernel, out_shape=(jax.ShapeDtypeStruct((2 * n_ctx...  99.5 us
    dot_general x12, matrix products, dot(): lax.dot_general(left, right, (((left_dim,), (right_dim,)), ((), ())), pre...  74.8 us
    pallas_call x1, Pallas kernels, closing(): pl.pallas_call(closing_kernel, out_shape=(jax.ShapeDtypeStruct(block, F32...  72.3 us
    unnamed x108, local copies, waits for them, and re-layouts  47.3 us
    ppermute x2, waiting for transfers between devices, unspread(): lax.ppermute(pick(grad, 1 - x), 'x', shift_perm(2, 1))  45.9 us
    pallas_call x1, Pallas kernels, group_scatter(): pl.pallas_call(group_scatter_kernel, out_shape=jax.ShapeDtypeStruct(block...  45.4 us
    ppermute x2, waiting for transfers between devices, spread(): got = lax.ppermute(mine, 'h', shift_perm(n_h, step))  39.7 us
    ppermute x2, waiting for transfers between devices, unspread(): lax.ppermute(pick(line, lax.rem(h + step, n_h)), 'h', shift_perm(n_h, step))  31.2 us
  transfers between devices with their start and end apart: 25, of which 9 were waited for; matrix products, arithmetic and copies ran while one was open for 40% of the time, Pallas kernels for 37%

profile of v2, /device:TPU:0, one launch (start us, length us, event | category | flops | bytes accessed | tf_op | source)
XLA Modules:
  0.0 862.9 jit_solution(12528001013449546668)
XLA Ops:
  31.2 99.5 %opening.1 = (bf16[16,128,1600]{2,1,0:T(8,128)(2,1)}, bf16[2,8,112,384]{3,2,1,0:T(8,128)(2,1)}) custom-call(bf16[128,1600]{1,0:T(8,128)(2,1)} %bitcast.201, bf16[8,112,384]{2,1,0:T(8,128)(2,1)} %pad_maximum_fusion.blocks), custom_call_target="tpu_custom_call" | custom-call | tf_op jit(solution)/shard_map/opening/pallas_call | solution.py:450
  188.3 28.8 %collective-permute-done.3 = bf16[4,100,800]{2,0,1:T(4,128)(2,1)} collective-permute-done((bf16[4,100,800]{2,0,1:T(4,128)(2,1)S(1)}, bf16[4,100,800]{2,0,1:T(4,128)(2,1)}, u32[]{:S(2)}, u32[]{:S(2)}) %collective-permute-start.3) | collective-permute-done | bytes 640032 | tf_op jit(solution)/shard_map/ppermute | solution.py:742
  219.3 10.9 %collective-permute-done.8 = bf16[4,100,800]{2,0,1:T(4,128)(2,1)S(1)} collective-permute-done((bf16[4,100,800]{2,0,1:T(4,128)(2,1)S(1)}, bf16[4,100,800]{2,0,1:T(4,128)(2,1)S(1)}, u32[]{:S(2)}, u32[]{:S(2)}) %collective-permute-start.8) | collective-permute-done | bytes 640032 | tf_op jit(solution)/shard_map/ppermute | solution.py:742
  232.0 20.2 %attend.1 = (bf16[2048,128]{1,0:T(8,128)(2,1)}, f32[8,2,256]{2,1,0:T(2,128)}) custom-call(s32[16]{0:T(128)} %copy-done.41, s32[8]{0:T(128)} %and_select_fusion.low_ref, bf16[2048,384]{1,0:T(8,128)(2,1)} %add_convert_fusion.1.qkv_ref, s32[8,1,256]{2,1,0:T(1,128)} %bitcast.230), custom_call_target="tpu_custom_call" | custom-call | flops 1073741824 | bytes 2097152 | tf_op jit(solution)/shard_map/attend/pallas_call | solution.py:156
  252.2 12.0 %to_tokens.1 = bf16[128,2048]{1,0:T(8,128)(2,1)} custom-call(bf16[16,128,128]{2,1,0:T(8,128)(2,1)} %bitcast.216), custom_call_target="tpu_custom_call" | custom-call | tf_op jit(solution)/shard_map/to_tokens/pallas_call | solution.py:484
  286.7 8.1 reshape.324
  299.7 23.7 %group_gather.1 = bf16[8,128,1600]{2,1,0:T(8,128)(2,1)} custom-call(bf16[128,1600]{1,0:T(8,128)(2,1)} %add_convert_fusion.2.own), custom_call_target="tpu_custom_call" | custom-call | tf_op jit(solution)/shard_map/group_gather/pallas_call | solution.py:409
  323.4 6.3 fusion.49
  331.4 5.7 convolution_convert_fusion.3
  346.1 9.8 %fusion.48 = (f32[800]{0:T(1024)}, bf16[1024,800]{0,1:T(8,128)(2,1)S(1)}) fusion(f32[1024,800]{0,1:T(8,128)} %copy-done.42, f32[800]{0:T(1024)S(1)} %copy-done.31, bf16[1600,800]{1,0:T(8,128)(2,1)} %reshape.293, bf16[1,1024,1600]{1,2,0:T(8,128)(2,1)} %all-gather.5.cloned.1.call-done), kind=kOutput, calls=%fused_computation.155 | convolution fusion | flops 2638642432 | bytes 10758400 | tf_op jit(solution)/shard_map/dot_general | solution.py:58
  367.8 45.4 %group_scatter.1 = f32[128,1600]{1,0:T(8,128)} custom-call(bf16[8,128,1600]{2,1,0:T(8,128)(2,1)} %bitcast.202), custom_call_target="tpu_custom_call" | custom-call | tf_op jit(solution)/shard_map/group_scatter/pallas_call | solution.py:604
  413.3 8.4 fusion.13
  421.7 15.5 %reshape.326 = bf16[2,2,4,100,800]{3,2,1,0,4:T(4,128)(2,1)} reshape(bf16[1600,800]{0,1:T(8,128)(2,1)} %fusion.13) | data formatting | bytes 5120000 | tf_op jit(solution)/shard_map/reshape | solution.py:854
  447.7 7.5 reshape.303
  455.2 5.5 pad.29
  460.8 7.1 convolution_convert_fusion.4
  467.9 15.6 %reshape.325 = bf16[2,2,4,100,800]{3,2,1,0,4:T(4,128)(2,1)} reshape(bf16[1600,800]{0,1:T(8,128)(2,1)} %convolution_convert_fusion.4) | data formatting | bytes 5120000 | tf_op jit(solution)/shard_map/reshape | solution.py:856
  483.5 5.9 constant_dynamic-slice_fusion.1
  497.0 6.3 collective-permute-start.10
  510.8 7.5 fusion.3
  527.0 17.5 %collective-permute-done.10 = bf16[2,4,100,800]{3,1,2,0:T(4,128)(2,1)} collective-permute-done((bf16[2,4,100,800]{3,1,2,0:T(4,128)(2,1)}, bf16[2,4,100,800]{3,1,2,0:T(4,128)(2,1)}, u32[]{:S(2)}, u32[]{:S(2)}) %collective-permute-start.10) | collective-permute-done | bytes 1280032 | tf_op jit(solution)/shard_map/ppermute | solution.py:755
  550.6 28.5 %collective-permute-done.15 = bf16[2,4,100,800]{3,1,2,0:T(4,128)(2,1)} collective-permute-done((bf16[2,4,100,800]{3,1,2,0:T(4,128)(2,1)}, bf16[2,4,100,800]{3,1,2,0:T(4,128)(2,1)}, u32[]{:S(2)}, u32[]{:S(2)}) %collective-permute-start.15) | collective-permute-done | bytes 1280032 | tf_op jit(solution)/shard_map/ppermute | solution.py:755
  587.0 19.8 %collective-permute-done.11 = bf16[4,100,800]{2,0,1:T(4,128)(2,1)S(1)} collective-permute-done((bf16[4,100,800]{2,0,1:T(4,128)(2,1)}, bf16[4,100,800]{2,0,1:T(4,128)(2,1)S(1)}, u32[]{:S(2)}, u32[]{:S(2)}) %collective-permute-start.11) | collective-permute-done | bytes 640032 | tf_op jit(solution)/shard_map/ppermute | solution.py:758
  610.8 11.4 %collective-permute-done.16 = bf16[4,100,800]{2,0,1:T(4,128)(2,1)S(1)} collective-permute-done((bf16[4,100,800]{2,0,1:T(4,128)(2,1)}, bf16[4,100,800]{2,0,1:T(4,128)(2,1)S(1)}, u32[]{:S(2)}, u32[]{:S(2)}) %collective-permute-start.16) | collective-permute-done | bytes 640032 | tf_op jit(solution)/shard_map/ppermute | solution.py:758
  677.8 12.7 %to_heads.1 = bf16[16,128,128]{2,1,0:T(8,128)(2,1)} custom-call(bf16[128,2048]{1,0:T(8,128)(2,1)} %pad.27.src), custom_call_target="tpu_custom_call" | custom-call | tf_op jit(solution)/shard_map/to_heads/pallas_call | solution.py:515
  690.5 21.6 %attend_back.1 = f32[2048,384]{1,0:T(8,128)} custom-call(s32[16]{0:T(128)} %copy-done.41, s32[8]{0:T(128)} %and_select_fusion.low_ref, bf16[2048,384]{1,0:T(8,128)(2,1)} %add_convert_fusion.1.qkv_ref, bf16[2048,128]{1,0:T(8,128)(2,1)} %get-tuple-element.24.out_ref, bf16[2048,128]{1,0:T(8,128)(2,1)} %bitcast.217, f32[8,2,256]{2,1,0:T(2,128)} %get-tuple-element.25.lse_ref, ...), custom_call_target="tpu_custom_call" | custom-call | flops 2684354560 | bytes 7864320 | tf_op jit(solution)/shard_map/attend_back/pallas_call | solution.py:256
  712.2 7.4 convolution_convert_fusion.1
  719.5 9.8 %copy.310 = bf16[2048,1600]{1,0:T(8,128)(2,1)} copy(bf16[2048,1600]{0,1:T(8,128)(2,1)} %convolution_convert_fusion.1) | data formatting | bytes 13107200 | tf_op jit(solution)/shard_map/convert_element_type | solution.py:871
  729.3 8.5 convolution_convert_fusion.6
  740.4 72.3 %closing.1 = (f32[128,1600]{1,0:T(8,128)}, bf16[2,8,112,384]{3,2,1,0:T(8,128)(2,1)}) custom-call(bf16[16,128,1600]{2,1,0:T(8,128)(2,1)} %bitcast.199, bf16[2,8,112,384]{3,2,1,0:T(8,128)(2,1)} %pad.28.grads), custom_call_target="tpu_custom_call" | custom-call | tf_op jit(solution)/shard_map/closing/pallas_call | solution.py:657
  831.6 11.2 %vectors_sum.1 = (f32[8,128]{1,0:T(8,128)}, f32[4,8,128]{2,1,0:T(8,128)}) custom-call(f32[16,16,128]{2,1,0:T(8,128)} %bitcast.219), custom_call_target="tpu_custom_call" | custom-call | tf_op jit(solution)/shard_map/vectors_sum/pallas_call | solution.py:707
  847.1 6.9 all-reduce.8.cloned.1.call-done
  (322 shorter events, 269.9 us)
Async XLA Ops:
  7.2 134.5 %copy-start = (s32[1,2048]{1,0:T(1,128)S(1)}, s32[1,2048]{1,0:T(1,128)}, u32[]{:S(2)}) copy-start(s32[1,2048]{1,0:T(1,128)} %param.17) | copy-start | bytes 24580
  7.2 279.5 %all-gather.7.cloned.1.call-start = ((), (), s32[]{:S(2)}) async-start(), calls=%async_computation.6 | async-start | bytes 5883904 | tf_op jit(solution)/shard_map/all_gather | solution.py:786
  7.9 338.2 %all-gather.5.cloned.1.call-start = ((), (), s32[]{:S(2)}) async-start(), calls=%async_computation.5 | async-start | bytes 3686400 | tf_op jit(solution)/shard_map/all_gather | solution.py:786
  12.5 142.8 %collective-permute-start = (bf16[100,800]{1,0:T(8,128)(2,1)}, bf16[100,800]{1,0:T(8,128)(2,1)}, u32[]{:S(2)}, u32[]{:S(2)}) collective-permute-start(bf16[100,800]{1,0:T(8,128)(2,1)} %bitcast.191), channel_id=1, source_target_pairs={{0,2},{2,0},{4,6},{6,4},{1,3},{3,1},{5,7},{7,5},{8,10},{10,8},{12,... | collective-permute-start | bytes 480008 | tf_op jit(solution)/shard_map/ppermute | solution.py:737
  13.6 143.0 %collective-permute-start.1 = (bf16[100,800]{1,0:T(8,128)(2,1)}, bf16[100,800]{1,0:T(8,128)(2,1)}, u32[]{:S(2)}, u32[]{:S(2)}) collective-permute-start(bf16[100,800]{1,0:T(8,128)(2,1)} %bitcast.190), channel_id=1, source_target_pairs={{0,4},{2,6},{4,0},{6,2},{1,5},{3,7},{5,1},{7,3},{8,12},{10,14},{12... | collective-permute-start | bytes 480008 | tf_op jit(solution)/shard_map/ppermute | solution.py:737
  16.9 140.9 %collective-permute-start.2 = (bf16[100,800]{1,0:T(8,128)(2,1)}, bf16[100,800]{1,0:T(8,128)(2,1)}, u32[]{:S(2)}, u32[]{:S(2)}) collective-permute-start(bf16[100,800]{1,0:T(8,128)(2,1)} %bitcast.189), channel_id=1, source_target_pairs={{0,6},{2,4},{4,2},{6,0},{1,7},{3,5},{5,3},{7,1},{8,14},{10,12},{12... | collective-permute-start | bytes 480008 | tf_op jit(solution)/shard_map/ppermute | solution.py:737
  20.6 149.1 %collective-permute-start.5 = (bf16[100,800]{1,0:T(8,128)(2,1)}, bf16[100,800]{1,0:T(8,128)(2,1)}, u32[]{:S(2)}, u32[]{:S(2)}) collective-permute-start(bf16[100,800]{1,0:T(8,128)(2,1)} %bitcast.194), channel_id=1, source_target_pairs={{0,2},{2,0},{4,6},{6,4},{1,3},{3,1},{5,7},{7,5},{8,10},{10,8},{12,... | collective-permute-start | bytes 480008 | tf_op jit(solution)/shard_map/ppermute | solution.py:737
  21.4 149.5 %collective-permute-start.6 = (bf16[100,800]{1,0:T(8,128)(2,1)}, bf16[100,800]{1,0:T(8,128)(2,1)}, u32[]{:S(2)}, u32[]{:S(2)}) collective-permute-start(bf16[100,800]{1,0:T(8,128)(2,1)} %bitcast.193), channel_id=1, source_target_pairs={{0,4},{2,6},{4,0},{6,2},{1,5},{3,7},{5,1},{7,3},{8,12},{10,14},{12... | collective-permute-start | bytes 480008 | tf_op jit(solution)/shard_map/ppermute | solution.py:737
  23.3 417.8 %reduce-scatter.3.cloned.1.call-start = ((), (), s32[]{:S(2)}) async-start(), calls=%async_computation.2 | async-start | bytes 3833856 | tf_op jit(solution)/shard_map/reduce_scatter | solution.py:846
  155.3 16.8 %collective-permute-start.7 = (bf16[100,800]{1,0:T(8,128)(2,1)S(1)}, bf16[100,800]{1,0:T(8,128)(2,1)S(1)}, u32[]{:S(2)}, u32[]{:S(2)}) collective-permute-start(bf16[100,800]{1,0:T(8,128)(2,1)S(1)} %bitcast.223), channel_id=1, source_target_pairs={{0,6},{2,4},{4,2},{6,0},{1,7},{3,5},{5,3},{7,1},{8,14},{10,12},{12... | collective-permute-start | bytes 480008 | tf_op jit(solution)/shard_map/ppermute | solution.py:737
  166.5 50.6 %collective-permute-start.3 = (bf16[4,100,800]{2,0,1:T(4,128)(2,1)S(1)}, bf16[4,100,800]{2,0,1:T(4,128)(2,1)}, u32[]{:S(2)}, u32[]{:S(2)}) collective-permute-start(bf16[4,100,800]{2,0,1:T(4,128)(2,1)S(1)} %dynamic_update_slice.84), channel_id=1, source_target_pairs={{0,8},{8,0},{1,9},{9,1},{2,10},{10,2},{3,11},{11,3},{4,12},{12,4},... | collective-permute-start | bytes 1920008 | tf_op jit(solution)/shard_map/ppermute | solution.py:742
  180.1 50.1 %collective-permute-start.8 = (bf16[4,100,800]{2,0,1:T(4,128)(2,1)S(1)}, bf16[4,100,800]{2,0,1:T(4,128)(2,1)S(1)}, u32[]{:S(2)}, u32[]{:S(2)}) collective-permute-start(bf16[4,100,800]{2,0,1:T(4,128)(2,1)S(1)} %dynamic_update_slice.92), channel_id=1, source_target_pairs={{0,8},{8,0},{1,9},{9,1},{2,10},{10,2},{3,11},{11,3},{4,12},{12,4},... | collective-permute-start | bytes 1920008 | tf_op jit(solution)/shard_map/ppermute | solution.py:742
  219.3 50.3 %collective-permute-start.4 = (bf16[2,4,100,800]{3,1,2,0:T(4,128)(2,1)}, bf16[2,4,100,800]{3,1,2,0:T(4,128)(2,1)}, u32[]{:S(2)}, u32[]{:S(2)}) collective-permute-start(bf16[2,4,100,800]{3,1,2,0:T(4,128)(2,1)} %bitcast_dynamic-update-slice_fusion.2), channel_id=1, source_target_pairs={{0,16},{16,0},{1,17},{17,1},{2,18},{18,2},{3,19},{19,3},{4,20},{20... | collective-permute-start | bytes 3840008 | tf_op jit(solution)/shard_map/ppermute | solution.py:745
  231.4 48.0 %collective-permute-start.9 = (bf16[2,4,100,800]{3,1,2,0:T(4,128)(2,1)}, bf16[2,4,100,800]{3,1,2,0:T(4,128)(2,1)}, u32[]{:S(2)}, u32[]{:S(2)}) collective-permute-start(bf16[2,4,100,800]{3,1,2,0:T(4,128)(2,1)} %bitcast_dynamic-update-slice_fusion), channel_id=1, source_target_pairs={{0,16},{16,0},{1,17},{17,1},{2,18},{18,2},{3,19},{19,3},{4,20},{20... | collective-permute-start | bytes 3840008 | tf_op jit(solution)/shard_map/ppermute | solution.py:745
  298.5 138.8 %copy-start.27 = (f32[128]{0:T(128)}, f32[128]{0:T(128)S(1)}, u32[]{:S(2)}) copy-start(f32[128]{0:T(128)S(1)} %broadcast_multiply_fusion.6) | copy-start | bytes 1540
  298.7 138.5 %copy-start.30 = (f32[128]{0:T(128)}, f32[128]{0:T(128)S(1)}, u32[]{:S(2)}) copy-start(f32[128]{0:T(128)S(1)} %add_rsqrt_fusion.2) | copy-start | bytes 1540
  342.6 486.5 %reduce-scatter.5.cloned.1.call-start = ((), (), s32[]{:S(2)}) async-start(), calls=%async_computation.3 | async-start | bytes 6336512 | tf_op jit(solution)/shard_map/reduce_scatter | solution.py:863
  460.7 393.3 %all-reduce.8.cloned.1.call-start = ((), (), s32[]{:S(2)}) async-start(), calls=%async_computation.4 | async-start | bytes 692224 | tf_op jit(solution)/shard_map/psum | solution.py:864
  497.0 47.6 %collective-permute-start.10 = (bf16[2,4,100,800]{3,1,2,0:T(4,128)(2,1)}, bf16[2,4,100,800]{3,1,2,0:T(4,128)(2,1)}, u32[]{:S(2)}, u32[]{:S(2)}) collective-permute-start(bf16[2,4,100,800]{3,1,2,0:T(4,128)(2,1)} %copy.315), channel_id=1, source_target_pairs={{0,16},{16,0},{1,17},{17,1},{2,18},{18,2},{3,19},{19,3},{4,20},{20... | collective-permute-start | bytes 3840008 | tf_op jit(solution)/shard_map/ppermute | solution.py:755
  510.7 68.3 %collective-permute-start.15 = (bf16[2,4,100,800]{3,1,2,0:T(4,128)(2,1)}, bf16[2,4,100,800]{3,1,2,0:T(4,128)(2,1)}, u32[]{:S(2)}, u32[]{:S(2)}) collective-permute-start(bf16[2,4,100,800]{3,1,2,0:T(4,128)(2,1)} %copy.324), channel_id=1, source_target_pairs={{0,16},{16,0},{1,17},{17,1},{2,18},{18,2},{3,19},{19,3},{4,20},{20... | collective-permute-start | bytes 3840008 | tf_op jit(solution)/shard_map/ppermute | solution.py:755
  527.0 52.0 %copy-start.9 = (bf16[1,2,4,100,800]{4,3,2,1,0:T(8,128)(2,1)S(1)}, bf16[1,2,4,100,800]{4,3,2,1,0:T(8,128)(2,1)}, u32[]{:S(2)}) copy-start(bf16[1,2,4,100,800]{4,3,2,1,0:T(8,128)(2,1)} %copy.348) | copy-start | bytes 3840004
  548.2 37.2 %copy-start.11 = (bf16[1,128,1600]{2,1,0:T(8,128)(2,1)S(1)}, bf16[1,128,1600]{2,1,0:T(8,128)(2,1)}, u32[]{:S(2)}) copy-start(bf16[1,128,1600]{2,1,0:T(8,128)(2,1)} %copy.307) | copy-start | bytes 1228804
  548.2 38.0 %copy-start.33 = (f32[128]{0:T(128)S(1)}, f32[128]{0:T(128)}, u32[]{:S(2)}) copy-start(f32[128]{0:T(128)} %fusion.30) | copy-start | bytes 1540
  548.2 58.7 %collective-permute-start.11 = (bf16[4,100,800]{2,0,1:T(4,128)(2,1)}, bf16[4,100,800]{2,0,1:T(4,128)(2,1)S(1)}, u32[]{:S(2)}, u32[]{:S(2)}) collective-permute-start(bf16[4,100,800]{2,0,1:T(4,128)(2,1)} %copy.317), channel_id=1, source_target_pairs={{0,8},{8,0},{1,9},{9,1},{2,10},{10,2},{3,11},{11,3},{4,12},{12,4},... | collective-permute-start | bytes 1920008 | tf_op jit(solution)/shard_map/ppermute | solution.py:758
  583.0 39.2 %collective-permute-start.16 = (bf16[4,100,800]{2,0,1:T(4,128)(2,1)}, bf16[4,100,800]{2,0,1:T(4,128)(2,1)S(1)}, u32[]{:S(2)}, u32[]{:S(2)}) collective-permute-start(bf16[4,100,800]{2,0,1:T(4,128)(2,1)} %copy.326), channel_id=1, source_target_pairs={{0,8},{8,0},{1,9},{9,1},{2,10},{10,2},{3,11},{11,3},{4,12},{12,4},... | collective-permute-start | bytes 1920008 | tf_op jit(solution)/shard_map/ppermute | solution.py:758
  609.0 20.6 %collective-permute-start.12 = (bf16[100,800]{1,0:T(8,128)(2,1)}, bf16[100,800]{1,0:T(8,128)(2,1)}, u32[]{:S(2)}, u32[]{:S(2)}) collective-permute-start(bf16[100,800]{1,0:T(8,128)(2,1)} %get-tuple-element.179), channel_id=1, source_target_pairs={{0,2},{2,0},{4,6},{6,4},{1,3},{3,1},{5,7},{7,5},{8,10},{10,8},{12,... | collective-permute-start | bytes 480008 | tf_op jit(solution)/shard_map/ppermute | solution.py:761
  609.0 23.6 %collective-permute-start.13 = (bf16[100,800]{1,0:T(8,128)(2,1)}, bf16[100,800]{1,0:T(8,128)(2,1)}, u32[]{:S(2)}, u32[]{:S(2)}) collective-permute-start(bf16[100,800]{1,0:T(8,128)(2,1)} %get-tuple-element.178), channel_id=1, source_target_pairs={{0,4},{2,6},{4,0},{6,2},{1,5},{3,7},{5,1},{7,3},{8,12},{10,14},{12... | collective-permute-start | bytes 480008 | tf_op jit(solution)/shard_map/ppermute | solution.py:761
  609.0 25.5 %collective-permute-start.14 = (bf16[100,800]{1,0:T(8,128)(2,1)}, bf16[100,800]{1,0:T(8,128)(2,1)S(1)}, u32[]{:S(2)}, u32[]{:S(2)}) collective-permute-start(bf16[100,800]{1,0:T(8,128)(2,1)} %get-tuple-element.177), channel_id=1, source_target_pairs={{0,6},{2,4},{4,2},{6,0},{1,7},{3,5},{5,3},{7,1},{8,14},{10,12},{12... | collective-permute-start | bytes 480008 | tf_op jit(solution)/shard_map/ppermute | solution.py:761
  623.8 28.9 %collective-permute-start.17 = (bf16[100,800]{1,0:T(8,128)(2,1)}, bf16[100,800]{1,0:T(8,128)(2,1)}, u32[]{:S(2)}, u32[]{:S(2)}) collective-permute-start(bf16[100,800]{1,0:T(8,128)(2,1)} %get-tuple-element.175), channel_id=1, source_target_pairs={{0,2},{2,0},{4,6},{6,4},{1,3},{3,1},{5,7},{7,5},{8,10},{10,8},{12,... | collective-permute-start | bytes 480008 | tf_op jit(solution)/shard_map/ppermute | solution.py:761
  623.8 30.1 %collective-permute-start.18 = (bf16[100,800]{1,0:T(8,128)(2,1)}, bf16[100,800]{1,0:T(8,128)(2,1)}, u32[]{:S(2)}, u32[]{:S(2)}) collective-permute-start(bf16[100,800]{1,0:T(8,128)(2,1)} %get-tuple-element.174), channel_id=1, source_target_pairs={{0,4},{2,6},{4,0},{6,2},{1,5},{3,7},{5,1},{7,3},{8,12},{10,14},{12... | collective-permute-start | bytes 480008 | tf_op jit(solution)/shard_map/ppermute | solution.py:761
  629.5 25.6 %collective-permute-start.19 = (bf16[100,800]{1,0:T(8,128)(2,1)}, bf16[100,800]{1,0:T(8,128)(2,1)}, u32[]{:S(2)}, u32[]{:S(2)}) collective-permute-start(bf16[100,800]{1,0:T(8,128)(2,1)} %get-tuple-element.173), channel_id=1, source_target_pairs={{0,6},{2,4},{4,2},{6,0},{1,7},{3,5},{5,3},{7,1},{8,14},{10,12},{12... | collective-permute-start | bytes 480008 | tf_op jit(solution)/shard_map/ppermute | solution.py:761
  740.4 72.4 %copy-start.29 = (f32[128]{0:T(128)S(1)}, f32[128]{0:T(128)}, u32[]{:S(2)}) copy-start(f32[128]{0:T(128)} %copy-done.28) | copy-start | bytes 1540
  (37 other events, 340.5 us)
Sparse Core Ops, SparseCore 0:
  10.3 101.1 all-gather.6
  113.0 31.6 all-gather.4
  342.7 98.4 reduce-scatter.2
  460.9 121.3 reduce-scatter.4
  830.9 23.0 all-reduce.7

commit v3 on v2

--- a/solution.py
+++ b/solution.py
@@ -38,19 +38,19 @@
     return (result, derivative)
 
 
-def norm_forward(values):
-    mean_value = jnp.mean(values, axis=-1, keepdims=True)
-    centered = values - mean_value
-    inv_sigma = lax.rsqrt(jnp.mean(centered * centered, axis=-1, keepdims=True) + NORM_EPS)
+def norm_forward(values, mask, feats):
+    mean_value = jnp.sum(values, axis=-1, keepdims=True) / feats
+    centered = (values - mean_value) * mask
+    inv_sigma = lax.rsqrt(jnp.sum(centered * centered, axis=-1, keepdims=True) / feats + NORM_EPS)
     return (centered * inv_sigma, inv_sigma)
 
 
-def norm_backward(upstream, normed, inv_sigma, norm_gain):
+def norm_backward(upstream, normed, inv_sigma, norm_gain, feats):
     scaled = upstream * norm_gain
     return inv_sigma * (
         scaled
-        - jnp.mean(scaled, axis=-1, keepdims=True)
-        - normed * jnp.mean(scaled * normed, axis=-1, keepdims=True)
+        - jnp.sum(scaled, axis=-1, keepdims=True) / feats
+        - normed * (jnp.sum(scaled * normed, axis=-1, keepdims=True) / feats)
     )
 
 
@@ -319,7 +319,8 @@
     def local(self, src, dst, sem=None):
         copy = pltpu.make_async_copy(src, dst, self.sems.at[len(self.begun)] if sem is None else sem)
         copy.start()
-        self.begun.append(copy.wait if sem is None else (lambda: None))
+        if sem is None:
+            self.begun.append(copy.wait)
         return copy
 
     def arrived(self, dst, recv, peer):
@@ -417,48 +418,100 @@
     )(value)
 
 
-def opening_kernel(own, blocks, out, blocks_all, send, recv, recv_w):
-    place = Place(True)
+def opening_kernel(
+    own, blocks, fc, proj, out_w, out, blocks_all, fc_all, proj_all, out_w_all, send, recv, recv_w, recv_f, recv_o, recv_p
+):
+    place, group = Place(True), Place(False)
     n_ctx = blocks.shape[0]
     copies = Copies(send)
-    peer_x = {"x": 1 - place.x}
+    peer_x, peer_y, peer_c = {"x": 1 - place.x}, {"y": 1 - place.y}, {"c": 1 - place.c}
     far_ctx = others(place.ctx, n_ctx)
-    meet([place.at_ctx(k) for k in far_ctx] + [{"y": 1 - place.y}, peer_x])
+    meet([place.at_ctx(k) for k in far_ctx] + [peer_y, peer_x])
     mine = blocks_all.at[place.x, place.ctx]
+    half = out_w.shape[1] // 2
 
     def sem_w(x, k):
         return recv_w.at[x * n_ctx + k]
 
+    def out_block(x, z, c, y):
+        at = (x * place.n_z + z) * 2 + c
+        ref = out_w_all.at[at, :, pl.ds(pl.multiple_of(y * half, half), half)]
+        return ref, recv_o.at[at * 2 + y]
+
+    def give_out(x, z, c, y, peer):
+        ref, sem = out_block(x, z, c, y)
+        copies.send(ref, ref, sem, peer)
+
+    def got_out(x, z, c, y, peer):
+        ref, sem = out_block(x, z, c, y)
+        copies.arrived(ref, sem, peer)
+
     gather_begin(place, own, out, copies, recv)
+    for k in others(group.ctx, 4):
+        copies.send(fc.at[k], fc_all.at[group.ctx], recv_f.at[group.ctx], group.at_ctx(k))
+        copies.send(proj.at[k], proj_all.at[group.ctx], recv_p.at[group.ctx], group.at_ctx(k))
+    copies.local(fc.at[group.ctx], fc_all.at[group.ctx])
+    copies.local(proj.at[group.ctx], proj_all.at[group.ctx])
     for k in far_ctx:
         copies.send(blocks.at[k], mine, sem_w(place.x, place.ctx), place.at_ctx(k))
     copies.local(blocks.at[place.ctx], mine)
     copies.send(blocks.at[place.ctx], mine, sem_w(place.x, place.ctx), peer_x)
+    own_out, own_sem = out_block(place.x, place.z, place.c, place.y)
+    own_half = out_w.at[:, pl.ds(pl.multiple_of(place.y * half, half), half)]
+    copies.local(own_half, own_out)
+    for z in place.far_z():
+        copies.send(own_half, own_out, own_sem, place.at_z(z))
+    for peer in (peer_x, peer_y, peer_c):
+        copies.send(own_half, own_out, own_sem, peer)
     gather_middle(place, out, copies, recv)
     for k in far_ctx:
         block = blocks_all.at[place.x, k]
         copies.arrived(block, sem_w(place.x, k), place.at_ctx(k))
         copies.send(block, block, sem_w(place.x, k), peer_x)
+    for z in place.far_z():
+        got_out(place.x, z, place.c, place.y, place.at_z(z))
+        for peer in (peer_x, peer_y, peer_c):
+            give_out(place.x, z, place.c, place.y, peer)
+    for z in [place.z] + place.far_z():
+        got_out(1 - place.x, z, place.c, place.y, peer_x)
+        for peer in (peer_y, peer_c):
+            give_out(1 - place.x, z, place.c, place.y, peer)
     gather_end(place, out, copies, recv)
+    for x in (place.x, 1 - place.x):
+        for z in [place.z] + place.far_z():
+            got_out(x, z, place.c, 1 - place.y, peer_y)
+            give_out(x, z, place.c, 1 - place.y, peer_c)
     for k in [place.ctx] + far_ctx:
         copies.arrived(blocks_all.at[1 - place.x, k], sem_w(1 - place.x, k), peer_x)
+    for k in others(group.ctx, 4):
+        copies.arrived(fc_all.at[k], recv_f.at[k], group.at_ctx(k))
+        copies.arrived(proj_all.at[k], recv_p.at[k], group.at_ctx(k))
+    for x in (place.x, 1 - place.x):
+        for z in [place.z] + place.far_z():
+            for y in (place.y, 1 - place.y):
+                got_out(x, z, 1 - place.c, y, peer_c)
     copies.finish()
 
 
-def opening(own, blocks):
+def opening(own, blocks, fc, proj, out_w):
     n_ctx = blocks.shape[0]
+    n_z = n_ctx // 2
+    sends = gather_copies(n_z) + 2 * n_ctx + 8 + (n_z - 1) + 4 + 3 * n_z + 2 * n_z + 2 * n_z
     return pl.pallas_call(
         opening_kernel,
         out_shape=(
             jax.ShapeDtypeStruct((2 * n_ctx,) + own.shape, own.dtype),
             jax.ShapeDtypeStruct((2,) + blocks.shape, blocks.dtype),
+            jax.ShapeDtypeStruct(fc.shape, fc.dtype),
+            jax.ShapeDtypeStruct(proj.shape, proj.dtype),
+            jax.ShapeDtypeStruct((2 * n_ctx,) + out_w.shape, out_w.dtype),
         ),
-        in_specs=[ANY, ANY],
-        out_specs=(ANY, ANY),
-        scratch_shapes=dma_sems(gather_copies(n_ctx // 2) + 2 * n_ctx, 2 * n_ctx, 2 * n_ctx),
+        in_specs=[ANY] * 5,
+        out_specs=(ANY,) * 5,
+        scratch_shapes=dma_sems(sends, 2 * n_ctx, 2 * n_ctx, 4, 4 * n_ctx, 4),
         compiler_params=comm_params(1),
         name="opening",
-    )(own, blocks)
+    )(own, blocks, fc, proj, out_w)
 
 
 def to_tokens_kernel(src, dst, send, recv):
@@ -538,23 +591,35 @@
                 self.copies.send(
                     self.part.at[p.slot_of(z, 1 - p.c, y)], self.from_c.at[at], self.rc.at[at], {"c": 1 - p.c}
                 )
-                self.copies.local(self.part.at[p.slot_of(z, p.c, y)], self.held.at[at], self.loads.at[at])
-
-    def add_c(self, z, y):
-        at = z * 2 + y
+        self.queue = [(z, y) for y in (1 - p.y, p.y) for z in self.order()]
+        for at in range(min(self.held.shape[0], len(self.queue))):
+            self.load(at)
+
+    def load(self, at):
+        p = self.place
+        z, y = self.queue[at]
+        at = at % self.held.shape[0]
+        self.copies.local(self.part.at[p.slot_of(z, p.c, y)], self.held.at[at], self.loads.at[at])
+
+    def add_c(self, step):
+        z, y = self.queue[step]
+        at, depth = z * 2 + y, self.held.shape[0]
+        own = step % depth
         self.copies.arrived(self.from_c.at[at], self.rc.at[at], {"c": 1 - self.place.c})
-        pltpu.make_async_copy(self.held.at[at], self.held.at[at], self.loads.at[at]).wait()
-        self.from_c[at] = self.from_c[at] + self.held[at]
+        pltpu.make_async_copy(self.held.at[own], self.held.at[own], self.loads.at[own]).wait()
+        self.from_c[at] = self.from_c[at] + self.held[own]
+        if step + depth < len(self.queue):
+            self.load(step + depth)
 
     def over_c_far(self):
         p = self.place
-        for z in self.order():
-            self.add_c(z, 1 - p.y)
+        for step, z in enumerate(self.order()):
+            self.add_c(step)
             self.copies.send(self.from_c.at[z * 2 + 1 - p.y], self.from_y.at[z], self.ry.at[z], {"y": 1 - p.y})
 
     def over_c_near(self):
-        for z in self.order():
-            self.add_c(z, self.place.y)
+        for step in range(self.place.n_z):
+            self.add_c(self.place.n_z + step)
 
     def over_y(self):
         p = self.place
@@ -575,7 +640,7 @@
 
 def scatter_scratch(n_z, block):
     return [
-        pltpu.VMEM((2 * n_z,) + block, B16),
+        pltpu.VMEM((min(8, 2 * n_z),) + block, B16),
         pltpu.VMEM((2 * n_z,) + block, B16),
         pltpu.VMEM((n_z,) + block, B16),
         pltpu.VMEM((n_z,) + block, B16),
@@ -583,7 +648,7 @@
 
 
 def scatter_sems(n_z, more=0):
-    return dma_sems(6 * n_z + more, 2 * n_z, 2 * n_z, n_z, n_z)
+    return dma_sems(4 * n_z + more, min(8, 2 * n_z), 2 * n_z, n_z, n_z)
 
 
 def group_scatter_kernel(part, out, held, from_c, from_y, from_z, send, loads, rc, ry, rz):
@@ -612,9 +677,78 @@
     )(part)
 
 
+class OutScatter:
+    def __init__(self, place, part, held, from_c, from_x, from_y, from_z, out, copies, loads, rc, rx, ry, rz, rg):
+        self.__dict__.update(locals())
+        self.half = out.shape[2]
+
+    def order(self):
+        return self.place.far_z() + [self.place.z]
+
+    def columns(self, y):
+        return pl.ds(pl.multiple_of(y * self.half, self.half), self.half)
+
+    def begin(self):
+        p = self.place
+        for x in (1 - p.x, p.x):
+            for z in self.order():
+                at = x * p.n_z + z
+                self.copies.send(self.part.at[at * 2 + 1 - p.c], self.from_c.at[at], self.rc.at[at], {"c": 1 - p.c})
+                self.copies.local(self.part.at[at * 2 + p.c], self.held.at[at], self.loads.at[at])
+
+    def add_c(self, x, z):
+        at = x * self.place.n_z + z
+        self.copies.arrived(self.from_c.at[at], self.rc.at[at], {"c": 1 - self.place.c})
+        pltpu.make_async_copy(self.held.at[at], self.held.at[at], self.loads.at[at]).wait()
+        self.from_c[at] = self.from_c[at] + self.held[at]
+
+    def over_c_far(self):
+        p = self.place
+        for z in self.order():
+            self.add_c(1 - p.x, z)
+            self.copies.send(
+                self.from_c.at[(1 - p.x) * p.n_z + z], self.from_x.at[z], self.rx.at[z], {"x": 1 - p.x}
+            )
+
+    def over_c_near(self):
+        for z in self.order():
+            self.add_c(self.place.x, z)
+
+    def over_x(self):
+        p = self.place
+        for z in self.order():
+            self.copies.arrived(self.from_x.at[z], self.rx.at[z], {"x": 1 - p.x})
+            self.from_x[z] = self.from_x[z] + self.from_c[p.x * p.n_z + z]
+            self.copies.send(
+                self.from_x.at[z, :, self.columns(1 - p.y)], self.from_y.at[z], self.ry.at[z], {"y": 1 - p.y}
+            )
+
+    def over_y(self):
+        p = self.place
+        for z in self.order():
+            self.copies.arrived(self.from_y.at[z], self.ry.at[z], {"y": 1 - p.y})
+            self.from_y[z] = self.from_y[z] + self.from_x[z, :, self.columns(p.y)]
+            if z is not p.z:
+                self.copies.send(self.from_y.at[z], self.from_z.at[p.z], self.rz.at[p.z], p.at_z(z))
+
+    def over_z(self):
+        p = self.place
+        total = self.from_y[p.z].astype(F32)
+        for z in p.far_z():
+            self.copies.arrived(self.from_z.at[z], self.rz.at[z], p.at_z(z))
+            total = total + self.from_z[z].astype(F32)
+        self.out[p.y] = total.astype(B16)
+        self.copies.send(self.out.at[p.y], self.out.at[p.y], self.rg.at[p.y], {"y": 1 - p.y})
+
+    def end(self):
+        p = self.place
+        self.copies.arrived(self.out.at[1 - p.y], self.rg.at[1 - p.y], {"y": 1 - p.y})
+
+
 def closing_kernel(
-    part, grads, out, grads_out, held, from_c, from_y, from_z, own_x, from_x,
-    send, loads, rc, ry, rz, load_x, rx, rk, rg,
+    part, grads, out_part, out, grads_out, out_w_out,
+    held, from_c, from_y, from_z, own_x, from_x, o_held, o_c, o_x, o_y, o_z,
+    send, loads, rc, ry, rz, load_x, rx, rk, rg, o_loads, orc, orx, ory, orz, org,
 ):
     place = Place(True)
     n_ctx = grads.shape[1]
@@ -623,10 +757,12 @@
     peer_x, peer_y = {"x": 1 - place.x}, {"y": 1 - place.y}
     meet([place.at_ctx(k) for k in far_ctx] + [peer_y, peer_x])
     sums = Scatter(place, part, held, from_c, from_y, from_z, out, copies, loads, rc, ry, rz)
+    outs = OutScatter(place, out_part, o_held, o_c, o_x, o_y, o_z, out_w_out, copies, o_loads, orc, orx, ory, orz, org)
     sums.begin()
     for k in far_ctx + [place.ctx]:
         copies.send(grads.at[1 - place.x, k], from_x.at[k], rx.at[k], peer_x)
         copies.local(grads.at[place.x, k], own_x.at[k], load_x.at[k])
+    outs.begin()
     sums.over_c_far()
     mine = grads_out.at[place.y, place.ctx]
     for k in far_ctx + [place.ctx]:
@@ -638,34 +774,49 @@
     copies.local(from_x.at[place.ctx], mine)
     copies.send(from_x.at[place.ctx], mine, rg.at[place.ctx], peer_y)
     sums.over_c_near()
+    outs.over_c_far()
+    outs.over_c_near()
     sums.over_y()
+    outs.over_x()
     for k in far_ctx:
         block = grads_out.at[place.y, k]
         copies.arrived(block, rk.at[k], place.at_ctx(k))
         copies.send(block, block, rg.at[k], peer_y)
+    outs.over_y()
     sums.over_z()
+    outs.over_z()
     for k in [place.ctx] + far_ctx:
         copies.arrived(grads_out.at[1 - place.y, k], rg.at[k], peer_y)
+    outs.end()
     copies.finish()
 
 
-def closing(part, grads):
+def closing(part, grads, out_part):
     block = part.shape[1:]
     n_ctx = grads.shape[1]
     n_z = n_ctx // 2
     piece = grads.shape[1:]
+    rows, width = out_part.shape[1:]
+    half = (rows, width // 2)
     return pl.pallas_call(
         closing_kernel,
-        out_shape=(jax.ShapeDtypeStruct(block, F32), jax.ShapeDtypeStruct((2,) + piece, B16)),
-        in_specs=[ANY, ANY],
-        out_specs=(IN_VMEM, ANY),
+        out_shape=(
+            jax.ShapeDtypeStruct(block, F32),
+            jax.ShapeDtypeStruct((2,) + piece, B16),
+            jax.ShapeDtypeStruct((2,) + half, B16),
+        ),
+        in_specs=[ANY] * 3,
+        out_specs=(IN_VMEM, ANY, IN_VMEM),
         scratch_shapes=scatter_scratch(n_z, block)
         + [pltpu.VMEM(piece, B16), pltpu.VMEM(piece, B16)]
-        + scatter_sems(n_z, 5 * n_ctx)
-        + dma_sems(n_ctx, n_ctx, n_ctx, n_ctx),
+        + [pltpu.VMEM((2 * n_z, rows, width), B16), pltpu.VMEM((2 * n_z, rows, width), B16)]
+        + [pltpu.VMEM((n_z, rows, width), B16), pltpu.VMEM((n_z,) + half, B16), pltpu.VMEM((n_z,) + half, B16)]
+        + scatter_sems(n_z, 3 * n_ctx + 6 * n_z)
+        + dma_sems(n_ctx, n_ctx, n_ctx, n_ctx)
+        + dma_sems(2 * n_z, 2 * n_z, n_z, n_z, n_z, 2),
         compiler_params=comm_params(4),
         name="closing",
-    )(part, grads)
+    )(part, grads, out_part)
 
 
 def vectors_kernel(src, own_out, ff_out, from_all, half, from_y, send, recv, ry):
@@ -720,47 +871,38 @@
     )(value)
 
 
-def shift_perm(count, step):
-    return [(i, (i + step) % count) for i in range(count)]
-
-
-def spread(blocks, n_h):
-    lc, h, x = lax.axis_index(("l", "c")), lax.axis_index("h"), lax.axis_index("x")
-
-    def pick(value, at):
-        return lax.dynamic_index_in_dim(value, at, 0, False)
-
-    whole = jnp.zeros((2, n_h) + blocks.shape, blocks.dtype)
-    mine = jnp.zeros(blocks.shape, blocks.dtype)
-    mine = lax.dynamic_update_index_in_dim(mine, pick(blocks, lc), lc, 0)
-    for step in range(1, 4):
-        got = lax.ppermute(pick(blocks, lc ^ step), ("l", "c"), [(i, i ^ step) for i in range(4)])
-        mine = lax.dynamic_update_index_in_dim(mine, got, lc ^ step, 0)
-    line = jnp.zeros((n_h,) + blocks.shape, blocks.dtype)
-    line = lax.dynamic_update_index_in_dim(line, mine, h, 0)
-    for step in range(1, n_h):
-        got = lax.ppermute(mine, "h", shift_perm(n_h, step))
-        line = lax.dynamic_update_index_in_dim(line, got, lax.rem(h + n_h - step, n_h), 0)
-    whole = lax.dynamic_update_index_in_dim(whole, line, x, 0)
-    got = lax.ppermute(line, "x", shift_perm(2, 1))
-    return lax.dynamic_update_index_in_dim(whole, got, 1 - x, 0)
-
-
-def unspread(grad, n_h):
-    lc, h, x = lax.axis_index(("l", "c")), lax.axis_index("h"), lax.axis_index("x")
-
-    def pick(value, at):
-        return lax.dynamic_index_in_dim(value, at, 0, False)
-
-    line = pick(grad, x) + lax.ppermute(pick(grad, 1 - x), "x", shift_perm(2, 1))
-    mine = pick(line, h)
-    for step in range(1, n_h):
-        mine = mine + lax.ppermute(pick(line, lax.rem(h + step, n_h)), "h", shift_perm(n_h, step))
-    out = lax.dynamic_update_index_in_dim(jnp.zeros_like(mine), pick(mine, lc), lc, 0)
-    for step in range(1, 4):
-        got = lax.ppermute(pick(mine, lc ^ step), ("l", "c"), [(i, i ^ step) for i in range(4)])
-        out = lax.dynamic_update_index_in_dim(out, got, lc ^ step, 0)
-    return out
+def project_kernel(feats, x_ref, gain_ref, shift_ref, mask_ref, w_ref, bias_ref, norm_ref, qkv_ref):
+    x = x_ref[...].astype(F32)
+    mean = jnp.sum(x, axis=1, keepdims=True) * (1.0 / feats)
+    centered = (x - mean) * mask_ref[...]
+    inv = lax.rsqrt(jnp.sum(centered * centered, axis=1, keepdims=True) * (1.0 / feats) + NORM_EPS)
+    norm = (centered * inv * gain_ref[...] + shift_ref[...]).astype(B16)
+    norm_ref[...] = norm
+    qkv_ref[...] = (dot(norm, w_ref[...], 1, 0) + bias_ref[...]).astype(B16)
+
+
+def project(x, gain, shift, mask, weight, bias, feats):
+    total, wide = x.shape
+    cols = weight.shape[1]
+    step = min(256, total)
+
+    def fixed(shape):
+        return pl.BlockSpec(shape, lambda i: (0, 0))
+
+    return pl.pallas_call(
+        functools.partial(project_kernel, feats),
+        grid=(total // step,),
+        in_specs=[pl.BlockSpec((step, wide), lambda i: (i, 0))]
+        + [fixed((1, wide))] * 3
+        + [fixed((wide, cols)), fixed((1, cols))],
+        out_specs=(pl.BlockSpec((step, wide), lambda i: (i, 0)), pl.BlockSpec((step, cols), lambda i: (i, 0))),
+        out_shape=(jax.ShapeDtypeStruct((total, wide), B16), jax.ShapeDtypeStruct((total, cols), B16)),
+        compiler_params=pltpu.CompilerParams(vmem_limit_bytes=VMEM_LIMIT),
+        cost_estimate=pl.CostEstimate(
+            flops=2 * total * wide * cols, bytes_accessed=4 * total * wide, transcendentals=total
+        ),
+        name="project",
+    )(x, gain[None], shift[None], mask[None], weight, bias[None])
 
 
 def on_device(
@@ -785,34 +927,48 @@
     def gather(value, axes):
         return lax.all_gather(value, axes, axis=0, tiled=True)
 
-    small = jnp.concatenate(
-        [
-            first_gain, first_shift, out_bias, second_gain, second_shift, proj_bias, qv_bias,
-        ]
-    )
-    row_pad = -rows % 16
+    tall = rows + (-rows % 16)
+    wide = n_shard * tall
+    row_pad = tall - rows
+
+    def widened(value):
+        lead = value.shape[:-1]
+        value = value.reshape(lead + (n_shard, rows))
+        return jnp.pad(value, [(0, 0)] * (len(lead) + 1) + [(0, row_pad)]).reshape(lead + (wide,))
+
+    def narrowed(value):
+        lead = value.shape[:-1]
+        return value.reshape(lead + (n_shard, tall))[..., :rows].reshape(lead + (feats,))
+
+    mask = jnp.asarray((np.arange(wide) % tall < rows).astype(np.float32))
+
+    small = jnp.concatenate([first_gain, first_shift, out_bias, second_gain, second_shift, proj_bias, qv_bias])
     packed = jnp.pad(qkv_weight.reshape(rows, 3, feats), ((0, 0), (0, 0), (0, padded - feats)))
     packed = lax.dynamic_index_in_dim(packed.reshape(rows, 3, n_ctx, n_y, pair), y_at, 3, False)
     packed = packed.transpose(2, 0, 1, 3).reshape(n_ctx, rows, 3 * pair)
     small = jnp.pad(small, (0, row_pad * 3 * pair - small.shape[0])).reshape(1, row_pad, 3 * pair)
     packed = jnp.concatenate([packed, jnp.broadcast_to(small, (n_ctx, row_pad, 3 * pair))], axis=1)
-    all_input, packed = opening(block_input[0], packed)
-    all_input = all_input.reshape(n_slot * slot_len, feats)
-    packed = packed.reshape(n_shard, rows + row_pad, 3 * pair)
-    w_qkv = packed[:, :rows].reshape(feats, 3 * pair)
+    fc_blocks = jnp.pad(fc_weight, ((0, row_pad), (0, 0))).reshape(tall, 4, ff_own).transpose(1, 0, 2)
+    proj_blocks = jnp.pad(proj_weight.T, ((0, row_pad), (0, 0))).reshape(tall, 4, ff_own).transpose(1, 0, 2)
+    own_input = widened(block_input[0])
+    grad_own = widened(out_grad[0])
+    grad_all = gather(grad_own, FFG)
+    all_input, packed, fc_blocks, proj_blocks, w_out = opening(
+        own_input, packed, fc_blocks, proj_blocks, widened(jnp.pad(out_weight, ((0, row_pad), (0, 0))))
+    )
+    w_fc = gather(fc_blocks.reshape(4 * tall, ff_own), ("x", "h"))
+    w_proj = gather(proj_blocks.reshape(4 * tall, ff_own), ("x", "h"))
+    w_out = w_out.reshape(wide, wide)
+    packed = packed.reshape(n_shard, tall, 3 * pair)
+    w_qkv = packed.reshape(wide, 3 * pair)
     smalls = packed[:, rows:].reshape(n_shard, -1)[:, : 8 * rows].astype(F32)
-    gain_one, shift_one, bias_out, gain_two, shift_two, bias_proj = [
-        smalls[:, i * rows : (i + 1) * rows].reshape(feats) for i in range(6)
-    ]
+    singles = jnp.pad(smalls[:, : 6 * rows].reshape(n_shard, 6, rows), ((0, 0), (0, 0), (0, row_pad)))
+    gain_one, shift_one, bias_out, gain_two, shift_two, bias_proj = singles.transpose(1, 0, 2).reshape(6, wide)
     bias_qv = smalls[:, 6 * rows :].reshape(2, feats)
     bias_pair = lax.dynamic_slice_in_dim(
         jnp.pad(bias_qv, ((0, 0), (0, padded - feats))), slot_at * pair, pair, 1
     )
     bias_qkv = jnp.concatenate([bias_pair[0], jnp.zeros((pair,), F32), bias_pair[1]])
-
-    w_fc = spread(fc_weight.reshape(rows, 4, ff_own).transpose(1, 0, 2), n_h).reshape(feats, ff_own)
-    w_proj = spread(proj_weight.reshape(4, ff_own, rows).transpose(0, 2, 1), n_h).reshape(feats, ff_own)
-    w_out = gather(out_weight, SHARD)
     b_fc = lax.dynamic_slice_in_dim(fc_bias, lc_at * ff_own, ff_own, 0).astype(F32)
 
     order = slot_order[0]
@@ -825,66 +981,62 @@
     start3 = starts.reshape(-1, 1, BLK)
     low = start3[:, 0, 0] // BLK
 
-    own_input = block_input[0]
     own_wide = own_input.astype(F32)
-    normed_all, unused = norm_forward(all_input.astype(F32))
-    norm_one = (normed_all * gain_one + shift_one).astype(B16)
-    qkv = (dot(norm_one, w_qkv, 1, 0) + bias_qkv).astype(B16)
+    norm_one, qkv = project(
+        all_input.reshape(n_slot * slot_len, wide), gain_one, shift_one, mask, w_qkv, bias_qkv, feats
+    )
     heads_out, lse = attend(inv, low, qkv, start3, slot_len, head)
-    attention = to_tokens(heads_out.reshape(n_slot, slot_len, pair))[:, :feats]
+    attention = widened(to_tokens(heads_out.reshape(n_slot, slot_len, pair))[:, :feats])
     hidden = own_wide + dot(attention, w_out, 1, 0) + bias_out
-    normed_two, inv_two = norm_forward(hidden)
+    normed_two, inv_two = norm_forward(hidden, mask, feats)
     norm_two = (normed_two * gain_two + shift_two).astype(B16)
-    grad_own = out_grad[0]
     grad_wide = grad_own.astype(F32)
-    grad_all = gather(grad_own, FFG)
-    norm_all = group_gather(norm_two, 6).reshape(-1, feats)
+    norm_all = group_gather(norm_two, 6).reshape(-1, wide)
     preact = dot(norm_all, w_fc, 1, 0) + b_fc
     activated, derivative = gelu_parts(preact)
     activation = activated.astype(B16)
     mlp_part = dot(activation, w_proj, 1, 1).astype(B16)
     mlp = lax.psum_scatter(mlp_part, FFG, scatter_dimension=0, tiled=True).astype(F32)
-    block_output = hidden + mlp + bias_proj
+    block_output = narrowed(hidden + mlp + bias_proj)
 
     dpreact = dot(grad_all, w_proj, 1, 0) * derivative
     dpreact_b = dpreact.astype(B16)
     dnorm_part = dot(dpreact_b, w_fc, 1, 1).astype(B16)
-    dnorm_two = group_scatter(dnorm_part.reshape(8, slot_len, feats), 7)
-    ffn_shape = (n_x, n_h, 4, rows, ff_own)
-    proj_grad = unspread(dot(grad_all, activation, 0, 0).astype(B16).reshape(ffn_shape), n_h)
-    proj_grad = proj_grad.transpose(0, 2, 1).reshape(4 * ff_own, rows).astype(F32)
-    fc_grad = unspread(dot(norm_all, dpreact_b, 0, 0).astype(B16).reshape(ffn_shape), n_h)
-    fc_grad = fc_grad.transpose(1, 0, 2).reshape(rows, 4 * ff_own).astype(F32)
-
-    dhidden = grad_wide + norm_backward(dnorm_two, normed_two, inv_two, gain_two)
+    dnorm_two = group_scatter(dnorm_part.reshape(8, slot_len, wide), 7)
+
+    def owner_sum(value):
+        value = lax.psum_scatter(value.astype(B16), ("x", "h"), scatter_dimension=0, tiled=True)
+        value = lax.all_to_all(value.reshape(4, tall, ff_own), ("l", "c"), 0, 0, tiled=True)
+        return value[:, :rows].astype(F32)
+
+    proj_grad = owner_sum(dot(grad_all, activation, 0, 0)).transpose(0, 2, 1).reshape(4 * ff_own, rows)
+    fc_grad = owner_sum(dot(norm_all, dpreact_b, 0, 0)).transpose(1, 0, 2).reshape(rows, 4 * ff_own)
+
+    dhidden = grad_wide + norm_backward(dnorm_two, normed_two, inv_two, gain_two, feats)
     dhidden_b = dhidden.astype(B16)
-    out_part = dot(attention, dhidden_b, 0, 0).astype(B16).reshape(n_shard, rows, feats)
-    out_part = jnp.pad(out_part, ((0, 0), (0, row_pad), (0, 0))).reshape(-1, feats)
-    out_grad_w = lax.psum_scatter(out_part, SHARD, scatter_dimension=0, tiled=True)[:rows]
-    out_grad_w = lax.psum(out_grad_w, "y").astype(F32)
-
-    dattention = dot(dhidden_b, w_out, 1, 1).astype(B16)
+    out_part = dot(attention, dhidden_b, 0, 0).astype(B16).reshape(n_shard, tall, wide)
+    dattention = narrowed(dot(dhidden_b, w_out, 1, 1).astype(B16))
     dattention = jnp.pad(dattention, ((0, 0), (0, padded - feats)))
     dattention = to_heads(dattention, n_slot).reshape(n_slot * slot_len, pair)
     dqkv = attend_back(inv, low, qkv, heads_out, dattention, lse, start3, slot_len, head)
     dqkv_b = dqkv.astype(B16)
     dnorm_one_part = dot(dqkv_b, w_qkv, 1, 1).astype(B16)
-    qkv_part = dot(norm_one, dqkv_b, 0, 0).astype(B16).reshape(n_x, n_ctx, rows, 3 * pair)
-    qkv_part = jnp.pad(qkv_part, ((0, 0), (0, 0), (0, row_pad), (0, 0)))
-    dnorm_one, qkv_all = closing(dnorm_one_part.reshape(n_slot, slot_len, feats), qkv_part)
+    qkv_part = dot(norm_one, dqkv_b, 0, 0).astype(B16).reshape(n_x, n_ctx, tall, 3 * pair)
+    dnorm_one, qkv_all, out_all = closing(dnorm_one_part.reshape(n_slot, slot_len, wide), qkv_part, out_part)
     qkv_all = qkv_all[:, :, :rows].reshape(n_y, n_ctx, rows, 3, pair)
     qkv_grad = qkv_all.transpose(2, 3, 1, 0, 4).reshape(rows, 3, padded)
     qkv_grad = qkv_grad[:, :, :feats].reshape(rows, 3 * feats).astype(F32)
-
-    normed_one, inv_one = norm_forward(own_wide)
-    input_grad = dhidden + norm_backward(dnorm_one, normed_one, inv_one, gain_one)
+    out_grad_w = narrowed(out_all[:, :rows].transpose(1, 0, 2).reshape(rows, wide)).astype(F32)
+
+    normed_one, inv_one = norm_forward(own_wide, mask, feats)
+    input_grad = narrowed(dhidden + norm_backward(dnorm_one, normed_one, inv_one, gain_one, feats))
 
     dq_sum, dv_sum = jnp.sum(dqkv[:, :pair], axis=0), jnp.sum(dqkv[:, 2 * pair :], axis=0)
 
     def placed(value, width, at):
-        return lax.dynamic_update_slice(jnp.zeros((width,), F32), value, (at,))
-
-    vectors = jnp.concatenate(
+        return lax.dynamic_update_slice(jnp.zeros((width,), F32), value, (at,))[:feats]
+
+    vectors = jnp.stack(
         [
             jnp.sum(dhidden, axis=0),
             jnp.sum(dnorm_one * normed_one, axis=0),
@@ -894,14 +1046,12 @@
             jnp.sum(grad_wide, axis=0),
         ]
     )
-    qv_sums = jnp.concatenate(
-        [placed(dq_sum, padded, slot_at * pair)[:feats], placed(dv_sum, padded, slot_at * pair)[:feats]]
-    )
+    qv_sums = jnp.concatenate([placed(dq_sum, padded, slot_at * pair), placed(dv_sum, padded, slot_at * pair)])
     vectors = jnp.concatenate(
         [
-            vectors.reshape(6, n_shard, rows).transpose(1, 0, 2).reshape(n_shard, 6 * rows),
+            vectors.reshape(6, n_shard, tall).transpose(1, 0, 2).reshape(n_shard, 6 * tall),
             qv_sums.reshape(n_shard, 2 * rows),
-            jnp.zeros((n_shard, 1024 - 8 * rows), F32),
+            jnp.zeros((n_shard, 1024 - 6 * tall - 2 * rows), F32),
             jnp.broadcast_to(jnp.sum(dpreact, axis=0)[None], (n_shard, ff_own)),
             jnp.zeros((n_shard, 1024 - ff_own), F32),
         ],
@@ -910,10 +1060,10 @@
     owned, ff_sums = vectors_sum(vectors.reshape(n_shard, 16, 128))
     owned = owned.reshape(1024)
     fc_bias_grad = ff_sums.reshape(4, 1024)[:, :ff_own].reshape(4 * ff_own)
-    qv_grad = owned[6 * rows : 8 * rows]
+    qv_grad = owned[6 * tall : 6 * tall + 2 * rows]
 
     def own(index):
-        return owned[index * rows : (index + 1) * rows]
+        return owned[index * tall : index * tall + rows]
 
     return (
         block_output[None],

time: 868 us -> 729 us (0.84)
  local copies, waits for them, and re-layouts: 253 us -> 58.6 us
  Pallas kernels: 319 us -> 464 us
  waiting for transfers between devices: 132 us -> 84.4 us
  other arithmetic: 46 us -> 17.9 us
  starting transfers between devices: 23.6 us -> 8.98 us
    ppermute x20 -> x0, waiting for transfers between devices: 121 us -> none  [the longest x2 45.9 us: unspread(): lax.ppermute(pick(grad, 1 - x), 'x', shift_perm(2, 1))]
    pallas_call x1, Pallas kernels: 72.3 us -> 152 us  [closing(): pl.pallas_call(closing_kernel, out_shape=(jax.ShapeDtypeStruct(block, F32...]
    all_gather x2 -> x3, waiting for transfers between devices: 0.01 us -> 62.5 us  [gather(): return lax.all_gather(value, axes, axis=0, tiled=True)]
    dynamic_update_slice x26 -> x2, local copies, waits for them, and re-layouts: 62.2 us -> 0.56 us  [placed(): lax.dynamic_update_slice(jnp.zeros((width,), F32), value, (at,))[:feats]]
    unnamed x108 -> x55, local copies, waits for them, and re-layouts: 47.3 us -> 7.47 us
    reshape x10 -> x15, local copies, waits for them, and re-layouts: 50.4 us -> 12.1 us  [the longest x3 3.21 us: widened(): jnp.pad(value, [(0, 0)] * (len(lead) + 1) + [(0, row_pad)])]
    convert_element_type x6 -> x2, local copies, waits for them, and re-layouts: 26.7 us -> 2.62 us  [the longest x1 2.37 us: on_device(): narrowed(out_all[:, :rows].transpose(1, 0, 2).reshape(rows, wide))]
    ppermute x20 -> x0, starting transfers between devices: 23.4 us -> none  [the longest x2 6.32 us: unspread(): lax.ppermute(pick(grad, 1 - x), 'x', shift_perm(2, 1))]
  transfers between devices with their start and end apart: 25 -> 8, of which waited for: 9 -> 4; matrix products, arithmetic and copies ran while one was open for 40% -> 17% of each run, Pallas kernels for 37% -> 49%
where the time goes in v3:
time: 729 us; the launch traced here: 724 us
  Pallas kernels  464 us (64%)
  waiting for transfers between devices  84.4 us (12%)
  matrix products  75.1 us (10%)
  local copies, waits for them, and re-layouts  58.6 us (8%)
  other arithmetic  17.9 us (2%)
  between operations  15.1 us (2%)
  starting transfers between devices  8.98 us (1%)
    pallas_call x1, Pallas kernels, closing(): pl.pallas_call(closing_kernel, out_shape=(jax.ShapeDtypeStruct(block, F32...  152 us
    pallas_call x1, Pallas kernels, opening(): pl.pallas_call(opening_kernel, out_shape=(jax.ShapeDtypeStruct((2 * n_ctx...  113 us
    dot_general x11, matrix products, dot(): lax.dot_general(left, right, (((left_dim,), (right_dim,)), ((), ())), pre...  75.1 us
    all_gather x3, waiting for transfers between devices, gather(): return lax.all_gather(value, axes, axis=0, tiled=True)  62.5 us
    pallas_call x1, Pallas kernels, group_scatter(): pl.pallas_call(group_scatter_kernel, out_shape=jax.ShapeDtypeStruct(block...  47.4 us
    pallas_call x1, Pallas kernels, group_gather(): pl.pallas_call(group_gather_kernel, out_shape=jax.ShapeDtypeStruct((8,) +...  36.7 us
    pallas_call x1, Pallas kernels, attend_back(): pl.pallas_call(functools.partial(attend_back_kernel, slot_len, head), out...  27.8 us
    pallas_call x1, Pallas kernels, attend(): pl.pallas_call(functools.partial(attend_kernel, slot_len, head), out_shap...  27.3 us
  transfers between devices with their start and end apart: 8, of which 4 were waited for; matrix products, arithmetic and copies ran while one was open for 17% of the time, Pallas kernels for 49%

profile of v3, /device:TPU:0, one launch (start us, length us, event | category | flops | bytes accessed | tf_op | source)
XLA Modules:
  0.0 724.2 jit_solution(11139539443450980776)
XLA Ops:
  7.3 4.8 concatenate.21
  24.9 2.5 copy_bitcast_fusion.1
  28.4 112.9 %opening.1 = (bf16[16,128,1792]{2,1,0:T(8,128)(2,1)}, bf16[2,8,112,384]{3,2,1,0:T(8,128)(2,1)}, bf16[4,112,800]{2,1,0:T(8,128)(2,1)}, bf16[4,112,800]{2,1,0:T(8,128)(2,1)}, bf16[16,112,1792]{2,1,0:T(8,128)(2,1)}) custom-call(bf16[128,1792]{1,0:T(8,128)(2,1)} %copy.80.own, bf16[8,112,384]{2,1,0:T(8,128)(2,1)} %pad_maximum_fusion.blocks, ...), custom_call_target="tpu_custom_call" | custom-call | tf_op jit(solution)/shard_map/opening/pallas_call | solution.py:500
  148.6 12.3 %project.1 = (bf16[2048,1792]{1,0:T(8,128)(2,1)}, bf16[2048,384]{1,0:T(8,128)(2,1)}) custom-call(bf16[2048,1792]{1,0:T(8,128)(2,1)} %bitcast.157, f32[1,1792]{1,0:T(1,128)} %unstack.23.gain_ref, f32[1,1792]{1,0:T(1,128)} %unstack.25.shift_ref, f32[1,1792]{1,0:T(1,128)} %constant.136.mask_ref, bf16[1792,384]{1,0:T(8,128)(2,1)} %bitcast.149, ...), custom_call_target="tpu_custom_call" | custom-call | flops 2818572288 | bytes 14680064 | tf_op jit(solution)/shard_map/project/pallas_call | solution.py:892
  160.9 27.3 %attend.1 = (bf16[2048,128]{1,0:T(8,128)(2,1)}, f32[8,2,256]{2,1,0:T(2,128)}) custom-call(s32[16]{0:T(128)} %copy-done.20, s32[8]{0:T(128)} %and_select_fusion.low_ref, bf16[2048,384]{1,0:T(8,128)(2,1)} %get-tuple-element.30.qkv_ref, s32[8,1,256]{2,1,0:T(1,128)} %bitcast.152), custom_call_target="tpu_custom_call" | custom-call | flops 1073741824 | bytes 2097152 | tf_op jit(solution)/shard_map/attend/pallas_call | solution.py:156
  188.2 13.7 %to_tokens.1 = bf16[128,2048]{1,0:T(8,128)(2,1)} custom-call(bf16[16,128,128]{2,1,0:T(8,128)(2,1)} %bitcast.137), custom_call_target="tpu_custom_call" | custom-call | tf_op jit(solution)/shard_map/to_tokens/pallas_call | solution.py:537
  203.3 4.0 fusion.32
  208.7 36.7 %group_gather.1 = bf16[8,128,1792]{2,1,0:T(8,128)(2,1)} custom-call(bf16[128,1792]{1,0:T(8,128)(2,1)} %add_convert_fusion.own), custom_call_target="tpu_custom_call" | custom-call | tf_op jit(solution)/shard_map/group_gather/pallas_call | solution.py:410
  246.1 8.0 %fusion.35 = f32[1024,800]{0,1:T(8,128)} fusion(bf16[1024,1792]{1,0:T(8,128)(2,1)} %bitcast.120, bf16[1792,800]{1,0:T(8,128)(2,1)} %all-gather.4.cloned.1.call-done), kind=kOutput, calls=%fused_computation.112 | convolution fusion | flops 2936012800 | bytes 9814016 | tf_op jit(solution)/shard_map/dot_general | solution.py:58
  254.1 39.4 %all-gather.6.cloned.1.call-done = bf16[1792,800]{1,0:T(8,128)(2,1)} async-done(((bf16[448,800]{1,0:T(8,128)(2,1)}), bf16[1792,800]{1,0:T(8,128)(2,1)}) %all-gather.6.cloned.1.call-update) | async-done | bytes 2867216 | tf_op jit(solution)/shard_map/all_gather | solution.py:928
  293.5 9.7 %convolution_convert_fusion.3 = bf16[1024,1792]{1,0:T(8,128)(2,1)} fusion(bf16[1792,800]{1,0:T(8,128)(2,1)} %all-gather.6.cloned.1.call-done, f32[1024,800]{0,1:T(8,128)} %fusion.35, f32[800]{0:T(1024)S(1)} %dynamic-slice_convert_fusion), kind=kOutput, calls=%fused_computation.6 | convolution fusion | flops 2946039808 | bytes 9817216 | tf_op jit(solution)/shard_map/dot_general | solution.py:58
  303.4 23.1 %all-gather.8.cloned.1.call-done = bf16[1024,1792]{0,1:T(8,128)(2,1)} async-done(((bf16[128,1792]{0,1:T(8,128)(2,1)}), bf16[1024,1792]{0,1:T(8,128)(2,1)}) %all-gather.8.cloned.1.call-update) | async-done | bytes 3670032 | tf_op jit(solution)/shard_map/all_gather | solution.py:928
  326.5 9.5 %fusion.33 = (f32[800]{0:T(1024)S(1)}, bf16[1024,800]{0,1:T(8,128)(2,1)S(1)}) fusion(f32[1024,800]{0,1:T(8,128)} %fusion.35, f32[800]{0:T(1024)S(1)} %dynamic-slice_convert_fusion, bf16[1024,1792]{0,1:T(8,128)(2,1)} %all-gather.8.cloned.1.call-done, bf16[1792,800]{1,0:T(8,128)(2,1)} %all-gather.6.cloned.1.call-done), kind=kOutput, calls=%fused_computation.110 | convolution fusion | flops 2953215232 | bytes 11458816 | tf_op jit(solution)/shard_map/dot_general | solution.py:58
  337.1 5.4 convolution_convert_fusion.5
  346.3 9.4 %convolution_convert_fusion.4 = bf16[1792,800]{1,0:T(8,128)(2,1)} fusion(bf16[1024,1792]{0,1:T(8,128)(2,1)} %all-gather.8.cloned.1.call-done, f32[1024,800]{0,1:T(8,128)} %fusion.35, f32[800]{0:T(1024)S(1)} %dynamic-slice_convert_fusion), kind=kOutput, calls=%fused_computation.7 | convolution fusion | flops 2945638400 | bytes 9817216 | tf_op jit(solution)/shard_map/dot_general | solution.py:58
  355.8 7.9 %convolution_convert_fusion.2 = bf16[1024,1792]{1,0:T(8,128)(2,1)} fusion(bf16[1792,800]{1,0:T(8,128)(2,1)} %all-gather.4.cloned.1.call-done, bf16[1024,800]{0,1:T(8,128)(2,1)S(1)} %copy-done.22), kind=kOutput, calls=%fused_computation.5 | convolution fusion | flops 2937847808 | bytes 8175616 | tf_op jit(solution)/shard_map/dot_general | solution.py:58
  363.7 47.4 %group_scatter.1 = f32[128,1792]{1,0:T(8,128)} custom-call(bf16[8,128,1792]{2,1,0:T(8,128)(2,1)} %bitcast.122), custom_call_target="tpu_custom_call" | custom-call | tf_op jit(solution)/shard_map/group_scatter/pallas_call | solution.py:669
  413.0 14.0 %reduce-scatter.4.cloned.1.call-done = bf16[128,1792]{1,0:T(8,128)(2,1)} async-done(((bf16[1024,1792]{1,0:T(8,128)(2,1)}), bf16[128,1792]{1,0:T(8,128)(2,1)}) %reduce-scatter.4.cloned.1.call-update) | async-done | bytes 458768 | tf_op jit(solution)/shard_map/reduce_scatter | solution.py:999
  427.0 2.7 fusion.30
  429.7 5.0 convolution_convert_fusion.7
  436.3 20.6 %to_heads.1 = bf16[16,128,128]{2,1,0:T(8,128)(2,1)} custom-call(bf16[128,2048]{1,0:T(8,128)(2,1)} %pad.56.src), custom_call_target="tpu_custom_call" | custom-call | tf_op jit(solution)/shard_map/to_heads/pallas_call | solution.py:568
  456.9 27.8 %attend_back.1 = f32[2048,384]{1,0:T(8,128)} custom-call(s32[16]{0:T(128)} %copy-done.20, s32[8]{0:T(128)} %and_select_fusion.low_ref, bf16[2048,384]{1,0:T(8,128)(2,1)} %get-tuple-element.30.qkv_ref, bf16[2048,128]{1,0:T(8,128)(2,1)} %get-tuple-element.31.out_ref, bf16[2048,128]{1,0:T(8,128)(2,1)} %bitcast.138, f32[8,2,256]{2,1,0:T(2,128)} %get-tuple-element.35.lse_ref, ...), custom_call_target="tpu_custom_call" | custom-call | flops 2684354560 | bytes 7864320 | tf_op jit(solution)/shard_map/attend_back/pallas_call | solution.py:256
  484.8 4.9 convolution_convert_fusion
  489.7 6.1 convolution_convert_fusion.1
  495.8 5.2 convolution_convert_fusion.6
  501.0 151.9 %closing.1 = (f32[128,1792]{1,0:T(8,128)}, bf16[2,8,112,384]{3,2,1,0:T(8,128)(2,1)}, bf16[2,112,896]{2,1,0:T(8,128)(2,1)}) custom-call(bf16[16,128,1792]{2,1,0:T(8,128)(2,1)} %bitcast.115, bf16[2,8,112,384]{3,2,1,0:T(8,128)(2,1)} %bitcast.130, bf16[16,112,1792]{2,1,0:T(8,128)(2,1)} %bitcast.113), custom_call_target="tpu_custom_call" | custom-call | tf_op jit(solution)/shard_map/closing/pallas_call | solution.py:801
  655.6 4.4 all-to-all-start
  664.8 7.0 all-to-all-done
  671.9 4.2 all-to-all-start.1
  684.0 13.5 %vectors_sum.1 = (f32[8,128]{1,0:T(8,128)}, f32[4,8,128]{2,1,0:T(8,128)}) custom-call(f32[16,16,128]{2,1,0:T(8,128)} %bitcast.140), custom_call_target="tpu_custom_call" | custom-call | tf_op jit(solution)/shard_map/vectors_sum/pallas_call | solution.py:858
  704.9 2.4 copy.96
  707.3 2.5 copy.100
  (194 shorter events, 62.8 us)
Async XLA Ops:
  7.2 139.7 %copy-start = (s32[1,2048]{1,0:T(1,128)S(1)}, s32[1,2048]{1,0:T(1,128)}, u32[]{:S(2)}) copy-start(s32[1,2048]{1,0:T(1,128)} %param.18) | copy-start | bytes 24580
  7.2 8.2 %copy-start.12 = (bf16[1,128,1600]{1,2,0:T(8,128)(2,1)S(1)}, bf16[1,128,1600]{1,2,0:T(8,128)(2,1)}, u32[]{:S(2)}) copy-start(bf16[1,128,1600]{1,2,0:T(8,128)(2,1)} %param.17) | copy-start | bytes 1228804
  7.2 9.3 %copy-start.11 = (bf16[100,3200]{1,0:T(8,128)(2,1)S(1)}, bf16[100,3200]{1,0:T(8,128)(2,1)}, u32[]{:S(2)}) copy-start(bf16[100,3200]{1,0:T(8,128)(2,1)} %param.28) | copy-start | bytes 1920004
  7.2 238.9 %all-gather.4.cloned.1.call-start = ((), (), s32[]{:S(2)}) async-start(), calls=%async_computation.5 | async-start | bytes 4014080 | tf_op jit(solution)/shard_map/all_gather | solution.py:928
  15.5 5.2 copy-start.10
  22.4 2.6 copy-start.6
  27.5 114.7 %copy-start.13 = (bf16[1,128,1600]{1,2,0:T(8,128)(2,1)S(1)}, bf16[1,128,1600]{1,2,0:T(8,128)(2,1)}, u32[]{:S(2)}) copy-start(bf16[1,128,1600]{1,2,0:T(8,128)(2,1)} %param.32) | copy-start | bytes 1228804
  141.3 5.5 copy-start.19
  141.3 152.1 %all-gather.6.cloned.1.call-start = ((), (), s32[]{:S(2)}) async-start(), calls=%async_computation.6 | async-start | bytes 4014080 | tf_op jit(solution)/shard_map/all_gather | solution.py:928
  142.1 184.4 %all-gather.8.cloned.1.call-start = ((), (), s32[]{:S(2)}) async-start(), calls=%async_computation.8 | async-start | bytes 4128768 | tf_op jit(solution)/shard_map/all_gather | solution.py:928
  143.0 284.0 %reduce-scatter.4.cloned.1.call-start = ((), (), s32[]{:S(2)}) async-start(), calls=%async_computation.7 | async-start | bytes 4128768 | tf_op jit(solution)/shard_map/reduce_scatter | solution.py:999
  146.9 14.0 %copy-start.20 = (s32[16]{0:T(128)}, s32[16]{0:T(128)S(1)}, u32[]{:S(2)}) copy-start(s32[16]{0:T(128)S(1)} %select_reduce_fusion.1.inv_ref) | copy-start | bytes 196
  147.8 13.1 %copy-start.16 = (s32[2048]{0:T(1024)}, s32[2048]{0:T(1024)S(1)}, u32[]{:S(2)}) copy-start(s32[2048]{0:T(1024)S(1)} %select_reduce_fusion) | copy-start | bytes 24580
  188.2 15.1 %copy-start.2 = (bf16[128,1792]{1,0:T(8,128)(2,1)S(1)}, bf16[128,1792]{1,0:T(8,128)(2,1)}, u32[]{:S(2)}) copy-start(bf16[128,1792]{1,0:T(8,128)(2,1)} %copy.80.own) | copy-start | bytes 1376260
  203.3 4.0 copy-start.14
  303.2 352.4 %reduce-scatter.6.cloned.1.call-start = ((), (), s32[]{:S(2)}) async-start(), calls=%async_computation.9 | async-start | bytes 4014080 | tf_op jit(solution)/shard_map/reduce_scatter | solution.py:1008
  326.5 10.6 %copy-start.4 = (bf16[8,128,1792]{2,1,0:T(8,128)(2,1)S(1)}, bf16[8,128,1792]{2,1,0:T(8,128)(2,1)}, u32[]{:S(2)}) copy-start(bf16[8,128,1792]{2,1,0:T(8,128)(2,1)} %group_gather.1) | copy-start | bytes 11010052
  336.0 1.2 copy-start.21
  342.5 3.4 copy-start.17
  342.6 322.2 %reduce-scatter.8.cloned.1.call-start = ((), (), s32[]{:S(2)}) async-start(), calls=%async_computation.10 | async-start | bytes 4014080 | tf_op jit(solution)/shard_map/reduce_scatter | solution.py:1008
  346.3 9.5 %copy-start.22 = (bf16[1024,800]{0,1:T(8,128)(2,1)S(1)}, bf16[1024,800]{0,1:T(8,128)(2,1)}, u32[]{:S(2)}) copy-start(bf16[1024,800]{0,1:T(8,128)(2,1)} %copy-done.21) | copy-start | bytes 4915204
  363.7 63.3 %copy-start.8 = (bf16[128,1792]{1,0:T(8,128)(2,1)S(1)}, bf16[128,1792]{1,0:T(8,128)(2,1)}, u32[]{:S(2)}) copy-start(bf16[128,1792]{1,0:T(8,128)(2,1)} %copy.90) | copy-start | bytes 1376260
  456.9 27.8 %copy-start.7 = (bf16[128,16,112]{0,2,1:T(8,128)(2,1)S(1)}, bf16[128,16,112]{0,2,1:T(8,128)(2,1)}, u32[]{:S(2)}) copy-start(bf16[128,16,112]{0,2,1:T(8,128)(2,1)} %pad.54) | copy-start | bytes 1376260
  484.7 4.9 copy-start.9
  484.7 4.9 copy-start.15
  484.8 11.0 %slice-start = ((s8[7340032]{0:T(1024)(128)(4,1)}), s8[4194304]{0:T(1024)(128)(4,1)S(1)}, s32[]{:S(2)}) async-start(s8[7340032]{0:T(1024)(128)(4,1)} %bitcast.159), calls=%async_computation.11 | async-start | bytes 8388608
  489.7 6.1 slice-start.1
  655.6 8.8 %copy-start.5 = (f32[128,1792]{1,0:T(8,128)S(1)}, f32[128,1792]{1,0:T(8,128)}, u32[]{:S(2)}) copy-start(f32[128,1792]{1,0:T(8,128)} %get-tuple-element.37) | copy-start | bytes 2752516
  655.6 16.3 %all-to-all-start = ((bf16[4,112,800]{2,1,0:T(8,128)(2,1)}), bf16[4,112,800]{2,1,0:T(8,128)(2,1)}, u32[]{:S(2)}, u32[]{:S(2)}) async-start(bf16[4,112,800]{2,1,0:T(8,128)(2,1)} %bitcast.134), calls=%async_computation.2 | async-start | bytes 1605632 | tf_op jit(solution)/shard_map/all_to_all | solution.py:1009
  671.9 41.9 %all-to-all-start.1 = ((bf16[4,112,800]{2,1,0:T(8,128)(2,1)}), bf16[4,112,800]{2,1,0:T(8,128)(2,1)}, u32[]{:S(2)}, u32[]{:S(2)}) async-start(bf16[4,112,800]{2,1,0:T(8,128)(2,1)} %bitcast.131), calls=%async_computation.4 | async-start | bytes 1605632 | tf_op jit(solution)/shard_map/all_to_all | solution.py:1009
  707.2 2.5 copy-start.18
  713.8 3.4 copy-start.1
  (1 other events, 1.0 us)
Sparse Core Ops, SparseCore 0:
  141.4 79.8 all-gather.3
  223.2 70.2 all-gather.5
  295.5 30.9 all-gather.7
  328.7 98.3 reduce-scatter.3
  429.9 83.2 reduce-scatter.5
  516.0 129.3 reduce-scatter.7

commit v4 on v3

--- a/solution.py
+++ b/solution.py
@@ -419,7 +419,7 @@
 
 
 def opening_kernel(
-    own, blocks, fc, proj, out_w, out, blocks_all, fc_all, proj_all, out_w_all, send, recv, recv_w, recv_f, recv_o, recv_p
+    own, blocks, ffn, out_w, out, blocks_all, ffn_all, out_w_all, send, recv, recv_w, recv_f, recv_o
 ):
     place, group = Place(True), Place(False)
     n_ctx = blocks.shape[0]
@@ -448,10 +448,8 @@
 
     gather_begin(place, own, out, copies, recv)
     for k in others(group.ctx, 4):
-        copies.send(fc.at[k], fc_all.at[group.ctx], recv_f.at[group.ctx], group.at_ctx(k))
-        copies.send(proj.at[k], proj_all.at[group.ctx], recv_p.at[group.ctx], group.at_ctx(k))
-    copies.local(fc.at[group.ctx], fc_all.at[group.ctx])
-    copies.local(proj.at[group.ctx], proj_all.at[group.ctx])
+        copies.send(ffn.at[:, k], ffn_all.at[:, group.ctx], recv_f.at[group.ctx], group.at_ctx(k))
+    copies.local(ffn.at[:, group.ctx], ffn_all.at[:, group.ctx])
     for k in far_ctx:
         copies.send(blocks.at[k], mine, sem_w(place.x, place.ctx), place.at_ctx(k))
     copies.local(blocks.at[place.ctx], mine)
@@ -484,8 +482,7 @@
     for k in [place.ctx] + far_ctx:
         copies.arrived(blocks_all.at[1 - place.x, k], sem_w(1 - place.x, k), peer_x)
     for k in others(group.ctx, 4):
-        copies.arrived(fc_all.at[k], recv_f.at[k], group.at_ctx(k))
-        copies.arrived(proj_all.at[k], recv_p.at[k], group.at_ctx(k))
+        copies.arrived(ffn_all.at[:, k], recv_f.at[k], group.at_ctx(k))
     for x in (place.x, 1 - place.x):
         for z in [place.z] + place.far_z():
             for y in (place.y, 1 - place.y):
@@ -493,7 +490,7 @@
     copies.finish()
 
 
-def opening(own, blocks, fc, proj, out_w):
+def opening(own, blocks, ffn, out_w):
     n_ctx = blocks.shape[0]
     n_z = n_ctx // 2
     sends = gather_copies(n_z) + 2 * n_ctx + 8 + (n_z - 1) + 4 + 3 * n_z + 2 * n_z + 2 * n_z
@@ -502,16 +499,15 @@
         out_shape=(
             jax.ShapeDtypeStruct((2 * n_ctx,) + own.shape, own.dtype),
             jax.ShapeDtypeStruct((2,) + blocks.shape, blocks.dtype),
-            jax.ShapeDtypeStruct(fc.shape, fc.dtype),
-            jax.ShapeDtypeStruct(proj.shape, proj.dtype),
+            jax.ShapeDtypeStruct(ffn.shape, ffn.dtype),
             jax.ShapeDtypeStruct((2 * n_ctx,) + out_w.shape, out_w.dtype),
         ),
-        in_specs=[ANY] * 5,
-        out_specs=(ANY,) * 5,
-        scratch_shapes=dma_sems(sends, 2 * n_ctx, 2 * n_ctx, 4, 4 * n_ctx, 4),
+        in_specs=[ANY] * 4,
+        out_specs=(ANY,) * 4,
+        scratch_shapes=dma_sems(sends, 2 * n_ctx, 2 * n_ctx, 4, 4 * n_ctx),
         compiler_params=comm_params(1),
         name="opening",
-    )(own, blocks, fc, proj, out_w)
+    )(own, blocks, ffn, out_w)
 
 
 def to_tokens_kernel(src, dst, send, recv):
@@ -746,11 +742,11 @@
 
 
 def closing_kernel(
-    part, grads, out_part, out, grads_out, out_w_out,
+    part, grads, out_part, fc, proj, out, grads_out, out_w_out, fc_out, proj_out,
     held, from_c, from_y, from_z, own_x, from_x, o_held, o_c, o_x, o_y, o_z,
-    send, loads, rc, ry, rz, load_x, rx, rk, rg, o_loads, orc, orx, ory, orz, org,
+    send, loads, rc, ry, rz, load_x, rx, rk, rg, o_loads, orc, orx, ory, orz, org, rfc, rproj,
 ):
-    place = Place(True)
+    place, group = Place(True), Place(False)
     n_ctx = grads.shape[1]
     copies = Copies(send)
     far_ctx = others(place.ctx, n_ctx)
@@ -763,6 +759,11 @@
         copies.send(grads.at[1 - place.x, k], from_x.at[k], rx.at[k], peer_x)
         copies.local(grads.at[place.x, k], own_x.at[k], load_x.at[k])
     outs.begin()
+    for k in others(group.ctx, 4):
+        copies.send(fc.at[k], fc_out.at[group.ctx], rfc.at[group.ctx], group.at_ctx(k))
+        copies.send(proj.at[k], proj_out.at[group.ctx], rproj.at[group.ctx], group.at_ctx(k))
+    copies.local(fc.at[group.ctx], fc_out.at[group.ctx])
+    copies.local(proj.at[group.ctx], proj_out.at[group.ctx])
     sums.over_c_far()
     mine = grads_out.at[place.y, place.ctx]
     for k in far_ctx + [place.ctx]:
@@ -788,10 +789,13 @@
     for k in [place.ctx] + far_ctx:
         copies.arrived(grads_out.at[1 - place.y, k], rg.at[k], peer_y)
     outs.end()
+    for k in others(group.ctx, 4):
+        copies.arrived(fc_out.at[k], rfc.at[k], group.at_ctx(k))
+        copies.arrived(proj_out.at[k], rproj.at[k], group.at_ctx(k))
     copies.finish()
 
 
-def closing(part, grads, out_part):
+def closing(part, grads, out_part, fc, proj):
     block = part.shape[1:]
     n_ctx = grads.shape[1]
     n_z = n_ctx // 2
@@ -804,19 +808,21 @@
             jax.ShapeDtypeStruct(block, F32),
             jax.ShapeDtypeStruct((2,) + piece, B16),
             jax.ShapeDtypeStruct((2,) + half, B16),
+            jax.ShapeDtypeStruct(fc.shape, fc.dtype),
+            jax.ShapeDtypeStruct(proj.shape, proj.dtype),
         ),
-        in_specs=[ANY] * 3,
-        out_specs=(IN_VMEM, ANY, IN_VMEM),
+        in_specs=[ANY] * 5,
+        out_specs=(IN_VMEM, ANY, IN_VMEM, ANY, ANY),
         scratch_shapes=scatter_scratch(n_z, block)
         + [pltpu.VMEM(piece, B16), pltpu.VMEM(piece, B16)]
         + [pltpu.VMEM((2 * n_z, rows, width), B16), pltpu.VMEM((2 * n_z, rows, width), B16)]
         + [pltpu.VMEM((n_z, rows, width), B16), pltpu.VMEM((n_z,) + half, B16), pltpu.VMEM((n_z,) + half, B16)]
-        + scatter_sems(n_z, 3 * n_ctx + 6 * n_z)
+        + scatter_sems(n_z, 3 * n_ctx + 6 * n_z + 8)
         + dma_sems(n_ctx, n_ctx, n_ctx, n_ctx)
-        + dma_sems(2 * n_z, 2 * n_z, n_z, n_z, n_z, 2),
+        + dma_sems(2 * n_z, 2 * n_z, n_z, n_z, n_z, 2, 4, 4),
         compiler_params=comm_params(4),
         name="closing",
-    )(part, grads, out_part)
+    )(part, grads, out_part, fc, proj)
 
 
 def vectors_kernel(src, own_out, ff_out, from_all, half, from_y, send, recv, ry):
@@ -905,6 +911,15 @@
     )(x, gain[None], shift[None], mask[None], weight, bias[None])
 
 
+def after(value, other, unpack=False):
+    value, other = lax.optimization_barrier((value, other))
+    return (*value, other) if unpack else (value, other)
+
+
+def shift_perm(count, step):
+    return [(i, (i + step) % count) for i in range(count)]
+
+
 def on_device(
     sizes, block_input, segment_ids, slot_order, first_gain, first_shift, qkv_weight, qv_bias, out_weight, out_bias,
     second_gain, second_shift, fc_weight, fc_bias, proj_weight, proj_bias, out_grad,
@@ -923,6 +938,7 @@
     ctx_at = lax.axis_index(CTX)
     slot_at = lax.axis_index(ROW)
     lc_at = lax.axis_index(("l", "c"))
+    x_at, h_at = lax.axis_index("x"), lax.axis_index("h")
 
     def gather(value, axes):
         return lax.all_gather(value, axes, axis=0, tiled=True)
@@ -948,16 +964,18 @@
     packed = packed.transpose(2, 0, 1, 3).reshape(n_ctx, rows, 3 * pair)
     small = jnp.pad(small, (0, row_pad * 3 * pair - small.shape[0])).reshape(1, row_pad, 3 * pair)
     packed = jnp.concatenate([packed, jnp.broadcast_to(small, (n_ctx, row_pad, 3 * pair))], axis=1)
-    fc_blocks = jnp.pad(fc_weight, ((0, row_pad), (0, 0))).reshape(tall, 4, ff_own).transpose(1, 0, 2)
-    proj_blocks = jnp.pad(proj_weight.T, ((0, row_pad), (0, 0))).reshape(tall, 4, ff_own).transpose(1, 0, 2)
+    ffn_blocks = jnp.stack([fc_weight, proj_weight.T])
+    ffn_blocks = jnp.pad(ffn_blocks, ((0, 0), (0, row_pad), (0, 0))).reshape(2, tall, 4, ff_own).transpose(0, 2, 1, 3)
     own_input = widened(block_input[0])
     grad_own = widened(out_grad[0])
-    grad_all = gather(grad_own, FFG)
-    all_input, packed, fc_blocks, proj_blocks, w_out = opening(
-        own_input, packed, fc_blocks, proj_blocks, widened(jnp.pad(out_weight, ((0, row_pad), (0, 0))))
+    all_input, packed, ffn_blocks, w_out = opening(
+        own_input, packed, ffn_blocks, widened(jnp.pad(out_weight, ((0, row_pad), (0, 0))))
     )
-    w_fc = gather(fc_blocks.reshape(4 * tall, ff_own), ("x", "h"))
-    w_proj = gather(proj_blocks.reshape(4 * tall, ff_own), ("x", "h"))
+    grad_late, all_input = after(grad_own, all_input)
+    grad_all = gather(grad_late, FFG)
+    ffn_blocks = ffn_blocks.reshape(2, 4 * tall, ff_own)
+    along_h = [lax.ppermute(ffn_blocks, "h", shift_perm(n_h, step)) for step in range(1, n_h)]
+    along_x = lax.ppermute(ffn_blocks, "x", shift_perm(n_x, 1))
     w_out = w_out.reshape(wide, wide)
     packed = packed.reshape(n_shard, tall, 3 * pair)
     w_qkv = packed.reshape(wide, 3 * pair)
@@ -991,38 +1009,75 @@
     normed_two, inv_two = norm_forward(hidden, mask, feats)
     norm_two = (normed_two * gain_two + shift_two).astype(B16)
     grad_wide = grad_own.astype(F32)
+    along_h, grad_all, norm_two = after((along_h, grad_all), norm_two, True)
+    along_both = [lax.ppermute(value, "x", shift_perm(n_x, 1)) for value in along_h]
     norm_all = group_gather(norm_two, 6).reshape(-1, wide)
+    w_ffn = jnp.zeros((2, n_x, n_h, 4 * tall, ff_own), B16)
+
+    def put(whole, value, x, h):
+        return lax.dynamic_update_slice(whole, value[:, None, None], (0, x, h, 0, 0))
+
+    w_ffn = put(put(w_ffn, ffn_blocks, x_at, h_at), along_x, 1 - x_at, h_at)
+    for step in range(1, n_h):
+        h_from = lax.rem(h_at + n_h - step, n_h)
+        w_ffn = put(put(w_ffn, along_h[step - 1], x_at, h_from), along_both[step - 1], 1 - x_at, h_from)
+    w_fc, w_proj = w_ffn[0].reshape(wide, ff_own), w_ffn[1].reshape(wide, ff_own)
     preact = dot(norm_all, w_fc, 1, 0) + b_fc
     activated, derivative = gelu_parts(preact)
     activation = activated.astype(B16)
     mlp_part = dot(activation, w_proj, 1, 1).astype(B16)
-    mlp = lax.psum_scatter(mlp_part, FFG, scatter_dimension=0, tiled=True).astype(F32)
-    block_output = narrowed(hidden + mlp + bias_proj)
 
     dpreact = dot(grad_all, w_proj, 1, 0) * derivative
     dpreact_b = dpreact.astype(B16)
     dnorm_part = dot(dpreact_b, w_fc, 1, 1).astype(B16)
     dnorm_two = group_scatter(dnorm_part.reshape(8, slot_len, wide), 7)
 
-    def owner_sum(value):
-        value = lax.psum_scatter(value.astype(B16), ("x", "h"), scatter_dimension=0, tiled=True)
-        value = lax.all_to_all(value.reshape(4, tall, ff_own), ("l", "c"), 0, 0, tiled=True)
-        return value[:, :rows].astype(F32)
-
-    proj_grad = owner_sum(dot(grad_all, activation, 0, 0)).transpose(0, 2, 1).reshape(4 * ff_own, rows)
-    fc_grad = owner_sum(dot(norm_all, dpreact_b, 0, 0)).transpose(1, 0, 2).reshape(rows, 4 * ff_own)
-
+    def pick(value, at):
+        return lax.dynamic_index_in_dim(value, at, 0, False)
+
+    def by_owner(value):
+        return value.astype(B16).reshape(n_x, n_h, 4 * tall, ff_own)
+
+    proj_part = by_owner(dot(grad_all, activation, 0, 0))
+    proj_x = lax.ppermute(pick(proj_part, 1 - x_at), "x", shift_perm(n_x, 1))
+    fc_part = by_owner(dot(norm_all, dpreact_b, 0, 0))
+    fc_x = lax.ppermute(pick(fc_part, 1 - x_at), "x", shift_perm(n_x, 1))
+
+    def over_h(value):
+        gives = [pick(value, lax.rem(h_at + step, n_h)) for step in range(1, n_h)]
+        return [lax.ppermute(give, "h", shift_perm(n_h, step + 1)) for step, give in enumerate(gives)]
+
+    def total(value, received):
+        value = pick(value, h_at).astype(F32)
+        for other in received:
+            value = value + other
+        return value.astype(B16).reshape(4, tall, ff_own)
+
+    proj_x, mlp_part, dnorm_two = after((proj_x, mlp_part), dnorm_two, True)
+    proj_line = pick(proj_part, x_at) + proj_x
+    proj_h = over_h(proj_line)
+    mlp = lax.psum_scatter(mlp_part, FFG, scatter_dimension=0, tiled=True)
     dhidden = grad_wide + norm_backward(dnorm_two, normed_two, inv_two, gain_two, feats)
     dhidden_b = dhidden.astype(B16)
     out_part = dot(attention, dhidden_b, 0, 0).astype(B16).reshape(n_shard, tall, wide)
     dattention = narrowed(dot(dhidden_b, w_out, 1, 1).astype(B16))
     dattention = jnp.pad(dattention, ((0, 0), (0, padded - feats)))
     dattention = to_heads(dattention, n_slot).reshape(n_slot * slot_len, pair)
+    fc_x, dattention = after(fc_x, dattention)
+    fc_line = pick(fc_part, x_at) + fc_x
+    fc_h = over_h(fc_line)
     dqkv = attend_back(inv, low, qkv, heads_out, dattention, lse, start3, slot_len, head)
     dqkv_b = dqkv.astype(B16)
     dnorm_one_part = dot(dqkv_b, w_qkv, 1, 1).astype(B16)
     qkv_part = dot(norm_one, dqkv_b, 0, 0).astype(B16).reshape(n_x, n_ctx, tall, 3 * pair)
-    dnorm_one, qkv_all, out_all = closing(dnorm_one_part.reshape(n_slot, slot_len, wide), qkv_part, out_part)
+    proj_h, fc_h, dnorm_one_part = after((proj_h, fc_h), dnorm_one_part, True)
+    dnorm_one, qkv_all, out_all, fc_all, proj_all = closing(
+        dnorm_one_part.reshape(n_slot, slot_len, wide), qkv_part, out_part, total(fc_line, fc_h), total(proj_line, proj_h)
+    )
+    mlp, dnorm_one = after(mlp, dnorm_one)
+    block_output = narrowed(hidden + mlp.astype(F32) + bias_proj)
+    proj_grad = proj_all[:, :rows].astype(F32).transpose(0, 2, 1).reshape(4 * ff_own, rows)
+    fc_grad = fc_all[:, :rows].astype(F32).transpose(1, 0, 2).reshape(rows, 4 * ff_own)
     qkv_all = qkv_all[:, :, :rows].reshape(n_y, n_ctx, rows, 3, pair)
     qkv_grad = qkv_all.transpose(2, 3, 1, 0, 4).reshape(rows, 3, padded)
     qkv_grad = qkv_grad[:, :, :feats].reshape(rows, 3 * feats).astype(F32)

time: 729 us -> 635 us (0.87)
  Pallas kernels: 464 us -> 384 us
  waiting for transfers between devices: 84.4 us -> 28.5 us
  local copies, waits for them, and re-layouts: 58.6 us -> 98.3 us
    all_gather x3 -> x1, waiting for transfers between devices: 62.5 us -> 0.01 us  [gather(): return lax.all_gather(value, axes, axis=0, tiled=True)]
    pallas_call x1, Pallas kernels: 152 us -> 94.9 us  [closing(): pl.pallas_call(closing_kernel, out_shape=(jax.ShapeDtypeStruct(block, F32...]
    ppermute x0 -> x7, waiting for transfers between devices: none -> 28.5 us  [the longest x2 17.5 us: over_h(): lax.ppermute(give, 'h', shift_perm(n_h, step + 1))]
    pallas_call x1, Pallas kernels: 13.7 us -> 38.1 us  [to_tokens(): pl.pallas_call(to_tokens_kernel, out_shape=jax.ShapeDtypeStruct((tokens,...]
    pallas_call x1, Pallas kernels: 47.4 us -> 29.5 us  [group_scatter(): pl.pallas_call(group_scatter_kernel, out_shape=jax.ShapeDtypeStruct(block...]
    reduce_scatter x3 -> x1, waiting for transfers between devices: 14.1 us -> 0.01 us  [on_device(): mlp = lax.psum_scatter(mlp_part, FFG, scatter_dimension=0, tiled=True)]
    convert_element_type x0 -> x2, local copies, waits for them, and re-layouts: none -> 11.2 us  [by_owner(): return value.astype(B16).reshape(n_x, n_h, 4 * tall, ff_own)]
    all_to_all x2 -> x0, starting transfers between devices: 8.56 us -> none  [owner_sum(): lax.all_to_all(value.reshape(4, tall, ff_own), ('l', 'c'), 0, 0, tiled=True)]
  transfers between devices with their start and end apart: 8 -> 9, of which waited for: 4 -> 3; matrix products, arithmetic and copies ran while one was open for 17% -> 21% of each run, Pallas kernels for 49% -> 41%
where the time goes in v4:
time: 635 us; the launch traced here: 629 us
  Pallas kernels  384 us (60%)
  local copies, waits for them, and re-layouts  98.3 us (15%)
  matrix products  71.8 us (11%)
  waiting for transfers between devices  28.5 us (4%)
  other arithmetic  23.9 us (4%)
  between operations  15.3 us (2%)
  starting transfers between devices  7.22 us (1%)
    pallas_call x1, Pallas kernels, opening(): pl.pallas_call(opening_kernel, out_shape=(jax.ShapeDtypeStruct((2 * n_ctx...  113 us
    pallas_call x1, Pallas kernels, closing(): pl.pallas_call(closing_kernel, out_shape=(jax.ShapeDtypeStruct(block, F32...  94.9 us
    dot_general x11, matrix products, dot(): lax.dot_general(left, right, (((left_dim,), (right_dim,)), ((), ())), pre...  71.8 us
    pallas_call x1, Pallas kernels, to_tokens(): pl.pallas_call(to_tokens_kernel, out_shape=jax.ShapeDtypeStruct((tokens,...  38.1 us
    pallas_call x1, Pallas kernels, group_gather(): pl.pallas_call(group_gather_kernel, out_shape=jax.ShapeDtypeStruct((8,) +...  29.6 us
    pallas_call x1, Pallas kernels, group_scatter(): pl.pallas_call(group_scatter_kernel, out_shape=jax.ShapeDtypeStruct(block...  29.5 us
    pallas_call x1, Pallas kernels, attend_back(): pl.pallas_call(functools.partial(attend_back_kernel, slot_len, head), out...  21.6 us
    pallas_call x1, Pallas kernels, attend(): pl.pallas_call(functools.partial(attend_kernel, slot_len, head), out_shap...  20.3 us
  transfers between devices with their start and end apart: 9, of which 3 were waited for; matrix products, arithmetic and copies ran while one was open for 21% of the time, Pallas kernels for 41%

profile of v4, /device:TPU:0, one launch (start us, length us, event | category | flops | bytes accessed | tf_op | source)
XLA Modules:
  0.0 628.7 jit_solution(3463287664558500846)
XLA Ops:
  7.3 4.8 concatenate.21
  22.9 3.7 reshape.292
  28.9 112.8 %opening.1 = (bf16[16,128,1792]{2,1,0:T(8,128)(2,1)}, bf16[2,8,112,384]{3,2,1,0:T(8,128)(2,1)}, bf16[2,4,112,800]{3,2,1,0:T(8,128)(2,1)}, bf16[16,112,1792]{2,1,0:T(8,128)(2,1)}) custom-call(bf16[128,1792]{1,0:T(8,128)(2,1)} %copy.84.own, bf16[8,112,384]{2,1,0:T(8,128)(2,1)} %pad_maximum_fusion.blocks, bf16[2,4,112,800]{3,2,1,0:T(8,128)(2,1)} %bitcast.150, ...), custom_call_target="tpu_custom_call" | custom-call | tf_op jit(solution)/shard_map/opening/pallas_call | solution.py:497
  148.7 12.3 %project.1 = (bf16[2048,1792]{1,0:T(8,128)(2,1)}, bf16[2048,384]{1,0:T(8,128)(2,1)}) custom-call(bf16[2048,1792]{1,0:T(8,128)(2,1)} %bitcast.198, f32[1,1792]{1,0:T(1,128)} %unstack.23.gain_ref, f32[1,1792]{1,0:T(1,128)} %unstack.25.shift_ref, f32[1,1792]{1,0:T(1,128)} %constant.168.mask_ref, bf16[1792,384]{1,0:T(8,128)(2,1)} %bitcast.190, ...), custom_call_target="tpu_custom_call" | custom-call | flops 2818572288 | bytes 14680064 | tf_op jit(solution)/shard_map/project/pallas_call | solution.py:898
  161.0 20.3 %attend.1 = (bf16[2048,128]{1,0:T(8,128)(2,1)}, f32[8,2,256]{2,1,0:T(2,128)}) custom-call(s32[16]{0:T(128)} %copy-done.42, s32[8]{0:T(128)} %and_select_fusion.low_ref, bf16[2048,384]{1,0:T(8,128)(2,1)} %get-tuple-element.47.qkv_ref, s32[8,1,256]{2,1,0:T(1,128)} %bitcast.193), custom_call_target="tpu_custom_call" | custom-call | flops 1073741824 | bytes 2097152 | tf_op jit(solution)/shard_map/attend/pallas_call | solution.py:156
  181.4 38.1 %to_tokens.1 = bf16[128,2048]{1,0:T(8,128)(2,1)} custom-call(bf16[16,128,128]{2,1,0:T(8,128)(2,1)} %bitcast.178), custom_call_target="tpu_custom_call" | custom-call | tf_op jit(solution)/shard_map/to_tokens/pallas_call | solution.py:533
  220.9 4.1 fusion.38
  228.5 3.6 broadcast_in_dim.101
  236.7 29.6 %group_gather.1 = bf16[8,128,1792]{2,1,0:T(8,128)(2,1)} custom-call(bf16[128,1792]{1,0:T(8,128)(2,1)} %add_convert_fusion.own), custom_call_target="tpu_custom_call" | custom-call | tf_op jit(solution)/shard_map/group_gather/pallas_call | solution.py:410
  270.4 3.5 fusion.36
  274.3 3.3 fusion.41
  278.3 5.6 convolution_convert_fusion.5
  283.8 6.9 %fusion.39 = (f32[800]{0:T(1024)}, bf16[1024,800]{0,1:T(8,128)(2,1)}) fusion(f32[1024,800]{0,1:T(8,128)S(1)} %fusion.41, f32[800]{0:T(1024)S(1)} %dynamic-slice_convert_fusion, bf16[1024,1792]{0,1:T(8,128)(2,1)S(1)} %copy-done.40, bf16[1792,800]{1,0:T(8,128)(2,1)S(1)} %bitcast.161), kind=kOutput, calls=%fused_computation.128 | convolution fusion | flops 2953215232 | bytes 11458816 | tf_op jit(solution)/shard_map/dot_general | solution.py:58
  290.8 5.5 copy.92
  300.6 7.8 %convolution_convert_fusion.2 = bf16[1024,1792]{1,0:T(8,128)(2,1)} fusion(bf16[1792,800]{1,0:T(8,128)(2,1)S(1)} %bitcast.164, bf16[1024,800]{0,1:T(8,128)(2,1)} %get-tuple-element.148), kind=kOutput, calls=%fused_computation.5 | convolution fusion | flops 2937847808 | bytes 8175616 | tf_op jit(solution)/shard_map/dot_general | solution.py:58
  308.4 29.5 %group_scatter.1 = f32[128,1792]{1,0:T(8,128)} custom-call(bf16[8,128,1792]{2,1,0:T(8,128)(2,1)} %bitcast.157), custom_call_target="tpu_custom_call" | custom-call | tf_op jit(solution)/shard_map/group_scatter/pallas_call | solution.py:665
  337.9 9.6 %convolution_convert_fusion.3 = bf16[1024,1792]{1,0:T(8,128)(2,1)} fusion(bf16[1792,800]{1,0:T(8,128)(2,1)} %bitcast.162, f32[1024,800]{0,1:T(8,128)} %copy-done.43, f32[800]{0:T(1024)S(1)} %dynamic-slice_convert_fusion), kind=kOutput, calls=%fused_computation.6 | convolution fusion | flops 2946039808 | bytes 9817216 | tf_op jit(solution)/shard_map/dot_general | solution.py:58
  348.7 7.3 %convolution_convert_fusion.4 = bf16[1792,800]{0,1:T(8,128)(2,1)} fusion(bf16[1024,1792]{1,0:T(8,128)(2,1)} %bitcast.155, bf16[1024,800]{0,1:T(8,128)(2,1)} %get-tuple-element.148), kind=kOutput, calls=%fused_computation.7 | convolution fusion | flops 2937446400 | bytes 8175616 | tf_op jit(solution)/shard_map/dot_general | solution.py:58
  356.0 5.7 copy.93
  370.9 5.0 convolution_convert_fusion.7
  377.4 13.1 %to_heads.1 = bf16[16,128,128]{2,1,0:T(8,128)(2,1)} custom-call(bf16[128,2048]{1,0:T(8,128)(2,1)} %pad.52.src), custom_call_target="tpu_custom_call" | custom-call | tf_op jit(solution)/shard_map/to_heads/pallas_call | solution.py:564
  390.5 11.0 %collective-permute-done.5 = bf16[2,448,800]{2,1,0:T(8,128)(2,1)} collective-permute-done((bf16[2,448,800]{2,1,0:T(8,128)(2,1)}, bf16[2,448,800]{2,1,0:T(8,128)(2,1)}, u32[]{:S(2)}, u32[]{:S(2)}) %collective-permute-start.5) | collective-permute-done | bytes 1433632 | tf_op jit(solution)/shard_map/ppermute | solution.py:1044
  410.8 21.6 %attend_back.1 = f32[2048,384]{1,0:T(8,128)} custom-call(s32[16]{0:T(128)} %copy-done.42, s32[8]{0:T(128)} %and_select_fusion.low_ref, bf16[2048,384]{1,0:T(8,128)(2,1)} %get-tuple-element.47.qkv_ref, bf16[2048,128]{1,0:T(8,128)(2,1)} %get-tuple-element.48.out_ref, bf16[2048,128]{1,0:T(8,128)(2,1)} %bitcast.179, f32[8,2,256]{2,1,0:T(2,128)} %get-tuple-element.60.lse_ref, ...), custom_call_target="tpu_custom_call" | custom-call | flops 2684354560 | bytes 7864320 | tf_op jit(solution)/shard_map/attend_back/pallas_call | solution.py:256
  432.3 4.5 convolution_convert_fusion
  436.9 8.2 %convolution_convert_fusion.6 = bf16[1792,384]{1,0:T(8,128)(2,1)} fusion(bf16[2048,1792]{1,0:T(8,128)(2,1)} %get-tuple-element.62, f32[2048,384]{1,0:T(8,128)S(1)} %copy-done.21), kind=kOutput, calls=%fused_computation.19 | convolution fusion | flops 2820046848 | bytes 11862016 | tf_op jit(solution)/shard_map/dot_general | solution.py:58
  448.9 9.4 %convolution_convert_fusion.1 = bf16[2048,1792]{1,0:T(8,128)(2,1)} fusion(bf16[1792,384]{1,0:T(8,128)(2,1)} %bitcast.191, f32[2048,384]{1,0:T(8,128)} %attend_back.1), kind=kOutput, calls=%fused_computation.2 | convolution fusion | flops 2823028736 | bytes 11862016 | tf_op jit(solution)/shard_map/dot_general | solution.py:58
  459.1 16.6 %collective-permute-done.6 = bf16[448,800]{1,0:T(8,128)(2,1)} collective-permute-done((bf16[448,800]{1,0:T(8,128)(2,1)}, bf16[448,800]{1,0:T(8,128)(2,1)}, u32[]{:S(2)}, u32[]{:S(2)}) %collective-permute-start.6) | collective-permute-done | bytes 716832 | tf_op jit(solution)/shard_map/ppermute | solution.py:1048
  478.5 94.9 %closing.1 = (f32[128,1792]{1,0:T(8,128)}, bf16[2,8,112,384]{3,2,1,0:T(8,128)(2,1)}, bf16[2,112,896]{2,1,0:T(8,128)(2,1)}, bf16[4,112,800]{2,1,0:T(8,128)(2,1)}, bf16[4,112,800]{2,1,0:T(8,128)(2,1)}) custom-call(bf16[16,128,1792]{2,1,0:T(8,128)(2,1)} %bitcast.149, bf16[2,8,112,384]{3,2,1,0:T(8,128)(2,1)} %bitcast.174, bf16[16,112,1792]{2,1,0:T(8,128)(2,1)} %bitcast.143, ...), custom_call_target="tpu_custom_call" | custom-call | tf_op jit(solution)/shard_map/closing/pallas_call | solution.py:805
  583.9 3.2 copy.101
  587.1 3.2 copy.105
  591.9 3.1 reshape.335
  601.2 11.4 %vectors_sum.1 = (f32[8,128]{1,0:T(8,128)}, f32[4,8,128]{2,1,0:T(8,128)}) custom-call(f32[16,16,128]{2,1,0:T(8,128)} %bitcast.181), custom_call_target="tpu_custom_call" | custom-call | tf_op jit(solution)/shard_map/vectors_sum/pallas_call | solution.py:864
  (243 shorter events, 94.1 us)
Async XLA Ops:
  7.2 139.9 %copy-start = (s32[1,2048]{1,0:T(1,128)S(1)}, s32[1,2048]{1,0:T(1,128)}, u32[]{:S(2)}) copy-start(s32[1,2048]{1,0:T(1,128)} %param.18) | copy-start | bytes 24580
  7.2 8.2 %copy-start.25 = (bf16[1,128,1600]{1,2,0:T(8,128)(2,1)S(1)}, bf16[1,128,1600]{1,2,0:T(8,128)(2,1)}, u32[]{:S(2)}) copy-start(bf16[1,128,1600]{1,2,0:T(8,128)(2,1)} %param.17) | copy-start | bytes 1228804
  7.2 9.3 %copy-start.26 = (bf16[1,128,1600]{1,2,0:T(8,128)(2,1)S(1)}, bf16[1,128,1600]{1,2,0:T(8,128)(2,1)}, u32[]{:S(2)}) copy-start(bf16[1,128,1600]{1,2,0:T(8,128)(2,1)} %param.32) | copy-start | bytes 1228804
  7.2 219.6 %all-gather.2.cloned.1.call-start = ((), (), s32[]{:S(2)}) async-start(), calls=%async_computation.1 | async-start | bytes 4128768 | tf_op jit(solution)/shard_map/all_gather | solution.py:944
  27.9 119.0 %copy-start.41 = (s32[1,16]{1,0:T(1,128)S(1)}, s32[1,16]{1,0:T(1,128)}, u32[]{:S(2)}) copy-start(s32[1,16]{1,0:T(1,128)} %param.19) | copy-start | bytes 196
  141.7 457.8 %reduce-scatter.2.cloned.1.call-start = ((), (), s32[]{:S(2)}) async-start(), calls=%async_computation.2 | async-start | bytes 4128768 | tf_op jit(solution)/shard_map/reduce_scatter | solution.py:1059
  142.0 92.0 %collective-permute-start.1 = (bf16[2,448,800]{2,1,0:T(8,128)(2,1)}, bf16[2,448,800]{2,1,0:T(8,128)(2,1)}, u32[]{:S(2)}, u32[]{:S(2)}) collective-permute-start(bf16[2,448,800]{2,1,0:T(8,128)(2,1)} %bitcast.171), channel_id=1, source_target_pairs={{0,16},{16,0},{1,17},{17,1},{2,18},{18,2},{3,19},{19,3},{4,20},{20... | collective-permute-start | bytes 4300808 | tf_op jit(solution)/shard_map/ppermute | solution.py:978
  143.4 83.4 %collective-permute-start = (bf16[2,448,800]{2,1,0:T(8,128)(2,1)}, bf16[2,448,800]{2,1,0:T(8,128)(2,1)}, u32[]{:S(2)}, u32[]{:S(2)}) collective-permute-start(bf16[2,448,800]{2,1,0:T(8,128)(2,1)} %bitcast.172), channel_id=1, source_target_pairs={{0,8},{8,0},{1,9},{9,1},{2,10},{10,2},{3,11},{11,3},{4,12},{12,4},... | collective-permute-start | bytes 4300808 | tf_op jit(solution)/shard_map/ppermute | solution.py:977
  147.0 14.0 %copy-start.42 = (s32[16]{0:T(128)}, s32[16]{0:T(128)S(1)}, u32[]{:S(2)}) copy-start(s32[16]{0:T(128)S(1)} %select_reduce_fusion.1.inv_ref) | copy-start | bytes 196
  147.9 13.1 %copy-start.33 = (s32[2048]{0:T(1024)}, s32[2048]{0:T(1024)S(1)}, u32[]{:S(2)}) copy-start(s32[2048]{0:T(1024)S(1)} %select_reduce_fusion) | copy-start | bytes 24580
  181.4 39.5 %copy-start.3 = (bf16[128,1792]{1,0:T(8,128)(2,1)S(1)}, bf16[128,1792]{1,0:T(8,128)(2,1)}, u32[]{:S(2)}) copy-start(bf16[128,1792]{1,0:T(8,128)(2,1)} %copy.84.own) | copy-start | bytes 1376260
  220.9 7.3 %copy-start.35 = (f32[16,112]{1,0:T(8,128)S(1)}, f32[16,112]{1,0:T(8,128)}, u32[]{:S(2)}) copy-start(f32[16,112]{1,0:T(8,128)} %constant.169) | copy-start | bytes 21508
  226.8 42.2 %collective-permute-start.2 = (bf16[2,448,800]{2,1,0:T(8,128)(2,1)}, bf16[2,448,800]{2,1,0:T(8,128)(2,1)S(1)}, u32[]{:S(2)}, u32[]{:S(2)}) collective-permute-start(bf16[2,448,800]{2,1,0:T(8,128)(2,1)} %collective-permute-done), channel_id=1, source_target_pairs={{0,16},{16,0},{1,17},{17,1},{2,18},{18,2},{3,19},{19,3},{4,20},{20... | collective-permute-start | bytes 4300808 | tf_op jit(solution)/shard_map/ppermute | solution.py:1013
  273.9 9.9 %copy-start.15 = (bf16[1,2,2,448,800]{4,3,0,2,1:T(8,128)(2,1)}, bf16[1,2,2,448,800]{4,3,0,2,1:T(8,128)(2,1)S(1)}, u32[]{:S(2)}) copy-start(bf16[1,2,2,448,800]{4,3,0,2,1:T(8,128)(2,1)S(1)} %get-tuple-element.134) | copy-start | bytes 8601604
  278.3 5.6 copy-start.43
  299.2 48.3 %collective-permute-start.3 = (bf16[2,448,800]{2,1,0:T(8,128)(2,1)}, bf16[2,448,800]{2,1,0:T(8,128)(2,1)S(1)}, u32[]{:S(2)}, u32[]{:S(2)}) collective-permute-start(bf16[2,448,800]{2,1,0:T(8,128)(2,1)} %dynamic-slice_bitcast_fusion.1), channel_id=1, source_target_pairs={{0,16},{16,0},{1,17},{17,1},{2,18},{18,2},{3,19},{19,3},{4,20},{20... | collective-permute-start | bytes 4300808 | tf_op jit(solution)/shard_map/ppermute | solution.py:1042
  356.0 9.1 %copy-start.11 = (bf16[128,16,100]{0,2,1:T(8,128)(2,1)S(1)}, bf16[128,16,100]{0,2,1:T(8,128)(2,1)}, u32[]{:S(2)}) copy-start(bf16[128,16,100]{0,2,1:T(8,128)(2,1)} %copy-done.10) | copy-start | bytes 1228804
  361.7 7.2 %copy-start.4 = (f32[128,1792]{1,0:T(8,128)S(1)}, f32[128,1792]{1,0:T(8,128)}, u32[]{:S(2)}) copy-start(f32[128,1792]{1,0:T(8,128)} %group_scatter.1) | copy-start | bytes 2752516
  364.5 37.0 %collective-permute-start.5 = (bf16[2,448,800]{2,1,0:T(8,128)(2,1)}, bf16[2,448,800]{2,1,0:T(8,128)(2,1)}, u32[]{:S(2)}, u32[]{:S(2)}) collective-permute-start(bf16[2,448,800]{2,1,0:T(8,128)(2,1)} %dynamic-slice_bitcast_fusion), channel_id=1, source_target_pairs={{0,16},{16,0},{1,17},{17,1},{2,18},{18,2},{3,19},{19,3},{4,20},{20... | collective-permute-start | bytes 4300808 | tf_op jit(solution)/shard_map/ppermute | solution.py:1044
  401.5 5.3 copy-start.2
  403.7 4.6 copy-start.5
  404.8 54.3 %collective-permute-start.4 = (bf16[448,800]{1,0:T(8,128)(2,1)}, bf16[448,800]{1,0:T(8,128)(2,1)S(1)}, u32[]{:S(2)}, u32[]{:S(2)}) collective-permute-start(bf16[448,800]{1,0:T(8,128)(2,1)} %dynamic-slice_bitcast_fusion.3), channel_id=1, source_target_pairs={{0,8},{8,0},{1,9},{9,1},{2,10},{10,2},{3,11},{11,3},{4,12},{12,4},... | collective-permute-start | bytes 2150408 | tf_op jit(solution)/shard_map/ppermute | solution.py:1048
  409.8 66.0 %collective-permute-start.6 = (bf16[448,800]{1,0:T(8,128)(2,1)}, bf16[448,800]{1,0:T(8,128)(2,1)}, u32[]{:S(2)}, u32[]{:S(2)}) collective-permute-start(bf16[448,800]{1,0:T(8,128)(2,1)} %dynamic-slice_bitcast_fusion.2), channel_id=1, source_target_pairs={{0,8},{8,0},{1,9},{9,1},{2,10},{10,2},{3,11},{11,3},{4,12},{12,4},... | collective-permute-start | bytes 2150408 | tf_op jit(solution)/shard_map/ppermute | solution.py:1048
  410.8 21.6 %copy-start.18 = (bf16[128,16,112]{0,2,1:T(8,128)(2,1)S(1)}, bf16[128,16,112]{0,2,1:T(8,128)(2,1)}, u32[]{:S(2)}) copy-start(bf16[128,16,112]{0,2,1:T(8,128)(2,1)} %pad.51) | copy-start | bytes 1376260
  448.9 26.9 %copy-start.6 = (bf16[2,448,800]{2,1,0:T(8,128)(2,1)S(1)}, bf16[2,448,800]{2,1,0:T(8,128)(2,1)}, u32[]{:S(2)}) copy-start(bf16[2,448,800]{2,1,0:T(8,128)(2,1)} %copy-done.5) | copy-start | bytes 4300804
  448.9 26.9 %copy-start.8 = (bf16[2,448,800]{2,1,0:T(8,128)(2,1)S(1)}, bf16[2,448,800]{2,1,0:T(8,128)(2,1)}, u32[]{:S(2)}) copy-start(bf16[2,448,800]{2,1,0:T(8,128)(2,1)} %copy-done.7) | copy-start | bytes 4300804
  595.1 5.1 copy-start.29
  595.1 5.1 copy-start.30
  595.1 5.1 copy-start.31
  595.1 5.1 copy-start.32
  595.2 5.3 copy-start.38
  595.2 5.3 copy-start.28
  (21 other events, 74.0 us)
Sparse Core Ops, SparseCore 0:
  141.9 56.6 all-gather.1
  347.6 82.1 reduce-scatter.1

commit v5 on v4

--- a/solution.py
+++ b/solution.py
@@ -6,6 +6,7 @@
 import numpy as np
 from jax import lax
 from jax.experimental import pallas as pl
+from jax.experimental.layout import Layout, with_layout_constraint
 from jax.experimental.pallas import tpu as pltpu
 from jax.sharding import Mesh
 from jax.sharding import PartitionSpec as P
@@ -167,9 +168,6 @@
             pltpu.VMEM((2 * head, total), B16),
         ],
         compiler_params=pltpu.CompilerParams(vmem_limit_bytes=VMEM_LIMIT),
-        cost_estimate=pl.CostEstimate(
-            flops=4 * total * total * head, bytes_accessed=8 * total * head * 2, transcendentals=total * total
-        ),
         name="attend",
     )(inv, low, qkv, start3)
 
@@ -263,9 +261,6 @@
             pltpu.VMEM((total, pair), F32), pltpu.VMEM((total, pair), F32),
         ],
         compiler_params=pltpu.CompilerParams(vmem_limit_bytes=VMEM_LIMIT),
-        cost_estimate=pl.CostEstimate(
-            flops=10 * total * total * head, bytes_accessed=30 * total * head * 2, transcendentals=total * total
-        ),
         name="attend_back",
     )(inv, low, qkv, out, grad, lse, start3)
 
@@ -303,7 +298,7 @@
         self.sems = sems
         self.begun = []
 
-    def send(self, src, dst, recv, peer):
+    def send(self, src, dst, recv, peer, when=None):
         at = len(self.begun)
         copy = pltpu.make_async_remote_copy(
             src_ref=src,
@@ -313,8 +308,12 @@
             device_id=peer,
             device_id_type=pl.DeviceIdType.MESH,
         )
-        copy.start()
-        self.begun.append(copy.wait_send)
+        if when is None:
+            copy.start()
+            self.begun.append(copy.wait_send)
+        else:
+            pl.when(when)(copy.start)
+            self.begun.append(lambda: pl.when(when)(copy.wait_send))
 
     def local(self, src, dst, sem=None):
         copy = pltpu.make_async_copy(src, dst, self.sems.at[len(self.begun)] if sem is None else sem)
@@ -363,26 +362,68 @@
     )
 
 
+class Line:
+    def __init__(self, place, copies, block):
+        self.place, self.copies, self.block = place, copies, block
+
+    def pass_on(self, src, z, step, when):
+        p = self.place
+        ref, sem = self.block(z)
+        peer = p.at_z(jnp.clip(p.z + step, 0, p.n_z - 1))
+        self.copies.send(ref if src is None else src, ref, sem, peer, when)
+
+    def begin(self, own):
+        p = self.place
+        self.pass_on(own, p.z, 1, p.z < p.n_z - 1)
+        self.pass_on(own, p.z, -1, p.z > 0)
+
+    def arrive(self, distance, then):
+        p = self.place
+        for side in (1, -1):
+            z = p.z + side * distance
+            here = jnp.logical_and(z >= 0, z < p.n_z)
+            z = jnp.clip(z, 0, p.n_z - 1)
+            ref, sem = self.block(z)
+            peer = p.at_z(jnp.clip(p.z + side, 0, p.n_z - 1))
+            pl.when(here)(lambda: self.copies.arrived(ref, sem, peer))
+            beyond = p.z - side
+            beyond = jnp.logical_and(beyond >= 0, beyond < p.n_z)
+            self.pass_on(None, z, -side, jnp.logical_and(here, beyond))
+            then(z, here)
+
+
+def row_line(place, out, copies, recv):
+    def block(z):
+        at = place.slot_of(z, place.c, place.y)
+        return out.at[at], recv.at[at]
+
+    return Line(place, copies, block)
+
+
 def gather_begin(place, own, out, copies, recv):
     peer_y, peer_c = {"y": 1 - place.y}, {"c": 1 - place.c}
     copies.local(own, out.at[place.slot])
-    for z in place.far_z():
-        copies.send(own, out.at[place.slot], recv.at[place.slot], place.at_z(z))
+    line = row_line(place, out, copies, recv)
+    line.begin(own)
     copies.send(own, out.at[place.slot], recv.at[place.slot], peer_y)
     copies.send(own, out.at[place.slot], recv.at[place.slot], peer_c)
-
-
-def gather_middle(place, out, copies, recv):
-    peer_y, peer_c = {"y": 1 - place.y}, {"c": 1 - place.c}
-    for z in place.far_z():
-        at = place.slot_of(z, place.c, place.y)
-        copies.arrived(out.at[at], recv.at[at], place.at_z(z))
-        copies.send(out.at[at], out.at[at], recv.at[at], peer_y)
-        copies.send(out.at[at], out.at[at], recv.at[at], peer_c)
+    return line
+
+
+def gather_step(place, line, copies, distance):
+    def then(z, here):
+        ref, sem = line.block(z)
+        copies.send(ref, ref, sem, {"y": 1 - place.y}, here)
+        copies.send(ref, ref, sem, {"c": 1 - place.c}, here)
+
+    line.arrive(distance, then)
+
+
+def gather_cross(place, out, copies, recv):
     for z in [place.z] + place.far_z():
         at = place.slot_of(z, place.c, 1 - place.y)
-        copies.arrived(out.at[at], recv.at[at], peer_y)
-        copies.send(out.at[at], out.at[at], recv.at[at], peer_c)
+        copies.arrived(out.at[at], recv.at[at], {"y": 1 - place.y})
+        copies.send(out.at[at], out.at[at], recv.at[at], {"c": 1 - place.c})
 
 
 def gather_end(place, out, copies, recv):
@@ -393,15 +434,16 @@
 
 
 def gather_copies(n_z):
-    return 4 * n_z
+    return 7 * n_z
 
 
 def group_gather_kernel(own, out, send, recv):
     place = Place(False)
     copies = Copies(send)
     meet([place.at_z(1 - place.z), {"y": 1 - place.y}, {"c": 1 - place.c}])
-    gather_begin(place, own, out, copies, recv)
-    gather_middle(place, out, copies, recv)
+    line = gather_begin(place, own, out, copies, recv)
+    gather_step(place, line, copies, 1)
+    gather_cross(place, out, copies, recv)
     gather_end(place, out, copies, recv)
     copies.finish()
 
@@ -424,7 +466,7 @@
     place, group = Place(True), Place(False)
     n_ctx = blocks.shape[0]
     copies = Copies(send)
-    peer_x, peer_y, peer_c = {"x": 1 - place.x}, {"y": 1 - place.y}, {"c": 1 - place.c}
+    peer_x, peer_y = {"x": 1 - place.x}, {"y": 1 - place.y}
     far_ctx = others(place.ctx, n_ctx)
     meet([place.at_ctx(k) for k in far_ctx] + [peer_y, peer_x])
     mine = blocks_all.at[place.x, place.ctx]
@@ -433,78 +475,63 @@
     def sem_w(x, k):
         return recv_w.at[x * n_ctx + k]
 
-    def out_block(x, z, c, y):
-        at = (x * place.n_z + z) * 2 + c
-        ref = out_w_all.at[at, :, pl.ds(pl.multiple_of(y * half, half), half)]
-        return ref, recv_o.at[at * 2 + y]
-
-    def give_out(x, z, c, y, peer):
-        ref, sem = out_block(x, z, c, y)
-        copies.send(ref, ref, sem, peer)
-
-    def got_out(x, z, c, y, peer):
-        ref, sem = out_block(x, z, c, y)
-        copies.arrived(ref, sem, peer)
-
-    gather_begin(place, own, out, copies, recv)
-    for k in others(group.ctx, 4):
-        copies.send(ffn.at[:, k], ffn_all.at[:, group.ctx], recv_f.at[group.ctx], group.at_ctx(k))
-    copies.local(ffn.at[:, group.ctx], ffn_all.at[:, group.ctx])
+    def out_block(z, x=place.x):
+        at = x * place.n_z + z
+        return out_w_all.at[at], recv_o.at[at]
+
+    line = gather_begin(place, own, out, copies, recv)
     for k in far_ctx:
         copies.send(blocks.at[k], mine, sem_w(place.x, place.ctx), place.at_ctx(k))
     copies.local(blocks.at[place.ctx], mine)
     copies.send(blocks.at[place.ctx], mine, sem_w(place.x, place.ctx), peer_x)
-    own_out, own_sem = out_block(place.x, place.z, place.c, place.y)
+    own_out, own_sem = out_block(place.z)
     own_half = out_w.at[:, pl.ds(pl.multiple_of(place.y * half, half), half)]
     copies.local(own_half, own_out)
-    for z in place.far_z():
-        copies.send(own_half, own_out, own_sem, place.at_z(z))
-    for peer in (peer_x, peer_y, peer_c):
-        copies.send(own_half, own_out, own_sem, peer)
-    gather_middle(place, out, copies, recv)
+    out_line = Line(place, copies, out_block)
+    out_line.begin(own_half)
+    copies.send(own_half, own_out, own_sem, peer_x)
+    for k in others(group.ctx, 4):
+        copies.send(ffn.at[:, k], ffn_all.at[:, group.ctx], recv_f.at[group.ctx], group.at_ctx(k))
+    copies.local(ffn.at[:, group.ctx], ffn_all.at[:, group.ctx])
+
+    def out_over_x(z, here):
+        ref, sem = out_block(z)
+        copies.send(ref, ref, sem, peer_x, here)
+
+    for distance in range(1, place.n_z):
+        gather_step(place, line, copies, distance)
+        out_line.arrive(distance, out_over_x)
     for k in far_ctx:
         block = blocks_all.at[place.x, k]
         copies.arrived(block, sem_w(place.x, k), place.at_ctx(k))
         copies.send(block, block, sem_w(place.x, k), peer_x)
-    for z in place.far_z():
-        got_out(place.x, z, place.c, place.y, place.at_z(z))
-        for peer in (peer_x, peer_y, peer_c):
-            give_out(place.x, z, place.c, place.y, peer)
-    for z in [place.z] + place.far_z():
-        got_out(1 - place.x, z, place.c, place.y, peer_x)
-        for peer in (peer_y, peer_c):
-            give_out(1 - place.x, z, place.c, place.y, peer)
+    gather_cross(place, out, copies, recv)
     gather_end(place, out, copies, recv)
-    for x in (place.x, 1 - place.x):
-        for z in [place.z] + place.far_z():
-            got_out(x, z, place.c, 1 - place.y, peer_y)
-            give_out(x, z, place.c, 1 - place.y, peer_c)
     for k in [place.ctx] + far_ctx:
         copies.arrived(blocks_all.at[1 - place.x, k], sem_w(1 - place.x, k), peer_x)
     for k in others(group.ctx, 4):
         copies.arrived(ffn_all.at[:, k], recv_f.at[k], group.at_ctx(k))
-    for x in (place.x, 1 - place.x):
-        for z in [place.z] + place.far_z():
-            for y in (place.y, 1 - place.y):
-                got_out(x, z, 1 - place.c, y, peer_c)
+    for z in [place.z] + place.far_z():
+        ref, sem = out_block(z, 1 - place.x)
+        copies.arrived(ref, sem, peer_x)
     copies.finish()
 
 
 def opening(own, blocks, ffn, out_w):
     n_ctx = blocks.shape[0]
     n_z = n_ctx // 2
-    sends = gather_copies(n_z) + 2 * n_ctx + 8 + (n_z - 1) + 4 + 3 * n_z + 2 * n_z + 2 * n_z
+    sends = gather_copies(n_z) + 2 * n_ctx + 4 + 5 * n_z
     return pl.pallas_call(
         opening_kernel,
         out_shape=(
             jax.ShapeDtypeStruct((2 * n_ctx,) + own.shape, own.dtype),
             jax.ShapeDtypeStruct((2,) + blocks.shape, blocks.dtype),
             jax.ShapeDtypeStruct(ffn.shape, ffn.dtype),
-            jax.ShapeDtypeStruct((2 * n_ctx,) + out_w.shape, out_w.dtype),
+            jax.ShapeDtypeStruct((n_ctx, out_w.shape[0], out_w.shape[1] // 2), out_w.dtype),
         ),
         in_specs=[ANY] * 4,
         out_specs=(ANY,) * 4,
-        scratch_shapes=dma_sems(sends, 2 * n_ctx, 2 * n_ctx, 4, 4 * n_ctx),
+        scratch_shapes=dma_sems(sends, 2 * n_ctx, 2 * n_ctx, 4, n_ctx),
         compiler_params=comm_params(1),
         name="opening",
     )(own, blocks, ffn, out_w)
@@ -674,7 +701,7 @@
 
 
 class OutScatter:
-    def __init__(self, place, part, held, from_c, from_x, from_y, from_z, out, copies, loads, rc, rx, ry, rz, rg):
+    def __init__(self, place, part, held, from_x, from_y, from_z, out, copies, loads, rx, ry, rz, rg):
         self.__dict__.update(locals())
         self.half = out.shape[2]
 
@@ -686,35 +713,16 @@
 
     def begin(self):
         p = self.place
-        for x in (1 - p.x, p.x):
-            for z in self.order():
-                at = x * p.n_z + z
-                self.copies.send(self.part.at[at * 2 + 1 - p.c], self.from_c.at[at], self.rc.at[at], {"c": 1 - p.c})
-                self.copies.local(self.part.at[at * 2 + p.c], self.held.at[at], self.loads.at[at])
-
-    def add_c(self, x, z):
-        at = x * self.place.n_z + z
-        self.copies.arrived(self.from_c.at[at], self.rc.at[at], {"c": 1 - self.place.c})
-        pltpu.make_async_copy(self.held.at[at], self.held.at[at], self.loads.at[at]).wait()
-        self.from_c[at] = self.from_c[at] + self.held[at]
-
-    def over_c_far(self):
-        p = self.place
         for z in self.order():
-            self.add_c(1 - p.x, z)
-            self.copies.send(
-                self.from_c.at[(1 - p.x) * p.n_z + z], self.from_x.at[z], self.rx.at[z], {"x": 1 - p.x}
-            )
-
-    def over_c_near(self):
-        for z in self.order():
-            self.add_c(self.place.x, z)
+            self.copies.send(self.part.at[(1 - p.x) * p.n_z + z], self.from_x.at[z], self.rx.at[z], {"x": 1 - p.x})
+            self.copies.local(self.part.at[p.x * p.n_z + z], self.held.at[z], self.loads.at[z])
 
     def over_x(self):
         p = self.place
         for z in self.order():
             self.copies.arrived(self.from_x.at[z], self.rx.at[z], {"x": 1 - p.x})
-            self.from_x[z] = self.from_x[z] + self.from_c[p.x * p.n_z + z]
+            pltpu.make_async_copy(self.held.at[z], self.held.at[z], self.loads.at[z]).wait()
+            self.from_x[z] = self.from_x[z] + self.held[z]
             self.copies.send(
                 self.from_x.at[z, :, self.columns(1 - p.y)], self.from_y.at[z], self.ry.at[z], {"y": 1 - p.y}
             )
@@ -743,8 +751,8 @@
 
 def closing_kernel(
     part, grads, out_part, fc, proj, out, grads_out, out_w_out, fc_out, proj_out,
-    held, from_c, from_y, from_z, own_x, from_x, o_held, o_c, o_x, o_y, o_z,
-    send, loads, rc, ry, rz, load_x, rx, rk, rg, o_loads, orc, orx, ory, orz, org, rfc, rproj,
+    held, from_c, from_y, from_z, own_x, from_x, o_held, o_x, o_y, o_z,
+    send, loads, rc, ry, rz, load_x, rx, rk, rg, o_loads, orx, ory, orz, org, rfc, rproj,
 ):
     place, group = Place(True), Place(False)
     n_ctx = grads.shape[1]
@@ -753,7 +761,7 @@
     peer_x, peer_y = {"x": 1 - place.x}, {"y": 1 - place.y}
     meet([place.at_ctx(k) for k in far_ctx] + [peer_y, peer_x])
     sums = Scatter(place, part, held, from_c, from_y, from_z, out, copies, loads, rc, ry, rz)
-    outs = OutScatter(place, out_part, o_held, o_c, o_x, o_y, o_z, out_w_out, copies, o_loads, orc, orx, ory, orz, org)
+    outs = OutScatter(place, out_part, o_held, o_x, o_y, o_z, out_w_out, copies, o_loads, orx, ory, orz, org)
     sums.begin()
     for k in far_ctx + [place.ctx]:
         copies.send(grads.at[1 - place.x, k], from_x.at[k], rx.at[k], peer_x)
@@ -775,8 +783,6 @@
     copies.local(from_x.at[place.ctx], mine)
     copies.send(from_x.at[place.ctx], mine, rg.at[place.ctx], peer_y)
     sums.over_c_near()
-    outs.over_c_far()
-    outs.over_c_near()
     sums.over_y()
     outs.over_x()
     for k in far_ctx:
@@ -815,11 +821,11 @@
         out_specs=(IN_VMEM, ANY, IN_VMEM, ANY, ANY),
         scratch_shapes=scatter_scratch(n_z, block)
         + [pltpu.VMEM(piece, B16), pltpu.VMEM(piece, B16)]
-        + [pltpu.VMEM((2 * n_z, rows, width), B16), pltpu.VMEM((2 * n_z, rows, width), B16)]
-        + [pltpu.VMEM((n_z, rows, width), B16), pltpu.VMEM((n_z,) + half, B16), pltpu.VMEM((n_z,) + half, B16)]
-        + scatter_sems(n_z, 3 * n_ctx + 6 * n_z + 8)
+        + [pltpu.VMEM((n_z, rows, width), B16), pltpu.VMEM((n_z, rows, width), B16)]
+        + [pltpu.VMEM((n_z,) + half, B16), pltpu.VMEM((n_z,) + half, B16)]
+        + scatter_sems(n_z, 3 * n_ctx + 4 * n_z + 8)
         + dma_sems(n_ctx, n_ctx, n_ctx, n_ctx)
-        + dma_sems(2 * n_z, 2 * n_z, n_z, n_z, n_z, 2, 4, 4),
+        + dma_sems(n_z, n_z, n_z, n_z, 2, 4, 4),
         compiler_params=comm_params(4),
         name="closing",
     )(part, grads, out_part, fc, proj)
@@ -904,11 +910,63 @@
         out_specs=(pl.BlockSpec((step, wide), lambda i: (i, 0)), pl.BlockSpec((step, cols), lambda i: (i, 0))),
         out_shape=(jax.ShapeDtypeStruct((total, wide), B16), jax.ShapeDtypeStruct((total, cols), B16)),
         compiler_params=pltpu.CompilerParams(vmem_limit_bytes=VMEM_LIMIT),
-        cost_estimate=pl.CostEstimate(
-            flops=2 * total * wide * cols, bytes_accessed=4 * total * wide, transcendentals=total
-        ),
         name="project",
     )(x, gain[None], shift[None], mask[None], weight, bias[None])
+
+
+def feed_kernel(count, at_ref, *refs):
+    pieces, refs = refs[:count], refs[count:]
+    norm_ref, grad_ref, bias_ref, act_ref, dpre_ref, dnorm_ref, mlp_ref, sum_ref, w_fc, w_proj, sems = refs
+
+    @pl.when(pl.program_id(0) == 0)
+    def begin():
+        rows = pieces[0].shape[1]
+        copies = []
+        for i, piece in enumerate(pieces):
+            to = pl.ds(pl.multiple_of(at_ref[i], 16), rows)
+            copies.append(pltpu.make_async_copy(piece.at[0], w_fc.at[to, :], sems.at[2 * i]))
+            copies.append(pltpu.make_async_copy(piece.at[1], w_proj.at[to, :], sems.at[2 * i + 1]))
+        for copy in copies:
+            copy.start()
+        for copy in copies:
+            copy.wait()
+        sum_ref[...] = jnp.zeros_like(sum_ref)
+
+    preact = dot(norm_ref[...], w_fc[...], 1, 0) + bias_ref[...]
+    activated, derivative = gelu_parts(preact)
+    activation = activated.astype(B16)
+    act_ref[...] = activation
+    dpre = dot(grad_ref[...], w_proj[...], 1, 0) * derivative
+    sum_ref[...] += jnp.sum(dpre, axis=0, keepdims=True)
+    dpre_b = dpre.astype(B16)
+    dpre_ref[...] = dpre_b
+    dnorm_ref[...] = dot(dpre_b, w_fc[...], 1, 1).astype(B16)
+    mlp_ref[...] = dot(activation, w_proj[...], 1, 1).astype(B16)
+
+
+def feed(pieces, places, norm, grad, bias):
+    total, wide = norm.shape
+    ff = bias.shape[0]
+    step = 256
+    tokens = pl.BlockSpec((step, wide), lambda i: (i, 0))
+    hidden = pl.BlockSpec((step, ff), lambda i: (i, 0))
+    single = pl.BlockSpec((1, ff), lambda i: (0, 0))
+    return pl.pallas_call(
+        functools.partial(feed_kernel, len(pieces)),
+        grid=(total // step,),
+        in_specs=[pl.BlockSpec(memory_space=pltpu.SMEM)] + [ANY] * len(pieces) + [tokens, tokens, single],
+        out_specs=(hidden, hidden, tokens, tokens, single),
+        out_shape=(
+            jax.ShapeDtypeStruct((total, ff), B16),
+            jax.ShapeDtypeStruct((total, ff), B16),
+            jax.ShapeDtypeStruct((total, wide), B16),
+            jax.ShapeDtypeStruct((total, wide), B16),
+            jax.ShapeDtypeStruct((1, ff), F32),
+        ),
+        scratch_shapes=[pltpu.VMEM((wide, ff), B16), pltpu.VMEM((wide, ff), B16)] + dma_sems(2 * len(pieces)),
+        compiler_params=pltpu.CompilerParams(vmem_limit_bytes=VMEM_LIMIT),
+        name="feed",
+    )(places, *pieces, norm, grad, bias[None])
 
 
 def after(value, other, unpack=False):
@@ -971,12 +1029,13 @@
     all_input, packed, ffn_blocks, w_out = opening(
         own_input, packed, ffn_blocks, widened(jnp.pad(out_weight, ((0, row_pad), (0, 0))))
     )
-    grad_late, all_input = after(grad_own, all_input)
-    grad_all = gather(grad_late, FFG)
     ffn_blocks = ffn_blocks.reshape(2, 4 * tall, ff_own)
     along_h = [lax.ppermute(ffn_blocks, "h", shift_perm(n_h, step)) for step in range(1, n_h)]
     along_x = lax.ppermute(ffn_blocks, "x", shift_perm(n_x, 1))
-    w_out = w_out.reshape(wide, wide)
+    grad_late, all_input = after(grad_own, all_input)
+    grad_all = gather(grad_late, FFG)
+    w_out = lax.all_gather(w_out.reshape(wide // 2, wide // 2), ("c", "y"), axis=0, tiled=False)
+    w_out = w_out.reshape(2, n_y, wide // 2, wide // 2)
     packed = packed.reshape(n_shard, tall, 3 * pair)
     w_qkv = packed.reshape(wide, 3 * pair)
     smalls = packed[:, rows:].reshape(n_shard, -1)[:, : 8 * rows].astype(F32)
@@ -1005,43 +1064,38 @@
     )
     heads_out, lse = attend(inv, low, qkv, start3, slot_len, head)
     attention = widened(to_tokens(heads_out.reshape(n_slot, slot_len, pair))[:, :feats])
-    hidden = own_wide + dot(attention, w_out, 1, 0) + bias_out
+    by_core = attention.reshape(slot_len, n_shard // 2, 2, tall)
+    by_core = [by_core[:, :, part].reshape(slot_len, wide // 2) for part in range(2)]
+    hidden = [dot(by_core[0], w_out[0, y], 1, 0) + dot(by_core[1], w_out[1, y], 1, 0) for y in range(n_y)]
+    hidden = own_wide + jnp.concatenate(hidden, axis=1) + bias_out
     normed_two, inv_two = norm_forward(hidden, mask, feats)
     norm_two = (normed_two * gain_two + shift_two).astype(B16)
     grad_wide = grad_own.astype(F32)
-    along_h, grad_all, norm_two = after((along_h, grad_all), norm_two, True)
+    along_h, norm_two = after(along_h, norm_two)
     along_both = [lax.ppermute(value, "x", shift_perm(n_x, 1)) for value in along_h]
     norm_all = group_gather(norm_two, 6).reshape(-1, wide)
-    w_ffn = jnp.zeros((2, n_x, n_h, 4 * tall, ff_own), B16)
-
-    def put(whole, value, x, h):
-        return lax.dynamic_update_slice(whole, value[:, None, None], (0, x, h, 0, 0))
-
-    w_ffn = put(put(w_ffn, ffn_blocks, x_at, h_at), along_x, 1 - x_at, h_at)
+    pieces, places = [ffn_blocks, along_x], [(x_at, h_at), (1 - x_at, h_at)]
     for step in range(1, n_h):
         h_from = lax.rem(h_at + n_h - step, n_h)
-        w_ffn = put(put(w_ffn, along_h[step - 1], x_at, h_from), along_both[step - 1], 1 - x_at, h_from)
-    w_fc, w_proj = w_ffn[0].reshape(wide, ff_own), w_ffn[1].reshape(wide, ff_own)
-    preact = dot(norm_all, w_fc, 1, 0) + b_fc
-    activated, derivative = gelu_parts(preact)
-    activation = activated.astype(B16)
-    mlp_part = dot(activation, w_proj, 1, 1).astype(B16)
-
-    dpreact = dot(grad_all, w_proj, 1, 0) * derivative
-    dpreact_b = dpreact.astype(B16)
-    dnorm_part = dot(dpreact_b, w_fc, 1, 1).astype(B16)
-    dnorm_two = group_scatter(dnorm_part.reshape(8, slot_len, wide), 7)
+        pieces += [along_h[step - 1], along_both[step - 1]]
+        places += [(x_at, h_from), (1 - x_at, h_from)]
+    places = jnp.stack([(x * n_h + h) * (4 * tall) for x, h in places]).astype(jnp.int32)
+    activation, dpreact_b, dnorm_part, mlp_part, dpreact_sum = feed(pieces, places, norm_all, grad_all, b_fc)
 
     def pick(value, at):
         return lax.dynamic_index_in_dim(value, at, 0, False)
 
     def by_owner(value):
-        return value.astype(B16).reshape(n_x, n_h, 4 * tall, ff_own)
+        value = with_layout_constraint(value.astype(B16), Layout(major_to_minor=(0, 1)))
+        return value.reshape(n_x, n_h, 4 * tall, ff_own)
 
     proj_part = by_owner(dot(grad_all, activation, 0, 0))
     proj_x = lax.ppermute(pick(proj_part, 1 - x_at), "x", shift_perm(n_x, 1))
     fc_part = by_owner(dot(norm_all, dpreact_b, 0, 0))
     fc_x = lax.ppermute(pick(fc_part, 1 - x_at), "x", shift_perm(n_x, 1))
+
+    proj_part, fc_part, dnorm_part = after((proj_part, fc_part), dnorm_part, True)
+    dnorm_two = group_scatter(dnorm_part.reshape(8, slot_len, wide), 7)
 
     def over_h(value):
         gives = [pick(value, lax.rem(h_at + step, n_h)) for step in range(1, n_h)]
@@ -1059,11 +1113,18 @@
     mlp = lax.psum_scatter(mlp_part, FFG, scatter_dimension=0, tiled=True)
     dhidden = grad_wide + norm_backward(dnorm_two, normed_two, inv_two, gain_two, feats)
     dhidden_b = dhidden.astype(B16)
-    out_part = dot(attention, dhidden_b, 0, 0).astype(B16).reshape(n_shard, tall, wide)
-    dattention = narrowed(dot(dhidden_b, w_out, 1, 1).astype(B16))
+    c_at = lax.axis_index("c")
+    out_give = dot(jnp.where(c_at == 0, by_core[1], by_core[0]), dhidden_b, 0, 0).astype(B16)
+    out_give = lax.ppermute(out_give, "c", shift_perm(2, 1))
+    out_keep = dot(jnp.where(c_at == 0, by_core[0], by_core[1]), dhidden_b, 0, 0)
+    grad_y = [dhidden_b[:, : wide // 2], dhidden_b[:, wide // 2 :]]
+    datt = [dot(grad_y[0], w_out[c, 0], 1, 1) + dot(grad_y[1], w_out[c, 1], 1, 1) for c in range(2)]
+    datt = [value.astype(B16).reshape(slot_len, -1, 1, tall) for value in datt]
+    dattention = narrowed(jnp.concatenate(datt, axis=2).reshape(slot_len, wide))
     dattention = jnp.pad(dattention, ((0, 0), (0, padded - feats)))
     dattention = to_heads(dattention, n_slot).reshape(n_slot * slot_len, pair)
-    fc_x, dattention = after(fc_x, dattention)
+    out_give, fc_x, dattention = after((out_give, fc_x), dattention, True)
+    out_part = (out_keep + out_give).astype(B16).reshape(n_shard // 2, tall, wide)
     fc_line = pick(fc_part, x_at) + fc_x
     fc_h = over_h(fc_line)
     dqkv = attend_back(inv, low, qkv, heads_out, dattention, lse, start3, slot_len, head)
@@ -1107,7 +1168,7 @@
             vectors.reshape(6, n_shard, tall).transpose(1, 0, 2).reshape(n_shard, 6 * tall),
             qv_sums.reshape(n_shard, 2 * rows),
             jnp.zeros((n_shard, 1024 - 6 * tall - 2 * rows), F32),
-            jnp.broadcast_to(jnp.sum(dpreact, axis=0)[None], (n_shard, ff_own)),
+            jnp.broadcast_to(dpreact_sum, (n_shard, ff_own)),
             jnp.zeros((n_shard, 1024 - ff_own), F32),
         ],
         axis=1,

time: 635 us -> 593 us (0.934)
  local copies, waits for them, and re-layouts: 98.3 us -> 61.1 us
  matrix products: 71.8 us -> 52 us
  Pallas kernels: 384 us -> 398 us
    pallas_call x0 -> x1, Pallas kernels: none -> 21.7 us  [feed(): pl.pallas_call(functools.partial(feed_kernel, len(pieces)), grid=(total /...]
    dot_general x11 -> x14, matrix products: 71.8 us -> 52 us  [dot(): lax.dot_general(left, right, (((left_dim,), (right_dim,)), ((), ())), pre...]
    pallas_call x1, Pallas kernels: 113 us -> 98.2 us  [opening(): pl.pallas_call(opening_kernel, out_shape=(jax.ShapeDtypeStruct((2 * n_ctx...]
    convert_element_type x3 -> x2, local copies, waits for them, and re-layouts: 11.5 us -> 0.34 us  [on_device(): datt = [value.astype(B16).reshape(slot_len, -1, 1, tall) for value in datt]]
    ppermute x1, waiting for transfers between devices: 11 us -> 1.46 us  [on_device(): fc_x = lax.ppermute(pick(fc_part, 1 - x_at), 'x', shift_perm(n_x, 1))]
    dynamic_update_slice x4 -> x0, local copies, waits for them, and re-layouts: 8.17 us -> none  [put(): lax.dynamic_update_slice(whole, value[:, None, None], (0, x, h, 0, 0))]
    pallas_call x1, Pallas kernels: 38.1 us -> 31.2 us  [to_tokens(): pl.pallas_call(to_tokens_kernel, out_shape=jax.ShapeDtypeStruct((tokens,...]
    pallas_call x1, Pallas kernels: 20.3 us -> 26.8 us  [attend(): pl.pallas_call(functools.partial(attend_kernel, slot_len, head), out_shap...]
  transfers between devices with their start and end apart: 9 -> 11, of which waited for: 3 -> 3; matrix products, arithmetic and copies ran while one was open for 21% -> 17% of each run, Pallas kernels for 41% -> 46%
where the time goes in v5:
time: 593 us; the launch traced here: 588 us
  Pallas kernels  398 us (67%)
  local copies, waits for them, and re-layouts  61.1 us (10%)
  matrix products  52 us (9%)
  other arithmetic  30.2 us (5%)
  waiting for transfers between devices  22.7 us (4%)
  between operations  14.9 us (3%)
  starting transfers between devices  9.23 us (2%)
    pallas_call x1, Pallas kernels, opening(): pl.pallas_call(opening_kernel, out_shape=(jax.ShapeDtypeStruct((2 * n_ctx...  98.2 us
    pallas_call x1, Pallas kernels, closing(): pl.pallas_call(closing_kernel, out_shape=(jax.ShapeDtypeStruct(block, F32...  95.5 us
    dot_general x14, matrix products, dot(): lax.dot_general(left, right, (((left_dim,), (right_dim,)), ((), ())), pre...  52 us
    pallas_call x1, Pallas kernels, to_tokens(): pl.pallas_call(to_tokens_kernel, out_shape=jax.ShapeDtypeStruct((tokens,...  31.2 us
    pallas_call x1, Pallas kernels, group_gather(): pl.pallas_call(group_gather_kernel, out_shape=jax.ShapeDtypeStruct((8,) +...  30 us
    pallas_call x1, Pallas kernels, group_scatter(): pl.pallas_call(group_scatter_kernel, out_shape=jax.ShapeDtypeStruct(block...  30 us
    pallas_call x1, Pallas kernels, attend_back(): pl.pallas_call(functools.partial(attend_back_kernel, slot_len, head), out...  27.6 us
    pallas_call x1, Pallas kernels, attend(): pl.pallas_call(functools.partial(attend_kernel, slot_len, head), out_shap...  26.8 us
  transfers between devices with their start and end apart: 11, of which 3 were waited for; matrix products, arithmetic and copies ran while one was open for 17% of the time, Pallas kernels for 46%

profile of v5, /device:TPU:0, one launch (start us, length us, event | category | flops | bytes accessed | tf_op | source)
XLA Modules:
  0.0 588.1 jit_solution(2392689286489894456)
XLA Ops:
  7.2 2.3 copy.117
  13.4 4.6 reshape.313
  18.0 2.8 copy.154
  24.1 98.2 %opening.1 = (bf16[16,128,1792]{2,1,0:T(8,128)(2,1)}, bf16[2,8,112,384]{3,2,1,0:T(8,128)(2,1)}, bf16[2,4,112,800]{3,2,1,0:T(8,128)(2,1)}, bf16[8,112,896]{2,1,0:T(8,128)(2,1)}) custom-call(bf16[128,1792]{1,0:T(8,128)(2,1)} %copy.116.own, bf16[8,112,384]{2,1,0:T(8,128)(2,1)} %pad_maximum_fusion.blocks, bf16[2,4,112,800]{3,2,1,0:T(8,128)(2,1)} %bitcast.192, ...), custom_call_target="tpu_custom_call" | custom-call | tf_op jit(solution)/shard_map/opening/pallas_call | solution.py:524
  129.0 12.6 %project.1 = (bf16[2048,1792]{1,0:T(8,128)(2,1)}, bf16[2048,384]{1,0:T(8,128)(2,1)}) custom-call(bf16[2048,1792]{1,0:T(8,128)(2,1)} %bitcast.183, f32[1,1792]{1,0:T(1,128)} %unstack.23.gain_ref, f32[1,1792]{1,0:T(1,128)} %unstack.25.shift_ref, f32[1,1792]{1,0:T(1,128)} %constant.159.mask_ref, bf16[1792,384]{1,0:T(8,128)(2,1)} %bitcast.217, ...), custom_call_target="tpu_custom_call" | custom-call | tf_op jit(solution)/shard_map/project/pallas_call | solution.py:904
  142.7 26.8 %attend.1 = (bf16[2048,128]{1,0:T(8,128)(2,1)}, f32[8,2,256]{2,1,0:T(2,128)}) custom-call(s32[16]{0:T(128)} %copy-done.25, s32[8]{0:T(128)} %and_select_fusion.low_ref, bf16[2048,384]{1,0:T(8,128)(2,1)} %get-tuple-element.55.qkv_ref, s32[8,1,256]{2,1,0:T(1,128)} %bitcast.235), custom_call_target="tpu_custom_call" | custom-call | tf_op jit(solution)/shard_map/attend/pallas_call | solution.py:157
  169.5 31.2 %to_tokens.1 = bf16[128,2048]{1,0:T(8,128)(2,1)} custom-call(bf16[16,128,128]{2,1,0:T(8,128)(2,1)} %bitcast.212), custom_call_target="tpu_custom_call" | custom-call | tf_op jit(solution)/shard_map/to_tokens/pallas_call | solution.py:560
  217.4 30.0 %group_gather.1 = bf16[8,128,1792]{2,1,0:T(8,128)(2,1)} custom-call(bf16[128,1792]{1,0:T(8,128)(2,1)} %add_convert_fusion.1.own), custom_call_target="tpu_custom_call" | custom-call | tf_op jit(solution)/shard_map/group_gather/pallas_call | solution.py:452
  247.4 5.4 collective-permute-done.2.refs_3_
  252.8 21.7 %feed.1 = (bf16[1024,800]{1,0:T(8,128)(2,1)}, bf16[1024,800]{1,0:T(8,128)(2,1)}, bf16[1024,1792]{1,0:T(8,128)(2,1)}, bf16[1024,1792]{1,0:T(8,128)(2,1)}, f32[1,800]{1,0:T(1,128)}) custom-call(s32[4]{0:T(128)} %pad_add_fusion.at_ref, bf16[2,448,800]{2,1,0:T(8,128)(2,1)} %bitcast.222, bf16[2,448,800]{2,1,0:T(8,128)(2,1)} %collective-permute-done.refs_1_, ...), custom_call_target="tpu_custom_call" | custom-call | tf_op jit(solution)/shard_map/feed/pallas_call | solution.py:954
  274.5 6.6 %convolution_convert_fusion.3 = bf16[1792,800]{1,0:T(8,128)(2,1)S(1)} fusion(bf16[1024,1792]{1,0:T(8,128)(2,1)} %all-gather.5.cloned.1.call-done.refs_5_, bf16[1024,800]{1,0:T(8,128)(2,1)} %get-tuple-element.62), kind=kOutput, calls=%fused_computation.5 | convolution fusion | flops 2937446400 | bytes 8175616 | tf_op jit(solution)/shard_map/dot_general | solution.py:59
  284.4 8.4 %convolution_convert_fusion.2 = bf16[1792,800]{1,0:T(8,128)(2,1)} fusion(bf16[1024,1792]{1,0:T(8,128)(2,1)} %bitcast.171, bf16[1024,800]{1,0:T(8,128)(2,1)} %get-tuple-element.64), kind=kOutput, calls=%fused_computation.4 | convolution fusion | flops 2937446400 | bytes 8175616 | tf_op jit(solution)/shard_map/dot_general | solution.py:59
  292.8 30.0 %group_scatter.1 = f32[128,1792]{1,0:T(8,128)} custom-call(bf16[8,128,1792]{2,1,0:T(8,128)(2,1)} %bitcast.201), custom_call_target="tpu_custom_call" | custom-call | tf_op jit(solution)/shard_map/group_scatter/pallas_call | solution.py:692
  326.2 2.7 convolution_convert_fusion.1
  329.1 2.7 dynamic-slice_bitcast_fusion
  339.7 2.2 fusion.18
  343.4 14.3 %to_heads.1 = bf16[16,128,128]{2,1,0:T(8,128)(2,1)} custom-call(bf16[128,2048]{1,0:T(8,128)(2,1)} %pad.52.src), custom_call_target="tpu_custom_call" | custom-call | tf_op jit(solution)/shard_map/to_heads/pallas_call | solution.py:591
  357.7 2.1 bitcast_add_fusion.1
  361.9 2.4 collective-permute-start.4
  364.6 3.6 fusion.37
  369.6 27.6 %attend_back.1 = f32[2048,384]{1,0:T(8,128)} custom-call(s32[16]{0:T(128)} %copy-done.25, s32[8]{0:T(128)} %and_select_fusion.low_ref, bf16[2048,384]{1,0:T(8,128)(2,1)} %get-tuple-element.55.qkv_ref, bf16[2048,128]{1,0:T(8,128)(2,1)} %get-tuple-element.56.out_ref, bf16[2048,128]{1,0:T(8,128)(2,1)} %bitcast.213, f32[8,2,256]{2,1,0:T(2,128)} %get-tuple-element.74.lse_ref, ...), custom_call_target="tpu_custom_call" | custom-call | tf_op jit(solution)/shard_map/attend_back/pallas_call | solution.py:254
  399.8 2.2 bitcast_add_fusion
  402.2 2.6 collective-permute-start.7
  404.7 6.4 %convolution_convert_fusion = bf16[2048,1792]{1,0:T(8,128)(2,1)} fusion(bf16[1792,384]{1,0:T(8,128)(2,1)S(1)} %bitcast.218, f32[2048,384]{1,0:T(8,128)S(1)} %copy-done.3), kind=kOutput, calls=%fused_computation.1 | convolution fusion | flops 2823028736 | bytes 11862016 | tf_op jit(solution)/shard_map/dot_general | solution.py:59
  411.1 8.4 %convolution_convert_fusion.4 = bf16[1792,384]{1,0:T(8,128)(2,1)} fusion(bf16[2048,1792]{1,0:T(8,128)(2,1)} %get-tuple-element.76, f32[2048,384]{1,0:T(8,128)S(1)} %copy-done.3), kind=kOutput, calls=%fused_computation.9 | convolution fusion | flops 2820046848 | bytes 11862016 | tf_op jit(solution)/shard_map/dot_general | solution.py:59
  419.5 4.5 add_convert_fusion
  424.1 15.8 %collective-permute-done.7 = bf16[448,800]{1,0:T(8,128)(2,1)S(1)} collective-permute-done((bf16[448,800]{1,0:T(8,128)(2,1)S(1)}, bf16[448,800]{1,0:T(8,128)(2,1)S(1)}, u32[]{:S(2)}, u32[]{:S(2)}) %collective-permute-start.7) | collective-permute-done | bytes 716832 | tf_op jit(solution)/shard_map/ppermute | solution.py:1102
  442.0 95.5 %closing.1 = (f32[128,1792]{1,0:T(8,128)}, bf16[2,8,112,384]{3,2,1,0:T(8,128)(2,1)}, bf16[2,112,896]{2,1,0:T(8,128)(2,1)}, bf16[4,112,800]{2,1,0:T(8,128)(2,1)}, bf16[4,112,800]{2,1,0:T(8,128)(2,1)}) custom-call(bf16[16,128,1792]{2,1,0:T(8,128)(2,1)} %bitcast.182, bf16[2,8,112,384]{3,2,1,0:T(8,128)(2,1)} %bitcast.224, bf16[8,112,1792]{2,1,0:T(8,128)(2,1)} %bitcast.172, ...), custom_call_target="tpu_custom_call" | custom-call | tf_op jit(solution)/shard_map/closing/pallas_call | solution.py:811
  543.6 2.1 copy.138
  545.7 3.6 copy.142
  560.7 10.1 %vectors_sum.1 = (f32[8,128]{1,0:T(8,128)}, f32[4,8,128]{2,1,0:T(8,128)}) custom-call(f32[16,16,128]{2,1,0:T(8,128)} %bitcast.231), custom_call_target="tpu_custom_call" | custom-call | tf_op jit(solution)/shard_map/vectors_sum/pallas_call | solution.py:870
  575.0 2.7 fusion.28
  (239 shorter events, 81.1 us)
Async XLA Ops:
  7.2 121.2 %copy-start = (s32[1,2048]{1,0:T(1,128)S(1)}, s32[1,2048]{1,0:T(1,128)}, u32[]{:S(2)}) copy-start(s32[1,2048]{1,0:T(1,128)} %param.18) | copy-start | bytes 24580
  7.2 195.2 %all-gather.3.cloned.1.call-start = ((), (), s32[]{:S(2)}) async-start(), calls=%async_computation.1 | async-start | bytes 8028160 | tf_op jit(solution)/shard_map/all_gather | solution.py:1037
  18.0 2.8 copy-start.19
  24.1 99.0 %copy-start.18 = (bf16[1,128,1600]{1,2,0:T(8,128)(2,1)S(1)}, bf16[1,128,1600]{1,2,0:T(8,128)(2,1)}, u32[]{:S(2)}) copy-start(bf16[1,128,1600]{1,2,0:T(8,128)(2,1)} %param.32) | copy-start | bytes 1228804
  122.3 125.1 %all-gather.5.cloned.1.call-start = ((), (), s32[]{:S(2)}) async-start(), calls=%async_computation.2 | async-start | bytes 4128768 | tf_op jit(solution)/shard_map/all_gather | solution.py:1002
  122.4 92.5 %collective-permute-start.1 = (bf16[2,448,800]{2,1,0:T(8,128)(2,1)}, bf16[2,448,800]{2,1,0:T(8,128)(2,1)}, u32[]{:S(2)}, u32[]{:S(2)}) collective-permute-start(bf16[2,448,800]{2,1,0:T(8,128)(2,1)} %bitcast.220), channel_id=1, source_target_pairs={{0,8},{8,0},{1,9},{9,1},{2,10},{10,2},{3,11},{11,3},{4,12},{12,4},... | collective-permute-start | bytes 4300808 | tf_op jit(solution)/shard_map/ppermute | solution.py:1033
  122.5 124.9 %collective-permute-start = (bf16[2,448,800]{2,1,0:T(8,128)(2,1)}, bf16[2,448,800]{2,1,0:T(8,128)(2,1)}, u32[]{:S(2)}, u32[]{:S(2)}) collective-permute-start(bf16[2,448,800]{2,1,0:T(8,128)(2,1)} %bitcast.221), channel_id=1, source_target_pairs={{0,16},{16,0},{1,17},{17,1},{2,18},{18,2},{3,19},{19,3},{4,20},{20... | collective-permute-start | bytes 4300808 | tf_op jit(solution)/shard_map/ppermute | solution.py:1034
  123.1 2.8 copy-start.10
  123.2 5.0 copy-start.33
  124.2 434.8 %reduce-scatter.2.cloned.1.call-start = ((), (), s32[]{:S(2)}) async-start(), calls=%async_computation.3 | async-start | bytes 4128768 | tf_op jit(solution)/shard_map/reduce_scatter | solution.py:1113
  128.4 13.2 %copy-start.25 = (s32[16]{0:T(128)}, s32[16]{0:T(128)S(1)}, u32[]{:S(2)}) copy-start(s32[16]{0:T(128)S(1)} %select_reduce_fusion.1.inv_ref) | copy-start | bytes 196
  210.3 2.7 copy-start.23
  211.3 2.5 copy-start.2
  211.3 2.5 copy-start.21
  214.8 37.9 %collective-permute-start.2 = (bf16[2,448,800]{2,1,0:T(8,128)(2,1)}, bf16[2,448,800]{2,1,0:T(8,128)(2,1)}, u32[]{:S(2)}, u32[]{:S(2)}) collective-permute-start(bf16[2,448,800]{2,1,0:T(8,128)(2,1)} %collective-permute-done.1.refs_2_), channel_id=1, source_target_pairs={{0,16},{16,0},{1,17},{17,1},{2,18},{18,2},{3,19},{19,3},{4,20},{20... | collective-permute-start | bytes 4300808 | tf_op jit(solution)/shard_map/ppermute | solution.py:1075
  281.1 2.3 copy-start.12
  283.4 39.4 %collective-permute-start.3 = (bf16[2,448,800]{2,1,0:T(8,128)(2,1)}, bf16[2,448,800]{2,1,0:T(8,128)(2,1)}, u32[]{:S(2)}, u32[]{:S(2)}) collective-permute-start(bf16[2,448,800]{2,1,0:T(8,128)(2,1)} %dynamic-slice_bitcast_fusion.1), channel_id=1, source_target_pairs={{0,16},{16,0},{1,17},{17,1},{2,18},{18,2},{3,19},{19,3},{4,20},{20... | collective-permute-start | bytes 4300808 | tf_op jit(solution)/shard_map/ppermute | solution.py:1093
  322.8 1.8 copy-start.6
  328.9 40.7 %collective-permute-start.5 = (bf16[896,1792]{1,0:T(8,128)(2,1)}, bf16[896,1792]{1,0:T(8,128)(2,1)}, u32[]{:S(2)}, u32[]{:S(2)}) collective-permute-start(bf16[896,1792]{1,0:T(8,128)(2,1)} %convolution_convert_fusion.1), channel_id=1, source_target_pairs={{0,2},{2,0},{1,3},{3,1},{4,6},{6,4},{5,7},{7,5},{8,10},{10,8},{9,1... | collective-permute-start | bytes 9633800 | tf_op jit(solution)/shard_map/ppermute | solution.py:1118
  329.1 4.3 copy-start.24
  331.8 37.8 %collective-permute-start.6 = (bf16[2,448,800]{2,1,0:T(8,128)(2,1)}, bf16[2,448,800]{2,1,0:T(8,128)(2,1)}, u32[]{:S(2)}, u32[]{:S(2)}) collective-permute-start(bf16[2,448,800]{2,1,0:T(8,128)(2,1)} %dynamic-slice_bitcast_fusion), channel_id=1, source_target_pairs={{0,16},{16,0},{1,17},{17,1},{2,18},{18,2},{3,19},{19,3},{4,20},{20... | collective-permute-start | bytes 4300808 | tf_op jit(solution)/shard_map/ppermute | solution.py:1095
  361.9 62.2 %collective-permute-start.4 = (bf16[448,800]{1,0:T(8,128)(2,1)}, bf16[448,800]{1,0:T(8,128)(2,1)S(1)}, u32[]{:S(2)}, u32[]{:S(2)}) collective-permute-start(bf16[448,800]{1,0:T(8,128)(2,1)} %dynamic-slice_bitcast_fusion.3), channel_id=1, source_target_pairs={{0,8},{8,0},{1,9},{9,1},{2,10},{10,2},{3,11},{11,3},{4,12},{12,4},... | collective-permute-start | bytes 2150408 | tf_op jit(solution)/shard_map/ppermute | solution.py:1102
  399.8 4.9 copy-start.3
  402.1 2.7 copy-start.13
  402.2 37.7 %collective-permute-start.7 = (bf16[448,800]{1,0:T(8,128)(2,1)S(1)}, bf16[448,800]{1,0:T(8,128)(2,1)S(1)}, u32[]{:S(2)}, u32[]{:S(2)}) collective-permute-start(bf16[448,800]{1,0:T(8,128)(2,1)S(1)} %dynamic-slice_bitcast_fusion.2), channel_id=1, source_target_pairs={{0,8},{8,0},{1,9},{9,1},{2,10},{10,2},{3,11},{11,3},{4,12},{12,4},... | collective-permute-start | bytes 2150408 | tf_op jit(solution)/shard_map/ppermute | solution.py:1102
  404.7 14.8 %slice-start = ((s8[6422528]{0:T(1024)(128)(4,1)}), s8[4194304]{0:T(1024)(128)(4,1)S(1)}, s32[]{:S(2)}) async-start(s8[6422528]{0:T(1024)(128)(4,1)} %bitcast.168), calls=%async_computation.4 | async-start | bytes 8388608
  411.1 8.4 %slice-start.1 = ((s8[6422528]{0:T(1024)(128)(4,1)}), s8[2228224]{0:T(1024)(128)(4,1)S(1)}, s32[]{:S(2)}) async-start(s8[6422528]{0:T(1024)(128)(4,1)} %bitcast.168), calls=%async_computation.5 | async-start | bytes 4456448
  419.5 20.4 %copy-start.8 = (bf16[2,448,800]{2,1,0:T(8,128)(2,1)S(1)}, bf16[2,448,800]{2,1,0:T(8,128)(2,1)}, u32[]{:S(2)}) copy-start(bf16[2,448,800]{2,1,0:T(8,128)(2,1)} %copy-done.7) | copy-start | bytes 4300804
  545.7 3.6 copy-start.14
  553.3 1.8 copy-start.20
  555.4 3.6 copy-start.11
  559.1 15.9 %copy-start.5 = (f32[128,1792]{1,0:T(8,128)S(1)}, f32[128,1792]{1,0:T(8,128)}, u32[]{:S(2)}) copy-start(f32[128,1792]{1,0:T(8,128)} %copy-done.4) | copy-start | bytes 2752516
  (15 other events, 14.3 us)
Sparse Core Ops, SparseCore 0:
  122.5 45.2 all-gather.2
  169.9 50.8 all-gather.4
  329.2 83.7 reduce-scatter.1

commit v6 on v5

--- a/solution.py
+++ b/solution.py
@@ -750,16 +750,41 @@
 
 
 def closing_kernel(
-    part, grads, out_part, fc, proj, out, grads_out, out_w_out, fc_out, proj_out,
+    part, grads, out_part, fc, proj, sums_in, gain_in, shift_in, pair_in, ff_in,
+    out, grads_out, out_w_out, fc_out, proj_out, owned, pairs_out, ff_out,
     held, from_c, from_y, from_z, own_x, from_x, o_held, o_x, o_y, o_z,
     send, loads, rc, ry, rz, load_x, rx, rk, rg, o_loads, orx, ory, orz, org, rfc, rproj,
+    terms, terms_all, half, pairs_half, half_y, pairs_y, rv, rvy,
 ):
     place, group = Place(True), Place(False)
     n_ctx = grads.shape[1]
     copies = Copies(send)
     far_ctx = others(place.ctx, n_ctx)
     peer_x, peer_y = {"x": 1 - place.x}, {"y": 1 - place.y}
-    meet([place.at_ctx(k) for k in far_ctx] + [peer_y, peer_x])
+    count = 2 * n_ctx
+    me = place.x * n_ctx + place.ctx
+    far_shards = others(me, count)
+
+    def at_shard(k):
+        return dict(place.at_ctx(lax.rem(k, n_ctx)), x=k // n_ctx)
+
+    meet([at_shard(k) for k in far_shards] + [peer_y])
+    tall = grads.shape[2]
+    terms[...] = jnp.zeros_like(terms)
+    for k in range(count):
+        cols = slice(k * tall, (k + 1) * tall)
+        terms[k, 0:4, 0:tall] = sums_in[:, cols]
+        terms[k, 4:5, 0:tall] = gain_in[:, cols]
+        terms[k, 5:6, 0:tall] = shift_in[:, cols]
+        pair = pair_in.shape[1] // 3
+        terms[k, 6:7, 0:pair] = pair_in[:, 0:pair]
+        terms[k, 7:8, 0:pair] = pair_in[:, 2 * pair :]
+        for row in range(-(-ff_in.shape[1] // 128)):
+            width = min(128, ff_in.shape[1] - row * 128)
+            terms[k, 8 + row : 9 + row, 0:width] = ff_in[:, row * 128 : row * 128 + width]
+    for k in far_shards:
+        copies.send(terms.at[k], terms_all.at[me], rv.at[me], at_shard(k))
+    terms_all[me] = terms[me]
     sums = Scatter(place, part, held, from_c, from_y, from_z, out, copies, loads, rc, ry, rz)
     outs = OutScatter(place, out_part, o_held, o_x, o_y, o_z, out_w_out, copies, o_loads, orx, ory, orz, org)
     sums.begin()
@@ -792,6 +817,26 @@
     outs.over_y()
     sums.over_z()
     outs.over_z()
+    for k in far_shards:
+        copies.arrived(terms_all.at[k], rv.at[k], at_shard(k))
+    total = terms_all[0, 0:8, :]
+    for k in range(1, count):
+        total = total + terms_all[k, 0:8, :]
+    half[...] = total
+    for k in range(n_ctx):
+        pairs_half[k] = terms_all[k, 6:8, :] + terms_all[n_ctx + k, 6:8, :]
+    copies.send(half, half_y, rvy.at[0], peer_y)
+    copies.send(pairs_half, pairs_y, rvy.at[1], peer_y)
+    for part in range(4):
+        total = terms_all[part, 8:16, :]
+        for k in range(part + 4, count, 4):
+            total = total + terms_all[k, 8:16, :]
+        ff_out[part] = total
+    copies.arrived(half_y, rvy.at[0], peer_y)
+    owned[...] = half[...] + half_y[...]
+    copies.arrived(pairs_y, rvy.at[1], peer_y)
+    pairs_out[place.y] = pairs_half[...]
+    pairs_out[1 - place.y] = pairs_y[...]
     for k in [place.ctx] + far_ctx:
         copies.arrived(grads_out.at[1 - place.y, k], rg.at[k], peer_y)
     outs.end()
@@ -801,7 +846,7 @@
     copies.finish()
 
 
-def closing(part, grads, out_part, fc, proj):
+def closing(part, grads, out_part, fc, proj, *vectors):
     block = part.shape[1:]
     n_ctx = grads.shape[1]
     n_z = n_ctx // 2
@@ -816,102 +861,248 @@
             jax.ShapeDtypeStruct((2,) + half, B16),
             jax.ShapeDtypeStruct(fc.shape, fc.dtype),
             jax.ShapeDtypeStruct(proj.shape, proj.dtype),
+            jax.ShapeDtypeStruct((8, 128), F32),
+            jax.ShapeDtypeStruct((2, n_ctx, 2, 128), F32),
+            jax.ShapeDtypeStruct((4, 8, 128), F32),
         ),
-        in_specs=[ANY] * 5,
-        out_specs=(IN_VMEM, ANY, IN_VMEM, ANY, ANY),
+        in_specs=[ANY] * 5 + [IN_VMEM] * 5,
+        out_specs=(IN_VMEM, ANY, IN_VMEM, ANY, ANY, IN_VMEM, IN_VMEM, IN_VMEM),
         scratch_shapes=scatter_scratch(n_z, block)
         + [pltpu.VMEM(piece, B16), pltpu.VMEM(piece, B16)]
         + [pltpu.VMEM((n_z, rows, width), B16), pltpu.VMEM((n_z, rows, width), B16)]
         + [pltpu.VMEM((n_z,) + half, B16), pltpu.VMEM((n_z,) + half, B16)]
-        + scatter_sems(n_z, 3 * n_ctx + 4 * n_z + 8)
+        + scatter_sems(n_z, 5 * n_ctx + 4 * n_z + 10)
         + dma_sems(n_ctx, n_ctx, n_ctx, n_ctx)
-        + dma_sems(n_z, n_z, n_z, n_z, 2, 4, 4),
+        + dma_sems(n_z, n_z, n_z, n_z, 2, 4, 4)
+        + [pltpu.VMEM((2 * n_ctx, 16, 128), F32), pltpu.VMEM((2 * n_ctx, 16, 128), F32)]
+        + [pltpu.VMEM((8, 128), F32), pltpu.VMEM((n_ctx, 2, 128), F32)]
+        + [pltpu.VMEM((8, 128), F32), pltpu.VMEM((n_ctx, 2, 128), F32)]
+        + dma_sems(2 * n_ctx, 2),
         compiler_params=comm_params(4),
         name="closing",
-    )(part, grads, out_part, fc, proj)
-
-
-def vectors_kernel(src, own_out, ff_out, from_all, half, from_y, send, recv, ry):
-    place = Place(True)
-    count = src.shape[0]
-    n_ctx = count // 2
-    copies = Copies(send)
-    me = place.x * n_ctx + place.ctx
-    far = others(me, count)
-    peer_y = {"y": 1 - place.y}
-
-    def peer(k):
-        return dict(place.at_ctx(lax.rem(k, n_ctx)), x=k // n_ctx)
-
-    meet([peer(k) for k in far] + [peer_y])
-    for k in far:
-        copies.send(src.at[k], from_all.at[me], recv.at[me], peer(k))
-    from_all[me] = src[me]
-    for k in far:
-        copies.arrived(from_all.at[k], recv.at[k], peer(k))
-    total = from_all[0, 0:8, :]
-    for k in range(1, count):
-        total = total + from_all[k, 0:8, :]
-    half[...] = total
-    copies.send(half, from_y, ry.at[0], peer_y)
-    for part in range(4):
-        total = from_all[part, 8:16, :]
-        for k in range(part + 4, count, 4):
-            total = total + from_all[k, 8:16, :]
-        ff_out[part] = total
-    copies.arrived(from_y, ry.at[0], peer_y)
-    own_out[...] = half[...] + from_y[...]
-    copies.finish()
-
-
-def vectors_sum(value):
-    count = value.shape[0]
-    flat = jax.ShapeDtypeStruct((8, 128), F32)
+    )(part, grads, out_part, fc, proj, *vectors)
+
+
+def laid_wide(value, count, rows, tall):
+    zeros = jnp.zeros((value.shape[0], tall - rows), value.dtype)
+    parts = []
+    for k in range(count):
+        parts += [value[:, k * rows : (k + 1) * rows], zeros]
+    return jnp.concatenate(parts, axis=1)
+
+
+def laid_narrow(value, count, rows, tall):
+    return jnp.concatenate([value[:, k * tall : k * tall + rows] for k in range(count)], axis=1)
+
+
+def prepare_kernel(count, at_ref, x, grad, qkv, fc, proj, out_w, *refs):
+    singles, qv, (x_out, grad_out, blocks, ffn, out_out) = refs[:6], refs[6], refs[7:]
+    rows, feats = out_w.shape
+    n_ctx, tall, cols = blocks.shape
+    pair, ff = cols // 3, ffn.shape[3]
+    x_out[...] = laid_wide(x[...].astype(F32), count, rows, tall).astype(B16)
+    grad_out[...] = laid_wide(grad[...].astype(F32), count, rows, tall).astype(B16)
+    below = jnp.zeros((tall - rows, feats), F32)
+    out_out[...] = laid_wide(
+        jnp.concatenate([out_w[...].astype(F32), below], axis=0), count, rows, tall
+    ).astype(B16)
+    below = jnp.zeros((tall - rows, ff), F32)
+    for k in range(4):
+        ffn[0, k] = jnp.concatenate([fc[:, k * ff : (k + 1) * ff].astype(F32), below], axis=0).astype(B16)
+        ffn[1, k] = jnp.concatenate([proj[k * ff : (k + 1) * ff, :].astype(F32).T, below], axis=0).astype(B16)
+    small = [jnp.concatenate([ref[...].astype(F32), jnp.zeros((1, cols - rows), F32)], axis=1) for ref in singles]
+    small.append(jnp.concatenate([qv[...].astype(F32), jnp.zeros((1, cols - 2 * rows), F32)], axis=1))
+    if tall - rows > 7:
+        small.append(jnp.zeros((tall - rows - 7, cols), F32))
+    small = jnp.concatenate(small, axis=0)
+    first = at_ref[0] == 0
+    whole = qkv[...].astype(F32)
+
+    def columns(part, p):
+        width = min(pair, feats - p * pair)
+        if width <= 0:
+            return jnp.zeros((rows, pair), F32)
+        value = whole[:, part * feats + p * pair : part * feats + p * pair + width]
+        if width < pair:
+            value = jnp.concatenate([value, jnp.zeros((rows, pair - width), F32)], axis=1)
+        return value
+
+    for k in range(n_ctx):
+        value = [jnp.where(first, columns(part, 2 * k), columns(part, 2 * k + 1)) for part in range(3)]
+        blocks[k] = jnp.concatenate([jnp.concatenate(value, axis=1), small], axis=0).astype(B16)
+
+
+def prepare(y_at, x, grad, qkv, fc, proj, out_w, singles, qv, n_ctx, tall, pair):
+    rows, feats = out_w.shape
+    count = feats // rows
+    wide = count * tall
+    tokens = x.shape[0]
+    vmem = pl.BlockSpec(memory_space=pltpu.VMEM)
     return pl.pallas_call(
-        vectors_kernel,
-        out_shape=(flat, jax.ShapeDtypeStruct((4, 8, 128), F32)),
-        in_specs=[IN_VMEM],
-        out_specs=(IN_VMEM, IN_VMEM),
-        scratch_shapes=[
-            pltpu.VMEM(value.shape, F32),
-            pltpu.VMEM((8, 128), F32),
-            pltpu.VMEM((8, 128), F32),
-        ]
-        + dma_sems(count + 1, count, 1),
-        compiler_params=comm_params(5),
-        name="vectors_sum",
-    )(value)
-
-
-def project_kernel(feats, x_ref, gain_ref, shift_ref, mask_ref, w_ref, bias_ref, norm_ref, qkv_ref):
+        functools.partial(prepare_kernel, count),
+        in_specs=[pl.BlockSpec(memory_space=pltpu.SMEM)] + [vmem] * 13,
+        out_shape=(
+            jax.ShapeDtypeStruct((tokens, wide), B16),
+            jax.ShapeDtypeStruct((tokens, wide), B16),
+            jax.ShapeDtypeStruct((n_ctx, tall, 3 * pair), B16),
+            jax.ShapeDtypeStruct((2, 4, tall, fc.shape[1] // 4), B16),
+            jax.ShapeDtypeStruct((tall, wide), B16),
+        ),
+        compiler_params=pltpu.CompilerParams(vmem_limit_bytes=VMEM_LIMIT),
+        name="prepare",
+    )(y_at, x, grad, qkv, fc, proj, out_w, *[value[None] for value in singles], qv[None])
+
+
+def project_kernel(
+    rows, feats, at_ref, x_ref, packed_ref, mask_ref, w_ref, norm_ref, qkv_ref, single_ref, bias_s, held_s
+):
+    count, tall, cols = packed_ref.shape
+    pair = cols // 3
+
+    @pl.when(pl.program_id(0) == 0)
+    def begin():
+        held_s[...] = jnp.zeros_like(held_s)
+        vectors = []
+        for row in range(6):
+            at = rows + row
+            vectors.append(
+                jnp.concatenate([packed_ref[k, at : at + 1, 0:tall].astype(F32) for k in range(count)], axis=1)
+            )
+        single_ref[...] = jnp.concatenate(vectors + [jnp.zeros((2, count * tall), F32)], axis=0)
+        for part in range(2):
+            blocks = range(part * count // 2, (part + 1) * count // 2)
+            at = rows + 6
+            held_s[part : part + 1, 0:feats] = jnp.concatenate(
+                [packed_ref[k, at : at + 1, 0 : 2 * rows].astype(F32) for k in blocks], axis=1
+            )
+        own = pl.ds(pl.multiple_of(at_ref[0] * pair, pair), pair)
+        bias_s[...] = jnp.concatenate([held_s[0:1, own], jnp.zeros((1, pair), F32), held_s[1:2, own]], axis=1)
+
     x = x_ref[...].astype(F32)
     mean = jnp.sum(x, axis=1, keepdims=True) * (1.0 / feats)
     centered = (x - mean) * mask_ref[...]
     inv = lax.rsqrt(jnp.sum(centered * centered, axis=1, keepdims=True) * (1.0 / feats) + NORM_EPS)
-    norm = (centered * inv * gain_ref[...] + shift_ref[...]).astype(B16)
+    norm = (centered * inv * single_ref[0:1, :] + single_ref[1:2, :]).astype(B16)
     norm_ref[...] = norm
-    qkv_ref[...] = (dot(norm, w_ref[...], 1, 0) + bias_ref[...]).astype(B16)
-
-
-def project(x, gain, shift, mask, weight, bias, feats):
+    qkv_ref[...] = (dot(norm, w_ref[...], 1, 0) + bias_s[...]).astype(B16)
+
+
+def project(slot_at, x, packed, mask, rows, feats, padded):
+    total, wide = x.shape
+    cols = packed.shape[2]
+    step = min(256, total)
+
+    def fixed(shape):
+        return pl.BlockSpec(shape, lambda i: (0,) * len(shape))
+
+    return pl.pallas_call(
+        functools.partial(project_kernel, rows, feats),
+        grid=(total // step,),
+        in_specs=[pl.BlockSpec(memory_space=pltpu.SMEM), pl.BlockSpec((step, wide), lambda i: (i, 0))]
+        + [fixed(packed.shape), fixed((1, wide)), fixed((wide, cols))],
+        out_specs=(
+            pl.BlockSpec((step, wide), lambda i: (i, 0)),
+            pl.BlockSpec((step, cols), lambda i: (i, 0)),
+            fixed((8, wide)),
+        ),
+        out_shape=(
+            jax.ShapeDtypeStruct((total, wide), B16),
+            jax.ShapeDtypeStruct((total, cols), B16),
+            jax.ShapeDtypeStruct((8, wide), F32),
+        ),
+        scratch_shapes=[pltpu.VMEM((1, cols), F32), pltpu.VMEM((2, padded), F32)],
+        compiler_params=pltpu.CompilerParams(vmem_limit_bytes=VMEM_LIMIT),
+        name="project",
+    )(slot_at, x, packed, mask[None], packed.reshape(wide, cols))
+
+
+def project_back_kernel(feats, x_ref, grad_ref, mask_ref, w_ref, part_ref, gradb_ref, gain_ref, shift_ref, pair_ref):
+    @pl.when(pl.program_id(0) == 0)
+    def begin():
+        gain_ref[...] = jnp.zeros_like(gain_ref)
+        shift_ref[...] = jnp.zeros_like(shift_ref)
+        pair_ref[...] = jnp.zeros_like(pair_ref)
+
+    grad = grad_ref[...]
+    pair_ref[...] += jnp.sum(grad, axis=0, keepdims=True)
+    grad = grad.astype(B16)
+    gradb_ref[...] = grad
+    part = dot(grad, w_ref[...], 1, 1)
+    part_ref[...] = part.astype(B16)
+    x = x_ref[...].astype(F32)
+    mean = jnp.sum(x, axis=1, keepdims=True) * (1.0 / feats)
+    centered = (x - mean) * mask_ref[...]
+    inv = lax.rsqrt(jnp.sum(centered * centered, axis=1, keepdims=True) * (1.0 / feats) + NORM_EPS)
+    gain_ref[...] += jnp.sum(part * (centered * inv), axis=0, keepdims=True)
+    shift_ref[...] += jnp.sum(part, axis=0, keepdims=True)
+
+
+def project_back(x, grad, mask, weight, feats):
     total, wide = x.shape
     cols = weight.shape[1]
     step = min(256, total)
 
     def fixed(shape):
-        return pl.BlockSpec(shape, lambda i: (0, 0))
+        return pl.BlockSpec(shape, lambda i: (0,) * len(shape))
+
+    def moving(width):
+        return pl.BlockSpec((step, width), lambda i: (i, 0))
 
     return pl.pallas_call(
-        functools.partial(project_kernel, feats),
+        functools.partial(project_back_kernel, feats),
         grid=(total // step,),
-        in_specs=[pl.BlockSpec((step, wide), lambda i: (i, 0))]
-        + [fixed((1, wide))] * 3
-        + [fixed((wide, cols)), fixed((1, cols))],
-        out_specs=(pl.BlockSpec((step, wide), lambda i: (i, 0)), pl.BlockSpec((step, cols), lambda i: (i, 0))),
-        out_shape=(jax.ShapeDtypeStruct((total, wide), B16), jax.ShapeDtypeStruct((total, cols), B16)),
+        in_specs=[moving(wide), moving(cols), fixed((1, wide)), fixed((wide, cols))],
+        out_specs=(moving(wide), moving(cols), fixed((1, wide)), fixed((1, wide)), fixed((1, cols))),
+        out_shape=(
+            jax.ShapeDtypeStruct((total, wide), B16),
+            jax.ShapeDtypeStruct((total, cols), B16),
+            jax.ShapeDtypeStruct((1, wide), F32),
+            jax.ShapeDtypeStruct((1, wide), F32),
+            jax.ShapeDtypeStruct((1, cols), F32),
+        ),
         compiler_params=pltpu.CompilerParams(vmem_limit_bytes=VMEM_LIMIT),
-        name="project",
-    )(x, gain[None], shift[None], mask[None], weight, bias[None])
+        name="project_back",
+    )(x, grad, mask[None], weight)
+
+
+def deliver_kernel(
+    rows, feats, qkv, out_w, fc, proj, mlp, hidden, dnorm, dhidden, x_ref, single, mask,
+    qkv_out, out_out, fc_out, proj_out, block_out, grad_out,
+):
+    n_y, n_ctx, tall, cols = qkv.shape
+    pair, ff, count = cols // 3, fc.shape[2], feats // rows
+    parts = []
+    for part in range(3):
+        for p in range(-(-feats // pair)):
+            width = min(pair, feats - p * pair)
+            parts.append(qkv[p % n_y, p // n_y, :, part * pair : part * pair + width].astype(F32))
+    qkv_out[...] = jnp.concatenate(parts, axis=1)[:rows]
+    halves = jnp.concatenate([out_w[y].astype(F32) for y in range(2)], axis=1)
+    out_out[...] = laid_narrow(halves, count, rows, tall)[:rows]
+    fc_out[...] = jnp.concatenate([fc[k].astype(F32) for k in range(4)], axis=1)[:rows]
+    for k in range(4):
+        proj_out[k * ff : (k + 1) * ff, :] = proj[k].astype(F32).T[:, :rows]
+    block_out[...] = laid_narrow(hidden[...] + mlp[...].astype(F32) + single[5:6, :], count, rows, tall)
+    normed, inv = norm_forward(x_ref[...].astype(F32), mask[...], feats)
+    grad = dhidden[...] + norm_backward(dnorm[...], normed, inv, single[0:1, :], feats)
+    grad_out[...] = laid_narrow(grad, count, rows, tall)
+
+
+def deliver(qkv, out_w, fc, proj, mlp, hidden, dnorm, dhidden, x, single, mask, rows, feats):
+    tokens, ff = x.shape[0], fc.shape[2]
+    return pl.pallas_call(
+        functools.partial(deliver_kernel, rows, feats),
+        out_shape=(
+            jax.ShapeDtypeStruct((rows, 3 * feats), F32),
+            jax.ShapeDtypeStruct((rows, feats), F32),
+            jax.ShapeDtypeStruct((rows, 4 * ff), F32),
+            jax.ShapeDtypeStruct((4 * ff, rows), F32),
+            jax.ShapeDtypeStruct((tokens, feats), F32),
+            jax.ShapeDtypeStruct((tokens, feats), F32),
+        ),
+        compiler_params=pltpu.CompilerParams(vmem_limit_bytes=VMEM_LIMIT),
+        name="deliver",
+    )(qkv, out_w, fc, proj, mlp, hidden, dnorm, dhidden, x, single, mask[None])
 
 
 def feed_kernel(count, at_ref, *refs):
@@ -1016,18 +1207,13 @@
 
     mask = jnp.asarray((np.arange(wide) % tall < rows).astype(np.float32))
 
-    small = jnp.concatenate([first_gain, first_shift, out_bias, second_gain, second_shift, proj_bias, qv_bias])
-    packed = jnp.pad(qkv_weight.reshape(rows, 3, feats), ((0, 0), (0, 0), (0, padded - feats)))
-    packed = lax.dynamic_index_in_dim(packed.reshape(rows, 3, n_ctx, n_y, pair), y_at, 3, False)
-    packed = packed.transpose(2, 0, 1, 3).reshape(n_ctx, rows, 3 * pair)
-    small = jnp.pad(small, (0, row_pad * 3 * pair - small.shape[0])).reshape(1, row_pad, 3 * pair)
-    packed = jnp.concatenate([packed, jnp.broadcast_to(small, (n_ctx, row_pad, 3 * pair))], axis=1)
-    ffn_blocks = jnp.stack([fc_weight, proj_weight.T])
-    ffn_blocks = jnp.pad(ffn_blocks, ((0, 0), (0, row_pad), (0, 0))).reshape(2, tall, 4, ff_own).transpose(0, 2, 1, 3)
-    own_input = widened(block_input[0])
-    grad_own = widened(out_grad[0])
+    singles = (first_gain, first_shift, out_bias, second_gain, second_shift, proj_bias)
+    own_input, grad_own, packed, ffn_blocks, w_out = prepare(
+        y_at.astype(jnp.int32)[None], block_input[0], out_grad[0], qkv_weight, fc_weight, proj_weight, out_weight,
+        singles, qv_bias, n_ctx, tall, pair,
+    )
     all_input, packed, ffn_blocks, w_out = opening(
-        own_input, packed, ffn_blocks, widened(jnp.pad(out_weight, ((0, row_pad), (0, 0))))
+        own_input, packed, ffn_blocks, w_out
     )
     ffn_blocks = ffn_blocks.reshape(2, 4 * tall, ff_own)
     along_h = [lax.ppermute(ffn_blocks, "h", shift_perm(n_h, step)) for step in range(1, n_h)]
@@ -1038,14 +1224,6 @@
     w_out = w_out.reshape(2, n_y, wide // 2, wide // 2)
     packed = packed.reshape(n_shard, tall, 3 * pair)
     w_qkv = packed.reshape(wide, 3 * pair)
-    smalls = packed[:, rows:].reshape(n_shard, -1)[:, : 8 * rows].astype(F32)
-    singles = jnp.pad(smalls[:, : 6 * rows].reshape(n_shard, 6, rows), ((0, 0), (0, 0), (0, row_pad)))
-    gain_one, shift_one, bias_out, gain_two, shift_two, bias_proj = singles.transpose(1, 0, 2).reshape(6, wide)
-    bias_qv = smalls[:, 6 * rows :].reshape(2, feats)
-    bias_pair = lax.dynamic_slice_in_dim(
-        jnp.pad(bias_qv, ((0, 0), (0, padded - feats))), slot_at * pair, pair, 1
-    )
-    bias_qkv = jnp.concatenate([bias_pair[0], jnp.zeros((pair,), F32), bias_pair[1]])
     b_fc = lax.dynamic_slice_in_dim(fc_bias, lc_at * ff_own, ff_own, 0).astype(F32)
 
     order = slot_order[0]
@@ -1059,9 +1237,11 @@
     low = start3[:, 0, 0] // BLK
 
     own_wide = own_input.astype(F32)
-    norm_one, qkv = project(
-        all_input.reshape(n_slot * slot_len, wide), gain_one, shift_one, mask, w_qkv, bias_qkv, feats
+    all_input = all_input.reshape(n_slot * slot_len, wide)
+    norm_one, qkv, singles = project(
+        slot_at.astype(jnp.int32)[None], all_input, packed, mask, rows, feats, padded
     )
+    bias_out, gain_two, shift_two = singles[2], singles[3], singles[4]
     heads_out, lse = attend(inv, low, qkv, start3, slot_len, head)
     attention = widened(to_tokens(heads_out.reshape(n_slot, slot_len, pair))[:, :feats])
     by_core = attention.reshape(slot_len, n_shard // 2, 2, tall)
@@ -1128,58 +1308,31 @@
     fc_line = pick(fc_part, x_at) + fc_x
     fc_h = over_h(fc_line)
     dqkv = attend_back(inv, low, qkv, heads_out, dattention, lse, start3, slot_len, head)
-    dqkv_b = dqkv.astype(B16)
-    dnorm_one_part = dot(dqkv_b, w_qkv, 1, 1).astype(B16)
+    dnorm_one_part, dqkv_b, gain_sum, shift_sum, pair_sum = project_back(all_input, dqkv, mask, w_qkv, feats)
     qkv_part = dot(norm_one, dqkv_b, 0, 0).astype(B16).reshape(n_x, n_ctx, tall, 3 * pair)
     proj_h, fc_h, dnorm_one_part = after((proj_h, fc_h), dnorm_one_part, True)
-    dnorm_one, qkv_all, out_all, fc_all, proj_all = closing(
-        dnorm_one_part.reshape(n_slot, slot_len, wide), qkv_part, out_part, total(fc_line, fc_h), total(proj_line, proj_h)
-    )
-    mlp, dnorm_one = after(mlp, dnorm_one)
-    block_output = narrowed(hidden + mlp.astype(F32) + bias_proj)
-    proj_grad = proj_all[:, :rows].astype(F32).transpose(0, 2, 1).reshape(4 * ff_own, rows)
-    fc_grad = fc_all[:, :rows].astype(F32).transpose(1, 0, 2).reshape(rows, 4 * ff_own)
-    qkv_all = qkv_all[:, :, :rows].reshape(n_y, n_ctx, rows, 3, pair)
-    qkv_grad = qkv_all.transpose(2, 3, 1, 0, 4).reshape(rows, 3, padded)
-    qkv_grad = qkv_grad[:, :, :feats].reshape(rows, 3 * feats).astype(F32)
-    out_grad_w = narrowed(out_all[:, :rows].transpose(1, 0, 2).reshape(rows, wide)).astype(F32)
-
-    normed_one, inv_one = norm_forward(own_wide, mask, feats)
-    input_grad = narrowed(dhidden + norm_backward(dnorm_one, normed_one, inv_one, gain_one, feats))
-
-    dq_sum, dv_sum = jnp.sum(dqkv[:, :pair], axis=0), jnp.sum(dqkv[:, 2 * pair :], axis=0)
-
-    def placed(value, width, at):
-        return lax.dynamic_update_slice(jnp.zeros((width,), F32), value, (at,))[:feats]
-
-    vectors = jnp.stack(
+    token_sums = jnp.stack(
         [
             jnp.sum(dhidden, axis=0),
-            jnp.sum(dnorm_one * normed_one, axis=0),
-            jnp.sum(dnorm_one, axis=0),
             jnp.sum(dnorm_two * normed_two, axis=0),
             jnp.sum(dnorm_two, axis=0),
             jnp.sum(grad_wide, axis=0),
         ]
     )
-    qv_sums = jnp.concatenate([placed(dq_sum, padded, slot_at * pair), placed(dv_sum, padded, slot_at * pair)])
-    vectors = jnp.concatenate(
-        [
-            vectors.reshape(6, n_shard, tall).transpose(1, 0, 2).reshape(n_shard, 6 * tall),
-            qv_sums.reshape(n_shard, 2 * rows),
-            jnp.zeros((n_shard, 1024 - 6 * tall - 2 * rows), F32),
-            jnp.broadcast_to(dpreact_sum, (n_shard, ff_own)),
-            jnp.zeros((n_shard, 1024 - ff_own), F32),
-        ],
-        axis=1,
+    dnorm_one, qkv_all, out_all, fc_all, proj_all, owned, pair_sums, ff_sums = closing(
+        dnorm_one_part.reshape(n_slot, slot_len, wide), qkv_part, out_part, total(fc_line, fc_h), total(proj_line, proj_h),
+        token_sums, gain_sum, shift_sum, pair_sum, dpreact_sum,
     )
-    owned, ff_sums = vectors_sum(vectors.reshape(n_shard, 16, 128))
-    owned = owned.reshape(1024)
+    mlp, dnorm_one = after(mlp, dnorm_one)
+    qkv_grad, out_grad_w, fc_grad, proj_grad, block_output, input_grad = deliver(
+        qkv_all, out_all, fc_all, proj_all, mlp, hidden, dnorm_one, dhidden, own_input, singles, mask, rows, feats
+    )
     fc_bias_grad = ff_sums.reshape(4, 1024)[:, :ff_own].reshape(4 * ff_own)
-    qv_grad = owned[6 * tall : 6 * tall + 2 * rows]
+    pair_sums = pair_sums.transpose(2, 1, 0, 3).reshape(2, padded)[:, :feats].reshape(2 * feats)
+    qv_grad = lax.dynamic_slice_in_dim(pair_sums, lax.axis_index(SHARD) * 2 * rows, 2 * rows, 0)
 
     def own(index):
-        return owned[index * tall : index * tall + rows]
+        return owned[index, :rows]
 
     return (
         block_output[None],
@@ -1188,14 +1341,14 @@
         qv_grad,
         out_grad_w,
         own(0),
+        own(4),
+        own(5),
         own(1),
         own(2),
-        own(3),
-        own(4),
         fc_grad,
         fc_bias_grad,
         proj_grad,
-        own(5),
+        own(3),
     )
 
 

time: 593 us -> 560 us (0.944)
  local copies, waits for them, and re-layouts: 61.1 us -> 32.9 us
  Pallas kernels: 398 us -> 422 us
  other arithmetic: 30.2 us -> 18 us
  matrix products: 52 us -> 43.3 us
  waiting for transfers between devices: 22.7 us -> 16.2 us
    pallas_call x2 -> x4, Pallas kernels: 22.7 us -> 40 us  [the longest x1 13.5 us: project(): pl.pallas_call(functools.partial(project_kernel, rows, feats), grid=(tota...]
    reshape x14 -> x2, local copies, waits for them, and re-layouts: 16.4 us -> 0.11 us  [on_device(): pair_sums.transpose(2, 1, 0, 3).reshape(2, padded)[:, :feats]]
    dot_general x14 -> x13, matrix products: 52 us -> 43.3 us  [dot(): lax.dot_general(left, right, (((left_dim,), (right_dim,)), ((), ())), pre...]
    pallas_call x1, Pallas kernels: 31.2 us -> 39.3 us  [to_tokens(): pl.pallas_call(to_tokens_kernel, out_shape=jax.ShapeDtypeStruct((tokens,...]
    ppermute x2, waiting for transfers between devices: 15.8 us -> 8.71 us  [over_h(): lax.ppermute(give, 'h', shift_perm(n_h, step + 1))]
    unnamed x77 -> x49, local copies, waits for them, and re-layouts: 10.8 us -> 16.7 us
  transfers between devices with their start and end apart: 11 -> 11, of which waited for: 3 -> 4; matrix products, arithmetic and copies ran while one was open for 17% -> 12% of each run, Pallas kernels for 46% -> 52%
where the time goes in v6:
time: 560 us; the launch traced here: 555 us
  Pallas kernels  422 us (75%)
  matrix products  43.3 us (8%)
  local copies, waits for them, and re-layouts  32.9 us (6%)
  other arithmetic  18 us (3%)
  waiting for transfers between devices  16.2 us (3%)
  between operations  14.5 us (3%)
  starting transfers between devices  8.16 us (1%)
    pallas_call x1, Pallas kernels, closing(): pl.pallas_call(closing_kernel, out_shape=(jax.ShapeDtypeStruct(block, F32...  99.6 us
    pallas_call x1, Pallas kernels, opening(): pl.pallas_call(opening_kernel, out_shape=(jax.ShapeDtypeStruct((2 * n_ctx...  98.2 us
    dot_general x13, matrix products, dot(): lax.dot_general(left, right, (((left_dim,), (right_dim,)), ((), ())), pre...  43.3 us
    pallas_call x1, Pallas kernels, to_tokens(): pl.pallas_call(to_tokens_kernel, out_shape=jax.ShapeDtypeStruct((tokens,...  39.3 us
    pallas_call x1, Pallas kernels, group_scatter(): pl.pallas_call(group_scatter_kernel, out_shape=jax.ShapeDtypeStruct(block...  30.1 us
    pallas_call x1, Pallas kernels, group_gather(): pl.pallas_call(group_gather_kernel, out_shape=jax.ShapeDtypeStruct((8,) +...  30 us
    pallas_call x1, Pallas kernels, attend_back(): pl.pallas_call(functools.partial(attend_back_kernel, slot_len, head), out...  24.1 us
    pallas_call x1, Pallas kernels, attend(): pl.pallas_call(functools.partial(attend_kernel, slot_len, head), out_shap...  23.2 us
  transfers between devices with their start and end apart: 11, of which 4 were waited for; matrix products, arithmetic and copies ran while one was open for 12% of the time, Pallas kernels for 52%

profile of v6, /device:TPU:0, one launch (start us, length us, event | category | flops | bytes accessed | tf_op | source)
XLA Modules:
  0.0 555.5 jit_solution(3559931154615180995)
XLA Ops:
  13.7 5.2 prepare.1
  18.9 98.2 %opening.1 = (bf16[16,128,1792]{2,1,0:T(8,128)(2,1)}, bf16[2,8,112,384]{3,2,1,0:T(8,128)(2,1)}, bf16[2,4,112,800]{3,2,1,0:T(8,128)(2,1)}, bf16[8,112,896]{2,1,0:T(8,128)(2,1)}) custom-call(bf16[128,1792]{1,0:T(8,128)(2,1)} %get-tuple-element.71.own.x_ref, bf16[8,112,384]{2,1,0:T(8,128)(2,1)} %get-tuple-element.72.blocks, ...), custom_call_target="tpu_custom_call" | custom-call | tf_op jit(solution)/shard_map/opening/pallas_call | solution.py:524
  119.9 13.5 %project.1 = (bf16[2048,1792]{1,0:T(8,128)(2,1)}, bf16[2048,384]{1,0:T(8,128)(2,1)}, f32[8,1792]{1,0:T(8,128)}) custom-call(s32[1]{0:T(128)} %bitcast.20.at_ref, bf16[2048,1792]{1,0:T(8,128)(2,1)} %bitcast.134, bf16[16,112,384]{2,1,0:T(8,128)(2,1)} %bitcast.139, f32[1,1792]{1,0:T(1,128)} %constant.127.mask_ref.mask, bf16[1792,384]{1,0:T(8,128)(2,1)} %bitcast.140), custom_call_target="tpu_custom_call" | custom-call | tf_op jit(solution)/shard_map/project/pallas_call | solution.py:998
  134.4 23.2 %attend.1 = (bf16[2048,128]{1,0:T(8,128)(2,1)}, f32[8,2,256]{2,1,0:T(2,128)}) custom-call(s32[16]{0:T(128)} %copy-done.16, s32[8]{0:T(128)} %and_select_fusion.low_ref, bf16[2048,384]{1,0:T(8,128)(2,1)} %get-tuple-element.80.qkv_ref, s32[8,1,256]{2,1,0:T(1,128)} %bitcast.179), custom_call_target="tpu_custom_call" | custom-call | tf_op jit(solution)/shard_map/attend/pallas_call | solution.py:157
  157.6 39.3 %to_tokens.1 = bf16[128,2048]{1,0:T(8,128)(2,1)} custom-call(bf16[16,128,128]{2,1,0:T(8,128)(2,1)} %bitcast.166), custom_call_target="tpu_custom_call" | custom-call | tf_op jit(solution)/shard_map/to_tokens/pallas_call | solution.py:560
  211.6 30.0 %group_gather.1 = bf16[8,128,1792]{2,1,0:T(8,128)(2,1)} custom-call(bf16[128,1792]{1,0:T(8,128)(2,1)} %add_convert_fusion.1.own), custom_call_target="tpu_custom_call" | custom-call | tf_op jit(solution)/shard_map/group_gather/pallas_call | solution.py:452
  241.6 5.6 %collective-permute-done.2.refs_3_ = bf16[2,448,800]{2,1,0:T(8,128)(2,1)} collective-permute-done((bf16[2,448,800]{2,1,0:T(8,128)(2,1)}, bf16[2,448,800]{2,1,0:T(8,128)(2,1)}, u32[]{:S(2)}, u32[]{:S(2)}) %collective-permute-start.2) | collective-permute-done | bytes 1433632 | tf_op jit(solution)/shard_map/ppermute | solution.py:1255
  247.2 21.7 %feed.1 = (bf16[1024,800]{1,0:T(8,128)(2,1)}, bf16[1024,800]{1,0:T(8,128)(2,1)}, bf16[1024,1792]{1,0:T(8,128)(2,1)}, bf16[1024,1792]{1,0:T(8,128)(2,1)}, f32[1,800]{1,0:T(1,128)}) custom-call(s32[4]{0:T(128)} %pad_add_fusion.at_ref, bf16[2,448,800]{2,1,0:T(8,128)(2,1)} %bitcast.13.refs_0_, bf16[2,448,800]{2,1,0:T(8,128)(2,1)} %collective-permute-done.refs_1_, ...), custom_call_target="tpu_custom_call" | custom-call | tf_op jit(solution)/shard_map/feed/pallas_call | solution.py:1145
  268.9 6.8 %convolution_convert_fusion.2 = bf16[1792,800]{1,0:T(8,128)(2,1)S(1)} fusion(bf16[1024,1792]{1,0:T(8,128)(2,1)} %all-gather.3.cloned.1.call-done.refs_5_, bf16[1024,800]{1,0:T(8,128)(2,1)} %get-tuple-element.86), kind=kOutput, calls=%fused_computation.4 | convolution fusion | flops 2937446400 | bytes 8175616 | tf_op jit(solution)/shard_map/dot_general | solution.py:59
  278.6 5.6 %convolution_convert_fusion.1 = bf16[1792,800]{1,0:T(8,128)(2,1)} fusion(bf16[1024,1792]{1,0:T(8,128)(2,1)S(1)} %bitcast.137, bf16[1024,800]{1,0:T(8,128)(2,1)S(1)} %copy-done.17), kind=kOutput, calls=%fused_computation.3 | convolution fusion | flops 2937446400 | bytes 8175616 | tf_op jit(solution)/shard_map/dot_general | solution.py:59
  284.2 30.1 %group_scatter.1 = f32[128,1792]{1,0:T(8,128)} custom-call(bf16[8,128,1792]{2,1,0:T(8,128)(2,1)} %bitcast.159), custom_call_target="tpu_custom_call" | custom-call | tf_op jit(solution)/shard_map/group_scatter/pallas_call | solution.py:692
  317.3 2.6 convolution_convert_fusion
  320.0 2.7 dynamic-slice_bitcast_fusion
  325.3 2.0 fusion.15
  327.5 2.0 fusion.2
  329.5 2.0 fusion.14
  333.0 16.3 %to_heads.1 = bf16[16,128,128]{2,1,0:T(8,128)(2,1)} custom-call(bf16[128,2048]{1,0:T(8,128)(2,1)} %pad.9.src), custom_call_target="tpu_custom_call" | custom-call | tf_op jit(solution)/shard_map/to_heads/pallas_call | solution.py:591
  349.3 2.1 bitcast_add_fusion.1
  352.4 2.7 collective-permute-start.4
  355.8 3.7 fusion.18
  364.2 2.5 collective-permute-start.7
  366.7 24.1 %attend_back.1.grad_ref = f32[2048,384]{1,0:T(8,128)} custom-call(s32[16]{0:T(128)} %copy-done.16, s32[8]{0:T(128)} %and_select_fusion.low_ref, bf16[2048,384]{1,0:T(8,128)(2,1)} %get-tuple-element.80.qkv_ref, bf16[2048,128]{1,0:T(8,128)(2,1)} %get-tuple-element.81.out_ref, bf16[2048,128]{1,0:T(8,128)(2,1)} %bitcast.167, ...), custom_call_target="tpu_custom_call" | custom-call | tf_op jit(solution)/shard_map/attend_back/pallas_call | solution.py:254
  390.8 13.4 %project_back.1 = (bf16[2048,1792]{1,0:T(8,128)(2,1)}, bf16[2048,384]{1,0:T(8,128)(2,1)}, f32[1,1792]{1,0:T(1,128)}, f32[1,1792]{1,0:T(1,128)}, f32[1,384]{1,0:T(1,128)}) custom-call(bf16[2048,1792]{1,0:T(8,128)(2,1)} %bitcast.135, f32[2048,384]{1,0:T(8,128)} %attend_back.1.grad_ref, f32[1,1792]{1,0:T(1,128)} %constant.127.mask_ref.mask, ...), custom_call_target="tpu_custom_call" | custom-call | tf_op jit(solution)/shard_map/project_back/pallas_call | solution.py:1051
  404.2 8.7 %convolution_convert_fusion.3 = bf16[1792,384]{1,0:T(8,128)(2,1)} fusion(bf16[2048,1792]{1,0:T(8,128)(2,1)} %get-tuple-element.100, bf16[2048,384]{1,0:T(8,128)(2,1)} %get-tuple-element.101), kind=kOutput, calls=%fused_computation.5 | convolution fusion | flops 2819260416 | bytes 10289152 | tf_op jit(solution)/shard_map/dot_general | solution.py:59
  413.0 4.2 add_convert_fusion
  417.2 8.7 %collective-permute-done.7 = bf16[448,800]{1,0:T(8,128)(2,1)} collective-permute-done((bf16[448,800]{1,0:T(8,128)(2,1)}, bf16[448,800]{1,0:T(8,128)(2,1)}, u32[]{:S(2)}, u32[]{:S(2)}) %collective-permute-start.7) | collective-permute-done | bytes 716832 | tf_op jit(solution)/shard_map/ppermute | solution.py:1282
  425.9 2.2 fusion
  428.1 2.2 fusion.1
  430.3 99.6 %closing.1 = (f32[128,1792]{1,0:T(8,128)}, bf16[2,8,112,384]{3,2,1,0:T(8,128)(2,1)}, bf16[2,112,896]{2,1,0:T(8,128)(2,1)}, bf16[4,112,800]{2,1,0:T(8,128)(2,1)},...) custom-call(bf16[16,128,1792]{2,1,0:T(8,128)(2,1)} %bitcast.150, ...), custom_call_target="tpu_custom_call" | custom-call | tf_op jit(solution)/shard_map/closing/pallas_call | solution.py:856
  534.3 8.0 %deliver.1 = (f32[100,4800]{1,0:T(8,128)}, f32[100,1600]{1,0:T(8,128)}, f32[100,3200]{1,0:T(8,128)}, f32[3200,100]{1,0:T(8,128)}, f32[128,1600]{1,0:T(8,128)}, /*index=5*/f32[128,1600]{1,0:T(8,128)}) custom-call(bf16[2,8,112,384]{3,2,1,0:T(8,128)(2,1)} %get-tuple-element.109.qkv, bf16[2,112,896]{2,1,0:T(8,128)(2,1)} %get-tuple-element.110.out_w, ...), custom_call_target="tpu_custom_call" | custom-call | tf_op jit(solution)/shard_map/deliver/pallas_call | solution.py:1093
  542.3 2.5 copy.90
  544.7 2.3 copy.91
  (128 shorter events, 47.3 us)
Async XLA Ops:
  7.2 112.1 %copy-start = (s32[1,2048]{1,0:T(1,128)S(1)}, s32[1,2048]{1,0:T(1,128)}, u32[]{:S(2)}) copy-start(s32[1,2048]{1,0:T(1,128)} %param.18) | copy-start | bytes 24580
  7.2 5.3 copy-start.13
  7.2 192.1 %all-gather.5.cloned.1.call-start = ((), (), s32[]{:S(2)}) async-start(), calls=%async_computation.2 | async-start | bytes 8028160 | tf_op jit(solution)/shard_map/all_gather | solution.py:1223
  117.1 2.0 copy-start.18
  117.1 124.5 %all-gather.3.cloned.1.call-start = ((), (), s32[]{:S(2)}) async-start(), calls=%async_computation.1 | async-start | bytes 4128768 | tf_op jit(solution)/shard_map/all_gather | solution.py:1193
  117.9 416.3 %reduce-scatter.2.cloned.1.call-start = ((), (), s32[]{:S(2)}) async-start(), calls=%async_computation.3 | async-start | bytes 4128768 | tf_op jit(solution)/shard_map/reduce_scatter | solution.py:1293
  118.5 90.6 %collective-permute-start.1 = (bf16[2,448,800]{2,1,0:T(8,128)(2,1)}, bf16[2,448,800]{2,1,0:T(8,128)(2,1)}, u32[]{:S(2)}, u32[]{:S(2)}) collective-permute-start(bf16[2,448,800]{2,1,0:T(8,128)(2,1)} %bitcast.13.refs_0_), channel_id=1, source_target_pairs={{0,8},{8,0},{1,9},{9,1},{2,10},{10,2},{3,11},{11,3},{4,12},{12,4},... | collective-permute-start | bytes 4300808 | tf_op jit(solution)/shard_map/ppermute | solution.py:1219
  118.6 123.0 %collective-permute-start = (bf16[2,448,800]{2,1,0:T(8,128)(2,1)}, bf16[2,448,800]{2,1,0:T(8,128)(2,1)}, u32[]{:S(2)}, u32[]{:S(2)}) collective-permute-start(bf16[2,448,800]{2,1,0:T(8,128)(2,1)} %bitcast.13.refs_0_), channel_id=1, source_target_pairs={{0,16},{16,0},{1,17},{17,1},{2,18},{18,2},{3,19},{19,3},{4,20},{20... | collective-permute-start | bytes 4300808 | tf_op jit(solution)/shard_map/ppermute | solution.py:1220
  119.3 14.1 %copy-start.16 = (s32[16]{0:T(128)}, s32[16]{0:T(128)S(1)}, u32[]{:S(2)}) copy-start(s32[16]{0:T(128)S(1)} %select_reduce_fusion.1.inv_ref) | copy-start | bytes 196
  133.7 0.8 copy-start.15
  205.1 2.0 copy-start.8
  207.1 0.7 copy-start.14
  207.3 108.7 %copy-start.2 = (f32[128,1792]{1,0:T(8,128)}, f32[128,1792]{1,0:T(8,128)S(1)}, u32[]{:S(2)}) copy-start(f32[128,1792]{1,0:T(8,128)S(1)} %get-tuple-element.206.hidden) | copy-start | bytes 2752516
  209.1 38.1 %collective-permute-start.2 = (bf16[2,448,800]{2,1,0:T(8,128)(2,1)}, bf16[2,448,800]{2,1,0:T(8,128)(2,1)}, u32[]{:S(2)}, u32[]{:S(2)}) collective-permute-start(bf16[2,448,800]{2,1,0:T(8,128)(2,1)} %collective-permute-done.1.refs_2_), channel_id=1, source_target_pairs={{0,16},{16,0},{1,17},{17,1},{2,18},{18,2},{3,19},{19,3},{4,20},{20... | collective-permute-start | bytes 4300808 | tf_op jit(solution)/shard_map/ppermute | solution.py:1255
  268.9 8.6 %copy-start.3 = (bf16[8,128,1792]{2,1,0:T(8,128)(2,1)S(1)}, bf16[8,128,1792]{2,1,0:T(8,128)(2,1)}, u32[]{:S(2)}) copy-start(bf16[8,128,1792]{2,1,0:T(8,128)(2,1)} %group_gather.1) | copy-start | bytes 11010052
  275.7 8.5 %copy-start.10 = (bf16[1792,800]{1,0:T(8,128)(2,1)}, bf16[1792,800]{1,0:T(8,128)(2,1)S(1)}, u32[]{:S(2)}) copy-start(bf16[1792,800]{1,0:T(8,128)(2,1)S(1)} %convolution_convert_fusion.2) | copy-start | bytes 8601604
  275.7 2.9 copy-start.17
  277.0 37.4 %collective-permute-start.3 = (bf16[2,448,800]{2,1,0:T(8,128)(2,1)}, bf16[2,448,800]{2,1,0:T(8,128)(2,1)}, u32[]{:S(2)}, u32[]{:S(2)}) collective-permute-start(bf16[2,448,800]{2,1,0:T(8,128)(2,1)} %dynamic-slice_bitcast_fusion.1), channel_id=1, source_target_pairs={{0,16},{16,0},{1,17},{17,1},{2,18},{18,2},{3,19},{19,3},{4,20},{20... | collective-permute-start | bytes 4300808 | tf_op jit(solution)/shard_map/ppermute | solution.py:1273
  314.4 1.2 copy-start.5
  315.6 1.0 copy-start.11
  317.3 2.7 copy-start.4
  320.0 40.5 %collective-permute-start.5 = (bf16[896,1792]{1,0:T(8,128)(2,1)}, bf16[896,1792]{1,0:T(8,128)(2,1)}, u32[]{:S(2)}, u32[]{:S(2)}) collective-permute-start(bf16[896,1792]{1,0:T(8,128)(2,1)} %convolution_convert_fusion), channel_id=1, source_target_pairs={{0,2},{2,0},{1,3},{3,1},{4,6},{6,4},{5,7},{7,5},{8,10},{10,8},{9,1... | collective-permute-start | bytes 9633800 | tf_op jit(solution)/shard_map/ppermute | solution.py:1298
  322.7 37.8 %collective-permute-start.6 = (bf16[2,448,800]{2,1,0:T(8,128)(2,1)}, bf16[2,448,800]{2,1,0:T(8,128)(2,1)}, u32[]{:S(2)}, u32[]{:S(2)}) collective-permute-start(bf16[2,448,800]{2,1,0:T(8,128)(2,1)} %dynamic-slice_bitcast_fusion), channel_id=1, source_target_pairs={{0,16},{16,0},{1,17},{17,1},{2,18},{18,2},{3,19},{19,3},{4,20},{20... | collective-permute-start | bytes 4300808 | tf_op jit(solution)/shard_map/ppermute | solution.py:1275
  352.4 64.8 %collective-permute-start.4 = (bf16[448,800]{1,0:T(8,128)(2,1)}, bf16[448,800]{1,0:T(8,128)(2,1)}, u32[]{:S(2)}, u32[]{:S(2)}) collective-permute-start(bf16[448,800]{1,0:T(8,128)(2,1)} %dynamic-slice_bitcast_fusion.3), channel_id=1, source_target_pairs={{0,8},{8,0},{1,9},{9,1},{2,10},{10,2},{3,11},{11,3},{4,12},{12,4},... | collective-permute-start | bytes 2150408 | tf_op jit(solution)/shard_map/ppermute | solution.py:1282
  355.8 4.7 copy-start.9
  362.1 1.2 copy-start.6
  364.2 61.7 %collective-permute-start.7 = (bf16[448,800]{1,0:T(8,128)(2,1)}, bf16[448,800]{1,0:T(8,128)(2,1)}, u32[]{:S(2)}, u32[]{:S(2)}) collective-permute-start(bf16[448,800]{1,0:T(8,128)(2,1)} %dynamic-slice_bitcast_fusion.2), channel_id=1, source_target_pairs={{0,8},{8,0},{1,9},{9,1},{2,10},{10,2},{3,11},{11,3},{4,12},{12,4},... | collective-permute-start | bytes 2150408 | tf_op jit(solution)/shard_map/ppermute | solution.py:1282
  390.8 22.1 %slice-start = ((s8[6422528]{0:T(1024)(128)(4,1)}), s8[2228224]{0:T(1024)(128)(4,1)S(1)}, s32[]{:S(2)}) async-start(s8[6422528]{0:T(1024)(128)(4,1)} %bitcast.132), calls=%async_computation.4 | async-start | bytes 4456448
  404.2 8.7 %slice-start.1 = ((s8[6422528]{0:T(1024)(128)(4,1)}), s8[4194304]{0:T(1024)(128)(4,1)S(1)}, s32[]{:S(2)}) async-start(s8[6422528]{0:T(1024)(128)(4,1)} %bitcast.132), calls=%async_computation.5 | async-start | bytes 8388608
  417.2 10.9 %copy-start.7 = (bf16[2,448,800]{2,1,0:T(8,128)(2,1)S(1)}, bf16[2,448,800]{2,1,0:T(8,128)(2,1)}, u32[]{:S(2)}) copy-start(bf16[2,448,800]{2,1,0:T(8,128)(2,1)} %copy-done.6) | copy-start | bytes 4300804
  542.3 4.8 copy-start.12
  544.7 4.0 copy-start.1
Sparse Core Ops, SparseCore 0:
  117.3 45.3 all-gather.4
  164.8 52.5 all-gather.2
  314.6 86.8 reduce-scatter.1

commit v7 on v6

--- a/solution.py
+++ b/solution.py
@@ -440,11 +440,50 @@
 def group_gather_kernel(own, out, send, recv):
     place = Place(False)
     copies = Copies(send)
-    meet([place.at_z(1 - place.z), {"y": 1 - place.y}, {"c": 1 - place.c}])
-    line = gather_begin(place, own, out, copies, recv)
-    gather_step(place, line, copies, 1)
-    gather_cross(place, out, copies, recv)
-    gather_end(place, out, copies, recv)
+    peer_z, peer_y, peer_c = place.at_z(1 - place.z), {"y": 1 - place.y}, {"c": 1 - place.c}
+    meet([peer_z, peer_y, peer_c])
+    rows = own.shape[0] // 2
+
+    def part(at, half):
+        return out.at[at, pl.ds(half * rows, rows)], recv.at[2 * at + half]
+
+    def give(at, half, peer, src=None):
+        ref, sem = part(at, half)
+        copies.send(ref if src is None else src, ref, sem, peer)
+
+    def got(at, half, peer):
+        ref, sem = part(at, half)
+        copies.arrived(ref, sem, peer)
+
+    for half in range(2):
+        src = own.at[pl.ds(half * rows, rows)]
+        other = own.at[pl.ds((1 - half) * rows, rows)]
+        give(place.slot, half, peer_y, src)
+        give(place.slot, 1 - half, peer_z, other)
+    copies.local(own, out.at[place.slot])
+    for half in range(2):
+        give(place.slot, half, peer_c, own.at[pl.ds(half * rows, rows)])
+    near_y = place.slot_of(place.z, place.c, 1 - place.y)
+    near_z = place.slot_of(1 - place.z, place.c, place.y)
+    across = place.slot_of(1 - place.z, place.c, 1 - place.y)
+    got(near_y, 0, peer_y)
+    give(near_y, 0, peer_z)
+    got(near_z, 1, peer_z)
+    give(near_z, 1, peer_y)
+    give(near_y, 0, peer_c)
+    give(near_z, 1, peer_c)
+    got(near_y, 1, peer_y)
+    give(near_y, 1, peer_c)
+    got(near_z, 0, peer_z)
+    give(near_z, 0, peer_c)
+    got(across, 0, peer_z)
+    give(across, 0, peer_c)
+    got(across, 1, peer_y)
+    give(across, 1, peer_c)
+    for z in range(2):
+        for y in range(2):
+            for half in range(2):
+                got(place.slot_of(z, 1 - place.c, y), half, peer_c)
     copies.finish()
 
 
@@ -454,7 +493,7 @@
         out_shape=jax.ShapeDtypeStruct((8,) + value.shape, value.dtype),
         in_specs=[ANY],
         out_specs=ANY,
-        scratch_shapes=dma_sems(gather_copies(2), 8),
+        scratch_shapes=dma_sems(16, 16),
         compiler_params=comm_params(collective_id),
         name="group_gather",
     )(value)
@@ -488,11 +527,6 @@
     own_half = out_w.at[:, pl.ds(pl.multiple_of(place.y * half, half), half)]
     copies.local(own_half, own_out)
     out_line = Line(place, copies, out_block)
-    out_line.begin(own_half)
-    copies.send(own_half, own_out, own_sem, peer_x)
-    for k in others(group.ctx, 4):
-        copies.send(ffn.at[:, k], ffn_all.at[:, group.ctx], recv_f.at[group.ctx], group.at_ctx(k))
-    copies.local(ffn.at[:, group.ctx], ffn_all.at[:, group.ctx])
 
     def out_over_x(z, here):
         ref, sem = out_block(z)
@@ -500,7 +534,16 @@
 
     for distance in range(1, place.n_z):
         gather_step(place, line, copies, distance)
-        out_line.arrive(distance, out_over_x)
+        if distance == 1:
+            out_line.begin(own_half)
+            copies.send(own_half, own_out, own_sem, peer_x)
+            copies.local(ffn.at[:, group.ctx], ffn_all.at[:, group.ctx])
+        if distance == 2:
+            for k in others(group.ctx, 4):
+                copies.send(ffn.at[:, k], ffn_all.at[:, group.ctx], recv_f.at[group.ctx], group.at_ctx(k))
+        if distance > 1:
+            out_line.arrive(distance - 1, out_over_x)
+    out_line.arrive(place.n_z - 1, out_over_x)
     for k in far_ctx:
         block = blocks_all.at[place.x, k]
         copies.arrived(block, sem_w(place.x, k), place.at_ctx(k))
@@ -674,27 +717,66 @@
     return dma_sems(4 * n_z + more, min(8, 2 * n_z), 2 * n_z, n_z, n_z)
 
 
-def group_scatter_kernel(part, out, held, from_c, from_y, from_z, send, loads, rc, ry, rz):
+def group_scatter_kernel(part, out, held, from_c, over_y, over_z, last, send, loads, rc, ry, rz, rl):
     place = Place(False)
     copies = Copies(send)
-    meet([place.at_z(1 - place.z), {"y": 1 - place.y}, {"c": 1 - place.c}])
-    sums = Scatter(place, part, held, from_c, from_y, from_z, out, copies, loads, rc, ry, rz)
-    sums.begin()
-    sums.over_c_far()
-    sums.over_c_near()
-    sums.over_y()
-    sums.over_z()
+    peer_z, peer_y, peer_c = place.at_z(1 - place.z), {"y": 1 - place.y}, {"c": 1 - place.c}
+    meet([peer_z, peer_y, peer_c])
+    rows = part.shape[1] // 2
+    first, second = slice(0, rows), slice(rows, 2 * rows)
+    own_y, far_y, own_z, far_z = place.y, 1 - place.y, place.z, 1 - place.z
+    order = [(far_z, far_y), (far_z, own_y), (own_z, far_y), (own_z, own_y)]
+    for z, y in order:
+        at = z * 2 + y
+        copies.send(part.at[place.slot_of(z, 1 - place.c, y)], from_c.at[at], rc.at[at], peer_c)
+        copies.local(part.at[place.slot_of(z, place.c, y)], held.at[at], loads.at[at])
+
+    def over_c(z, y):
+        at = z * 2 + y
+        copies.arrived(from_c.at[at], rc.at[at], peer_c)
+        pltpu.make_async_copy(held.at[at], held.at[at], loads.at[at]).wait()
+        from_c[at] = from_c[at] + held[at]
+        return from_c.at[at]
+
+    across = over_c(far_z, far_y)
+    copies.send(across.at[first], over_y, ry.at[0], peer_y)
+    copies.send(across.at[second], over_z, rz.at[0], peer_z)
+    beside_z = over_c(far_z, own_y)
+    copies.send(beside_z.at[second], last.at[0], rl.at[0], peer_z)
+    beside_y = over_c(own_z, far_y)
+    copies.send(beside_y.at[first], last.at[1], rl.at[1], peer_y)
+    copies.arrived(over_y, ry.at[0], peer_y)
+    over_y[...] = over_y[...] + beside_z[first, :]
+    copies.send(over_y, last.at[2], rl.at[2], peer_z)
+    copies.arrived(over_z, rz.at[0], peer_z)
+    over_z[...] = over_z[...] + beside_y[second, :]
+    copies.send(over_z, last.at[3], rl.at[3], peer_y)
+    mine = over_c(own_z, own_y)
+    copies.arrived(last.at[1], rl.at[1], peer_y)
+    copies.arrived(last.at[0], rl.at[0], peer_z)
+    copies.arrived(last.at[2], rl.at[2], peer_z)
+    out[first, :] = mine[first, :].astype(F32) + last[1].astype(F32) + last[2].astype(F32)
+    copies.arrived(last.at[3], rl.at[3], peer_y)
+    out[second, :] = mine[second, :].astype(F32) + last[0].astype(F32) + last[3].astype(F32)
     copies.finish()
 
 
 def group_scatter(part, collective_id):
     block = part.shape[1:]
+    half = (block[0] // 2, block[1])
     return pl.pallas_call(
         group_scatter_kernel,
         out_shape=jax.ShapeDtypeStruct(block, F32),
         in_specs=[ANY],
         out_specs=IN_VMEM,
-        scratch_shapes=scatter_scratch(2, block) + scatter_sems(2),
+        scratch_shapes=[
+            pltpu.VMEM((4,) + block, B16),
+            pltpu.VMEM((4,) + block, B16),
+            pltpu.VMEM(half, B16),
+            pltpu.VMEM(half, B16),
+            pltpu.VMEM((4,) + half, B16),
+        ]
+        + dma_sems(10, 4, 4, 1, 1, 4),
         compiler_params=comm_params(collective_id),
         name="group_scatter",
     )(part)
@@ -891,6 +973,18 @@
     return jnp.concatenate(parts, axis=1)
 
 
+def laid_tall(value, count, rows, tall):
+    zeros = jnp.zeros((tall - rows, value.shape[1]), value.dtype)
+    parts = []
+    for k in range(count):
+        parts += [value[k * rows : (k + 1) * rows], zeros]
+    return jnp.concatenate(parts, axis=0)
+
+
+def laid_short(value, count, rows, tall):
+    return jnp.concatenate([value[k * tall : k * tall + rows] for k in range(count)], axis=0)
+
+
 def laid_narrow(value, count, rows, tall):
     return jnp.concatenate([value[:, k * tall : k * tall + rows] for k in range(count)], axis=1)
 
@@ -900,8 +994,8 @@
     rows, feats = out_w.shape
     n_ctx, tall, cols = blocks.shape
     pair, ff = cols // 3, ffn.shape[3]
-    x_out[...] = laid_wide(x[...].astype(F32), count, rows, tall).astype(B16)
-    grad_out[...] = laid_wide(grad[...].astype(F32), count, rows, tall).astype(B16)
+    x_out[...] = laid_tall(x[...].astype(F32), count, rows, tall).T.astype(B16)
+    grad_out[...] = laid_tall(grad[...].astype(F32), count, rows, tall).T.astype(B16)
     below = jnp.zeros((tall - rows, feats), F32)
     out_out[...] = laid_wide(
         jnp.concatenate([out_w[...].astype(F32), below], axis=0), count, rows, tall
@@ -909,7 +1003,7 @@
     below = jnp.zeros((tall - rows, ff), F32)
     for k in range(4):
         ffn[0, k] = jnp.concatenate([fc[:, k * ff : (k + 1) * ff].astype(F32), below], axis=0).astype(B16)
-        ffn[1, k] = jnp.concatenate([proj[k * ff : (k + 1) * ff, :].astype(F32).T, below], axis=0).astype(B16)
+        ffn[1, k] = jnp.concatenate([proj[:, k * ff : (k + 1) * ff].astype(F32), below], axis=0).astype(B16)
     small = [jnp.concatenate([ref[...].astype(F32), jnp.zeros((1, cols - rows), F32)], axis=1) for ref in singles]
     small.append(jnp.concatenate([qv[...].astype(F32), jnp.zeros((1, cols - 2 * rows), F32)], axis=1))
     if tall - rows > 7:
@@ -936,7 +1030,7 @@
     rows, feats = out_w.shape
     count = feats // rows
     wide = count * tall
-    tokens = x.shape[0]
+    tokens = x.shape[1]
     vmem = pl.BlockSpec(memory_space=pltpu.VMEM)
     return pl.pallas_call(
         functools.partial(prepare_kernel, count),
@@ -1081,11 +1175,12 @@
     out_out[...] = laid_narrow(halves, count, rows, tall)[:rows]
     fc_out[...] = jnp.concatenate([fc[k].astype(F32) for k in range(4)], axis=1)[:rows]
     for k in range(4):
-        proj_out[k * ff : (k + 1) * ff, :] = proj[k].astype(F32).T[:, :rows]
-    block_out[...] = laid_narrow(hidden[...] + mlp[...].astype(F32) + single[5:6, :], count, rows, tall)
+        proj_out[:, k * ff : (k + 1) * ff] = proj[k].astype(F32)[:rows]
+    block = hidden[...] + mlp[...].astype(F32) + single[5:6, :]
+    block_out[...] = laid_short(block.T, count, rows, tall)
     normed, inv = norm_forward(x_ref[...].astype(F32), mask[...], feats)
     grad = dhidden[...] + norm_backward(dnorm[...], normed, inv, single[0:1, :], feats)
-    grad_out[...] = laid_narrow(grad, count, rows, tall)
+    grad_out[...] = laid_short(grad.T, count, rows, tall)
 
 
 def deliver(qkv, out_w, fc, proj, mlp, hidden, dnorm, dhidden, x, single, mask, rows, feats):
@@ -1096,27 +1191,30 @@
             jax.ShapeDtypeStruct((rows, 3 * feats), F32),
             jax.ShapeDtypeStruct((rows, feats), F32),
             jax.ShapeDtypeStruct((rows, 4 * ff), F32),
-            jax.ShapeDtypeStruct((4 * ff, rows), F32),
-            jax.ShapeDtypeStruct((tokens, feats), F32),
-            jax.ShapeDtypeStruct((tokens, feats), F32),
+            jax.ShapeDtypeStruct((rows, 4 * ff), F32),
+            jax.ShapeDtypeStruct((feats, tokens), F32),
+            jax.ShapeDtypeStruct((feats, tokens), F32),
         ),
         compiler_params=pltpu.CompilerParams(vmem_limit_bytes=VMEM_LIMIT),
         name="deliver",
     )(qkv, out_w, fc, proj, mlp, hidden, dnorm, dhidden, x, single, mask[None])
 
 
-def feed_kernel(count, at_ref, *refs):
+def feed_kernel(pairs, singles, at_ref, *refs):
+    count = pairs + 2 * singles
     pieces, refs = refs[:count], refs[count:]
     norm_ref, grad_ref, bias_ref, act_ref, dpre_ref, dnorm_ref, mlp_ref, sum_ref, w_fc, w_proj, sems = refs
 
     @pl.when(pl.program_id(0) == 0)
     def begin():
         rows = pieces[0].shape[1]
+        parts = [(piece.at[0], piece.at[1]) for piece in pieces[:pairs]]
+        parts += list(zip(pieces[pairs : pairs + singles], pieces[pairs + singles :]))
         copies = []
-        for i, piece in enumerate(pieces):
+        for i, (fc, proj) in enumerate(parts):
             to = pl.ds(pl.multiple_of(at_ref[i], 16), rows)
-            copies.append(pltpu.make_async_copy(piece.at[0], w_fc.at[to, :], sems.at[2 * i]))
-            copies.append(pltpu.make_async_copy(piece.at[1], w_proj.at[to, :], sems.at[2 * i + 1]))
+            copies.append(pltpu.make_async_copy(fc, w_fc.at[to, :], sems.at[2 * i]))
+            copies.append(pltpu.make_async_copy(proj, w_proj.at[to, :], sems.at[2 * i + 1]))
         for copy in copies:
             copy.start()
         for copy in copies:
@@ -1135,7 +1233,8 @@
     mlp_ref[...] = dot(activation, w_proj[...], 1, 1).astype(B16)
 
 
-def feed(pieces, places, norm, grad, bias):
+def feed(pairs, fcs, projs, places, norm, grad, bias):
+    pieces = pairs + fcs + projs
     total, wide = norm.shape
     ff = bias.shape[0]
     step = 256
@@ -1143,7 +1242,7 @@
     hidden = pl.BlockSpec((step, ff), lambda i: (i, 0))
     single = pl.BlockSpec((1, ff), lambda i: (0, 0))
     return pl.pallas_call(
-        functools.partial(feed_kernel, len(pieces)),
+        functools.partial(feed_kernel, len(pairs), len(fcs)),
         grid=(total // step,),
         in_specs=[pl.BlockSpec(memory_space=pltpu.SMEM)] + [ANY] * len(pieces) + [tokens, tokens, single],
         out_specs=(hidden, hidden, tokens, tokens, single),
@@ -1209,14 +1308,14 @@
 
     singles = (first_gain, first_shift, out_bias, second_gain, second_shift, proj_bias)
     own_input, grad_own, packed, ffn_blocks, w_out = prepare(
-        y_at.astype(jnp.int32)[None], block_input[0], out_grad[0], qkv_weight, fc_weight, proj_weight, out_weight,
+        y_at.astype(jnp.int32)[None], block_input[0].T, out_grad[0].T, qkv_weight, fc_weight, proj_weight.T, out_weight,
         singles, qv_bias, n_ctx, tall, pair,
     )
     all_input, packed, ffn_blocks, w_out = opening(
         own_input, packed, ffn_blocks, w_out
     )
     ffn_blocks = ffn_blocks.reshape(2, 4 * tall, ff_own)
-    along_h = [lax.ppermute(ffn_blocks, "h", shift_perm(n_h, step)) for step in range(1, n_h)]
+    fc_h = [lax.ppermute(ffn_blocks[0], "h", shift_perm(n_h, step)) for step in range(1, n_h)]
     along_x = lax.ppermute(ffn_blocks, "x", shift_perm(n_x, 1))
     grad_late, all_input = after(grad_own, all_input)
     grad_all = gather(grad_late, FFG)
@@ -1243,6 +1342,9 @@
     )
     bias_out, gain_two, shift_two = singles[2], singles[3], singles[4]
     heads_out, lse = attend(inv, low, qkv, start3, slot_len, head)
+    fc_h, proj_late, heads_out = after((fc_h, ffn_blocks[1]), heads_out, True)
+    fc_xh = [lax.ppermute(value, "x", shift_perm(n_x, 1)) for value in fc_h]
+    proj_h = [lax.ppermute(proj_late, "h", shift_perm(n_h, step)) for step in range(1, n_h)]
     attention = widened(to_tokens(heads_out.reshape(n_slot, slot_len, pair))[:, :feats])
     by_core = attention.reshape(slot_len, n_shard // 2, 2, tall)
     by_core = [by_core[:, :, part].reshape(slot_len, wide // 2) for part in range(2)]
@@ -1251,16 +1353,21 @@
     normed_two, inv_two = norm_forward(hidden, mask, feats)
     norm_two = (normed_two * gain_two + shift_two).astype(B16)
     grad_wide = grad_own.astype(F32)
-    along_h, norm_two = after(along_h, norm_two)
-    along_both = [lax.ppermute(value, "x", shift_perm(n_x, 1)) for value in along_h]
+    proj_h, norm_two = after(proj_h, norm_two)
+    proj_xh = [lax.ppermute(value, "x", shift_perm(n_x, 1)) for value in proj_h]
     norm_all = group_gather(norm_two, 6).reshape(-1, wide)
-    pieces, places = [ffn_blocks, along_x], [(x_at, h_at), (1 - x_at, h_at)]
+    places = [(x_at, h_at), (1 - x_at, h_at)]
     for step in range(1, n_h):
         h_from = lax.rem(h_at + n_h - step, n_h)
-        pieces += [along_h[step - 1], along_both[step - 1]]
         places += [(x_at, h_from), (1 - x_at, h_from)]
+
+    def mixed(one, two):
+        return [value for both in zip(one, two) for value in both]
+
     places = jnp.stack([(x * n_h + h) * (4 * tall) for x, h in places]).astype(jnp.int32)
-    activation, dpreact_b, dnorm_part, mlp_part, dpreact_sum = feed(pieces, places, norm_all, grad_all, b_fc)
+    activation, dpreact_b, dnorm_part, mlp_part, dpreact_sum = feed(
+        [ffn_blocks, along_x], mixed(fc_h, fc_xh), mixed(proj_h, proj_xh), places, norm_all, grad_all, b_fc
+    )
 
     def pick(value, at):
         return lax.dynamic_index_in_dim(value, at, 0, False)
@@ -1296,7 +1403,7 @@
     c_at = lax.axis_index("c")
     out_give = dot(jnp.where(c_at == 0, by_core[1], by_core[0]), dhidden_b, 0, 0).astype(B16)
     out_give = lax.ppermute(out_give, "c", shift_perm(2, 1))
-    out_keep = dot(jnp.where(c_at == 0, by_core[0], by_core[1]), dhidden_b, 0, 0)
+    out_keep = dot(jnp.where(c_at == 0, by_core[0], by_core[1]), dhidden_b, 0, 0).astype(B16)
     grad_y = [dhidden_b[:, : wide // 2], dhidden_b[:, wide // 2 :]]
     datt = [dot(grad_y[0], w_out[c, 0], 1, 1) + dot(grad_y[1], w_out[c, 1], 1, 1) for c in range(2)]
     datt = [value.astype(B16).reshape(slot_len, -1, 1, tall) for value in datt]
@@ -1304,7 +1411,7 @@
     dattention = jnp.pad(dattention, ((0, 0), (0, padded - feats)))
     dattention = to_heads(dattention, n_slot).reshape(n_slot * slot_len, pair)
     out_give, fc_x, dattention = after((out_give, fc_x), dattention, True)
-    out_part = (out_keep + out_give).astype(B16).reshape(n_shard // 2, tall, wide)
+    out_part = (out_keep + out_give).reshape(n_shard // 2, tall, wide)
     fc_line = pick(fc_part, x_at) + fc_x
     fc_h = over_h(fc_line)
     dqkv = attend_back(inv, low, qkv, heads_out, dattention, lse, start3, slot_len, head)
@@ -1335,8 +1442,8 @@
         return owned[index, :rows]
 
     return (
-        block_output[None],
-        input_grad[None],
+        block_output.T[None],
+        input_grad.T[None],
         qkv_grad,
         qv_grad,
         out_grad_w,
@@ -1347,7 +1454,7 @@
         own(2),
         fc_grad,
         fc_bias_grad,
-        proj_grad,
+        proj_grad.T,
         own(3),
     )
 

time: 560 us -> 542 us (0.968); the launches traced: 555 us -> 531 us
  Pallas kernels: 422 us -> 377 us
  waiting for transfers between devices: 16.2 us -> 45.1 us
  local copies, waits for them, and re-layouts: 32.9 us -> 22.9 us
  starting transfers between devices: 8.16 us -> 13.8 us
    pallas_call x1, Pallas kernels: 39.3 us -> 14.4 us  [to_tokens(): pl.pallas_call(to_tokens_kernel, out_shape=jax.ShapeDtypeStruct((tokens,...]
    ppermute x2 -> x4, waiting for transfers between devices: 5.57 us -> 24.3 us  [the longest x1 24.3 us: on_device(): lax.ppermute(proj_late, 'h', shift_perm(n_h, step))]
    unnamed x49, local copies, waits for them, and re-layouts: 16.7 us -> 6.76 us
    pallas_call x1, Pallas kernels: 30 us -> 20.2 us  [group_gather(): pl.pallas_call(group_gather_kernel, out_shape=jax.ShapeDtypeStruct((8,) +...]
    pallas_call x1, Pallas kernels: 30.1 us -> 21.4 us  [group_scatter(): pl.pallas_call(group_scatter_kernel, out_shape=jax.ShapeDtypeStruct(block...]
    ppermute x1, waiting for transfers between devices: 0.15 us -> 8.24 us  [on_device(): proj_x = lax.ppermute(pick(proj_part, 1 - x_at), 'x', shift_perm(n_x, 1))]
    ppermute x2 -> x4, starting transfers between devices: 0.61 us -> 6.47 us  [the longest x1 3.47 us: on_device(): lax.ppermute(proj_late, 'h', shift_perm(n_h, step))]
  transfers between devices with their start and end apart: 11 -> 13, of which waited for: 4 -> 4; matrix products, arithmetic and copies ran while one was open for 12% -> 12% of each run, Pallas kernels for 52% -> 46%
where the time goes in v7:
time: 542 us; the launch traced here: 531 us
  Pallas kernels  377 us (70%)
  waiting for transfers between devices  45.1 us (8%)
  matrix products  40.1 us (7%)
  local copies, waits for them, and re-layouts  22.9 us (4%)
  other arithmetic  17.4 us (3%)
  between operations  14.8 us (3%)
  starting transfers between devices  13.8 us (3%)
    pallas_call x1, Pallas kernels, closing(): pl.pallas_call(closing_kernel, out_shape=(jax.ShapeDtypeStruct(block, F32...  99.8 us
    pallas_call x1, Pallas kernels, opening(): pl.pallas_call(opening_kernel, out_shape=(jax.ShapeDtypeStruct((2 * n_ctx...  99.5 us
    dot_general x13, matrix products, dot(): lax.dot_general(left, right, (((left_dim,), (right_dim,)), ((), ())), pre...  40.1 us
    pallas_call x1, Pallas kernels, attend_back(): pl.pallas_call(functools.partial(attend_back_kernel, slot_len, head), out...  24.4 us
    ppermute x1, waiting for transfers between devices, on_device(): lax.ppermute(proj_late, 'h', shift_perm(n_h, step))  24.3 us
    pallas_call x1, Pallas kernels, attend(): pl.pallas_call(functools.partial(attend_kernel, slot_len, head), out_shap...  23.2 us
    pallas_call x1, Pallas kernels, feed(): pl.pallas_call(functools.partial(feed_kernel, len(pairs), len(fcs)), grid...  21.9 us
    pallas_call x1, Pallas kernels, group_scatter(): pl.pallas_call(group_scatter_kernel, out_shape=jax.ShapeDtypeStruct(block...  21.4 us
  transfers between devices with their start and end apart: 13, of which 4 were waited for; matrix products, arithmetic and copies ran while one was open for 12% of the time, Pallas kernels for 46%

profile of v7, /device:TPU:0, one launch (start us, length us, event | category | flops | bytes accessed | tf_op | source)
XLA Modules:
  0.0 531.4 jit_solution(10239982118959565103)
XLA Ops:
  8.5 4.8 prepare.1
  13.2 99.5 %opening.1 = (bf16[16,128,1792]{2,1,0:T(8,128)(2,1)}, bf16[2,8,112,384]{3,2,1,0:T(8,128)(2,1)}, bf16[2,4,112,800]{3,2,1,0:T(8,128)(2,1)}, bf16[8,112,896]{2,1,0:T(8,128)(2,1)}) custom-call(bf16[128,1792]{1,0:T(8,128)(2,1)} %get-tuple-element.74.own.x_ref, bf16[8,112,384]{2,1,0:T(8,128)(2,1)} %get-tuple-element.75.blocks, ...), custom_call_target="tpu_custom_call" | custom-call | tf_op jit(solution)/shard_map/opening/pallas_call | solution.py:567
  116.5 13.6 %project.1 = (bf16[2048,1792]{1,0:T(8,128)(2,1)}, bf16[2048,384]{1,0:T(8,128)(2,1)}, f32[8,1792]{1,0:T(8,128)}) custom-call(s32[1]{0:T(128)} %bitcast.25.at_ref, bf16[2048,1792]{1,0:T(8,128)(2,1)} %bitcast.144, bf16[16,112,384]{2,1,0:T(8,128)(2,1)} %bitcast.149, f32[1,1792]{1,0:T(1,128)} %constant.127.mask_ref.mask, bf16[1792,384]{1,0:T(8,128)(2,1)} %bitcast.150), custom_call_target="tpu_custom_call" | custom-call | tf_op jit(solution)/shard_map/project/pallas_call | solution.py:1092
  131.1 23.2 %attend.1 = (bf16[2048,128]{1,0:T(8,128)(2,1)}, f32[8,2,256]{2,1,0:T(2,128)}) custom-call(s32[16]{0:T(128)} %copy-done.20, s32[8]{0:T(128)} %and_select_fusion.low_ref, bf16[2048,384]{1,0:T(8,128)(2,1)} %get-tuple-element.83.qkv_ref, s32[8,1,256]{2,1,0:T(1,128)} %bitcast.192), custom_call_target="tpu_custom_call" | custom-call | tf_op jit(solution)/shard_map/attend/pallas_call | solution.py:157
  156.2 14.4 %to_tokens.1 = bf16[128,2048]{1,0:T(8,128)(2,1)} custom-call(bf16[16,128,128]{2,1,0:T(8,128)(2,1)} %bitcast.178), custom_call_target="tpu_custom_call" | custom-call | tf_op jit(solution)/shard_map/to_tokens/pallas_call | solution.py:603
  171.9 3.5 collective-permute-start.3
  186.7 24.3 %collective-permute-done.3.refs_4_ = bf16[448,800]{1,0:T(8,128)(2,1)} collective-permute-done((bf16[448,800]{1,0:T(8,128)(2,1)}, bf16[448,800]{1,0:T(8,128)(2,1)}, u32[]{:S(2)}, u32[]{:S(2)}) %collective-permute-start.3) | collective-permute-done | bytes 716832 | tf_op jit(solution)/shard_map/ppermute | solution.py:1347
  214.4 20.2 %group_gather.1 = bf16[8,128,1792]{2,1,0:T(8,128)(2,1)} custom-call(bf16[128,1792]{1,0:T(8,128)(2,1)} %add_convert_fusion.own), custom_call_target="tpu_custom_call" | custom-call | tf_op jit(solution)/shard_map/group_gather/pallas_call | solution.py:491
  234.7 21.9 %feed.1 = (bf16[1024,800]{1,0:T(8,128)(2,1)}, bf16[1024,800]{1,0:T(8,128)(2,1)}, bf16[1024,1792]{1,0:T(8,128)(2,1)}, bf16[1024,1792]{1,0:T(8,128)(2,1)}, f32[1,800]{1,0:T(1,128)}) custom-call(s32[4]{0:T(128)} %pad_add_fusion.at_ref, bf16[2,448,800]{2,1,0:T(8,128)(2,1)} %bitcast.153, bf16[2,448,800]{2,1,0:T(8,128)(2,1)} %collective-permute-done.refs_1_, ...), custom_call_target="tpu_custom_call" | custom-call | tf_op jit(solution)/shard_map/feed/pallas_call | solution.py:1244
  256.6 6.8 %convolution_convert_fusion.3 = bf16[1792,800]{1,0:T(8,128)(2,1)S(1)} fusion(bf16[1024,1792]{1,0:T(8,128)(2,1)} %all-gather.3.cloned.1.call-done.refs_7_, bf16[1024,800]{1,0:T(8,128)(2,1)} %get-tuple-element.92), kind=kOutput, calls=%fused_computation.4 | convolution fusion | flops 2937446400 | bytes 8175616 | tf_op jit(solution)/shard_map/dot_general | solution.py:59
  266.0 5.5 %convolution_convert_fusion.2 = bf16[1792,800]{1,0:T(8,128)(2,1)} fusion(bf16[1024,1792]{1,0:T(8,128)(2,1)S(1)} %bitcast.147, bf16[1024,800]{1,0:T(8,128)(2,1)S(1)} %copy-done.21), kind=kOutput, calls=%fused_computation.3 | convolution fusion | flops 2937446400 | bytes 8175616 | tf_op jit(solution)/shard_map/dot_general | solution.py:59
  271.5 21.4 %group_scatter.1 = f32[128,1792]{1,0:T(8,128)} custom-call(bf16[8,128,1792]{2,1,0:T(8,128)(2,1)} %bitcast.171), custom_call_target="tpu_custom_call" | custom-call | tf_op jit(solution)/shard_map/group_scatter/pallas_call | solution.py:767
  292.9 8.2 %collective-permute-done.5 = bf16[2,448,800]{2,1,0:T(8,128)(2,1)} collective-permute-done((bf16[2,448,800]{2,1,0:T(8,128)(2,1)S(1)}, bf16[2,448,800]{2,1,0:T(8,128)(2,1)}, u32[]{:S(2)}, u32[]{:S(2)}) %collective-permute-start.5) | collective-permute-done | bytes 1433632 | tf_op jit(solution)/shard_map/ppermute | solution.py:1380
  303.5 2.7 convolution_convert_fusion.1
  306.2 2.8 dynamic-slice_bitcast_fusion
  309.4 2.0 fusion.4
  311.4 2.0 fusion.15
  313.5 2.0 fusion.2
  315.7 2.0 fusion.14
  319.3 13.9 %to_heads.1 = bf16[16,128,128]{2,1,0:T(8,128)(2,1)} custom-call(bf16[128,2048]{1,0:T(8,128)(2,1)} %pad.9.src), custom_call_target="tpu_custom_call" | custom-call | tf_op jit(solution)/shard_map/to_heads/pallas_call | solution.py:634
  333.2 2.1 bitcast_add_fusion.1
  336.3 2.8 collective-permute-start.6
  340.7 6.1 %collective-permute-done.8 = bf16[2,448,800]{2,1,0:T(8,128)(2,1)} collective-permute-done((bf16[2,448,800]{2,1,0:T(8,128)(2,1)}, bf16[2,448,800]{2,1,0:T(8,128)(2,1)}, u32[]{:S(2)}, u32[]{:S(2)}) %collective-permute-start.8) | collective-permute-done | bytes 1433632 | tf_op jit(solution)/shard_map/ppermute | solution.py:1382
  350.5 2.7 collective-permute-start.9
  353.2 24.4 %attend_back.1.grad_ref = f32[2048,384]{1,0:T(8,128)} custom-call(s32[16]{0:T(128)} %copy-done.20, s32[8]{0:T(128)} %and_select_fusion.low_ref, bf16[2048,384]{1,0:T(8,128)(2,1)} %get-tuple-element.83.qkv_ref, bf16[2048,128]{1,0:T(8,128)(2,1)} %get-tuple-element.87.out_ref, bf16[2048,128]{1,0:T(8,128)(2,1)} %bitcast.179, ...), custom_call_target="tpu_custom_call" | custom-call | tf_op jit(solution)/shard_map/attend_back/pallas_call | solution.py:254
  377.5 13.3 %project_back.1 = (bf16[2048,1792]{1,0:T(8,128)(2,1)}, bf16[2048,384]{1,0:T(8,128)(2,1)}, f32[1,1792]{1,0:T(1,128)}, f32[1,1792]{1,0:T(1,128)}, f32[1,384]{1,0:T(1,128)}) custom-call(bf16[2048,1792]{1,0:T(8,128)(2,1)} %bitcast.145, f32[2048,384]{1,0:T(8,128)} %attend_back.1.grad_ref, f32[1,1792]{1,0:T(1,128)} %constant.127.mask_ref.mask, ...), custom_call_target="tpu_custom_call" | custom-call | tf_op jit(solution)/shard_map/project_back/pallas_call | solution.py:1145
  390.8 4.7 add.178
  395.5 8.4 %convolution_convert_fusion.4 = bf16[1792,384]{1,0:T(8,128)(2,1)} fusion(bf16[2048,1792]{1,0:T(8,128)(2,1)} %get-tuple-element.106, bf16[2048,384]{1,0:T(8,128)(2,1)S(1)} %copy-done.22), kind=kOutput, calls=%fused_computation.5 | convolution fusion | flops 2819260416 | bytes 10289152 | tf_op jit(solution)/shard_map/dot_general | solution.py:59
  404.0 5.8 %collective-permute-done.9 = bf16[448,800]{1,0:T(8,128)(2,1)S(1)} collective-permute-done((bf16[448,800]{1,0:T(8,128)(2,1)}, bf16[448,800]{1,0:T(8,128)(2,1)S(1)}, u32[]{:S(2)}, u32[]{:S(2)}) %collective-permute-start.9) | collective-permute-done | bytes 716832 | tf_op jit(solution)/shard_map/ppermute | solution.py:1389
  409.7 2.2 fusion
  413.0 99.8 %closing.1 = (f32[128,1792]{1,0:T(8,128)}, bf16[2,8,112,384]{3,2,1,0:T(8,128)(2,1)}, bf16[2,112,896]{2,1,0:T(8,128)(2,1)}, bf16[4,112,800]{2,1,0:T(8,128)(2,1)},...) custom-call(bf16[16,128,1792]{2,1,0:T(8,128)(2,1)} %bitcast.152, ...), custom_call_target="tpu_custom_call" | custom-call | tf_op jit(solution)/shard_map/closing/pallas_call | solution.py:938
  517.2 7.2 %deliver.1 = (f32[100,4800]{1,0:T(8,128)}, f32[100,1600]{1,0:T(8,128)}, f32[100,3200]{1,0:T(8,128)}, f32[100,3200]{1,0:T(8,128)}, f32[1600,128]{1,0:T(8,128)}, /*index=5*/f32[1600,128]{1,0:T(8,128)}) custom-call(bf16[2,8,112,384]{3,2,1,0:T(8,128)(2,1)} %get-tuple-element.115.qkv, bf16[2,112,896]{2,1,0:T(8,128)(2,1)} %get-tuple-element.116.out_w, ...), custom_call_target="tpu_custom_call" | custom-call | tf_op jit(solution)/shard_map/deliver/pallas_call | solution.py:1188
  (132 shorter events, 42.6 us)
Async XLA Ops:
  7.2 108.7 %copy-start = (s32[1,2048]{1,0:T(1,128)S(1)}, s32[1,2048]{1,0:T(1,128)}, u32[]{:S(2)}) copy-start(s32[1,2048]{1,0:T(1,128)} %param.18) | copy-start | bytes 24580
  7.2 169.8 %all-gather.5.cloned.1.call-start = ((), (), s32[]{:S(2)}) async-start(), calls=%async_computation.2 | async-start | bytes 8028160 | tf_op jit(solution)/shard_map/all_gather | solution.py:1322
  112.7 1.4 copy-start.6
  112.8 121.9 %all-gather.3.cloned.1.call-start = ((), (), s32[]{:S(2)}) async-start(), calls=%async_computation.1 | async-start | bytes 4128768 | tf_op jit(solution)/shard_map/all_gather | solution.py:1292
  112.8 2.9 copy-start.23
  113.5 403.6 %reduce-scatter.2.cloned.1.call-start = ((), (), s32[]{:S(2)}) async-start(), calls=%async_computation.3 | async-start | bytes 4128768 | tf_op jit(solution)/shard_map/reduce_scatter | solution.py:1400
  115.2 40.1 %collective-permute-start.1 = (bf16[448,800]{1,0:T(8,128)(2,1)S(1)}, bf16[448,800]{1,0:T(8,128)(2,1)S(1)}, u32[]{:S(2)}, u32[]{:S(2)}) collective-permute-start(bf16[448,800]{1,0:T(8,128)(2,1)S(1)} %bitcast.187), channel_id=1, source_target_pairs={{0,8},{8,0},{1,9},{9,1},{2,10},{10,2},{3,11},{11,3},{4,12},{12,4},... | collective-permute-start | bytes 2150408 | tf_op jit(solution)/shard_map/ppermute | solution.py:1318
  115.2 119.4 %collective-permute-start = (bf16[2,448,800]{2,1,0:T(8,128)(2,1)S(1)}, bf16[2,448,800]{2,1,0:T(8,128)(2,1)}, u32[]{:S(2)}, u32[]{:S(2)}) collective-permute-start(bf16[2,448,800]{2,1,0:T(8,128)(2,1)S(1)} %bitcast.154), channel_id=1, source_target_pairs={{0,16},{16,0},{1,17},{17,1},{2,18},{18,2},{3,19},{19,3},{4,20},{20... | collective-permute-start | bytes 4300808 | tf_op jit(solution)/shard_map/ppermute | solution.py:1319
  115.8 14.3 %copy-start.20 = (s32[16]{0:T(128)}, s32[16]{0:T(128)S(1)}, u32[]{:S(2)}) copy-start(s32[16]{0:T(128)S(1)} %select_reduce_fusion.1.inv_ref) | copy-start | bytes 196
  171.9 39.1 %collective-permute-start.3 = (bf16[448,800]{1,0:T(8,128)(2,1)}, bf16[448,800]{1,0:T(8,128)(2,1)}, u32[]{:S(2)}, u32[]{:S(2)}) collective-permute-start(bf16[448,800]{1,0:T(8,128)(2,1)} %bitcast.186), channel_id=1, source_target_pairs={{0,8},{8,0},{1,9},{9,1},{2,10},{10,2},{3,11},{11,3},{4,12},{12,4},... | collective-permute-start | bytes 2150408 | tf_op jit(solution)/shard_map/ppermute | solution.py:1347
  175.4 59.2 %collective-permute-start.2 = (bf16[448,800]{1,0:T(8,128)(2,1)}, bf16[448,800]{1,0:T(8,128)(2,1)}, u32[]{:S(2)}, u32[]{:S(2)}) collective-permute-start(bf16[448,800]{1,0:T(8,128)(2,1)} %copy-done.17), channel_id=1, source_target_pairs={{0,16},{16,0},{1,17},{17,1},{2,18},{18,2},{3,19},{19,3},{4,20},{20... | collective-permute-start | bytes 2150408 | tf_op jit(solution)/shard_map/ppermute | solution.py:1346
  182.7 2.0 copy-start.13
  184.9 117.8 %copy-start.2 = (f32[128,1792]{1,0:T(8,128)}, f32[128,1792]{1,0:T(8,128)S(1)}, u32[]{:S(2)}) copy-start(f32[128,1792]{1,0:T(8,128)S(1)} %get-tuple-element.142.hidden) | copy-start | bytes 2752516
  211.0 23.7 %collective-permute-start.4 = (bf16[448,800]{1,0:T(8,128)(2,1)}, bf16[448,800]{1,0:T(8,128)(2,1)}, u32[]{:S(2)}, u32[]{:S(2)}) collective-permute-start(bf16[448,800]{1,0:T(8,128)(2,1)} %collective-permute-done.3.refs_4_), channel_id=1, source_target_pairs={{0,16},{16,0},{1,17},{17,1},{2,18},{18,2},{3,19},{19,3},{4,20},{20... | collective-permute-start | bytes 2150408 | tf_op jit(solution)/shard_map/ppermute | solution.py:1357
  256.6 7.5 %copy-start.3 = (bf16[8,128,1792]{2,1,0:T(8,128)(2,1)S(1)}, bf16[8,128,1792]{2,1,0:T(8,128)(2,1)}, u32[]{:S(2)}) copy-start(bf16[8,128,1792]{2,1,0:T(8,128)(2,1)} %group_gather.1) | copy-start | bytes 11010052
  263.4 8.1 %copy-start.15 = (bf16[1792,800]{1,0:T(8,128)(2,1)}, bf16[1792,800]{1,0:T(8,128)(2,1)S(1)}, u32[]{:S(2)}) copy-start(bf16[1792,800]{1,0:T(8,128)(2,1)S(1)} %convolution_convert_fusion.3) | copy-start | bytes 8601604
  263.4 2.7 copy-start.21
  263.5 37.6 %collective-permute-start.5 = (bf16[2,448,800]{2,1,0:T(8,128)(2,1)S(1)}, bf16[2,448,800]{2,1,0:T(8,128)(2,1)}, u32[]{:S(2)}, u32[]{:S(2)}) collective-permute-start(bf16[2,448,800]{2,1,0:T(8,128)(2,1)S(1)} %dynamic-slice_bitcast_fusion.1), channel_id=1, source_target_pairs={{0,16},{16,0},{1,17},{17,1},{2,18},{18,2},{3,19},{19,3},{4,20},{20... | collective-permute-start | bytes 4300808 | tf_op jit(solution)/shard_map/ppermute | solution.py:1380
  301.2 1.6 copy-start.16
  303.4 2.8 copy-start.4
  303.5 12.2 %copy-start.11 = (bf16[128,1792]{1,0:T(8,128)(2,1)}, bf16[128,1792]{1,0:T(8,128)(2,1)S(1)}, u32[]{:S(2)}) copy-start(bf16[128,1792]{1,0:T(8,128)(2,1)S(1)} %convert_element_type.71) | copy-start | bytes 1376260
  306.2 40.6 %collective-permute-start.7 = (bf16[896,1792]{1,0:T(8,128)(2,1)}, bf16[896,1792]{1,0:T(8,128)(2,1)}, u32[]{:S(2)}, u32[]{:S(2)}) collective-permute-start(bf16[896,1792]{1,0:T(8,128)(2,1)} %convolution_convert_fusion.1), channel_id=1, source_target_pairs={{0,2},{2,0},{1,3},{3,1},{4,6},{6,4},{5,7},{7,5},{8,10},{10,8},{9,1... | collective-permute-start | bytes 9633800 | tf_op jit(solution)/shard_map/ppermute | solution.py:1405
  309.0 37.8 %collective-permute-start.8 = (bf16[2,448,800]{2,1,0:T(8,128)(2,1)}, bf16[2,448,800]{2,1,0:T(8,128)(2,1)}, u32[]{:S(2)}, u32[]{:S(2)}) collective-permute-start(bf16[2,448,800]{2,1,0:T(8,128)(2,1)} %dynamic-slice_bitcast_fusion), channel_id=1, source_target_pairs={{0,16},{16,0},{1,17},{17,1},{2,18},{18,2},{3,19},{19,3},{4,20},{20... | collective-permute-start | bytes 4300808 | tf_op jit(solution)/shard_map/ppermute | solution.py:1382
  335.3 5.4 %copy-start.7 = (bf16[2,448,800]{2,1,0:T(8,128)(2,1)}, bf16[2,448,800]{2,1,0:T(8,128)(2,1)S(1)}, u32[]{:S(2)}) copy-start(bf16[2,448,800]{2,1,0:T(8,128)(2,1)S(1)} %bitcast_add_fusion.1) | copy-start | bytes 4300804
  335.3 4.4 copy-start.12
  336.3 67.7 %collective-permute-start.6 = (bf16[448,800]{1,0:T(8,128)(2,1)}, bf16[448,800]{1,0:T(8,128)(2,1)}, u32[]{:S(2)}, u32[]{:S(2)}) collective-permute-start(bf16[448,800]{1,0:T(8,128)(2,1)} %dynamic-slice_bitcast_fusion.3), channel_id=1, source_target_pairs={{0,8},{8,0},{1,9},{9,1},{2,10},{10,2},{3,11},{11,3},{4,12},{12,4},... | collective-permute-start | bytes 2150408 | tf_op jit(solution)/shard_map/ppermute | solution.py:1389
  339.7 7.1 %copy-start.14 = (bf16[1792,800]{1,0:T(8,128)(2,1)S(1)}, bf16[1792,800]{1,0:T(8,128)(2,1)}, u32[]{:S(2)}) copy-start(bf16[1792,800]{1,0:T(8,128)(2,1)} %convolution_convert_fusion.2) | copy-start | bytes 8601604
  350.5 59.2 %collective-permute-start.9 = (bf16[448,800]{1,0:T(8,128)(2,1)}, bf16[448,800]{1,0:T(8,128)(2,1)S(1)}, u32[]{:S(2)}, u32[]{:S(2)}) collective-permute-start(bf16[448,800]{1,0:T(8,128)(2,1)} %dynamic-slice_bitcast_fusion.2), channel_id=1, source_target_pairs={{0,8},{8,0},{1,9},{9,1},{2,10},{10,2},{3,11},{11,3},{4,12},{12,4},... | collective-permute-start | bytes 2150408 | tf_op jit(solution)/shard_map/ppermute | solution.py:1389
  390.8 4.8 copy-start.22
  395.5 14.2 %copy-start.8 = (bf16[2,448,800]{2,1,0:T(8,128)(2,1)S(1)}, bf16[2,448,800]{2,1,0:T(8,128)(2,1)}, u32[]{:S(2)}) copy-start(bf16[2,448,800]{2,1,0:T(8,128)(2,1)} %copy-done.7) | copy-start | bytes 4300804
  404.0 8.0 %copy-start.10 = (bf16[2,448,800]{2,1,0:T(8,128)(2,1)S(1)}, bf16[2,448,800]{2,1,0:T(8,128)(2,1)}, u32[]{:S(2)}) copy-start(bf16[2,448,800]{2,1,0:T(8,128)(2,1)} %copy-done.9) | copy-start | bytes 4300804
  517.1 7.3 %copy-start.1 = (s32[1,2048]{1,0:T(1,128)S(1)}, s32[1,2048]{1,0:T(1,128)}, u32[]{:S(2)}) copy-start(s32[1,2048]{1,0:T(1,128)} %param.18) | copy-start | bytes 24580
  (5 other events, 4.7 us)
Sparse Core Ops, SparseCore 0:
  112.9 46.1 all-gather.4
  161.2 51.3 all-gather.2
  301.3 84.5 reduce-scatter.1

commit v8 on v7

--- a/solution.py
+++ b/solution.py
@@ -87,13 +87,23 @@
     return pl.ds(pl.multiple_of(block * BLK, BLK), BLK)
 
 
-def mask_of(start_row, key_block, query_block, diagonal):
-    key_at = key_block * BLK + lax.broadcasted_iota(jnp.int32, (BLK, BLK), 0)
+def mask_of(start_row, first, query_block, diagonal):
+    key_at = first * BLK + lax.broadcasted_iota(jnp.int32, (2 * BLK, BLK), 0)
     allowed = key_at >= start_row
     if diagonal:
-        query_at = query_block * BLK + lax.broadcasted_iota(jnp.int32, (BLK, BLK), 1)
+        query_at = query_block * BLK + lax.broadcasted_iota(jnp.int32, (2 * BLK, BLK), 1)
         allowed = jnp.logical_and(allowed, key_at <= query_at)
     return allowed
+
+
+def two_rows(first):
+    return block_rows(jnp.maximum(first, 0)), block_rows(first + 1)
+
+
+def over_pairs(low, block, step, state):
+    earlier = (block - low) // 2
+    state = lax.fori_loop(0, earlier, lambda t, s: step(block - 1 - 2 * (earlier - t), s, False), state)
+    return step(block - 1, state, True)
 
 
 def attend_kernel(slot_len, head, inv_ref, low_ref, qkv_ref, start_ref, out_ref, lse_ref, q_s, k_s, vt_s):
@@ -114,10 +124,11 @@
         queries = q_s[block_rows(block), :]
         start_row = start_ref[block]
 
-        def step(key_block, state, diagonal):
-            allowed = mask_of(start_row, key_block, block, diagonal)
-            keys = k_s[block_rows(key_block), :]
-            values = vt_s[:, block_rows(key_block)]
+        def step(first, state, diagonal):
+            allowed = mask_of(start_row, first, block, diagonal)
+            rows = two_rows(first)
+            keys = jnp.concatenate([k_s[r, :] for r in rows], axis=0)
+            values = jnp.concatenate([vt_s[:, r] for r in rows], axis=1)
             fresh = []
             for part in range(2):
                 old_max, old_sum, old_acc = state[part]
@@ -140,8 +151,7 @@
             )
             for part in range(2)
         )
-        state = lax.fori_loop(low_ref[block], block, lambda j, s: step(j, s, False), first)
-        state = step(block, state, True)
+        state = over_pairs(low_ref[block], block, step, first)
         lse_ref[block] = jnp.concatenate([s[0] + jnp.log(s[1]) for s in state], axis=0)
         result = jnp.concatenate([s[2] / s[1] for s in state], axis=0)
         unsort_block(inv_ref, out_ref, result.T, block, slot_len)
@@ -201,12 +211,12 @@
         prod = (grads.astype(F32) * o_s[block_rows(block), :].astype(F32)).T
         delta = [jnp.sum(prod[part * head : (part + 1) * head], axis=0, keepdims=True) for part in range(2)]
 
-        def step(key_block, state, diagonal):
-            allowed = mask_of(start_row, key_block, block, diagonal)
-            rows = block_rows(key_block)
-            keys = k_s[rows, :]
-            values = v_s[rows, :]
-            flipped = kt_s[:, rows]
+        def step(first, state, diagonal):
+            allowed = mask_of(start_row, first, block, diagonal)
+            rows = two_rows(first)
+            keys = jnp.concatenate([k_s[r, :] for r in rows], axis=0)
+            values = jnp.concatenate([v_s[r, :] for r in rows], axis=0)
+            flipped = jnp.concatenate([kt_s[:, r] for r in rows], axis=1)
             fresh, dks, dvs = [], [], []
             for part in range(2):
                 cols = slice(part * head, (part + 1) * head)
@@ -217,13 +227,14 @@
                 dvs.append(dot(weights.astype(B16), grads[:, cols], 1, 0))
                 dks.append(dot(dscore, queries[:, cols], 1, 0))
                 fresh.append(state[part] + dot(flipped[cols, :], dscore, 1, 0))
-            dk_s[rows, :] += jnp.concatenate(dks, axis=1)
-            dv_s[rows, :] += jnp.concatenate(dvs, axis=1)
+            dk, dv = jnp.concatenate(dks, axis=1), jnp.concatenate(dvs, axis=1)
+            for i, r in enumerate(rows):
+                dk_s[r, :] += dk[i * BLK : (i + 1) * BLK]
+                dv_s[r, :] += dv[i * BLK : (i + 1) * BLK]
             return tuple(fresh)
 
         state = (jnp.zeros((head, BLK), F32), jnp.zeros((head, BLK), F32))
-        state = lax.fori_loop(low_ref[block], block, lambda j, s: step(j, s, False), state)
-        state = step(block, state, True)
+        state = over_pairs(low_ref[block], block, step, state)
         dq = jnp.concatenate(state, axis=0).T * scale
         for part in range(BLK // slot_len):
             slot = inv_ref[block * (BLK // slot_len) + part]
@@ -1200,63 +1211,176 @@
     )(qkv, out_w, fc, proj, mlp, hidden, dnorm, dhidden, x, single, mask[None])
 
 
-def feed_kernel(pairs, singles, at_ref, *refs):
+def hidden_kernel(rows, feats, att, w_out, x_ref, single, mask, by_core, hidden_out, norm_out):
+    half = w_out.shape[2]
+    count = feats // rows
+    tall = 2 * half // count
+    value = att[...].astype(F32)
+    zeros = jnp.zeros((value.shape[0], tall - rows), F32)
+    parts = []
+    for core in range(2):
+        blocks = []
+        for k in range(core, count, 2):
+            blocks += [value[:, k * rows : (k + 1) * rows], zeros]
+        parts.append(jnp.concatenate(blocks, axis=1).astype(B16))
+        by_core[core] = parts[core]
+    hidden = [dot(parts[0], w_out[0, y], 1, 0) + dot(parts[1], w_out[1, y], 1, 0) for y in range(2)]
+    hidden = x_ref[...].astype(F32) + jnp.concatenate(hidden, axis=1) + single[2:3, :]
+    hidden_out[...] = hidden
+    normed, unused = norm_forward(hidden, mask[...], feats)
+    norm_out[...] = (normed * single[3:4, :] + single[4:5, :]).astype(B16)
+
+
+def hidden_forward(att, w_out, x, single, mask, rows, feats):
+    tokens, wide = x.shape
+    return pl.pallas_call(
+        functools.partial(hidden_kernel, rows, feats),
+        out_shape=(
+            jax.ShapeDtypeStruct((2, tokens, wide // 2), B16),
+            jax.ShapeDtypeStruct((tokens, wide), F32),
+            jax.ShapeDtypeStruct((tokens, wide), B16),
+        ),
+        compiler_params=pltpu.CompilerParams(vmem_limit_bytes=VMEM_LIMIT),
+        name="hidden_forward",
+    )(att, w_out, x, single, mask[None])
+
+
+def hidden_back_kernel(
+    rows, feats, dnorm_ref, hidden, grad_ref, w_out, single, mask, dhidden_out, dhidden_b, sums, datt_out
+):
+    half = w_out.shape[2]
+    count = feats // rows
+    tall = 2 * half // count
+    dnorm = dnorm_ref[...]
+    grad = grad_ref[...].astype(F32)
+    normed, inv = norm_forward(hidden[...], mask[...], feats)
+    dhidden = grad + norm_backward(dnorm, normed, inv, single[3:4, :], feats)
+    dhidden_out[...] = dhidden
+    rounded = dhidden.astype(B16)
+    dhidden_b[...] = rounded
+    sums[0:1, :] = jnp.sum(dhidden, axis=0, keepdims=True)
+    sums[1:2, :] = jnp.sum(dnorm * normed, axis=0, keepdims=True)
+    sums[2:3, :] = jnp.sum(dnorm, axis=0, keepdims=True)
+    sums[3:4, :] = jnp.sum(grad, axis=0, keepdims=True)
+    grads = [rounded[:, :half], rounded[:, half:]]
+    datt = [dot(grads[0], w_out[c, 0], 1, 1) + dot(grads[1], w_out[c, 1], 1, 1) for c in range(2)]
+    parts = [datt[k % 2][:, k // 2 * tall : k // 2 * tall + rows] for k in range(count)]
+    if datt_out.shape[1] > feats:
+        parts.append(jnp.zeros((dnorm.shape[0], datt_out.shape[1] - feats), F32))
+    datt_out[...] = jnp.concatenate(parts, axis=1).astype(B16)
+
+
+def hidden_back(dnorm, hidden, grad, w_out, single, mask, rows, feats, padded):
+    tokens, wide = hidden.shape
+    return pl.pallas_call(
+        functools.partial(hidden_back_kernel, rows, feats),
+        out_shape=(
+            jax.ShapeDtypeStruct((tokens, wide), F32),
+            jax.ShapeDtypeStruct((tokens, wide), B16),
+            jax.ShapeDtypeStruct((4, wide), F32),
+            jax.ShapeDtypeStruct((tokens, padded), B16),
+        ),
+        compiler_params=pltpu.CompilerParams(vmem_limit_bytes=VMEM_LIMIT),
+        name="hidden_back",
+    )(dnorm, hidden, grad, w_out, single, mask[None])
+
+
+def load_pieces(at_ref, pieces, whole, sems, first=0):
+    rows = whole.shape[0] // len(pieces)
+    copies = []
+    for i, piece in enumerate(pieces):
+        to = whole.at[pl.ds(pl.multiple_of(at_ref[i], 16), rows), :]
+        copies.append(pltpu.make_async_copy(piece, to, sems.at[first + i]))
+    for copy in copies:
+        copy.start()
+    return copies
+
+
+def as_pieces(pairs, refs, which):
+    return [ref.at[which] for ref in refs[:pairs]] + list(refs[pairs:])
+
+
+def feed_up_kernel(pairs, count, at_ref, *refs):
+    pieces, (norm_ref, bias_ref, act_ref, slope_ref, w_fc, sems) = refs[:count], refs[count:]
+
+    @pl.when(pl.program_id(0) == 0)
+    def begin():
+        for copy in load_pieces(at_ref, as_pieces(pairs, pieces, 0), w_fc, sems):
+            copy.wait()
+
+    activated, slope = gelu_parts(dot(norm_ref[...], w_fc[...], 1, 0) + bias_ref[...])
+    act_ref[...] = activated.astype(B16)
+    slope_ref[...] = slope
+
+
+FEED_STEP = 256
+
+
+def feed_up(pairs, fcs, places, norm, bias):
+    pieces = pairs + fcs
+    total, wide = norm.shape
+    ff = bias.shape[0]
+    hidden = pl.BlockSpec((FEED_STEP, ff), lambda i: (i, 0))
+    return pl.pallas_call(
+        functools.partial(feed_up_kernel, len(pairs), len(pieces)),
+        grid=(total // FEED_STEP,),
+        in_specs=[pl.BlockSpec(memory_space=pltpu.SMEM)]
+        + [ANY] * len(pieces)
+        + [pl.BlockSpec((FEED_STEP, wide), lambda i: (i, 0)), pl.BlockSpec((1, ff), lambda i: (0, 0))],
+        out_specs=(hidden, hidden),
+        out_shape=(jax.ShapeDtypeStruct((total, ff), B16), jax.ShapeDtypeStruct((total, ff), F32)),
+        scratch_shapes=[pltpu.VMEM((wide, ff), B16)] + dma_sems(len(pieces)),
+        compiler_params=pltpu.CompilerParams(vmem_limit_bytes=VMEM_LIMIT),
+        name="feed_up",
+    )(places, *pieces, norm, bias[None])
+
+
+def feed_down_kernel(pairs, singles, at_ref, *refs):
     count = pairs + 2 * singles
     pieces, refs = refs[:count], refs[count:]
-    norm_ref, grad_ref, bias_ref, act_ref, dpre_ref, dnorm_ref, mlp_ref, sum_ref, w_fc, w_proj, sems = refs
+    grad_ref, act_ref, slope_ref, dpre_ref, dnorm_ref, mlp_ref, sum_ref, w_fc, w_proj, sems = refs
 
     @pl.when(pl.program_id(0) == 0)
     def begin():
-        rows = pieces[0].shape[1]
-        parts = [(piece.at[0], piece.at[1]) for piece in pieces[:pairs]]
-        parts += list(zip(pieces[pairs : pairs + singles], pieces[pairs + singles :]))
-        copies = []
-        for i, (fc, proj) in enumerate(parts):
-            to = pl.ds(pl.multiple_of(at_ref[i], 16), rows)
-            copies.append(pltpu.make_async_copy(fc, w_fc.at[to, :], sems.at[2 * i]))
-            copies.append(pltpu.make_async_copy(proj, w_proj.at[to, :], sems.at[2 * i + 1]))
-        for copy in copies:
-            copy.start()
+        fcs = as_pieces(pairs, pieces[: pairs + singles], 0)
+        projs = as_pieces(pairs, pieces[:pairs] + pieces[pairs + singles :], 1)
+        copies = load_pieces(at_ref, projs, w_proj, sems)
+        copies += load_pieces(at_ref, fcs, w_fc, sems, pairs + singles)
         for copy in copies:
             copy.wait()
         sum_ref[...] = jnp.zeros_like(sum_ref)
 
-    preact = dot(norm_ref[...], w_fc[...], 1, 0) + bias_ref[...]
-    activated, derivative = gelu_parts(preact)
-    activation = activated.astype(B16)
-    act_ref[...] = activation
-    dpre = dot(grad_ref[...], w_proj[...], 1, 0) * derivative
+    dpre = dot(grad_ref[...], w_proj[...], 1, 0) * slope_ref[...]
     sum_ref[...] += jnp.sum(dpre, axis=0, keepdims=True)
     dpre_b = dpre.astype(B16)
     dpre_ref[...] = dpre_b
     dnorm_ref[...] = dot(dpre_b, w_fc[...], 1, 1).astype(B16)
-    mlp_ref[...] = dot(activation, w_proj[...], 1, 1).astype(B16)
-
-
-def feed(pairs, fcs, projs, places, norm, grad, bias):
+    mlp_ref[...] = dot(act_ref[...], w_proj[...], 1, 1).astype(B16)
+
+
+def feed_down(pairs, fcs, projs, places, grad, act, slope):
     pieces = pairs + fcs + projs
-    total, wide = norm.shape
-    ff = bias.shape[0]
-    step = 256
-    tokens = pl.BlockSpec((step, wide), lambda i: (i, 0))
-    hidden = pl.BlockSpec((step, ff), lambda i: (i, 0))
+    total, wide = grad.shape
+    ff = act.shape[1]
+    tokens = pl.BlockSpec((FEED_STEP, wide), lambda i: (i, 0))
+    hidden = pl.BlockSpec((FEED_STEP, ff), lambda i: (i, 0))
     single = pl.BlockSpec((1, ff), lambda i: (0, 0))
     return pl.pallas_call(
-        functools.partial(feed_kernel, len(pairs), len(fcs)),
-        grid=(total // step,),
-        in_specs=[pl.BlockSpec(memory_space=pltpu.SMEM)] + [ANY] * len(pieces) + [tokens, tokens, single],
-        out_specs=(hidden, hidden, tokens, tokens, single),
+        functools.partial(feed_down_kernel, len(pairs), len(fcs)),
+        grid=(total // FEED_STEP,),
+        in_specs=[pl.BlockSpec(memory_space=pltpu.SMEM)] + [ANY] * len(pieces) + [tokens, hidden, hidden],
+        out_specs=(hidden, tokens, tokens, single),
         out_shape=(
-            jax.ShapeDtypeStruct((total, ff), B16),
             jax.ShapeDtypeStruct((total, ff), B16),
             jax.ShapeDtypeStruct((total, wide), B16),
             jax.ShapeDtypeStruct((total, wide), B16),
             jax.ShapeDtypeStruct((1, ff), F32),
         ),
-        scratch_shapes=[pltpu.VMEM((wide, ff), B16), pltpu.VMEM((wide, ff), B16)] + dma_sems(2 * len(pieces)),
+        scratch_shapes=[pltpu.VMEM((wide, ff), B16), pltpu.VMEM((wide, ff), B16)]
+        + dma_sems(2 * (len(pairs) + len(fcs))),
         compiler_params=pltpu.CompilerParams(vmem_limit_bytes=VMEM_LIMIT),
-        name="feed",
-    )(places, *pieces, norm, grad, bias[None])
+        name="feed_down",
+    )(places, *pieces, grad, act, slope)
 
 
 def after(value, other, unpack=False):
@@ -1295,15 +1419,6 @@
     wide = n_shard * tall
     row_pad = tall - rows
 
-    def widened(value):
-        lead = value.shape[:-1]
-        value = value.reshape(lead + (n_shard, rows))
-        return jnp.pad(value, [(0, 0)] * (len(lead) + 1) + [(0, row_pad)]).reshape(lead + (wide,))
-
-    def narrowed(value):
-        lead = value.shape[:-1]
-        return value.reshape(lead + (n_shard, tall))[..., :rows].reshape(lead + (feats,))
-
     mask = jnp.asarray((np.arange(wide) % tall < rows).astype(np.float32))
 
     singles = (first_gain, first_shift, out_bias, second_gain, second_shift, proj_bias)
@@ -1335,24 +1450,17 @@
     start3 = starts.reshape(-1, 1, BLK)
     low = start3[:, 0, 0] // BLK
 
-    own_wide = own_input.astype(F32)
     all_input = all_input.reshape(n_slot * slot_len, wide)
     norm_one, qkv, singles = project(
         slot_at.astype(jnp.int32)[None], all_input, packed, mask, rows, feats, padded
     )
-    bias_out, gain_two, shift_two = singles[2], singles[3], singles[4]
     heads_out, lse = attend(inv, low, qkv, start3, slot_len, head)
     fc_h, proj_late, heads_out = after((fc_h, ffn_blocks[1]), heads_out, True)
     fc_xh = [lax.ppermute(value, "x", shift_perm(n_x, 1)) for value in fc_h]
     proj_h = [lax.ppermute(proj_late, "h", shift_perm(n_h, step)) for step in range(1, n_h)]
-    attention = widened(to_tokens(heads_out.reshape(n_slot, slot_len, pair))[:, :feats])
-    by_core = attention.reshape(slot_len, n_shard // 2, 2, tall)
-    by_core = [by_core[:, :, part].reshape(slot_len, wide // 2) for part in range(2)]
-    hidden = [dot(by_core[0], w_out[0, y], 1, 0) + dot(by_core[1], w_out[1, y], 1, 0) for y in range(n_y)]
-    hidden = own_wide + jnp.concatenate(hidden, axis=1) + bias_out
-    normed_two, inv_two = norm_forward(hidden, mask, feats)
-    norm_two = (normed_two * gain_two + shift_two).astype(B16)
-    grad_wide = grad_own.astype(F32)
+    by_core, hidden, norm_two = hidden_forward(
+        to_tokens(heads_out.reshape(n_slot, slot_len, pair)), w_out, own_input, singles, mask, rows, feats
+    )
     proj_h, norm_two = after(proj_h, norm_two)
     proj_xh = [lax.ppermute(value, "x", shift_perm(n_x, 1)) for value in proj_h]
     norm_all = group_gather(norm_two, 6).reshape(-1, wide)
@@ -1365,9 +1473,8 @@
         return [value for both in zip(one, two) for value in both]
 
     places = jnp.stack([(x * n_h + h) * (4 * tall) for x, h in places]).astype(jnp.int32)
-    activation, dpreact_b, dnorm_part, mlp_part, dpreact_sum = feed(
-        [ffn_blocks, along_x], mixed(fc_h, fc_xh), mixed(proj_h, proj_xh), places, norm_all, grad_all, b_fc
-    )
+    pairs, fcs, projs = [ffn_blocks, along_x], mixed(fc_h, fc_xh), mixed(proj_h, proj_xh)
+    activation, slope = feed_up(pairs, fcs, places, norm_all, b_fc)
 
     def pick(value, at):
         return lax.dynamic_index_in_dim(value, at, 0, False)
@@ -1377,11 +1484,14 @@
         return value.reshape(n_x, n_h, 4 * tall, ff_own)
 
     proj_part = by_owner(dot(grad_all, activation, 0, 0))
-    proj_x = lax.ppermute(pick(proj_part, 1 - x_at), "x", shift_perm(n_x, 1))
+    proj_give = pick(proj_part, 1 - x_at)
+    proj_give, activation = after(proj_give, activation)
+    proj_x = lax.ppermute(proj_give, "x", shift_perm(n_x, 1))
+    dpreact_b, dnorm_part, mlp_part, dpreact_sum = feed_down(pairs, fcs, projs, places, grad_all, activation, slope)
+
     fc_part = by_owner(dot(norm_all, dpreact_b, 0, 0))
     fc_x = lax.ppermute(pick(fc_part, 1 - x_at), "x", shift_perm(n_x, 1))
-
-    proj_part, fc_part, dnorm_part = after((proj_part, fc_part), dnorm_part, True)
+    fc_part, dnorm_part = after(fc_part, dnorm_part)
     dnorm_two = group_scatter(dnorm_part.reshape(8, slot_len, wide), 7)
 
     def over_h(value):
@@ -1398,17 +1508,13 @@
     proj_line = pick(proj_part, x_at) + proj_x
     proj_h = over_h(proj_line)
     mlp = lax.psum_scatter(mlp_part, FFG, scatter_dimension=0, tiled=True)
-    dhidden = grad_wide + norm_backward(dnorm_two, normed_two, inv_two, gain_two, feats)
-    dhidden_b = dhidden.astype(B16)
+    dhidden, dhidden_b, token_sums, dattention = hidden_back(
+        dnorm_two, hidden, grad_own, w_out, singles, mask, rows, feats, padded
+    )
     c_at = lax.axis_index("c")
     out_give = dot(jnp.where(c_at == 0, by_core[1], by_core[0]), dhidden_b, 0, 0).astype(B16)
     out_give = lax.ppermute(out_give, "c", shift_perm(2, 1))
     out_keep = dot(jnp.where(c_at == 0, by_core[0], by_core[1]), dhidden_b, 0, 0).astype(B16)
-    grad_y = [dhidden_b[:, : wide // 2], dhidden_b[:, wide // 2 :]]
-    datt = [dot(grad_y[0], w_out[c, 0], 1, 1) + dot(grad_y[1], w_out[c, 1], 1, 1) for c in range(2)]
-    datt = [value.astype(B16).reshape(slot_len, -1, 1, tall) for value in datt]
-    dattention = narrowed(jnp.concatenate(datt, axis=2).reshape(slot_len, wide))
-    dattention = jnp.pad(dattention, ((0, 0), (0, padded - feats)))
     dattention = to_heads(dattention, n_slot).reshape(n_slot * slot_len, pair)
     out_give, fc_x, dattention = after((out_give, fc_x), dattention, True)
     out_part = (out_keep + out_give).reshape(n_shard // 2, tall, wide)
@@ -1418,14 +1524,6 @@
     dnorm_one_part, dqkv_b, gain_sum, shift_sum, pair_sum = project_back(all_input, dqkv, mask, w_qkv, feats)
     qkv_part = dot(norm_one, dqkv_b, 0, 0).astype(B16).reshape(n_x, n_ctx, tall, 3 * pair)
     proj_h, fc_h, dnorm_one_part = after((proj_h, fc_h), dnorm_one_part, True)
-    token_sums = jnp.stack(
-        [
-            jnp.sum(dhidden, axis=0),
-            jnp.sum(dnorm_two * normed_two, axis=0),
-            jnp.sum(dnorm_two, axis=0),
-            jnp.sum(grad_wide, axis=0),
-        ]
-    )
     dnorm_one, qkv_all, out_all, fc_all, proj_all, owned, pair_sums, ff_sums = closing(
         dnorm_one_part.reshape(n_slot, slot_len, wide), qkv_part, out_part, total(fc_line, fc_h), total(proj_line, proj_h),
         token_sums, gain_sum, shift_sum, pair_sum, dpreact_sum,

time: 542 us -> 525 us (0.969); the launches traced: 531 us -> 521 us
  Pallas kernels: 377 us -> 422 us
  waiting for transfers between devices: 45.1 us -> 17.9 us
  matrix products: 40.1 us -> 26.9 us
  local copies, waits for them, and re-layouts: 22.9 us -> 15.6 us
    pallas_call x1, Pallas kernels: 14.4 us -> 41.4 us  [to_tokens(): pl.pallas_call(to_tokens_kernel, out_shape=jax.ShapeDtypeStruct((tokens,...]
    ppermute x1, waiting for transfers between devices: 24.3 us -> 0.01 us  [on_device(): lax.ppermute(proj_late, 'h', shift_perm(n_h, step))]
    pallas_call x1 -> x4, Pallas kernels: 21.9 us -> 41.7 us  [the longest x1 18.4 us: feed_down(): pl.pallas_call(functools.partial(feed_down_kernel, len(pairs), len(fcs)),...]
    dot_general x13 -> x5, matrix products: 40.1 us -> 26.9 us  [dot(): lax.dot_general(left, right, (((left_dim,), (right_dim,)), ((), ())), pre...]
    ppermute x1, waiting for transfers between devices: 6.07 us -> 17.1 us  [on_device(): fc_x = lax.ppermute(pick(fc_part, 1 - x_at), 'x', shift_perm(n_x, 1))]
    ppermute x1, waiting for transfers between devices: 8.24 us -> 0.01 us  [on_device(): proj_x = lax.ppermute(proj_give, 'x', shift_perm(n_x, 1))]
    ppermute x2, waiting for transfers between devices: 5.76 us -> 0.01 us  [over_h(): lax.ppermute(give, 'h', shift_perm(n_h, step + 1))]
  transfers between devices with their start and end apart: 13 -> 13, of which waited for: 4 -> 1; matrix products, arithmetic and copies ran while one was open for 12% -> 10% of each run, Pallas kernels for 46% -> 60%
where the time goes in v8:
time: 525 us; the launch traced here: 521 us
  Pallas kernels  422 us (80%)
  matrix products  26.9 us (5%)
  waiting for transfers between devices  17.9 us (3%)
  local copies, waits for them, and re-layouts  15.6 us (3%)
  between operations  14.6 us (3%)
  other arithmetic  13.2 us (3%)
  starting transfers between devices  10.7 us (2%)
    pallas_call x1, Pallas kernels, opening(): pl.pallas_call(opening_kernel, out_shape=(jax.ShapeDtypeStruct((2 * n_ctx...  99.5 us
    pallas_call x1, Pallas kernels, closing(): pl.pallas_call(closing_kernel, out_shape=(jax.ShapeDtypeStruct(block, F32...  98.6 us
    pallas_call x1, Pallas kernels, to_tokens(): pl.pallas_call(to_tokens_kernel, out_shape=jax.ShapeDtypeStruct((tokens,...  41.4 us
    dot_general x5, matrix products, dot(): lax.dot_general(left, right, (((left_dim,), (right_dim,)), ((), ())), pre...  26.9 us
    pallas_call x1, Pallas kernels, attend_back(): pl.pallas_call(functools.partial(attend_back_kernel, slot_len, head), out...  23.2 us
    pallas_call x1, Pallas kernels, attend(): pl.pallas_call(functools.partial(attend_kernel, slot_len, head), out_shap...  22.9 us
    pallas_call x1, Pallas kernels, group_gather(): pl.pallas_call(group_gather_kernel, out_shape=jax.ShapeDtypeStruct((8,) +...  21.6 us
    pallas_call x1, Pallas kernels, group_scatter(): pl.pallas_call(group_scatter_kernel, out_shape=jax.ShapeDtypeStruct(block...  21.1 us
  transfers between devices with their start and end apart: 13, of which 1 were waited for; matrix products, arithmetic and copies ran while one was open for 10% of the time, Pallas kernels for 60%

profile of v8, /device:TPU:0, one launch (start us, length us, event | category | flops | bytes accessed | tf_op | source)
XLA Modules:
  0.0 521.3 jit_solution(1673899768297164499)
XLA Ops:
  8.5 4.8 prepare.1
  13.2 99.5 %opening.1 = (bf16[16,128,1792]{2,1,0:T(8,128)(2,1)}, bf16[2,8,112,384]{3,2,1,0:T(8,128)(2,1)}, bf16[2,4,112,800]{3,2,1,0:T(8,128)(2,1)}, bf16[8,112,896]{2,1,0:T(8,128)(2,1)}) custom-call(bf16[128,1792]{1,0:T(8,128)(2,1)} %get-tuple-element.83.own.x_ref, bf16[8,112,384]{2,1,0:T(8,128)(2,1)} %get-tuple-element.84.blocks, ...), custom_call_target="tpu_custom_call" | custom-call | tf_op jit(solution)/shard_map/opening/pallas_call | solution.py:578
  116.7 13.5 %project.1 = (bf16[2048,1792]{1,0:T(8,128)(2,1)}, bf16[2048,384]{1,0:T(8,128)(2,1)}, f32[8,1792]{1,0:T(8,128)}) custom-call(s32[1]{0:T(128)} %bitcast.25.at_ref, bf16[2048,1792]{1,0:T(8,128)(2,1)} %bitcast.104, bf16[16,112,384]{2,1,0:T(8,128)(2,1)} %bitcast.114, f32[1,1792]{1,0:T(1,128)} %constant.111.mask_ref.mask, bf16[1792,384]{1,0:T(8,128)(2,1)} %bitcast.115), custom_call_target="tpu_custom_call" | custom-call | tf_op jit(solution)/shard_map/project/pallas_call | solution.py:1103
  131.3 22.9 %attend.1 = (bf16[2048,128]{1,0:T(8,128)(2,1)}, f32[8,2,256]{2,1,0:T(2,128)}) custom-call(s32[16]{0:T(128)} %copy-done.17, s32[8]{0:T(128)} %and_select_fusion.low_ref, bf16[2048,384]{1,0:T(8,128)(2,1)} %get-tuple-element.92.qkv_ref, s32[8,1,256]{2,1,0:T(1,128)} %bitcast.134), custom_call_target="tpu_custom_call" | custom-call | tf_op jit(solution)/shard_map/attend/pallas_call | solution.py:167
  154.2 2.9 collective-permute-start.3
  159.1 41.4 %to_tokens.1.att = bf16[128,2048]{1,0:T(8,128)(2,1)} custom-call(bf16[16,128,128]{2,1,0:T(8,128)(2,1)} %bitcast.125), custom_call_target="tpu_custom_call" | custom-call | tf_op jit(solution)/shard_map/to_tokens/pallas_call | solution.py:614
  200.6 5.6 %hidden_forward.1 = (bf16[2,128,896]{2,1,0:T(8,128)(2,1)}, f32[128,1792]{1,0:T(8,128)}, bf16[128,1792]{1,0:T(8,128)(2,1)}) custom-call(bf16[128,2048]{1,0:T(8,128)(2,1)} %to_tokens.1.att, bf16[2,2,896,896]{3,2,1,0:T(8,128)(2,1)} %bitcast.106, bf16[128,1792]{1,0:T(8,128)(2,1)} %get-tuple-element.83.own.x_ref, f32[8,1792]{1,0:T(8,128)} %get-tuple-element.98.single, ...), custom_call_target="tpu_custom_call" | custom-call | tf_op jit(solution)/shard_map/hidden_forward/pallas_call | solution.py:1236
  206.2 21.6 %group_gather.1 = bf16[8,128,1792]{2,1,0:T(8,128)(2,1)} custom-call(bf16[128,1792]{1,0:T(8,128)(2,1)} %get-tuple-element.100.own), custom_call_target="tpu_custom_call" | custom-call | tf_op jit(solution)/shard_map/group_gather/pallas_call | solution.py:502
  229.0 10.7 %feed_up.1 = (bf16[1024,800]{1,0:T(8,128)(2,1)}, f32[1024,800]{1,0:T(8,128)}) custom-call(s32[4]{0:T(128)} %pad_add_fusion.at_ref, bf16[2,448,800]{2,1,0:T(8,128)(2,1)} %bitcast.110, bf16[2,448,800]{2,1,0:T(8,128)(2,1)} %copy-done.8, bf16[448,800]{1,0:T(8,128)(2,1)} %collective-permute-done.1.refs_2_, bf16[448,800]{1,0:T(8,128)(2,1)} %collective-permute-done.2.refs_3_, ...), custom_call_target="tpu_custom_call" | custom-call | tf_op jit(solution)/shard_map/feed_up/pallas_call | solution.py:1324
  239.8 6.6 %convolution_convert_fusion.3 = bf16[1792,800]{1,0:T(8,128)(2,1)S(1)} fusion(bf16[1024,1792]{1,0:T(8,128)(2,1)} %all-gather.3.cloned.1.call-done.refs_6_, bf16[1024,800]{1,0:T(8,128)(2,1)} %get-tuple-element.104.refs_7_), kind=kOutput, calls=%fused_computation.4 | convolution fusion | flops 2937446400 | bytes 8175616 | tf_op jit(solution)/shard_map/dot_general | solution.py:59
  246.4 1.4 dynamic-slice_bitcast_fusion.1
  247.8 1.7 collective-permute-start.4
  249.6 18.4 %feed_down.1 = (bf16[1024,800]{1,0:T(8,128)(2,1)}, bf16[1024,1792]{1,0:T(8,128)(2,1)}, bf16[1024,1792]{1,0:T(8,128)(2,1)}, f32[1,800]{1,0:T(1,128)}) custom-call(s32[4]{0:T(128)} %pad_add_fusion.at_ref, bf16[2,448,800]{2,1,0:T(8,128)(2,1)} %bitcast.111, bf16[2,448,800]{2,1,0:T(8,128)(2,1)} %copy-done.8, bf16[448,800]{1,0:T(8,128)(2,1)} %collective-permute-done.1.refs_2_, ...), custom_call_target="tpu_custom_call" | custom-call | tf_op jit(solution)/shard_map/feed_down/pallas_call | solution.py:1368
  268.0 6.9 %convolution_convert_fusion.2 = bf16[1792,800]{1,0:T(8,128)(2,1)} fusion(bf16[1024,1792]{1,0:T(8,128)(2,1)S(1)} %bitcast.109, bf16[1024,800]{1,0:T(8,128)(2,1)} %get-tuple-element.107), kind=kOutput, calls=%fused_computation.3 | convolution fusion | flops 2937446400 | bytes 8175616 | tf_op jit(solution)/shard_map/dot_general | solution.py:59
  274.9 21.1 %group_scatter.1.dnorm_ref = f32[128,1792]{1,0:T(8,128)} custom-call(bf16[8,128,1792]{2,1,0:T(8,128)(2,1)} %bitcast.118), custom_call_target="tpu_custom_call" | custom-call | tf_op jit(solution)/shard_map/group_scatter/pallas_call | solution.py:778
  296.0 7.0 %hidden_back.1 = (f32[128,1792]{1,0:T(8,128)}, bf16[128,1792]{1,0:T(8,128)(2,1)}, f32[4,1792]{1,0:T(4,128)}, bf16[128,2048]{1,0:T(8,128)(2,1)}) custom-call(f32[128,1792]{1,0:T(8,128)} %group_scatter.1.dnorm_ref, f32[128,1792]{1,0:T(8,128)} %get-tuple-element.114.hidden, bf16[128,1792]{1,0:T(8,128)(2,1)} %get-tuple-element.88.grad_ref, ...), custom_call_target="tpu_custom_call" | custom-call | tf_op jit(solution)/shard_map/hidden_back/pallas_call | solution.py:1275
  303.0 3.9 convolution_convert_fusion.1
  307.0 1.3 dynamic-slice_bitcast_fusion
  309.0 13.7 %to_heads.1 = bf16[16,128,128]{2,1,0:T(8,128)(2,1)} custom-call(bf16[128,2048]{1,0:T(8,128)(2,1)} %get-tuple-element.116.src), custom_call_target="tpu_custom_call" | custom-call | tf_op jit(solution)/shard_map/to_heads/pallas_call | solution.py:645
  322.7 1.7 bitcast_add_fusion.1
  325.5 2.4 collective-permute-start.6
  328.9 17.1 %collective-permute-done.8 = bf16[2,448,800]{2,1,0:T(8,128)(2,1)} collective-permute-done((bf16[2,448,800]{2,1,0:T(8,128)(2,1)}, bf16[2,448,800]{2,1,0:T(8,128)(2,1)}, u32[]{:S(2)}, u32[]{:S(2)}) %collective-permute-start.8) | collective-permute-done | bytes 1433632 | tf_op jit(solution)/shard_map/ppermute | solution.py:1493
  346.0 1.6 bitcast_add_fusion
  349.8 2.1 collective-permute-start.9
  351.8 23.2 %attend_back.1.grad_ref = f32[2048,384]{1,0:T(8,128)} custom-call(s32[16]{0:T(128)} %copy-done.17, s32[8]{0:T(128)} %and_select_fusion.low_ref, bf16[2048,384]{1,0:T(8,128)(2,1)} %get-tuple-element.92.qkv_ref, bf16[2048,128]{1,0:T(8,128)(2,1)} %get-tuple-element.96.out_ref, bf16[2048,128]{1,0:T(8,128)(2,1)} %bitcast.126, ...), custom_call_target="tpu_custom_call" | custom-call | tf_op jit(solution)/shard_map/attend_back/pallas_call | solution.py:265
  375.0 13.1 %project_back.1 = (bf16[2048,1792]{1,0:T(8,128)(2,1)}, bf16[2048,384]{1,0:T(8,128)(2,1)}, f32[1,1792]{1,0:T(1,128)}, f32[1,1792]{1,0:T(1,128)}, f32[1,384]{1,0:T(1,128)}) custom-call(bf16[2048,1792]{1,0:T(8,128)(2,1)} %bitcast.105, f32[2048,384]{1,0:T(8,128)} %attend_back.1.grad_ref, f32[1,1792]{1,0:T(1,128)} %constant.111.mask_ref.mask, ...), custom_call_target="tpu_custom_call" | custom-call | tf_op jit(solution)/shard_map/project_back/pallas_call | solution.py:1156
  388.1 4.8 add.111
  392.9 8.4 %convolution_convert_fusion.4 = bf16[1792,384]{1,0:T(8,128)(2,1)} fusion(bf16[2048,1792]{1,0:T(8,128)(2,1)} %get-tuple-element.122, bf16[2048,384]{1,0:T(8,128)(2,1)S(1)} %copy-done.18), kind=kOutput, calls=%fused_computation.5 | convolution fusion | flops 2819260416 | bytes 10289152 | tf_op jit(solution)/shard_map/dot_general | solution.py:59
  401.3 2.7 fusion
  404.1 98.6 %closing.1 = (f32[128,1792]{1,0:T(8,128)}, bf16[2,8,112,384]{3,2,1,0:T(8,128)(2,1)}, bf16[2,112,896]{2,1,0:T(8,128)(2,1)}, bf16[4,112,800]{2,1,0:T(8,128)(2,1)},...) custom-call(bf16[16,128,1792]{2,1,0:T(8,128)(2,1)} %bitcast.117, ...), custom_call_target="tpu_custom_call" | custom-call | tf_op jit(solution)/shard_map/closing/pallas_call | solution.py:949
  505.6 1.4 slice_bitcast_fusion
  507.0 7.2 %deliver.1 = (f32[100,4800]{1,0:T(8,128)}, f32[100,1600]{1,0:T(8,128)}, f32[100,3200]{1,0:T(8,128)}, f32[100,3200]{1,0:T(8,128)}, f32[1600,128]{1,0:T(8,128)}, /*index=5*/f32[1600,128]{1,0:T(8,128)}) custom-call(bf16[2,8,112,384]{3,2,1,0:T(8,128)(2,1)} %get-tuple-element.132.qkv, bf16[2,112,896]{2,1,0:T(8,128)(2,1)} %get-tuple-element.133.out_w, ...), custom_call_target="tpu_custom_call" | custom-call | tf_op jit(solution)/shard_map/deliver/pallas_call | solution.py:1199
  (90 shorter events, 17.2 us)
Async XLA Ops:
  7.2 109.0 %copy-start = (s32[1,2048]{1,0:T(1,128)S(1)}, s32[1,2048]{1,0:T(1,128)}, u32[]{:S(2)}) copy-start(s32[1,2048]{1,0:T(1,128)} %param.18) | copy-start | bytes 24580
  7.2 193.4 %all-gather.5.cloned.1.call-start = ((), (), s32[]{:S(2)}) async-start(), calls=%async_computation.2 | async-start | bytes 8028160 | tf_op jit(solution)/shard_map/all_gather | solution.py:1437
  112.7 1.4 copy-start.3
  112.8 127.0 %all-gather.3.cloned.1.call-start = ((), (), s32[]{:S(2)}) async-start(), calls=%async_computation.1 | async-start | bytes 4128768 | tf_op jit(solution)/shard_map/all_gather | solution.py:1416
  112.8 3.2 copy-start.19
  113.5 393.5 %reduce-scatter.2.cloned.1.call-start = ((), (), s32[]{:S(2)}) async-start(), calls=%async_computation.3 | async-start | bytes 4128768 | tf_op jit(solution)/shard_map/reduce_scatter | solution.py:1510
  115.4 38.8 %collective-permute-start.1 = (bf16[448,800]{1,0:T(8,128)(2,1)}, bf16[448,800]{1,0:T(8,128)(2,1)}, u32[]{:S(2)}, u32[]{:S(2)}) collective-permute-start(bf16[448,800]{1,0:T(8,128)(2,1)} %bitcast.17), channel_id=1, source_target_pairs={{0,8},{8,0},{1,9},{9,1},{2,10},{10,2},{3,11},{11,3},{4,12},{12,4},... | collective-permute-start | bytes 2150408 | tf_op jit(solution)/shard_map/ppermute | solution.py:1433
  115.4 112.4 %collective-permute-start = (bf16[2,448,800]{2,1,0:T(8,128)(2,1)S(1)}, bf16[2,448,800]{2,1,0:T(8,128)(2,1)S(1)}, u32[]{:S(2)}, u32[]{:S(2)}) collective-permute-start(bf16[2,448,800]{2,1,0:T(8,128)(2,1)S(1)} %bitcast.112), channel_id=1, source_target_pairs={{0,16},{16,0},{1,17},{17,1},{2,18},{18,2},{3,19},{19,3},{4,20},{20... | collective-permute-start | bytes 4300808 | tf_op jit(solution)/shard_map/ppermute | solution.py:1434
  116.1 14.1 %copy-start.17 = (s32[16]{0:T(128)}, s32[16]{0:T(128)S(1)}, u32[]{:S(2)}) copy-start(s32[16]{0:T(128)S(1)} %select_reduce_fusion.1.inv_ref) | copy-start | bytes 196
  154.2 51.9 %collective-permute-start.3 = (bf16[448,800]{1,0:T(8,128)(2,1)}, bf16[448,800]{1,0:T(8,128)(2,1)}, u32[]{:S(2)}, u32[]{:S(2)}) collective-permute-start(bf16[448,800]{1,0:T(8,128)(2,1)} %bitcast.129), channel_id=1, source_target_pairs={{0,8},{8,0},{1,9},{9,1},{2,10},{10,2},{3,11},{11,3},{4,12},{12,4},... | collective-permute-start | bytes 2150408 | tf_op jit(solution)/shard_map/ppermute | solution.py:1460
  157.2 70.7 %collective-permute-start.2 = (bf16[448,800]{1,0:T(8,128)(2,1)}, bf16[448,800]{1,0:T(8,128)(2,1)}, u32[]{:S(2)}, u32[]{:S(2)}) collective-permute-start(bf16[448,800]{1,0:T(8,128)(2,1)} %collective-permute-done.1.refs_2_), channel_id=1, source_target_pairs={{0,16},{16,0},{1,17},{17,1},{2,18},{18,2},{3,19},{19,3},{4,20},{20... | collective-permute-start | bytes 2150408 | tf_op jit(solution)/shard_map/ppermute | solution.py:1459
  206.2 43.4 %collective-permute-start.5 = (bf16[448,800]{1,0:T(8,128)(2,1)}, bf16[448,800]{1,0:T(8,128)(2,1)}, u32[]{:S(2)}, u32[]{:S(2)}) collective-permute-start(bf16[448,800]{1,0:T(8,128)(2,1)} %collective-permute-done.3.refs_4_), channel_id=1, source_target_pairs={{0,16},{16,0},{1,17},{17,1},{2,18},{18,2},{3,19},{19,3},{4,20},{20... | collective-permute-start | bytes 2150408 | tf_op jit(solution)/shard_map/ppermute | solution.py:1465
  227.8 1.2 copy-start.8
  246.4 3.2 copy-start.9
  247.8 48.1 %collective-permute-start.4 = (bf16[2,448,800]{2,1,0:T(8,128)(2,1)}, bf16[2,448,800]{2,1,0:T(8,128)(2,1)}, u32[]{:S(2)}, u32[]{:S(2)}) collective-permute-start(bf16[2,448,800]{2,1,0:T(8,128)(2,1)} %dynamic-slice_bitcast_fusion.1), channel_id=1, source_target_pairs={{0,16},{16,0},{1,17},{17,1},{2,18},{18,2},{3,19},{19,3},{4,20},{20... | collective-permute-start | bytes 4300808 | tf_op jit(solution)/shard_map/ppermute | solution.py:1489
  249.6 18.4 %copy-start.2 = (bf16[8,128,1792]{2,1,0:T(8,128)(2,1)S(1)}, bf16[8,128,1792]{2,1,0:T(8,128)(2,1)}, u32[]{:S(2)}) copy-start(bf16[8,128,1792]{2,1,0:T(8,128)(2,1)} %group_gather.1) | copy-start | bytes 11010052
  296.0 7.0 %copy-start.14 = (bf16[2,128,896]{2,1,0:T(8,128)(2,1)S(1)}, bf16[2,128,896]{2,1,0:T(8,128)(2,1)}, u32[]{:S(2)}) copy-start(bf16[2,128,896]{2,1,0:T(8,128)(2,1)} %get-tuple-element.112) | copy-start | bytes 1376260
  303.0 4.0 copy-start.11
  306.9 15.8 %copy-start.10 = (bf16[1792,800]{1,0:T(8,128)(2,1)S(1)}, bf16[1792,800]{1,0:T(8,128)(2,1)}, u32[]{:S(2)}) copy-start(bf16[1792,800]{1,0:T(8,128)(2,1)} %copy-done.9) | copy-start | bytes 8601604
  306.9 39.1 %collective-permute-start.7 = (bf16[896,1792]{1,0:T(8,128)(2,1)}, bf16[896,1792]{1,0:T(8,128)(2,1)}, u32[]{:S(2)}, u32[]{:S(2)}) collective-permute-start(bf16[896,1792]{1,0:T(8,128)(2,1)} %convolution_convert_fusion.1), channel_id=1, source_target_pairs={{0,2},{2,0},{1,3},{3,1},{4,6},{6,4},{5,7},{7,5},{8,10},{10,8},{9,1... | collective-permute-start | bytes 9633800 | tf_op jit(solution)/shard_map/ppermute | solution.py:1516
  308.3 37.7 %collective-permute-start.8 = (bf16[2,448,800]{2,1,0:T(8,128)(2,1)}, bf16[2,448,800]{2,1,0:T(8,128)(2,1)}, u32[]{:S(2)}, u32[]{:S(2)}) collective-permute-start(bf16[2,448,800]{2,1,0:T(8,128)(2,1)} %dynamic-slice_bitcast_fusion), channel_id=1, source_target_pairs={{0,16},{16,0},{1,17},{17,1},{2,18},{18,2},{3,19},{19,3},{4,20},{20... | collective-permute-start | bytes 4300808 | tf_op jit(solution)/shard_map/ppermute | solution.py:1493
  322.7 5.2 copy-start.15
  324.5 4.4 copy-start.4
  324.5 3.4 copy-start.13
  325.5 20.6 %copy-start.12 = (bf16[1792,800]{1,0:T(8,128)(2,1)S(1)}, bf16[1792,800]{1,0:T(8,128)(2,1)}, u32[]{:S(2)}) copy-start(bf16[1792,800]{1,0:T(8,128)(2,1)} %convolution_convert_fusion.2) | copy-start | bytes 8601604
  325.5 75.8 %collective-permute-start.6 = (bf16[448,800]{1,0:T(8,128)(2,1)}, bf16[448,800]{1,0:T(8,128)(2,1)S(1)}, u32[]{:S(2)}, u32[]{:S(2)}) collective-permute-start(bf16[448,800]{1,0:T(8,128)(2,1)} %dynamic-slice_bitcast_fusion.3), channel_id=1, source_target_pairs={{0,8},{8,0},{1,9},{9,1},{2,10},{10,2},{3,11},{11,3},{4,12},{12,4},... | collective-permute-start | bytes 2150408 | tf_op jit(solution)/shard_map/ppermute | solution.py:1499
  347.6 1.2 copy-start.6
  349.8 51.5 %collective-permute-start.9 = (bf16[448,800]{1,0:T(8,128)(2,1)}, bf16[448,800]{1,0:T(8,128)(2,1)}, u32[]{:S(2)}, u32[]{:S(2)}) collective-permute-start(bf16[448,800]{1,0:T(8,128)(2,1)} %dynamic-slice_bitcast_fusion.2), channel_id=1, source_target_pairs={{0,8},{8,0},{1,9},{9,1},{2,10},{10,2},{3,11},{11,3},{4,12},{12,4},... | collective-permute-start | bytes 2150408 | tf_op jit(solution)/shard_map/ppermute | solution.py:1499
  388.1 4.8 copy-start.18
  392.9 8.4 %copy-start.5 = (bf16[2,448,800]{2,1,0:T(8,128)(2,1)S(1)}, bf16[2,448,800]{2,1,0:T(8,128)(2,1)}, u32[]{:S(2)}) copy-start(bf16[2,448,800]{2,1,0:T(8,128)(2,1)} %copy-done.4) | copy-start | bytes 4300804
  392.9 8.4 %copy-start.7 = (bf16[2,448,800]{2,1,0:T(8,128)(2,1)S(1)}, bf16[2,448,800]{2,1,0:T(8,128)(2,1)}, u32[]{:S(2)}) copy-start(bf16[2,448,800]{2,1,0:T(8,128)(2,1)} %copy-done.6) | copy-start | bytes 4300804
  507.0 7.3 %copy-start.1 = (s32[1,2048]{1,0:T(1,128)S(1)}, s32[1,2048]{1,0:T(1,128)}, u32[]{:S(2)}) copy-start(s32[1,2048]{1,0:T(1,128)} %param.18) | copy-start | bytes 24580
  (1 other events, 0.8 us)
Sparse Core Ops, SparseCore 0:
  112.9 46.1 all-gather.4
  161.2 49.1 all-gather.2
  296.1 82.3 reduce-scatter.1

commit v9 on v8

--- a/solution.py
+++ b/solution.py
@@ -1455,15 +1455,17 @@
         slot_at.astype(jnp.int32)[None], all_input, packed, mask, rows, feats, padded
     )
     heads_out, lse = attend(inv, low, qkv, start3, slot_len, head)
-    fc_h, proj_late, heads_out = after((fc_h, ffn_blocks[1]), heads_out, True)
+    fc_h, along_x, heads_out = after((fc_h, along_x), heads_out, True)
     fc_xh = [lax.ppermute(value, "x", shift_perm(n_x, 1)) for value in fc_h]
+    tokens_out = to_tokens(heads_out.reshape(n_slot, slot_len, pair))
+    proj_late, tokens_out = after(ffn_blocks[1], tokens_out)
     proj_h = [lax.ppermute(proj_late, "h", shift_perm(n_h, step)) for step in range(1, n_h)]
     by_core, hidden, norm_two = hidden_forward(
-        to_tokens(heads_out.reshape(n_slot, slot_len, pair)), w_out, own_input, singles, mask, rows, feats
+        tokens_out, w_out, own_input, singles, mask, rows, feats
     )
-    proj_h, norm_two = after(proj_h, norm_two)
+    norm_all = group_gather(norm_two, 6).reshape(-1, wide)
+    proj_h, norm_all = after(proj_h, norm_all)
     proj_xh = [lax.ppermute(value, "x", shift_perm(n_x, 1)) for value in proj_h]
-    norm_all = group_gather(norm_two, 6).reshape(-1, wide)
     places = [(x_at, h_at), (1 - x_at, h_at)]
     for step in range(1, n_h):
         h_from = lax.rem(h_at + n_h - step, n_h)

time: 525 us -> 516 us (0.983)
  Pallas kernels: 422 us -> 403 us
  starting transfers between devices: 10.7 us -> 17.6 us
    pallas_call x1, Pallas kernels: 41.4 us -> 12.4 us  [to_tokens(): pl.pallas_call(to_tokens_kernel, out_shape=jax.ShapeDtypeStruct((tokens,...]
    pallas_call x1, Pallas kernels: 21.6 us -> 40 us  [group_gather(): pl.pallas_call(group_gather_kernel, out_shape=jax.ShapeDtypeStruct((8,) +...]
    pallas_call x1, Pallas kernels: 22.9 us -> 17.6 us  [attend(): pl.pallas_call(functools.partial(attend_kernel, slot_len, head), out_shap...]
  transfers between devices with their start and end apart: 13 -> 13, of which waited for: 1 -> 3; matrix products, arithmetic and copies ran while one was open for 10% -> 10% of each run, Pallas kernels for 60% -> 57%
where the time goes in v9:
time: 516 us; the launch traced here: 513 us
  Pallas kernels  403 us (78%)
  matrix products  26.8 us (5%)
  waiting for transfers between devices  21.7 us (4%)
  starting transfers between devices  17.6 us (3%)
  local copies, waits for them, and re-layouts  16.3 us (3%)
  between operations  14.6 us (3%)
  other arithmetic  13 us (3%)
    pallas_call x1, Pallas kernels, opening(): pl.pallas_call(opening_kernel, out_shape=(jax.ShapeDtypeStruct((2 * n_ctx...  99.5 us
    pallas_call x1, Pallas kernels, closing(): pl.pallas_call(closing_kernel, out_shape=(jax.ShapeDtypeStruct(block, F32...  99.2 us
    pallas_call x1, Pallas kernels, group_gather(): pl.pallas_call(group_gather_kernel, out_shape=jax.ShapeDtypeStruct((8,) +...  40 us
    dot_general x5, matrix products, dot(): lax.dot_general(left, right, (((left_dim,), (right_dim,)), ((), ())), pre...  26.8 us
    pallas_call x1, Pallas kernels, group_scatter(): pl.pallas_call(group_scatter_kernel, out_shape=jax.ShapeDtypeStruct(block...  21.3 us
    pallas_call x1, Pallas kernels, attend_back(): pl.pallas_call(functools.partial(attend_back_kernel, slot_len, head), out...  18.5 us
    pallas_call x1, Pallas kernels, feed_down(): pl.pallas_call(functools.partial(feed_down_kernel, len(pairs), len(fcs)),...  18.3 us
    pallas_call x1, Pallas kernels, attend(): pl.pallas_call(functools.partial(attend_kernel, slot_len, head), out_shap...  17.6 us
  transfers between devices with their start and end apart: 13, of which 3 were waited for; matrix products, arithmetic and copies ran while one was open for 10% of the time, Pallas kernels for 57%

profile of v9, /device:TPU:0, one launch (start us, length us, event | category | flops | bytes accessed | tf_op | source)
XLA Modules:
  0.0 513.1 jit_solution(14016133365776067701)
XLA Ops:
  8.5 4.8 prepare.1
  13.2 99.5 %opening.1 = (bf16[16,128,1792]{2,1,0:T(8,128)(2,1)}, bf16[2,8,112,384]{3,2,1,0:T(8,128)(2,1)}, bf16[2,4,112,800]{3,2,1,0:T(8,128)(2,1)}, bf16[8,112,896]{2,1,0:T(8,128)(2,1)}) custom-call(bf16[128,1792]{1,0:T(8,128)(2,1)} %get-tuple-element.85.own.x_ref, bf16[8,112,384]{2,1,0:T(8,128)(2,1)} %get-tuple-element.86.blocks, ...), custom_call_target="tpu_custom_call" | custom-call | tf_op jit(solution)/shard_map/opening/pallas_call | solution.py:578
  116.7 13.5 %project.1 = (bf16[2048,1792]{1,0:T(8,128)(2,1)}, bf16[2048,384]{1,0:T(8,128)(2,1)}, f32[8,1792]{1,0:T(8,128)}) custom-call(s32[1]{0:T(128)} %bitcast.24.at_ref, bf16[2048,1792]{1,0:T(8,128)(2,1)} %bitcast.104, bf16[16,112,384]{2,1,0:T(8,128)(2,1)} %bitcast.114, f32[1,1792]{1,0:T(1,128)} %constant.111.mask_ref.mask, bf16[1792,384]{1,0:T(8,128)(2,1)} %bitcast.115), custom_call_target="tpu_custom_call" | custom-call | tf_op jit(solution)/shard_map/project/pallas_call | solution.py:1103
  131.3 17.6 %attend.1 = (bf16[2048,128]{1,0:T(8,128)(2,1)}, f32[8,2,256]{2,1,0:T(2,128)}) custom-call(s32[16]{0:T(128)} %copy-done.20, s32[8]{0:T(128)} %and_select_fusion.low_ref, bf16[2048,384]{1,0:T(8,128)(2,1)} %get-tuple-element.94.qkv_ref, s32[8,1,256]{2,1,0:T(1,128)} %bitcast.134), custom_call_target="tpu_custom_call" | custom-call | tf_op jit(solution)/shard_map/attend/pallas_call | solution.py:167
  148.9 2.8 collective-permute-done.refs_2_
  151.8 12.4 %to_tokens.1.att = bf16[128,2048]{1,0:T(8,128)(2,1)} custom-call(bf16[16,128,128]{2,1,0:T(8,128)(2,1)} %bitcast.125), custom_call_target="tpu_custom_call" | custom-call | tf_op jit(solution)/shard_map/to_tokens/pallas_call | solution.py:614
  164.1 4.3 collective-permute-start.3
  168.4 3.5 collective-permute-start.2
  173.8 5.6 %hidden_forward.1 = (bf16[2,128,896]{2,1,0:T(8,128)(2,1)}, f32[128,1792]{1,0:T(8,128)}, bf16[128,1792]{1,0:T(8,128)(2,1)}) custom-call(bf16[128,2048]{1,0:T(8,128)(2,1)} %to_tokens.1.att, bf16[2,2,896,896]{3,2,1,0:T(8,128)(2,1)} %bitcast.106, bf16[128,1792]{1,0:T(8,128)(2,1)} %get-tuple-element.85.own.x_ref, f32[8,1792]{1,0:T(8,128)} %get-tuple-element.102.single, ...), custom_call_target="tpu_custom_call" | custom-call | tf_op jit(solution)/shard_map/hidden_forward/pallas_call | solution.py:1236
  179.4 40.0 %group_gather.1 = bf16[8,128,1792]{2,1,0:T(8,128)(2,1)} custom-call(bf16[128,1792]{1,0:T(8,128)(2,1)} %get-tuple-element.103.own), custom_call_target="tpu_custom_call" | custom-call | tf_op jit(solution)/shard_map/group_gather/pallas_call | solution.py:502
  220.9 10.8 %feed_up.1 = (bf16[1024,800]{1,0:T(8,128)(2,1)}, f32[1024,800]{1,0:T(8,128)}) custom-call(s32[4]{0:T(128)} %pad_add_fusion.at_ref, bf16[2,448,800]{2,1,0:T(8,128)(2,1)} %bitcast.110, bf16[2,448,800]{2,1,0:T(8,128)(2,1)} %copy-done.8, bf16[448,800]{1,0:T(8,128)(2,1)} %collective-permute-done.refs_2_, bf16[448,800]{1,0:T(8,128)(2,1)} %copy-done.13, ...), custom_call_target="tpu_custom_call" | custom-call | tf_op jit(solution)/shard_map/feed_up/pallas_call | solution.py:1324
  231.8 6.6 %convolution_convert_fusion.3 = bf16[1792,800]{1,0:T(8,128)(2,1)S(1)} fusion(bf16[1024,1792]{1,0:T(8,128)(2,1)} %all-gather.3.cloned.1.call-done.refs_6_, bf16[1024,800]{1,0:T(8,128)(2,1)} %get-tuple-element.108.refs_7_), kind=kOutput, calls=%fused_computation.4 | convolution fusion | flops 2937446400 | bytes 8175616 | tf_op jit(solution)/shard_map/dot_general | solution.py:59
  239.8 1.5 collective-permute-start.4
  242.2 18.3 %feed_down.1 = (bf16[1024,800]{1,0:T(8,128)(2,1)}, bf16[1024,1792]{1,0:T(8,128)(2,1)}, bf16[1024,1792]{1,0:T(8,128)(2,1)}, f32[1,800]{1,0:T(1,128)}) custom-call(s32[4]{0:T(128)} %pad_add_fusion.at_ref, bf16[2,448,800]{2,1,0:T(8,128)(2,1)} %bitcast.111, bf16[2,448,800]{2,1,0:T(8,128)(2,1)} %copy-done.8, bf16[448,800]{1,0:T(8,128)(2,1)} %collective-permute-done.refs_2_, ...), custom_call_target="tpu_custom_call" | custom-call | tf_op jit(solution)/shard_map/feed_down/pallas_call | solution.py:1368
  260.5 6.9 %convolution_convert_fusion.2 = bf16[1792,800]{1,0:T(8,128)(2,1)} fusion(bf16[1024,1792]{1,0:T(8,128)(2,1)S(1)} %bitcast.109, bf16[1024,800]{1,0:T(8,128)(2,1)} %get-tuple-element.111), kind=kOutput, calls=%fused_computation.3 | convolution fusion | flops 2937446400 | bytes 8175616 | tf_op jit(solution)/shard_map/dot_general | solution.py:59
  267.4 21.3 %group_scatter.1.dnorm_ref = f32[128,1792]{1,0:T(8,128)} custom-call(bf16[8,128,1792]{2,1,0:T(8,128)(2,1)} %bitcast.118), custom_call_target="tpu_custom_call" | custom-call | tf_op jit(solution)/shard_map/group_scatter/pallas_call | solution.py:778
  288.8 7.0 %hidden_back.1 = (f32[128,1792]{1,0:T(8,128)}, bf16[128,1792]{1,0:T(8,128)(2,1)}, f32[4,1792]{1,0:T(4,128)}, bf16[128,2048]{1,0:T(8,128)(2,1)}) custom-call(f32[128,1792]{1,0:T(8,128)} %group_scatter.1.dnorm_ref, f32[128,1792]{1,0:T(8,128)} %get-tuple-element.118.hidden, bf16[128,1792]{1,0:T(8,128)(2,1)} %get-tuple-element.90.grad_ref, ...), custom_call_target="tpu_custom_call" | custom-call | tf_op jit(solution)/shard_map/hidden_back/pallas_call | solution.py:1275
  295.8 3.9 convolution_convert_fusion.1
  302.4 14.4 %to_heads.1 = bf16[16,128,128]{2,1,0:T(8,128)(2,1)} custom-call(bf16[128,2048]{1,0:T(8,128)(2,1)} %get-tuple-element.120.src), custom_call_target="tpu_custom_call" | custom-call | tf_op jit(solution)/shard_map/to_heads/pallas_call | solution.py:645
  316.8 1.7 bitcast_add_fusion.1
  319.5 2.5 collective-permute-start.6
  323.1 15.8 %collective-permute-done.8 = bf16[2,448,800]{2,1,0:T(8,128)(2,1)} collective-permute-done((bf16[2,448,800]{2,1,0:T(8,128)(2,1)}, bf16[2,448,800]{2,1,0:T(8,128)(2,1)}, u32[]{:S(2)}, u32[]{:S(2)}) %collective-permute-start.8) | collective-permute-done | bytes 1433632 | tf_op jit(solution)/shard_map/ppermute | solution.py:1495
  338.9 1.6 bitcast_add_fusion
  342.6 3.1 collective-permute-start.9
  345.7 18.5 %attend_back.1.grad_ref = f32[2048,384]{1,0:T(8,128)} custom-call(s32[16]{0:T(128)} %copy-done.20, s32[8]{0:T(128)} %and_select_fusion.low_ref, bf16[2048,384]{1,0:T(8,128)(2,1)} %get-tuple-element.94.qkv_ref, bf16[2048,128]{1,0:T(8,128)(2,1)} %get-tuple-element.98.out_ref, bf16[2048,128]{1,0:T(8,128)(2,1)} %bitcast.126, ...), custom_call_target="tpu_custom_call" | custom-call | tf_op jit(solution)/shard_map/attend_back/pallas_call | solution.py:265
  364.2 13.0 %project_back.1 = (bf16[2048,1792]{1,0:T(8,128)(2,1)}, bf16[2048,384]{1,0:T(8,128)(2,1)}, f32[1,1792]{1,0:T(1,128)}, f32[1,1792]{1,0:T(1,128)}, f32[1,384]{1,0:T(1,128)}) custom-call(bf16[2048,1792]{1,0:T(8,128)(2,1)} %bitcast.105, f32[2048,384]{1,0:T(8,128)} %attend_back.1.grad_ref, f32[1,1792]{1,0:T(1,128)} %constant.111.mask_ref.mask, ...), custom_call_target="tpu_custom_call" | custom-call | tf_op jit(solution)/shard_map/project_back/pallas_call | solution.py:1156
  377.2 4.7 add.111
  381.9 8.3 %convolution_convert_fusion.4 = bf16[1792,384]{1,0:T(8,128)(2,1)} fusion(bf16[2048,1792]{1,0:T(8,128)(2,1)} %get-tuple-element.126, bf16[2048,384]{1,0:T(8,128)(2,1)S(1)} %copy-done.21), kind=kOutput, calls=%fused_computation.5 | convolution fusion | flops 2819260416 | bytes 10289152 | tf_op jit(solution)/shard_map/dot_general | solution.py:59
  390.2 2.3 collective-permute-done.9
  392.6 2.7 fusion
  395.3 99.2 %closing.1 = (f32[128,1792]{1,0:T(8,128)}, bf16[2,8,112,384]{3,2,1,0:T(8,128)(2,1)}, bf16[2,112,896]{2,1,0:T(8,128)(2,1)}, bf16[4,112,800]{2,1,0:T(8,128)(2,1)},...) custom-call(bf16[16,128,1792]{2,1,0:T(8,128)(2,1)} %bitcast.117, ...), custom_call_target="tpu_custom_call" | custom-call | tf_op jit(solution)/shard_map/closing/pallas_call | solution.py:949
  498.9 7.2 %deliver.1 = (f32[100,4800]{1,0:T(8,128)}, f32[100,1600]{1,0:T(8,128)}, f32[100,3200]{1,0:T(8,128)}, f32[100,3200]{1,0:T(8,128)}, f32[1600,128]{1,0:T(8,128)}, /*index=5*/f32[1600,128]{1,0:T(8,128)}) custom-call(bf16[2,8,112,384]{3,2,1,0:T(8,128)(2,1)} %get-tuple-element.136.qkv, bf16[2,112,896]{2,1,0:T(8,128)(2,1)} %get-tuple-element.137.out_w, ...), custom_call_target="tpu_custom_call" | custom-call | tf_op jit(solution)/shard_map/deliver/pallas_call | solution.py:1199
  (96 shorter events, 23.2 us)
Async XLA Ops:
  7.2 109.0 %copy-start = (s32[1,2048]{1,0:T(1,128)S(1)}, s32[1,2048]{1,0:T(1,128)}, u32[]{:S(2)}) copy-start(s32[1,2048]{1,0:T(1,128)} %param.18) | copy-start | bytes 24580
  7.2 166.6 %all-gather.5.cloned.1.call-start = ((), (), s32[]{:S(2)}) async-start(), calls=%async_computation.2 | async-start | bytes 8028160 | tf_op jit(solution)/shard_map/all_gather | solution.py:1437
  112.7 1.4 copy-start.3
  112.8 119.0 %all-gather.3.cloned.1.call-start = ((), (), s32[]{:S(2)}) async-start(), calls=%async_computation.1 | async-start | bytes 4128768 | tf_op jit(solution)/shard_map/all_gather | solution.py:1416
  112.8 3.2 copy-start.22
  113.5 385.3 %reduce-scatter.2.cloned.1.call-start = ((), (), s32[]{:S(2)}) async-start(), calls=%async_computation.3 | async-start | bytes 4128768 | tf_op jit(solution)/shard_map/reduce_scatter | solution.py:1512
  115.4 36.3 %collective-permute-start = (bf16[448,800]{1,0:T(8,128)(2,1)}, bf16[448,800]{1,0:T(8,128)(2,1)}, u32[]{:S(2)}, u32[]{:S(2)}) collective-permute-start(bf16[448,800]{1,0:T(8,128)(2,1)} %bitcast.17), channel_id=1, source_target_pairs={{0,8},{8,0},{1,9},{9,1},{2,10},{10,2},{3,11},{11,3},{4,12},{12,4},... | collective-permute-start | bytes 2150408 | tf_op jit(solution)/shard_map/ppermute | solution.py:1433
  115.4 36.3 %collective-permute-start.1 = (bf16[2,448,800]{2,1,0:T(8,128)(2,1)S(1)}, bf16[2,448,800]{2,1,0:T(8,128)(2,1)S(1)}, u32[]{:S(2)}, u32[]{:S(2)}) collective-permute-start(bf16[2,448,800]{2,1,0:T(8,128)(2,1)S(1)} %bitcast.112), channel_id=1, source_target_pairs={{0,16},{16,0},{1,17},{17,1},{2,18},{18,2},{3,19},{19,3},{4,20},{20... | collective-permute-start | bytes 4300808 | tf_op jit(solution)/shard_map/ppermute | solution.py:1434
  116.1 14.1 %copy-start.20 = (s32[16]{0:T(128)}, s32[16]{0:T(128)S(1)}, u32[]{:S(2)}) copy-start(s32[16]{0:T(128)S(1)} %select_reduce_fusion.1.inv_ref) | copy-start | bytes 196
  151.8 27.6 %copy-start.8 = (bf16[2,448,800]{2,1,0:T(8,128)(2,1)}, bf16[2,448,800]{2,1,0:T(8,128)(2,1)S(1)}, u32[]{:S(2)}) copy-start(bf16[2,448,800]{2,1,0:T(8,128)(2,1)S(1)} %collective-permute-done.1.refs_1_) | copy-start | bytes 4300804
  164.1 55.2 %collective-permute-start.3 = (bf16[448,800]{1,0:T(8,128)(2,1)}, bf16[448,800]{1,0:T(8,128)(2,1)S(1)}, u32[]{:S(2)}, u32[]{:S(2)}) collective-permute-start(bf16[448,800]{1,0:T(8,128)(2,1)} %bitcast.129), channel_id=1, source_target_pairs={{0,8},{8,0},{1,9},{9,1},{2,10},{10,2},{3,11},{11,3},{4,12},{12,4},... | collective-permute-start | bytes 2150408 | tf_op jit(solution)/shard_map/ppermute | solution.py:1462
  168.4 51.6 %collective-permute-start.2 = (bf16[448,800]{1,0:T(8,128)(2,1)}, bf16[448,800]{1,0:T(8,128)(2,1)S(1)}, u32[]{:S(2)}, u32[]{:S(2)}) collective-permute-start(bf16[448,800]{1,0:T(8,128)(2,1)} %collective-permute-done.refs_2_), channel_id=1, source_target_pairs={{0,16},{16,0},{1,17},{17,1},{2,18},{18,2},{3,19},{19,3},{4,20},{20... | collective-permute-start | bytes 2150408 | tf_op jit(solution)/shard_map/ppermute | solution.py:1459
  219.4 19.0 %copy-start.15 = (bf16[448,800]{1,0:T(8,128)(2,1)}, bf16[448,800]{1,0:T(8,128)(2,1)S(1)}, u32[]{:S(2)}) copy-start(bf16[448,800]{1,0:T(8,128)(2,1)S(1)} %collective-permute-done.3.refs_4_) | copy-start | bytes 2150404
  219.4 21.9 %collective-permute-start.5 = (bf16[448,800]{1,0:T(8,128)(2,1)S(1)}, bf16[448,800]{1,0:T(8,128)(2,1)S(1)}, u32[]{:S(2)}, u32[]{:S(2)}) collective-permute-start(bf16[448,800]{1,0:T(8,128)(2,1)S(1)} %collective-permute-done.3.refs_4_), channel_id=1, source_target_pairs={{0,16},{16,0},{1,17},{17,1},{2,18},{18,2},{3,19},{19,3},{4,20},{20... | collective-permute-start | bytes 2150408 | tf_op jit(solution)/shard_map/ppermute | solution.py:1468
  238.4 2.9 copy-start.9
  239.8 48.9 %collective-permute-start.4 = (bf16[2,448,800]{2,1,0:T(8,128)(2,1)}, bf16[2,448,800]{2,1,0:T(8,128)(2,1)}, u32[]{:S(2)}, u32[]{:S(2)}) collective-permute-start(bf16[2,448,800]{2,1,0:T(8,128)(2,1)} %dynamic-slice_bitcast_fusion.1), channel_id=1, source_target_pairs={{0,16},{16,0},{1,17},{17,1},{2,18},{18,2},{3,19},{19,3},{4,20},{20... | collective-permute-start | bytes 4300808 | tf_op jit(solution)/shard_map/ppermute | solution.py:1491
  242.2 18.3 %copy-start.2 = (bf16[8,128,1792]{2,1,0:T(8,128)(2,1)S(1)}, bf16[8,128,1792]{2,1,0:T(8,128)(2,1)}, u32[]{:S(2)}) copy-start(bf16[8,128,1792]{2,1,0:T(8,128)(2,1)} %group_gather.1) | copy-start | bytes 11010052
  288.8 7.0 %copy-start.17 = (bf16[2,128,896]{2,1,0:T(8,128)(2,1)S(1)}, bf16[2,128,896]{2,1,0:T(8,128)(2,1)}, u32[]{:S(2)}) copy-start(bf16[2,128,896]{2,1,0:T(8,128)(2,1)} %get-tuple-element.116) | copy-start | bytes 1376260
  295.8 3.9 copy-start.11
  299.7 17.1 %copy-start.10 = (bf16[1792,800]{1,0:T(8,128)(2,1)S(1)}, bf16[1792,800]{1,0:T(8,128)(2,1)}, u32[]{:S(2)}) copy-start(bf16[1792,800]{1,0:T(8,128)(2,1)} %copy-done.9) | copy-start | bytes 8601604
  299.7 39.2 %collective-permute-start.7 = (bf16[896,1792]{1,0:T(8,128)(2,1)}, bf16[896,1792]{1,0:T(8,128)(2,1)}, u32[]{:S(2)}, u32[]{:S(2)}) collective-permute-start(bf16[896,1792]{1,0:T(8,128)(2,1)} %convolution_convert_fusion.1), channel_id=1, source_target_pairs={{0,2},{2,0},{1,3},{3,1},{4,6},{6,4},{5,7},{7,5},{8,10},{10,8},{9,1... | collective-permute-start | bytes 9633800 | tf_op jit(solution)/shard_map/ppermute | solution.py:1518
  301.0 37.8 %collective-permute-start.8 = (bf16[2,448,800]{2,1,0:T(8,128)(2,1)}, bf16[2,448,800]{2,1,0:T(8,128)(2,1)}, u32[]{:S(2)}, u32[]{:S(2)}) collective-permute-start(bf16[2,448,800]{2,1,0:T(8,128)(2,1)} %dynamic-slice_bitcast_fusion), channel_id=1, source_target_pairs={{0,16},{16,0},{1,17},{17,1},{2,18},{18,2},{3,19},{19,3},{4,20},{20... | collective-permute-start | bytes 4300808 | tf_op jit(solution)/shard_map/ppermute | solution.py:1495
  316.8 5.2 %copy-start.18 = (bf16[2,128,896]{2,1,0:T(8,128)(2,1)S(1)}, bf16[2,128,896]{2,1,0:T(8,128)(2,1)}, u32[]{:S(2)}) copy-start(bf16[2,128,896]{2,1,0:T(8,128)(2,1)} %get-tuple-element.116) | copy-start | bytes 1376260
  318.5 4.5 copy-start.4
  318.5 3.5 copy-start.14
  319.5 19.3 %copy-start.12 = (bf16[1792,800]{1,0:T(8,128)(2,1)S(1)}, bf16[1792,800]{1,0:T(8,128)(2,1)}, u32[]{:S(2)}) copy-start(bf16[1792,800]{1,0:T(8,128)(2,1)} %convolution_convert_fusion.2) | copy-start | bytes 8601604
  319.5 70.7 %collective-permute-start.6 = (bf16[448,800]{1,0:T(8,128)(2,1)}, bf16[448,800]{1,0:T(8,128)(2,1)S(1)}, u32[]{:S(2)}, u32[]{:S(2)}) collective-permute-start(bf16[448,800]{1,0:T(8,128)(2,1)} %dynamic-slice_bitcast_fusion.3), channel_id=1, source_target_pairs={{0,8},{8,0},{1,9},{9,1},{2,10},{10,2},{3,11},{11,3},{4,12},{12,4},... | collective-permute-start | bytes 2150408 | tf_op jit(solution)/shard_map/ppermute | solution.py:1501
  342.6 50.0 %collective-permute-start.9 = (bf16[448,800]{1,0:T(8,128)(2,1)}, bf16[448,800]{1,0:T(8,128)(2,1)}, u32[]{:S(2)}, u32[]{:S(2)}) collective-permute-start(bf16[448,800]{1,0:T(8,128)(2,1)} %dynamic-slice_bitcast_fusion.2), channel_id=1, source_target_pairs={{0,8},{8,0},{1,9},{9,1},{2,10},{10,2},{3,11},{11,3},{4,12},{12,4},... | collective-permute-start | bytes 2150408 | tf_op jit(solution)/shard_map/ppermute | solution.py:1501
  377.2 4.7 copy-start.21
  381.9 10.7 %copy-start.5 = (bf16[2,448,800]{2,1,0:T(8,128)(2,1)S(1)}, bf16[2,448,800]{2,1,0:T(8,128)(2,1)}, u32[]{:S(2)}) copy-start(bf16[2,448,800]{2,1,0:T(8,128)(2,1)} %copy-done.4) | copy-start | bytes 4300804
  381.9 10.7 %copy-start.7 = (bf16[2,448,800]{2,1,0:T(8,128)(2,1)S(1)}, bf16[2,448,800]{2,1,0:T(8,128)(2,1)}, u32[]{:S(2)}) copy-start(bf16[2,448,800]{2,1,0:T(8,128)(2,1)} %copy-done.6) | copy-start | bytes 4300804
  498.8 7.3 %copy-start.1 = (s32[1,2048]{1,0:T(1,128)S(1)}, s32[1,2048]{1,0:T(1,128)}, u32[]{:S(2)}) copy-start(s32[1,2048]{1,0:T(1,128)} %param.18) | copy-start | bytes 24580
  (4 other events, 3.7 us)
Sparse Core Ops, SparseCore 0:
  112.9 50.5 all-gather.4
  165.6 56.1 all-gather.2
  288.9 83.6 reduce-scatter.1

commit v10 on v9

--- a/solution.py
+++ b/solution.py
@@ -1095,7 +1095,7 @@
 def project(slot_at, x, packed, mask, rows, feats, padded):
     total, wide = x.shape
     cols = packed.shape[2]
-    step = min(256, total)
+    step = min(512, total)
 
     def fixed(shape):
         return pl.BlockSpec(shape, lambda i: (0,) * len(shape))
@@ -1145,7 +1145,7 @@
 def project_back(x, grad, mask, weight, feats):
     total, wide = x.shape
     cols = weight.shape[1]
-    step = min(256, total)
+    step = min(512, total)
 
     def fixed(shape):
         return pl.BlockSpec(shape, lambda i: (0,) * len(shape))

time: 516 us -> 524 us (1.016); the launches traced: 513 us -> 515 us
  Pallas kernels: 403 us -> 413 us
    pallas_call x1, Pallas kernels: 17.6 us -> 22.9 us  [attend(): pl.pallas_call(functools.partial(attend_kernel, slot_len, head), out_shap...]
  transfers between devices with their start and end apart: 13 -> 13, of which waited for: 3 -> 1; matrix products, arithmetic and copies ran while one was open for 10% -> 10% of each run, Pallas kernels for 57% -> 59%
where the time goes in v10:
time: 524 us; the launch traced here: 515 us
  Pallas kernels  413 us (79%)
  matrix products  27 us (5%)
  local copies, waits for them, and re-layouts  16.9 us (3%)
  waiting for transfers between devices  16.5 us (3%)
  between operations  14.6 us (3%)
  starting transfers between devices  13.9 us (3%)
  other arithmetic  13.1 us (2%)
    pallas_call x1, Pallas kernels, opening(): pl.pallas_call(opening_kernel, out_shape=(jax.ShapeDtypeStruct((2 * n_ctx...  99.5 us
    pallas_call x1, Pallas kernels, closing(): pl.pallas_call(closing_kernel, out_shape=(jax.ShapeDtypeStruct(block, F32...  97.9 us
    pallas_call x1, Pallas kernels, group_gather(): pl.pallas_call(group_gather_kernel, out_shape=jax.ShapeDtypeStruct((8,) +...  40.7 us
    dot_general x5, matrix products, dot(): lax.dot_general(left, right, (((left_dim,), (right_dim,)), ((), ())), pre...  27 us
    pallas_call x1, Pallas kernels, attend_back(): pl.pallas_call(functools.partial(attend_back_kernel, slot_len, head), out...  22.9 us
    pallas_call x1, Pallas kernels, attend(): pl.pallas_call(functools.partial(attend_kernel, slot_len, head), out_shap...  22.9 us
    pallas_call x1, Pallas kernels, group_scatter(): pl.pallas_call(group_scatter_kernel, out_shape=jax.ShapeDtypeStruct(block...  21.5 us
    pallas_call x1, Pallas kernels, feed_down(): pl.pallas_call(functools.partial(feed_down_kernel, len(pairs), len(fcs)),...  18 us
  transfers between devices with their start and end apart: 13, of which 1 were waited for; matrix products, arithmetic and copies ran while one was open for 10% of the time, Pallas kernels for 59%

profile of v10, /device:TPU:0, one launch (start us, length us, event | category | flops | bytes accessed | tf_op | source)
XLA Modules:
  0.0 514.8 jit_solution(17665358456923787134)
XLA Ops:
  8.5 4.8 prepare.1
  13.2 99.5 %opening.1 = (bf16[16,128,1792]{2,1,0:T(8,128)(2,1)}, bf16[2,8,112,384]{3,2,1,0:T(8,128)(2,1)}, bf16[2,4,112,800]{3,2,1,0:T(8,128)(2,1)}, bf16[8,112,896]{2,1,0:T(8,128)(2,1)}) custom-call(bf16[128,1792]{1,0:T(8,128)(2,1)} %get-tuple-element.85.own.x_ref, bf16[8,112,384]{2,1,0:T(8,128)(2,1)} %get-tuple-element.86.blocks, ...), custom_call_target="tpu_custom_call" | custom-call | tf_op jit(solution)/shard_map/opening/pallas_call | solution.py:578
  116.7 12.8 %project.1 = (bf16[2048,1792]{1,0:T(8,128)(2,1)}, bf16[2048,384]{1,0:T(8,128)(2,1)}, f32[8,1792]{1,0:T(8,128)}) custom-call(s32[1]{0:T(128)} %bitcast.24.at_ref, bf16[2048,1792]{1,0:T(8,128)(2,1)} %bitcast.104, bf16[16,112,384]{2,1,0:T(8,128)(2,1)} %bitcast.114, f32[1,1792]{1,0:T(1,128)} %constant.111.mask_ref.mask, bf16[1792,384]{1,0:T(8,128)(2,1)} %bitcast.115), custom_call_target="tpu_custom_call" | custom-call | tf_op jit(solution)/shard_map/project/pallas_call | solution.py:1103
  130.6 22.9 %attend.1 = (bf16[2048,128]{1,0:T(8,128)(2,1)}, f32[8,2,256]{2,1,0:T(2,128)}) custom-call(s32[16]{0:T(128)} %copy-done.20, s32[8]{0:T(128)} %and_select_fusion.low_ref, bf16[2048,384]{1,0:T(8,128)(2,1)} %get-tuple-element.94.qkv_ref, s32[8,1,256]{2,1,0:T(1,128)} %bitcast.134), custom_call_target="tpu_custom_call" | custom-call | tf_op jit(solution)/shard_map/attend/pallas_call | solution.py:167
  153.5 14.0 %to_tokens.1.att = bf16[128,2048]{1,0:T(8,128)(2,1)} custom-call(bf16[16,128,128]{2,1,0:T(8,128)(2,1)} %bitcast.125), custom_call_target="tpu_custom_call" | custom-call | tf_op jit(solution)/shard_map/to_tokens/pallas_call | solution.py:614
  167.5 4.2 collective-permute-start.3
  173.7 5.4 %hidden_forward.1 = (bf16[2,128,896]{2,1,0:T(8,128)(2,1)}, f32[128,1792]{1,0:T(8,128)}, bf16[128,1792]{1,0:T(8,128)(2,1)}) custom-call(bf16[128,2048]{1,0:T(8,128)(2,1)} %to_tokens.1.att, bf16[2,2,896,896]{3,2,1,0:T(8,128)(2,1)} %bitcast.106, bf16[128,1792]{1,0:T(8,128)(2,1)} %get-tuple-element.85.own.x_ref, f32[8,1792]{1,0:T(8,128)} %get-tuple-element.102.single, ...), custom_call_target="tpu_custom_call" | custom-call | tf_op jit(solution)/shard_map/hidden_forward/pallas_call | solution.py:1236
  179.1 40.7 %group_gather.1 = bf16[8,128,1792]{2,1,0:T(8,128)(2,1)} custom-call(bf16[128,1792]{1,0:T(8,128)(2,1)} %get-tuple-element.103.own), custom_call_target="tpu_custom_call" | custom-call | tf_op jit(solution)/shard_map/group_gather/pallas_call | solution.py:502
  219.9 1.9 collective-permute-start.5
  222.7 10.9 %feed_up.1 = (bf16[1024,800]{1,0:T(8,128)(2,1)}, f32[1024,800]{1,0:T(8,128)}) custom-call(s32[4]{0:T(128)} %pad_add_fusion.at_ref, bf16[2,448,800]{2,1,0:T(8,128)(2,1)} %bitcast.110, bf16[2,448,800]{2,1,0:T(8,128)(2,1)} %copy-done.8, bf16[448,800]{1,0:T(8,128)(2,1)} %collective-permute-done.refs_2_, bf16[448,800]{1,0:T(8,128)(2,1)} %copy-done.13, ...), custom_call_target="tpu_custom_call" | custom-call | tf_op jit(solution)/shard_map/feed_up/pallas_call | solution.py:1324
  233.7 6.6 %convolution_convert_fusion.3 = bf16[1792,800]{1,0:T(8,128)(2,1)S(1)} fusion(bf16[1024,1792]{1,0:T(8,128)(2,1)} %all-gather.3.cloned.1.call-done.refs_6_, bf16[1024,800]{1,0:T(8,128)(2,1)} %get-tuple-element.108.refs_7_), kind=kOutput, calls=%fused_computation.4 | convolution fusion | flops 2937446400 | bytes 8175616 | tf_op jit(solution)/shard_map/dot_general | solution.py:59
  240.3 1.4 dynamic-slice_bitcast_fusion.1
  243.3 18.0 %feed_down.1 = (bf16[1024,800]{1,0:T(8,128)(2,1)}, bf16[1024,1792]{1,0:T(8,128)(2,1)}, bf16[1024,1792]{1,0:T(8,128)(2,1)}, f32[1,800]{1,0:T(1,128)}) custom-call(s32[4]{0:T(128)} %pad_add_fusion.at_ref, bf16[2,448,800]{2,1,0:T(8,128)(2,1)} %bitcast.111, bf16[2,448,800]{2,1,0:T(8,128)(2,1)} %copy-done.8, bf16[448,800]{1,0:T(8,128)(2,1)} %collective-permute-done.refs_2_, ...), custom_call_target="tpu_custom_call" | custom-call | tf_op jit(solution)/shard_map/feed_down/pallas_call | solution.py:1368
  261.4 7.1 %convolution_convert_fusion.2 = bf16[1792,800]{1,0:T(8,128)(2,1)} fusion(bf16[1024,1792]{1,0:T(8,128)(2,1)S(1)} %bitcast.109, bf16[1024,800]{1,0:T(8,128)(2,1)} %get-tuple-element.111), kind=kOutput, calls=%fused_computation.3 | convolution fusion | flops 2937446400 | bytes 8175616 | tf_op jit(solution)/shard_map/dot_general | solution.py:59
  268.5 21.5 %group_scatter.1.dnorm_ref = f32[128,1792]{1,0:T(8,128)} custom-call(bf16[8,128,1792]{2,1,0:T(8,128)(2,1)} %bitcast.118), custom_call_target="tpu_custom_call" | custom-call | tf_op jit(solution)/shard_map/group_scatter/pallas_call | solution.py:778
  290.1 7.0 %hidden_back.1 = (f32[128,1792]{1,0:T(8,128)}, bf16[128,1792]{1,0:T(8,128)(2,1)}, f32[4,1792]{1,0:T(4,128)}, bf16[128,2048]{1,0:T(8,128)(2,1)}) custom-call(f32[128,1792]{1,0:T(8,128)} %group_scatter.1.dnorm_ref, f32[128,1792]{1,0:T(8,128)} %get-tuple-element.118.hidden, bf16[128,1792]{1,0:T(8,128)(2,1)} %get-tuple-element.90.grad_ref, ...), custom_call_target="tpu_custom_call" | custom-call | tf_op jit(solution)/shard_map/hidden_back/pallas_call | solution.py:1275
  297.1 3.9 convolution_convert_fusion.1
  301.0 1.3 dynamic-slice_bitcast_fusion
  303.4 14.8 %to_heads.1 = bf16[16,128,128]{2,1,0:T(8,128)(2,1)} custom-call(bf16[128,2048]{1,0:T(8,128)(2,1)} %get-tuple-element.120.src), custom_call_target="tpu_custom_call" | custom-call | tf_op jit(solution)/shard_map/to_heads/pallas_call | solution.py:645
  318.2 1.7 bitcast_add_fusion.1
  320.9 2.5 collective-permute-start.6
  324.5 15.7 %collective-permute-done.8 = bf16[2,448,800]{2,1,0:T(8,128)(2,1)} collective-permute-done((bf16[2,448,800]{2,1,0:T(8,128)(2,1)}, bf16[2,448,800]{2,1,0:T(8,128)(2,1)}, u32[]{:S(2)}, u32[]{:S(2)}) %collective-permute-start.8) | collective-permute-done | bytes 1433632 | tf_op jit(solution)/shard_map/ppermute | solution.py:1495
  340.2 1.6 bitcast_add_fusion
  343.9 3.4 collective-permute-start.9
  347.3 22.9 %attend_back.1.grad_ref = f32[2048,384]{1,0:T(8,128)} custom-call(s32[16]{0:T(128)} %copy-done.20, s32[8]{0:T(128)} %and_select_fusion.low_ref, bf16[2048,384]{1,0:T(8,128)(2,1)} %get-tuple-element.94.qkv_ref, bf16[2048,128]{1,0:T(8,128)(2,1)} %get-tuple-element.98.out_ref, bf16[2048,128]{1,0:T(8,128)(2,1)} %bitcast.126, ...), custom_call_target="tpu_custom_call" | custom-call | tf_op jit(solution)/shard_map/attend_back/pallas_call | solution.py:265
  370.2 12.3 %project_back.1 = (bf16[2048,1792]{1,0:T(8,128)(2,1)}, bf16[2048,384]{1,0:T(8,128)(2,1)}, f32[1,1792]{1,0:T(1,128)}, f32[1,1792]{1,0:T(1,128)}, f32[1,384]{1,0:T(1,128)}) custom-call(bf16[2048,1792]{1,0:T(8,128)(2,1)} %bitcast.105, f32[2048,384]{1,0:T(8,128)} %attend_back.1.grad_ref, f32[1,1792]{1,0:T(1,128)} %constant.111.mask_ref.mask, ...), custom_call_target="tpu_custom_call" | custom-call | tf_op jit(solution)/shard_map/project_back/pallas_call | solution.py:1156
  382.5 4.7 add.111
  387.2 8.3 %convolution_convert_fusion.4 = bf16[1792,384]{1,0:T(8,128)(2,1)} fusion(bf16[2048,1792]{1,0:T(8,128)(2,1)} %get-tuple-element.126, bf16[2048,384]{1,0:T(8,128)(2,1)S(1)} %copy-done.21), kind=kOutput, calls=%fused_computation.5 | convolution fusion | flops 2819260416 | bytes 10289152 | tf_op jit(solution)/shard_map/dot_general | solution.py:59
  395.6 2.7 fusion
  398.3 97.9 %closing.1 = (f32[128,1792]{1,0:T(8,128)}, bf16[2,8,112,384]{3,2,1,0:T(8,128)(2,1)}, bf16[2,112,896]{2,1,0:T(8,128)(2,1)}, bf16[4,112,800]{2,1,0:T(8,128)(2,1)},...) custom-call(bf16[16,128,1792]{2,1,0:T(8,128)(2,1)} %bitcast.117, ...), custom_call_target="tpu_custom_call" | custom-call | tf_op jit(solution)/shard_map/closing/pallas_call | solution.py:949
  499.1 1.4 slice_bitcast_fusion
  500.6 7.2 %deliver.1 = (f32[100,4800]{1,0:T(8,128)}, f32[100,1600]{1,0:T(8,128)}, f32[100,3200]{1,0:T(8,128)}, f32[100,3200]{1,0:T(8,128)}, f32[1600,128]{1,0:T(8,128)}, /*index=5*/f32[1600,128]{1,0:T(8,128)}) custom-call(bf16[2,8,112,384]{3,2,1,0:T(8,128)(2,1)} %get-tuple-element.136.qkv, bf16[2,112,896]{2,1,0:T(8,128)(2,1)} %get-tuple-element.137.out_w, ...), custom_call_target="tpu_custom_call" | custom-call | tf_op jit(solution)/shard_map/deliver/pallas_call | solution.py:1199
  (96 shorter events, 18.7 us)
Async XLA Ops:
  7.2 109.0 %copy-start = (s32[1,2048]{1,0:T(1,128)S(1)}, s32[1,2048]{1,0:T(1,128)}, u32[]{:S(2)}) copy-start(s32[1,2048]{1,0:T(1,128)} %param.18) | copy-start | bytes 24580
  7.2 166.5 %all-gather.5.cloned.1.call-start = ((), (), s32[]{:S(2)}) async-start(), calls=%async_computation.2 | async-start | bytes 8028160 | tf_op jit(solution)/shard_map/all_gather | solution.py:1437
  112.7 1.4 copy-start.3
  112.8 120.9 %all-gather.3.cloned.1.call-start = ((), (), s32[]{:S(2)}) async-start(), calls=%async_computation.1 | async-start | bytes 4128768 | tf_op jit(solution)/shard_map/all_gather | solution.py:1416
  112.8 3.2 copy-start.22
  113.5 387.0 %reduce-scatter.2.cloned.1.call-start = ((), (), s32[]{:S(2)}) async-start(), calls=%async_computation.3 | async-start | bytes 4128768 | tf_op jit(solution)/shard_map/reduce_scatter | solution.py:1512
  115.4 38.1 %collective-permute-start = (bf16[448,800]{1,0:T(8,128)(2,1)}, bf16[448,800]{1,0:T(8,128)(2,1)}, u32[]{:S(2)}, u32[]{:S(2)}) collective-permute-start(bf16[448,800]{1,0:T(8,128)(2,1)} %bitcast.17), channel_id=1, source_target_pairs={{0,8},{8,0},{1,9},{9,1},{2,10},{10,2},{3,11},{11,3},{4,12},{12,4},... | collective-permute-start | bytes 2150408 | tf_op jit(solution)/shard_map/ppermute | solution.py:1433
  115.4 38.1 %collective-permute-start.1 = (bf16[2,448,800]{2,1,0:T(8,128)(2,1)S(1)}, bf16[2,448,800]{2,1,0:T(8,128)(2,1)S(1)}, u32[]{:S(2)}, u32[]{:S(2)}) collective-permute-start(bf16[2,448,800]{2,1,0:T(8,128)(2,1)S(1)} %bitcast.112), channel_id=1, source_target_pairs={{0,16},{16,0},{1,17},{17,1},{2,18},{18,2},{3,19},{19,3},{4,20},{20... | collective-permute-start | bytes 4300808 | tf_op jit(solution)/shard_map/ppermute | solution.py:1434
  116.1 13.4 %copy-start.20 = (s32[16]{0:T(128)}, s32[16]{0:T(128)S(1)}, u32[]{:S(2)}) copy-start(s32[16]{0:T(128)S(1)} %select_reduce_fusion.1.inv_ref) | copy-start | bytes 196
  153.5 25.6 %copy-start.8 = (bf16[2,448,800]{2,1,0:T(8,128)(2,1)}, bf16[2,448,800]{2,1,0:T(8,128)(2,1)S(1)}, u32[]{:S(2)}) copy-start(bf16[2,448,800]{2,1,0:T(8,128)(2,1)S(1)} %collective-permute-done.1.refs_1_) | copy-start | bytes 4300804
  167.5 52.3 %collective-permute-start.3 = (bf16[448,800]{1,0:T(8,128)(2,1)}, bf16[448,800]{1,0:T(8,128)(2,1)S(1)}, u32[]{:S(2)}, u32[]{:S(2)}) collective-permute-start(bf16[448,800]{1,0:T(8,128)(2,1)} %bitcast.129), channel_id=1, source_target_pairs={{0,8},{8,0},{1,9},{9,1},{2,10},{10,2},{3,11},{11,3},{4,12},{12,4},... | collective-permute-start | bytes 2150408 | tf_op jit(solution)/shard_map/ppermute | solution.py:1462
  171.7 50.1 %collective-permute-start.2 = (bf16[448,800]{1,0:T(8,128)(2,1)}, bf16[448,800]{1,0:T(8,128)(2,1)S(1)}, u32[]{:S(2)}, u32[]{:S(2)}) collective-permute-start(bf16[448,800]{1,0:T(8,128)(2,1)} %collective-permute-done.refs_2_), channel_id=1, source_target_pairs={{0,16},{16,0},{1,17},{17,1},{2,18},{18,2},{3,19},{19,3},{4,20},{20... | collective-permute-start | bytes 2150408 | tf_op jit(solution)/shard_map/ppermute | solution.py:1459
  219.9 20.5 %copy-start.15 = (bf16[448,800]{1,0:T(8,128)(2,1)}, bf16[448,800]{1,0:T(8,128)(2,1)S(1)}, u32[]{:S(2)}) copy-start(bf16[448,800]{1,0:T(8,128)(2,1)S(1)} %collective-permute-done.3.refs_4_) | copy-start | bytes 2150404
  219.9 22.1 %collective-permute-start.5 = (bf16[448,800]{1,0:T(8,128)(2,1)S(1)}, bf16[448,800]{1,0:T(8,128)(2,1)S(1)}, u32[]{:S(2)}, u32[]{:S(2)}) collective-permute-start(bf16[448,800]{1,0:T(8,128)(2,1)S(1)} %collective-permute-done.3.refs_4_), channel_id=1, source_target_pairs={{0,16},{16,0},{1,17},{17,1},{2,18},{18,2},{3,19},{19,3},{4,20},{20... | collective-permute-start | bytes 2150408 | tf_op jit(solution)/shard_map/ppermute | solution.py:1468
  240.3 2.1 copy-start.9
  241.8 48.3 %collective-permute-start.4 = (bf16[2,448,800]{2,1,0:T(8,128)(2,1)}, bf16[2,448,800]{2,1,0:T(8,128)(2,1)}, u32[]{:S(2)}, u32[]{:S(2)}) collective-permute-start(bf16[2,448,800]{2,1,0:T(8,128)(2,1)} %dynamic-slice_bitcast_fusion.1), channel_id=1, source_target_pairs={{0,16},{16,0},{1,17},{17,1},{2,18},{18,2},{3,19},{19,3},{4,20},{20... | collective-permute-start | bytes 4300808 | tf_op jit(solution)/shard_map/ppermute | solution.py:1491
  243.3 18.1 %copy-start.2 = (bf16[8,128,1792]{2,1,0:T(8,128)(2,1)S(1)}, bf16[8,128,1792]{2,1,0:T(8,128)(2,1)}, u32[]{:S(2)}) copy-start(bf16[8,128,1792]{2,1,0:T(8,128)(2,1)} %group_gather.1) | copy-start | bytes 11010052
  290.1 7.0 %copy-start.17 = (bf16[2,128,896]{2,1,0:T(8,128)(2,1)S(1)}, bf16[2,128,896]{2,1,0:T(8,128)(2,1)}, u32[]{:S(2)}) copy-start(bf16[2,128,896]{2,1,0:T(8,128)(2,1)} %get-tuple-element.116) | copy-start | bytes 1376260
  297.1 3.9 copy-start.11
  301.0 17.2 %copy-start.10 = (bf16[1792,800]{1,0:T(8,128)(2,1)S(1)}, bf16[1792,800]{1,0:T(8,128)(2,1)}, u32[]{:S(2)}) copy-start(bf16[1792,800]{1,0:T(8,128)(2,1)} %copy-done.9) | copy-start | bytes 8601604
  301.0 39.2 %collective-permute-start.7 = (bf16[896,1792]{1,0:T(8,128)(2,1)}, bf16[896,1792]{1,0:T(8,128)(2,1)}, u32[]{:S(2)}, u32[]{:S(2)}) collective-permute-start(bf16[896,1792]{1,0:T(8,128)(2,1)} %convolution_convert_fusion.1), channel_id=1, source_target_pairs={{0,2},{2,0},{1,3},{3,1},{4,6},{6,4},{5,7},{7,5},{8,10},{10,8},{9,1... | collective-permute-start | bytes 9633800 | tf_op jit(solution)/shard_map/ppermute | solution.py:1518
  302.4 37.8 %collective-permute-start.8 = (bf16[2,448,800]{2,1,0:T(8,128)(2,1)}, bf16[2,448,800]{2,1,0:T(8,128)(2,1)}, u32[]{:S(2)}, u32[]{:S(2)}) collective-permute-start(bf16[2,448,800]{2,1,0:T(8,128)(2,1)} %dynamic-slice_bitcast_fusion), channel_id=1, source_target_pairs={{0,16},{16,0},{1,17},{17,1},{2,18},{18,2},{3,19},{19,3},{4,20},{20... | collective-permute-start | bytes 4300808 | tf_op jit(solution)/shard_map/ppermute | solution.py:1495
  318.2 5.2 %copy-start.18 = (bf16[2,128,896]{2,1,0:T(8,128)(2,1)S(1)}, bf16[2,128,896]{2,1,0:T(8,128)(2,1)}, u32[]{:S(2)}) copy-start(bf16[2,128,896]{2,1,0:T(8,128)(2,1)} %get-tuple-element.116) | copy-start | bytes 1376260
  320.0 4.5 copy-start.4
  320.0 3.5 copy-start.14
  320.9 19.3 %copy-start.12 = (bf16[1792,800]{1,0:T(8,128)(2,1)S(1)}, bf16[1792,800]{1,0:T(8,128)(2,1)}, u32[]{:S(2)}) copy-start(bf16[1792,800]{1,0:T(8,128)(2,1)} %convolution_convert_fusion.2) | copy-start | bytes 8601604
  320.9 74.6 %collective-permute-start.6 = (bf16[448,800]{1,0:T(8,128)(2,1)}, bf16[448,800]{1,0:T(8,128)(2,1)S(1)}, u32[]{:S(2)}, u32[]{:S(2)}) collective-permute-start(bf16[448,800]{1,0:T(8,128)(2,1)} %dynamic-slice_bitcast_fusion.3), channel_id=1, source_target_pairs={{0,8},{8,0},{1,9},{9,1},{2,10},{10,2},{3,11},{11,3},{4,12},{12,4},... | collective-permute-start | bytes 2150408 | tf_op jit(solution)/shard_map/ppermute | solution.py:1501
  343.9 51.7 %collective-permute-start.9 = (bf16[448,800]{1,0:T(8,128)(2,1)}, bf16[448,800]{1,0:T(8,128)(2,1)}, u32[]{:S(2)}, u32[]{:S(2)}) collective-permute-start(bf16[448,800]{1,0:T(8,128)(2,1)} %dynamic-slice_bitcast_fusion.2), channel_id=1, source_target_pairs={{0,8},{8,0},{1,9},{9,1},{2,10},{10,2},{3,11},{11,3},{4,12},{12,4},... | collective-permute-start | bytes 2150408 | tf_op jit(solution)/shard_map/ppermute | solution.py:1501
  382.5 4.7 copy-start.21
  387.2 8.4 %copy-start.5 = (bf16[2,448,800]{2,1,0:T(8,128)(2,1)S(1)}, bf16[2,448,800]{2,1,0:T(8,128)(2,1)}, u32[]{:S(2)}) copy-start(bf16[2,448,800]{2,1,0:T(8,128)(2,1)} %copy-done.4) | copy-start | bytes 4300804
  387.2 8.4 %copy-start.7 = (bf16[2,448,800]{2,1,0:T(8,128)(2,1)S(1)}, bf16[2,448,800]{2,1,0:T(8,128)(2,1)}, u32[]{:S(2)}) copy-start(bf16[2,448,800]{2,1,0:T(8,128)(2,1)} %copy-done.6) | copy-start | bytes 4300804
  500.5 7.3 %copy-start.1 = (s32[1,2048]{1,0:T(1,128)S(1)}, s32[1,2048]{1,0:T(1,128)}, u32[]{:S(2)}) copy-start(s32[1,2048]{1,0:T(1,128)} %param.18) | copy-start | bytes 24580
  (4 other events, 3.7 us)
Sparse Core Ops, SparseCore 0:
  112.9 46.1 all-gather.4
  161.3 61.3 all-gather.2
  290.2 83.7 reduce-scatter.1
